TPU v7x, 32 devices: a whole 2x2x4 slice. The times are simulated.
32 devices in a mesh: term: 8 (over z, core), doc: 4 (over y, x).
Axes of the slice: x: 2, y: 2, z: 4, core: 2. Of those that a mesh axis runs over, the one named last changes fastest.
Arguments:
- tiles: float32 [4096, 128, 128], P(('term', 'doc')), may hold values from 0.01 to 1
- tile_coords: int32 [4096, 2], P(('term', 'doc')), may hold values from 0 to 63, as said below
- sketch_matrix: float32 [8192, 256], P('doc'), may hold values from -0.1875 to 0.1875
- anchor_terms: int32 [64], replicated, may hold values from 0 to 8191, as said below
Outputs:
- coefficients: float32 [8192, 64], P(('term', 'doc'))
- residual: float32 [8192, 256], P(('term', 'doc'))
Inputs may be any that keep to these rules, and one draw needn't show every extreme that they name: `tile_coords`: column 0 is a term block below 64, column 1 a document block below 64. The tiles of the k-th device along term+doc (doc fastest) lie in document blocks j * 16 to j * 16 + 15, j being that device's doc index, and that device holds a tile of each of them. The term blocks fall in groups of 2 consecutive ones, the rows of one device along term+doc; the tiles of one device touch at most one term block of each group. Every term block holds a tile. Coordinates may repeat; such tiles add. `anchor_terms`: 64 distinct term rows; the last term row is always among them.
All inputs are finite; a program needn't handle non-finite values.
Results may differ from a plain program's by a relative error of at most 0.0003.
Values sent between devices are 32-bit elements; how exact they have to be, the bound alone decides.
No kernel may reach another device: no remote copies, remote signals or barrier semaphores. Data moves between devices by JAX's collectives and lax.ppermute only.
A program may use at most 256 MiB of HBM per device.

v0:
```python
import math

import jax
import jax.numpy as jnp
from jax import lax
from jax.sharding import PartitionSpec as P

ROWS_DEV = 256


def local_products(tiles, tile_coords, sketch_matrix, slots, slot_of):
    tile = tiles.shape[1]
    width = sketch_matrix.shape[1]
    g_blocks = sketch_matrix.reshape(-1, tile, width)
    doc_base = lax.axis_index("doc") * g_blocks.shape[0]
    group = math.gcd(tiles.shape[0], 32)
    steps = tiles.shape[0] // group
    tile_groups = tiles.reshape(steps, group, tile, tile)
    coord_groups = tile_coords.reshape(steps, group, 2)
    slot_ids = jnp.arange(slots, dtype=jnp.int32)

    def step(total, inputs):
        pieces, coords = inputs
        chosen = jnp.take(g_blocks, coords[:, 1] - doc_base, axis=0)
        prods = jnp.einsum("kab,kbc->kac", pieces, chosen, precision=lax.Precision.HIGHEST)
        onehot = (slot_of(coords[:, 0])[None, :] == slot_ids[:, None]).astype(jnp.float32)
        added = jnp.einsum("bk,kac->bac", onehot, prods, precision=lax.Precision.HIGHEST)
        return (total + added, None)

    start = jnp.zeros((slots, tile, width), jnp.float32)
    summed, unused = lax.scan(step, start, (tile_groups, coord_groups))
    return summed


def body(tiles, tile_coords, sketch_matrix, anchor_terms):
    n_term = lax.axis_size("term")
    n_doc = lax.axis_size("doc")
    devices = n_term * n_doc
    tile = tiles.shape[1]
    width = sketch_matrix.shape[1]
    owned_rows = ROWS_DEV
    all_rows = owned_rows * devices
    partial_value = local_products(
        tiles, tile_coords, sketch_matrix, all_rows // tile, lambda ids: ids
    ).reshape(all_rows, width)
    owned = lax.psum_scatter(partial_value, ("term", "doc"), scatter_dimension=0, tiled=True)
    row_start = lax.axis_index(("term", "doc")) * owned_rows
    positions = jnp.arange(owned_rows, dtype=jnp.int32)
    picker = (anchor_terms[:, None] - row_start == positions[None, :]).astype(jnp.float32)
    own_part = jnp.dot(picker, owned, precision=lax.Precision.HIGHEST)
    anchor_rows = lax.psum(own_part, ("term", "doc"))
    anchor_count = anchor_rows.shape[0]
    gram = jnp.dot(anchor_rows, anchor_rows.T, precision=lax.Precision.HIGHEST)
    ridge = 0.001 * jnp.trace(gram) / anchor_count
    gram = gram + ridge * jnp.eye(anchor_count, dtype=jnp.float32)
    factor = jnp.linalg.cholesky(gram)
    project = jnp.dot(owned, anchor_rows.T, precision=lax.Precision.HIGHEST)
    coefficients = jax.scipy.linalg.cho_solve((factor, True), project.T).T
    residual = owned - jnp.dot(coefficients, anchor_rows, precision=lax.Precision.HIGHEST)
    return (coefficients, residual)


def solution(mesh):
    in_specs = (P(("term", "doc"), None, None), P(("term", "doc"), None), P("doc", None), P())
    out_specs = (P(("term", "doc"), None), P(("term", "doc"), None))
    return jax.shard_map(body, mesh=mesh, in_specs=in_specs, out_specs=out_specs, check_vma=False)
```

profile of v0, /device:TPU:0, one launch (start us, length us, event | category | flops | bytes accessed | tf_op | source)
XLA Modules:
  0.0 446.6 jit_solution(10826765747947884470)
XLA Ops:
  7.2 0.8 reshape.37
  8.0 90.6 %while.11 = (s32[]{:T(128)}, f32[64,128,256]{2,0,1:T(8,128)}, s32[4,32,2]{1,0,2:T(4,128)S(1)}, f32[4,32,128,128]{3,2,1,0:T(8,128)}, s32[]{:T(128)}, /*index=5*/f32[16,128,256]{2,1,0:T(8,128)}, s32[]{:T(128)}, s32[]{:T(128)}) while((s32[]{:T(128)}, f32[64,128,256]{2,0,1:T(8,128)}, s32[4,32,2]{1,0,2:T(4,128)S(1)}, ...), condition=%wide.region_1.2_spmd.clone, body=%wide.region_0.1_spmd.clone.sunk | while | flops 2421165312 | bytes 106960480 | solution.py:31
  8.0 4.3 gather_fusion
  12.4 7.4 %fusion.45 = f32[32,128,256]{2,1,0:T(8,128)S(1)} fusion(f32[32,128,256]{2,1,0:T(8,128)} %gather_fusion, f32[4,32,128,128]{3,2,1,0:T(8,128)} %get-tuple-element.145, s32[]{:T(128)S(6)} %copy.21, pred[32]{0:T(512)(128)(4,1)S(1)} %get-tuple-element.125), kind=kOutput, calls=%fused_computation.5.clone.1 | convolution fusion | flops 1611661312 | bytes 10485796 | tf_op jit(solution)/shard_map/while/body/eval_jaxpr/kab,kbc->kac/dot_general | solution.py:25
  19.8 7.6 %select_add_fusion.2 = f32[64,128,256]{2,0,1:T(8,128)S(1)} fusion(f32[64,128,256]{2,0,1:T(8,128)S(1)} %copy-done, pred[]{:T(512)S(6)} %compare.17, f32[32,128,256]{2,1,0:T(8,128)S(1)} %fusion.45, s32[32]{0:T(128)S(1)} %slice_bitcast_fusion.2), kind=kOutput, calls=%fused_computation.2.clone.1 | convolution fusion | flops 809502720 | bytes 20971648 | tf_op jit(solution)/shard_map/while/body/eval_jaxpr/bk,kac->bac/dot_general | solution.py:27
  27.4 3.2 copy-done.1
  30.7 4.3 gather_fusion
  35.0 7.4 %fusion.45 = f32[32,128,256]{2,1,0:T(8,128)S(1)} fusion(f32[32,128,256]{2,1,0:T(8,128)} %gather_fusion, f32[4,32,128,128]{3,2,1,0:T(8,128)} %get-tuple-element.145, s32[]{:T(128)S(6)} %copy.21, pred[32]{0:T(512)(128)(4,1)S(1)} %get-tuple-element.125), kind=kOutput, calls=%fused_computation.5.clone.1 | convolution fusion | flops 1611661312 | bytes 10485796 | tf_op jit(solution)/shard_map/while/body/eval_jaxpr/kab,kbc->kac/dot_general | solution.py:25
  42.4 7.6 %select_add_fusion.2 = f32[64,128,256]{2,0,1:T(8,128)S(1)} fusion(f32[64,128,256]{2,0,1:T(8,128)S(1)} %copy-done, pred[]{:T(512)S(6)} %compare.17, f32[32,128,256]{2,1,0:T(8,128)S(1)} %fusion.45, s32[32]{0:T(128)S(1)} %slice_bitcast_fusion.2), kind=kOutput, calls=%fused_computation.2.clone.1 | convolution fusion | flops 809502720 | bytes 20971648 | tf_op jit(solution)/shard_map/while/body/eval_jaxpr/bk,kac->bac/dot_general | solution.py:27
  50.1 3.2 copy-done.1
  53.3 4.3 gather_fusion
  57.7 7.4 %fusion.45 = f32[32,128,256]{2,1,0:T(8,128)S(1)} fusion(f32[32,128,256]{2,1,0:T(8,128)} %gather_fusion, f32[4,32,128,128]{3,2,1,0:T(8,128)} %get-tuple-element.145, s32[]{:T(128)S(6)} %copy.21, pred[32]{0:T(512)(128)(4,1)S(1)} %get-tuple-element.125), kind=kOutput, calls=%fused_computation.5.clone.1 | convolution fusion | flops 1611661312 | bytes 10485796 | tf_op jit(solution)/shard_map/while/body/eval_jaxpr/kab,kbc->kac/dot_general | solution.py:25
  65.1 7.6 %select_add_fusion.2 = f32[64,128,256]{2,0,1:T(8,128)S(1)} fusion(f32[64,128,256]{2,0,1:T(8,128)S(1)} %copy-done, pred[]{:T(512)S(6)} %compare.17, f32[32,128,256]{2,1,0:T(8,128)S(1)} %fusion.45, s32[32]{0:T(128)S(1)} %slice_bitcast_fusion.2), kind=kOutput, calls=%fused_computation.2.clone.1 | convolution fusion | flops 809502720 | bytes 20971648 | tf_op jit(solution)/shard_map/while/body/eval_jaxpr/bk,kac->bac/dot_general | solution.py:27
  72.8 3.2 copy-done.1
  76.0 4.3 gather_fusion
  80.3 7.4 %fusion.45 = f32[32,128,256]{2,1,0:T(8,128)S(1)} fusion(f32[32,128,256]{2,1,0:T(8,128)} %gather_fusion, f32[4,32,128,128]{3,2,1,0:T(8,128)} %get-tuple-element.145, s32[]{:T(128)S(6)} %copy.21, pred[32]{0:T(512)(128)(4,1)S(1)} %get-tuple-element.125), kind=kOutput, calls=%fused_computation.5.clone.1 | convolution fusion | flops 1611661312 | bytes 10485796 | tf_op jit(solution)/shard_map/while/body/eval_jaxpr/kab,kbc->kac/dot_general | solution.py:25
  87.8 7.6 %select_add_fusion.2 = f32[64,128,256]{2,0,1:T(8,128)S(1)} fusion(f32[64,128,256]{2,0,1:T(8,128)S(1)} %copy-done, pred[]{:T(512)S(6)} %compare.17, f32[32,128,256]{2,1,0:T(8,128)S(1)} %fusion.45, s32[32]{0:T(128)S(1)} %slice_bitcast_fusion.2), kind=kOutput, calls=%fused_computation.2.clone.1 | convolution fusion | flops 809502720 | bytes 20971648 | tf_op jit(solution)/shard_map/while/body/eval_jaxpr/bk,kac->bac/dot_general | solution.py:27
  95.4 3.2 copy-done.1
  98.6 11.5 %copy.9 = f32[64,128,256]{2,1,0:T(8,128)} copy(f32[64,128,256]{2,0,1:T(8,128)} %get-tuple-element.39) | data formatting | bytes 16777216 | tf_op jit(solution)/shard_map/while | solution.py:31
  110.2 0.6 copy-done.3
  110.7 185.7 %reduce-scatter.2.cloned.1.call-done = f32[256,256]{1,0:T(8,128)} async-done(((f32[8192,256]{1,0:T(8,128)}), f32[256,256]{1,0:T(8,128)}) %reduce-scatter.2.cloned.1.call-update) | async-done | bytes 262160 | tf_op jit(solution)/shard_map/reduce_scatter | solution.py:46
  296.4 1.8 fusion.17
  298.3 122.9 %all-reduce.2.cloned.1.call-done = f32[64,256]{1,0:T(8,128)} async-done(((f32[64,256]{1,0:T(8,128)}), f32[64,256]{1,0:T(8,128)}) %all-reduce.2.cloned.1.call-update) | async-done | bytes 65552 | tf_op jit(solution)/shard_map/psum | solution.py:51
  421.2 1.7 select_reduce_fusion.1
  423.6 5.8 %cholesky.17 = f32[64,64]{1,0:T(8,128)S(1)} custom-call(f32[64,64]{1,0:T(8,128)S(1)} %fusion.24), custom_call_target="Cholesky" | custom-call | tf_op jit(solution)/shard_map/jit(cholesky)/cholesky | solution.py:56
  429.5 0.6 compare_reduce_fusion
  430.2 0.7 fusion.18
  430.8 4.9 %custom-call.10 = f32[1,64,64]{1,2,0:T(8,128)S(1)} custom-call(f32[1,64,64]{2,1,0:T(8,128)S(1)} %fusion.18), custom_call_target="InvertDiagBlocksLowerTriangular" | custom-call | tf_op jit(solution)/shard_map/jit(_cho_solve)/triangular_solve | solution.py:58
  435.7 1.4 fusion.26
  437.1 0.3 fusion.21
  437.4 0.2 fusion.19
  437.6 2.1 convolution_subtract_fusion
  (40 shorter events, 0.4 us)
Async XLA Ops:
  7.2 289.3 %reduce-scatter.2.cloned.1.call-start = ((), (), s32[]{:S(2)}) async-start(), calls=%async_computation.1 | async-start | bytes 8650752 | tf_op jit(solution)/shard_map/reduce_scatter | solution.py:46
  12.4 7.4 %copy-start = (f32[64,128,256]{2,0,1:T(8,128)S(1)}, f32[64,128,256]{2,0,1:T(8,128)}, u32[]{:S(2)}) copy-start(f32[64,128,256]{2,0,1:T(8,128)} %get-tuple-element.135) | copy-start | bytes 25165828 | tf_op jit(solution)/shard_map/while
  27.4 3.2 copy-start.1
  35.0 7.4 %copy-start = (f32[64,128,256]{2,0,1:T(8,128)S(1)}, f32[64,128,256]{2,0,1:T(8,128)}, u32[]{:S(2)}) copy-start(f32[64,128,256]{2,0,1:T(8,128)} %get-tuple-element.135) | copy-start | bytes 25165828 | tf_op jit(solution)/shard_map/while
  50.1 3.2 copy-start.1
  57.7 7.4 %copy-start = (f32[64,128,256]{2,0,1:T(8,128)S(1)}, f32[64,128,256]{2,0,1:T(8,128)}, u32[]{:S(2)}) copy-start(f32[64,128,256]{2,0,1:T(8,128)} %get-tuple-element.135) | copy-start | bytes 25165828 | tf_op jit(solution)/shard_map/while
  72.8 3.2 copy-start.1
  80.3 7.4 %copy-start = (f32[64,128,256]{2,0,1:T(8,128)S(1)}, f32[64,128,256]{2,0,1:T(8,128)}, u32[]{:S(2)}) copy-start(f32[64,128,256]{2,0,1:T(8,128)} %get-tuple-element.135) | copy-start | bytes 25165828 | tf_op jit(solution)/shard_map/while
  95.4 3.2 copy-start.1
  110.1 0.7 copy-start.3
  110.1 311.1 %all-reduce.2.cloned.1.call-start = ((), (), s32[]{:S(2)}) async-start(), calls=%async_computation.2 | async-start | bytes 131072 | tf_op jit(solution)/shard_map/psum | solution.py:51
  437.6 2.1 copy-start.2
Sparse Core Ops, SparseCore 0:
  110.2 186.1 reduce-scatter.1
  302.6 118.5 all-reduce.1
where the time goes:
time: 448 us; the launch traced here: 447 us
  waiting for transfers between devices  309 us (69%)
  matrix products  67.7 us (15%)
  local copies, waits for them, and re-layouts  43.1 us (10%)
  between operations  14.8 us (3%)
  other arithmetic  12.1 us (3%)
    reduce_scatter x1, waiting for transfers between devices, body(): lax.psum_scatter(partial_value, ('term', 'doc'), scatter_dimension=0, til...  186 us
    psum x1, waiting for transfers between devices, body(): anchor_rows = lax.psum(own_part, ('term', 'doc'))  123 us
    dot_general x4, matrix products, step(): jnp.einsum('bk,kac->bac', onehot, prods, precision=lax.Precision.HIGHEST)  30.6 us
    dot_general x4, matrix products, step(): jnp.einsum('kab,kbc->kac', pieces, chosen, precision=lax.Precision.HIGHEST)  29.7 us
    gather x4, local copies, waits for them, and re-layouts, step(): chosen = jnp.take(g_blocks, coords[:, 1] - doc_base, axis=0)  17.3 us
    while x16, local copies, waits for them, and re-layouts  12.8 us
    while x1, local copies, waits for them, and re-layouts, local_products(): summed, unused = lax.scan(step, start, (tile_groups, coord_groups))  11.5 us
  transfers between devices with their start and end apart: 2, of which 2 were waited for; matrix products, arithmetic and copies ran while one was open for 0% of the time, Pallas kernels for 0%

commit v1 on v0

v1 whole, which is shorter than its diff:
```python
import functools

import jax
import jax.numpy as jnp
from jax import lax
from jax.experimental import pallas as pl
from jax.experimental.pallas import tpu as pltpu
from jax.sharding import PartitionSpec as P

ROWS_DEV = 256
NBUF = 8
F32 = jnp.float32
BF16 = jnp.bfloat16
AXES = ("term", "doc")


def split(v):
    hi = v.astype(BF16)
    lo = (v - hi.astype(F32)).astype(BF16)
    return hi, lo


def round8(n):
    return (n + 7) // 8 * 8


def chunk_kernel(geo, coords, anchors, me_ref, g_ref, tiles, *rest):
    (z_lo, nz, n_y, n_tiles, tile, half) = geo
    n_y_out = n_y - 1
    keep_x, send_x, keep_y = rest[:3]
    send_y = rest[3 : 3 + n_y_out]
    anchor_out = rest[3 + n_y_out]
    buf, order, acc_x, acc_y, flag_x, flag_y, in_sem, out_sem = rest[4 + n_y_out :]
    n_doc = 2 * n_y
    per = ROWS_DEV // tile
    sx = 2 * n_y * nz
    sy = 4 * nz
    fx = round8(sx)
    fy = round8(sy)
    me = me_ref[0]
    doc_base = me_ref[1]

    def place(block):
        rel = lax.bitwise_xor(block // per, me)
        dx = rel & 1
        dy = (rel >> 1) & (n_y - 1)
        dc = (rel // n_doc) & 1
        zi = (rel // (2 * n_doc)) - z_lo
        inside = jnp.logical_and(zi >= 0, zi < nz)
        in_x = (dc * n_y + dy) * nz + zi
        in_y = (dc * 2 + dx) * nz + zi
        return inside, dx, in_x, dy, in_y

    def fetch(index, slot):
        return pltpu.make_async_copy(tiles.at[index], buf.at[slot], in_sem.at[slot])

    def scan(k, count):
        inside = place(coords[k, 0])[0]

        @pl.when(inside)
        def _():
            order[count] = k

            @pl.when(count < NBUF)
            def _():
                fetch(k, count).start()

        return count + inside.astype(jnp.int32)

    count = lax.fori_loop(0, n_tiles, scan, jnp.int32(0))
    acc_x[...] = jnp.zeros_like(acc_x)
    acc_y[...] = jnp.zeros_like(acc_y)
    flag_x[...] = jnp.zeros_like(flag_x)
    flag_y[...] = jnp.zeros_like(flag_y)
    width = g_ref.shape[1]

    def step(i, carry):
        k = order[i]
        slot = lax.rem(i, NBUF)
        block = coords[k, 0]
        doc = coords[k, 1] - doc_base
        _, dx, in_x, dy, in_y = place(block)
        fetch(k, slot).wait()
        hi, lo = split(buf[slot])
        g_hi, g_lo = split(g_ref[pl.ds(pl.multiple_of(doc * tile, tile), tile), :])
        lhs = jnp.concatenate([hi, lo], axis=1)
        top = jnp.dot(lhs, jnp.concatenate([g_hi, g_hi], axis=0), preferred_element_type=F32)
        low = jnp.dot(lhs, jnp.concatenate([g_lo, g_lo], axis=0), preferred_element_type=F32)
        prod = top + low
        px = dx * sx + in_x
        py = dy * sy + in_y
        acc_x[px] += prod[:half]
        acc_y[py] += prod[half:]
        bit = jnp.full((1, width), lax.rem(block, per).astype(F32), F32)
        flag_x[pl.ds(dx * fx + in_x, 1), :] = bit
        flag_y[pl.ds(dy * fy + in_y, 1), :] = bit

        @pl.when(i + NBUF < count)
        def _():
            fetch(order[i + NBUF], slot).start()

        return carry

    lax.fori_loop(0, count, step, 0)
    copies = []

    def out(src, dst):
        copies.append(pltpu.make_async_copy(src, dst, out_sem.at[len(copies)]))
        copies[-1].start()

    for d, ref in enumerate((keep_x, send_x)):
        out(acc_x.at[pl.ds(d * sx, sx)], ref.at[pl.ds(0, sx)])
        out(flag_x.at[pl.ds(d * fx, fx)], ref.at[sx, pl.ds(0, fx)])
    for d, ref in enumerate((keep_y,) + tuple(send_y)):
        out(acc_y.at[pl.ds(d * sy, sy)], ref.at[pl.ds(0, sy)])
        out(flag_y.at[pl.ds(d * fy, fy)], ref.at[sy, pl.ds(0, fy)])

    def pick(i, carry):
        row = anchors[i]
        block = row // tile
        inside, dx, in_x, dy, in_y = place(block)
        line = lax.rem(row, tile)
        bit = lax.rem(block, per).astype(F32)

        @pl.when(jnp.logical_and(inside, line < half))
        def _():
            value = acc_x[dx * sx + in_x, pl.ds(line, 1), :]
            mine = flag_x[pl.ds(dx * fx + in_x, 1), :] == bit
            anchor_out[pl.ds(i, 1), :] = jnp.where(mine, value, 0.0)

        @pl.when(jnp.logical_and(inside, line >= half))
        def _():
            value = acc_y[dy * sy + in_y, pl.ds(line - half, 1), :]
            mine = flag_y[pl.ds(dy * fy + in_y, 1), :] == bit
            anchor_out[pl.ds(i, 1), :] = jnp.where(mine, value, 0.0)

        return carry

    anchor_out[...] = jnp.zeros_like(anchor_out)
    lax.fori_loop(0, anchors.shape[0], pick, 0)
    for copy in copies:
        copy.wait()


def chunk_products(z_lo, nz, n_y, coords, anchors, me, g, tiles):
    n_tiles, tile = tiles.shape[0], tiles.shape[1]
    width = g.shape[1]
    half = tile // 2
    sx, sy = 2 * n_y * nz, 4 * nz
    fx, fy = round8(sx), round8(sy)
    shape_x = jax.ShapeDtypeStruct((sx + 1, half, width), F32)
    shape_y = jax.ShapeDtypeStruct((sy + 1, half, width), F32)
    outs = [shape_x, shape_x] + [shape_y] * n_y + [jax.ShapeDtypeStruct((anchors.shape[0], width), F32)]
    anyspace = pl.BlockSpec(memory_space=pl.ANY)
    smem = pl.BlockSpec(memory_space=pltpu.SMEM)
    vmem = pl.BlockSpec(memory_space=pltpu.VMEM)
    return pl.pallas_call(
        functools.partial(chunk_kernel, (z_lo, nz, n_y, n_tiles, tile, half)),
        out_shape=outs,
        in_specs=[smem, smem, smem, vmem, anyspace],
        out_specs=[anyspace] * (2 + n_y) + [vmem],
        scratch_shapes=[
            pltpu.VMEM((NBUF, tile, tile), F32),
            pltpu.SMEM((n_tiles,), jnp.int32),
            pltpu.VMEM((2 * sx, half, width), F32),
            pltpu.VMEM((n_y * sy, half, width), F32),
            pltpu.VMEM((2 * fx, width), F32),
            pltpu.VMEM((n_y * fy, width), F32),
            pltpu.SemaphoreType.DMA((NBUF,)),
            pltpu.SemaphoreType.DMA((2 * (2 + n_y),)),
        ],
        compiler_params=pltpu.CompilerParams(vmem_limit_bytes=48 * 2**20),
        cost_estimate=pl.CostEstimate(flops=n_tiles * 2 * tile * tile * width, bytes_accessed=8 * 2**20, transcendentals=0),
    )(coords, anchors, me, g, tiles)


def spread_kernel(sx, sy, n_in, *refs):
    xs = refs[:2]
    ys = refs[2:n_in]
    keep, send = refs[n_in:]
    for parts, slots, base in ((xs, sx, 0), (ys, sy, sx // 2)):
        for j in range(slots):
            one = None
            zero = None
            for ref in parts:
                value = ref[j]
                flag = ref[slots, pl.ds(j, 1), :]
                up = value * flag
                down = value - up
                one = up if one is None else one + up
                zero = down if zero is None else zero + down
            core, rest = divmod(j, slots // 2)
            dst = send if core else keep
            dst[2 * (base + rest)] = zero
            dst[2 * (base + rest) + 1] = one


def spread(sx, sy, keep_x, recv_x, keep_y, recv_y):
    half, width = keep_x.shape[1:]
    shape = jax.ShapeDtypeStruct((sx + sy, half, width), F32)
    args = (keep_x, recv_x, keep_y) + tuple(recv_y)
    vmem = pl.BlockSpec(memory_space=pltpu.VMEM)
    return pl.pallas_call(
        functools.partial(spread_kernel, sx, sy, len(args)),
        out_shape=[shape, shape],
        in_specs=[vmem] * len(args),
        out_specs=[vmem, vmem],
        compiler_params=pltpu.CompilerParams(vmem_limit_bytes=48 * 2**20),
    )(*args)


def hdot(a, b, dims):
    return lax.dot_general(a, b, (dims, ((), ())), precision=lax.Precision.HIGHEST, preferred_element_type=F32)


def finish_kernel(n_whole, half, *refs):
    parts = refs[:n_whole]
    rows_ref, inv_ref, coef_ref, res_ref = refs[n_whole:]
    total = parts[0][...]
    for ref in parts[1:]:
        total = total + ref[...]
    owned = jnp.concatenate([total[0, 0], total[1, 0], total[0, 1], total[1, 1]], axis=0)
    rows = rows_ref[...]
    project = hdot(owned, rows, ((1,), (1,)))
    coef = hdot(project, inv_ref[...], ((1,), (0,)))
    coef_ref[...] = coef
    res_ref[...] = owned - hdot(coef, rows, ((1,), (0,)))


def finish(parts, rows, inv):
    half, width = parts[0].shape[2:]
    vmem = pl.BlockSpec(memory_space=pltpu.VMEM)
    return pl.pallas_call(
        functools.partial(finish_kernel, len(parts), half),
        out_shape=[jax.ShapeDtypeStruct((4 * half, rows.shape[0]), F32), jax.ShapeDtypeStruct((4 * half, width), F32)],
        in_specs=[vmem] * (len(parts) + 2),
        out_specs=[vmem, vmem],
        compiler_params=pltpu.CompilerParams(vmem_limit_bytes=32 * 2**20),
    )(*parts, rows, inv)


def make_chunks(n_z):
    step = max(1, n_z // 2)
    return [(lo, step) for lo in range(n_z - step, -1, -step)]


def body(n_term, n_doc, tiles, coords, sketch, anchors):
    devices = n_term * n_doc
    n_y, n_z = n_doc // 2, n_term // 2
    me = lax.axis_index(AXES).astype(jnp.int32)
    doc_base = lax.axis_index("doc").astype(jnp.int32) * (sketch.shape[0] // tiles.shape[1])
    me_arr = jnp.stack([me, doc_base])

    def swap(v, mask):
        return lax.ppermute(v, AXES, [(i, i ^ mask) for i in range(devices)])

    half, width = tiles.shape[1] // 2, sketch.shape[1]
    whole = [None] * n_z
    anchor_parts = []
    for z_lo, nz in make_chunks(n_z):
        sx, sy = 2 * n_y * nz, 4 * nz
        keep_x, send_x, keep_y, *rest = chunk_products(z_lo, nz, n_y, coords, anchors, me_arr, sketch, tiles)
        send_y, part = rest[:-1], rest[-1]
        anchor_parts.append(part)
        recv_x = swap(send_x, 1)
        recv_y = [swap(v, 2 * (k + 1)) for k, v in enumerate(send_y)]
        keep, send = spread(sx, sy, keep_x, recv_x, keep_y, recv_y)
        got = swap(send, n_doc)
        n = 2 * nz
        pieces = [keep[i * n : (i + 1) * n] + got[i * n : (i + 1) * n] for i in range(n_y + 2)]
        xs, ys = pieces[:n_y], pieces[n_y:]
        total_x = xs[0]
        for k in range(1, n_y):
            total_x = total_x + swap(xs[k], 2 * k)
        total_y = ys[0] + swap(ys[1], 1)
        both = jnp.stack([total_x.reshape(nz, 2, half, width), total_y.reshape(nz, 2, half, width)], axis=1)
        for zi in range(nz):
            dz = z_lo + zi
            whole[dz] = swap(both[zi], dz * 2 * n_doc) if dz else both[zi]
    rows = sum(anchor_parts[1:], anchor_parts[0])
    mask = n_doc
    while mask < devices:
        rows = rows + swap(rows, mask)
        mask *= 2
    mask = 1
    while mask < n_doc:
        rows = rows + swap(rows, mask)
        mask *= 2
    count = rows.shape[0]
    gram = jnp.dot(rows, rows.T, precision=lax.Precision.HIGHEST)
    ridge = 0.001 * jnp.trace(gram) / count
    eye = jnp.eye(count, dtype=F32)
    factor = jnp.linalg.cholesky(gram + ridge * eye)
    inv = jax.scipy.linalg.cho_solve((factor, True), eye)
    coef, res = finish(whole, rows, inv)
    return (coef, res)


def solution(mesh):
    in_specs = (P(("term", "doc"), None, None), P(("term", "doc"), None), P("doc", None), P())
    out_specs = (P(("term", "doc"), None), P(("term", "doc"), None))
    run = functools.partial(body, mesh.shape["term"], mesh.shape["doc"])
    return jax.shard_map(run, mesh=mesh, in_specs=in_specs, out_specs=out_specs, check_vma=False)
```

time: 448 us -> 129 us (0.29)
  waiting for transfers between devices: 309 us -> 31.4 us
  matrix products: 67.7 us -> 1.17 us
  Pallas kernels: 0 us -> 47.5 us
  local copies, waits for them, and re-layouts: 43.1 us -> 3.82 us
  starting transfers between devices: 0.08 us -> 23.5 us
  between operations: 14.8 us -> 1.46 us
  other arithmetic: 12.1 us -> 18.5 us
    reduce_scatter x1 -> x0, waiting for transfers between devices: 186 us -> none  [body(): lax.psum_scatter(partial_value, ('term', 'doc'), scatter_dimension=0, til...]
    psum x1 -> x0, waiting for transfers between devices: 123 us -> none  [body(): anchor_rows = lax.psum(own_part, ('term', 'doc'))]
    dot_general x12 -> x1, matrix products: 67.3 us -> 0.8 us  [body(): gram = jnp.dot(rows, rows.T, precision=lax.Precision.HIGHEST)]
    pallas_call x0 -> x5, Pallas kernels: none -> 47.5 us  [the longest x2 44.3 us: chunk_products(): pl.pallas_call(functools.partial(chunk_kernel, (z_lo, nz, n_y, n_tiles, t...]
    ppermute x0 -> x18, waiting for transfers between devices: none -> 31.4 us  [swap(): return lax.ppermute(v, AXES, [(i, i ^ mask) for i in range(devices)])]
    while x17 -> x0, local copies, waits for them, and re-layouts: 24.3 us -> none
    ppermute x0 -> x18, starting transfers between devices: none -> 23.5 us  [swap(): return lax.ppermute(v, AXES, [(i, i ^ mask) for i in range(devices)])]
    gather x4 -> x0, local copies, waits for them, and re-layouts: 17.3 us -> none  [step(): chosen = jnp.take(g_blocks, coords[:, 1] - doc_base, axis=0)]
  transfers between devices with their start and end apart: 2 -> 18, of which waited for: 2 -> 10; matrix products, arithmetic and copies ran while one was open for 0% -> 15% of each run, Pallas kernels for 0% -> 23%
where the time goes in v1:
time: 129 us; the launch traced here: 127 us
  Pallas kernels  47.5 us (37%)
  waiting for transfers between devices  31.4 us (24%)
  starting transfers between devices  23.5 us (18%)
  other arithmetic  18.5 us (14%)
  local copies, waits for them, and re-layouts  3.82 us (3%)
  between operations  1.46 us (1%)
    pallas_call x2, Pallas kernels, chunk_products(): pl.pallas_call(functools.partial(chunk_kernel, (z_lo, nz, n_y, n_tiles, t...  44.3 us
    ppermute x18, waiting for transfers between devices, swap(): return lax.ppermute(v, AXES, [(i, i ^ mask) for i in range(devices)])  31.4 us
    ppermute x18, starting transfers between devices, swap(): return lax.ppermute(v, AXES, [(i, i ^ mask) for i in range(devices)])  23.5 us
    another operation x3, other arithmetic, body(): factor = jnp.linalg.cholesky(gram + ridge * eye)  6.51 us
    another operation x2, other arithmetic, body(): inv = jax.scipy.linalg.cho_solve((factor, True), eye)  5.55 us
    unnamed x5, local copies, waits for them, and re-layouts  3.03 us
  transfers between devices with their start and end apart: 18, of which 10 were waited for; matrix products, arithmetic and copies ran while one was open for 15% of the time, Pallas kernels for 23%

profile of v1, /device:TPU:0, one launch (start us, length us, event | category | flops | bytes accessed | tf_op | source)
XLA Modules:
  0.0 127.4 jit_solution(12906895242351779121)
XLA Ops:
  0.6 0.8 copy.6.coords
  1.5 1.6 %copy-done = f32[2048,256]{1,0:T(8,128)S(1)} copy-done((f32[2048,256]{1,0:T(8,128)S(1)}, f32[2048,256]{1,0:T(8,128)}, u32[]{:S(2)}) %copy-start) | copy-done | bytes 2097176
  3.7 16.5 %shard_map.61 = (f32[9,64,256]{2,1,0:T(8,128)S(1)}, f32[9,64,256]{2,1,0:T(8,128)S(1)}, f32[9,64,256]{2,1,0:T(8,128)S(1)}, f32[9,64,256]{2,1,0:T(8,128)S(1)}, f32[64,256]{1,0:T(8,128)S(1)}) custom-call(s32[128,2]{1,0:T(8,128)S(1)} %copy.6.coords, s32[64]{0:T(128)S(1)} %copy-done.1, s32[2]{0:T(128)S(1)} %pad_add_fusion.me_ref, f32[2048,256]{1,0:T(8,128)S(1)} %copy-done, ...), custom_call_target="tpu_custom_call" | custom-call | flops 1073741824 | bytes 8388608 | tf_op jit(solution)/shard_map/pallas_call | solution.py:157
  20.2 1.0 collective-permute-start.6
  21.3 3.9 %collective-permute-start.7 = (f32[9,64,256]{2,1,0:T(8,128)S(1)}, f32[9,64,256]{2,1,0:T(8,128)S(1)}, u32[]{:S(2)}, u32[]{:S(2)}) collective-permute-start(f32[9,64,256]{2,1,0:T(8,128)S(1)} %get-tuple-element.25), channel_id=1, source_target_pairs={{0,2},{1,3},{2,0},{3,1},{4,6},{5,7},{6,4},{7,5},{8,10},{9,11},{10,... | collective-permute-start | bytes 1769480 | tf_op jit(solution)/shard_map/ppermute | solution.py:255
  25.2 27.8 %shard_map.59 = (f32[9,64,256]{2,1,0:T(8,128)S(1)}, f32[9,64,256]{2,1,0:T(8,128)S(1)}, f32[9,64,256]{2,1,0:T(8,128)S(1)}, f32[9,64,256]{2,1,0:T(8,128)S(1)}, f32[64,256]{1,0:T(8,128)S(1)}) custom-call(s32[128,2]{1,0:T(8,128)S(1)} %copy.6.coords, s32[64]{0:T(128)S(1)} %copy-done.1, s32[2]{0:T(128)S(1)} %pad_add_fusion.me_ref, f32[2048,256]{1,0:T(8,128)S(1)} %copy-done, ...), custom_call_target="tpu_custom_call" | custom-call | flops 1073741824 | bytes 8388608 | tf_op jit(solution)/shard_map/pallas_call | solution.py:157
  53.0 2.1 %collective-permute-start = (f32[9,64,256]{2,1,0:T(8,128)S(1)}, f32[9,64,256]{2,1,0:T(8,128)S(1)}, u32[]{:S(2)}, u32[]{:S(2)}) collective-permute-start(f32[9,64,256]{2,1,0:T(8,128)S(1)} %get-tuple-element.17), channel_id=1, source_target_pairs={{0,1},{1,0},{2,3},{3,2},{4,5},{5,4},{6,7},{7,6},{8,9},{9,8},{10,11... | collective-permute-start | bytes 1769480 | tf_op jit(solution)/shard_map/ppermute | solution.py:255
  56.2 1.8 %collective-permute-done.13 = f32[64,256]{1,0:T(8,128)S(1)} collective-permute-done((f32[64,256]{1,0:T(8,128)S(1)}, f32[64,256]{1,0:T(8,128)S(1)}, u32[]{:S(2)}, u32[]{:S(2)}) %collective-permute-start.13) | collective-permute-done | bytes 65568 | tf_op jit(solution)/shard_map/ppermute | solution.py:255
  58.0 2.6 %collective-permute-start.14 = (f32[64,256]{1,0:T(8,128)S(1)}, f32[64,256]{1,0:T(8,128)S(1)}, u32[]{:S(2)}, u32[]{:S(2)}) collective-permute-start(f32[64,256]{1,0:T(8,128)S(1)} %add.92), channel_id=1, source_target_pairs={{0,8},{1,9},{2,10},{3,11},{4,12},{5,13},{6,14},{7,15},{8,0},{9,1},... | collective-permute-start | bytes 196616 | tf_op jit(solution)/shard_map/ppermute | solution.py:255
  60.6 2.6 %collective-permute-done.14 = f32[64,256]{1,0:T(8,128)S(1)} collective-permute-done((f32[64,256]{1,0:T(8,128)S(1)}, f32[64,256]{1,0:T(8,128)S(1)}, u32[]{:S(2)}, u32[]{:S(2)}) %collective-permute-start.14) | collective-permute-done | bytes 65568 | tf_op jit(solution)/shard_map/ppermute | solution.py:255
  63.3 1.9 %collective-permute-start.15 = (f32[64,256]{1,0:T(8,128)S(1)}, f32[64,256]{1,0:T(8,128)S(1)}, u32[]{:S(2)}, u32[]{:S(2)}) collective-permute-start(f32[64,256]{1,0:T(8,128)S(1)} %add.93), channel_id=1, source_target_pairs={{0,16},{1,17},{2,18},{3,19},{4,20},{5,21},{6,22},{7,23},{8,24},{9,... | collective-permute-start | bytes 196616 | tf_op jit(solution)/shard_map/ppermute | solution.py:255
  65.1 3.8 %collective-permute-done.15 = f32[64,256]{1,0:T(8,128)S(1)} collective-permute-done((f32[64,256]{1,0:T(8,128)S(1)}, f32[64,256]{1,0:T(8,128)S(1)}, u32[]{:S(2)}, u32[]{:S(2)}) %collective-permute-start.15) | collective-permute-done | bytes 65568 | tf_op jit(solution)/shard_map/ppermute | solution.py:255
  69.8 1.1 shard_map.60
  70.9 2.4 %collective-permute-done.16 = f32[64,256]{1,0:T(8,128)S(1)} collective-permute-done((f32[64,256]{1,0:T(8,128)S(1)}, f32[64,256]{1,0:T(8,128)S(1)}, u32[]{:S(2)}, u32[]{:S(2)}) %collective-permute-start.16) | collective-permute-done | bytes 65568 | tf_op jit(solution)/shard_map/ppermute | solution.py:255
  73.3 1.4 %collective-permute-start.17 = (f32[64,256]{1,0:T(8,128)S(1)}, f32[64,256]{1,0:T(8,128)S(1)}, u32[]{:S(2)}, u32[]{:S(2)}) collective-permute-start(f32[64,256]{1,0:T(8,128)S(1)} %add.95), channel_id=1, source_target_pairs={{0,2},{1,3},{2,0},{3,1},{4,6},{5,7},{6,4},{7,5},{8,10},{9,11},{10,... | collective-permute-start | bytes 196616 | tf_op jit(solution)/shard_map/ppermute | solution.py:255
  74.7 3.0 %collective-permute-done.17 = f32[64,256]{1,0:T(8,128)S(1)} collective-permute-done((f32[64,256]{1,0:T(8,128)S(1)}, f32[64,256]{1,0:T(8,128)S(1)}, u32[]{:S(2)}, u32[]{:S(2)}) %collective-permute-start.17) | collective-permute-done | bytes 65568 | tf_op jit(solution)/shard_map/ppermute | solution.py:255
  77.7 0.8 select_reduce_fusion.1
  79.2 5.8 %cholesky.18 = f32[64,64]{1,0:T(8,128)S(1)} custom-call(f32[64,64]{1,0:T(8,128)S(1)} %fusion.16), custom_call_target="Cholesky" | custom-call | tf_op jit(solution)/shard_map/jit(cholesky)/cholesky | solution.py:293
  85.1 1.0 slice_add_fusion
  87.5 1.0 slice_add_fusion.4
  88.5 1.4 %collective-permute-start.4 = (f32[4,64,256]{2,1,0:T(8,128)S(1)}, f32[4,64,256]{2,1,0:T(8,128)S(1)}, u32[]{:S(2)}, u32[]{:S(2)}) collective-permute-start(f32[4,64,256]{2,1,0:T(8,128)S(1)} %slice_add_fusion.4), channel_id=1, source_target_pairs={{0,1},{1,0},{2,3},{3,2},{4,5},{5,4},{6,7},{7,6},{8,9},{9,8},{10,11... | collective-permute-start | bytes 786440 | tf_op jit(solution)/shard_map/ppermute | solution.py:255
  89.9 4.3 %collective-permute-done.10 = f32[4,64,256]{2,1,0:T(8,128)S(1)} collective-permute-done((f32[4,64,256]{2,1,0:T(8,128)S(1)}, f32[4,64,256]{2,1,0:T(8,128)S(1)}, u32[]{:S(2)}, u32[]{:S(2)}) %collective-permute-start.10) | collective-permute-done | bytes 262176 | tf_op jit(solution)/shard_map/ppermute | solution.py:255
  94.2 1.1 fusion.5
  95.3 1.5 %collective-permute-start.9 = (f32[4,64,256]{2,1,0:T(8,128)S(1)}, f32[4,64,256]{2,1,0:T(8,128)S(1)}, u32[]{:S(2)}, u32[]{:S(2)}) collective-permute-start(f32[4,64,256]{2,1,0:T(8,128)S(1)} %get-tuple-element.33), channel_id=1, source_target_pairs={{0,2},{1,3},{2,0},{3,1},{4,6},{5,7},{6,4},{7,5},{8,10},{9,11},{10,... | collective-permute-start | bytes 786440 | tf_op jit(solution)/shard_map/ppermute | solution.py:255
  97.5 4.9 %custom-call.10 = f32[1,64,64]{1,2,0:T(8,128)S(1)} custom-call(f32[1,64,64]{2,1,0:T(8,128)S(1)} %fusion.10), custom_call_target="InvertDiagBlocksLowerTriangular" | custom-call | tf_op jit(solution)/shard_map/jit(_cho_solve)/triangular_solve | solution.py:294
  102.4 1.1 fusion.8
  104.2 1.0 fusion.6
  105.2 4.1 %collective-permute-start.12 = (f32[2,2,64,256]{3,2,1,0:T(8,128)S(1)}, f32[2,2,64,256]{3,2,1,0:T(8,128)S(1)}, u32[]{:S(2)}, u32[]{:S(2)}) collective-permute-start(f32[2,2,64,256]{3,2,1,0:T(8,128)S(1)} %get-tuple-element.36), channel_id=1, source_target_pairs={{0,24},{1,25},{2,26},{3,27},{4,28},{5,29},{6,30},{7,31},{8,16},{9,... | collective-permute-start | bytes 786440 | tf_op jit(solution)/shard_map/ppermute | solution.py:255
  109.9 1.0 fusion.9
  111.9 4.1 %collective-permute-done.12.refs_3_ = f32[2,2,64,256]{3,2,1,0:T(8,128)S(1)} collective-permute-done((f32[2,2,64,256]{3,2,1,0:T(8,128)S(1)}, f32[2,2,64,256]{3,2,1,0:T(8,128)S(1)}, u32[]{:S(2)}, u32[]{:S(2)}) %collective-permute-start.12) | collective-permute-done | bytes 262176 | tf_op jit(solution)/shard_map/ppermute | solution.py:255
  116.1 8.7 %collective-permute-done.11.refs_2_ = f32[2,2,64,256]{3,2,1,0:T(8,128)S(1)} collective-permute-done((f32[2,2,64,256]{3,2,1,0:T(8,128)S(1)}, f32[2,2,64,256]{3,2,1,0:T(8,128)S(1)}, u32[]{:S(2)}, u32[]{:S(2)}) %collective-permute-start.11) | collective-permute-done | bytes 262176 | tf_op jit(solution)/shard_map/ppermute | solution.py:255
  124.8 2.0 %shard_map.63 = (f32[256,64]{1,0:T(8,128)S(1)}, f32[256,256]{1,0:T(8,128)}) custom-call(f32[2,2,64,256]{3,2,1,0:T(8,128)S(1)} %get-tuple-element.39.refs_0_, f32[2,2,64,256]{3,2,1,0:T(8,128)S(1)} %collective-permute-done.5.refs_1_, f32[2,2,64,256]{3,2,1,0:T(8,128)S(1)} %collective-permute-done.11.refs_2_, ...), custom_call_target="tpu_custom_call" | custom-call | tf_op jit(solution)/shard_map/pallas_call | solution.py:233
  (40 shorter events, 7.9 us)
Async XLA Ops:
  1.5 1.6 %copy-start = (f32[2048,256]{1,0:T(8,128)S(1)}, f32[2048,256]{1,0:T(8,128)}, u32[]{:S(2)}) copy-start(f32[2048,256]{1,0:T(8,128)} %g_ref.3) | copy-start | bytes 6291460
  3.1 0.7 copy-start.1
  20.2 35.1 %collective-permute-start.6 = (f32[9,64,256]{2,1,0:T(8,128)S(1)}, f32[9,64,256]{2,1,0:T(8,128)S(1)}, u32[]{:S(2)}, u32[]{:S(2)}) collective-permute-start(f32[9,64,256]{2,1,0:T(8,128)S(1)} %get-tuple-element.23), channel_id=1, source_target_pairs={{0,1},{1,0},{2,3},{3,2},{4,5},{5,4},{6,7},{7,6},{8,9},{9,8},{10,11... | collective-permute-start | bytes 1769480 | tf_op jit(solution)/shard_map/ppermute | solution.py:255
  21.3 34.0 %collective-permute-start.7 = (f32[9,64,256]{2,1,0:T(8,128)S(1)}, f32[9,64,256]{2,1,0:T(8,128)S(1)}, u32[]{:S(2)}, u32[]{:S(2)}) collective-permute-start(f32[9,64,256]{2,1,0:T(8,128)S(1)} %get-tuple-element.25), channel_id=1, source_target_pairs={{0,2},{1,3},{2,0},{3,1},{4,6},{5,7},{6,4},{7,5},{8,10},{9,11},{10,... | collective-permute-start | bytes 1769480 | tf_op jit(solution)/shard_map/ppermute | solution.py:255
  53.0 16.8 %collective-permute-start = (f32[9,64,256]{2,1,0:T(8,128)S(1)}, f32[9,64,256]{2,1,0:T(8,128)S(1)}, u32[]{:S(2)}, u32[]{:S(2)}) collective-permute-start(f32[9,64,256]{2,1,0:T(8,128)S(1)} %get-tuple-element.17), channel_id=1, source_target_pairs={{0,1},{1,0},{2,3},{3,2},{4,5},{5,4},{6,7},{7,6},{8,9},{9,8},{10,11... | collective-permute-start | bytes 1769480 | tf_op jit(solution)/shard_map/ppermute | solution.py:255
  55.1 14.7 %collective-permute-start.1 = (f32[9,64,256]{2,1,0:T(8,128)S(1)}, f32[9,64,256]{2,1,0:T(8,128)S(1)}, u32[]{:S(2)}, u32[]{:S(2)}) collective-permute-start(f32[9,64,256]{2,1,0:T(8,128)S(1)} %get-tuple-element.19), channel_id=1, source_target_pairs={{0,2},{1,3},{2,0},{3,1},{4,6},{5,7},{6,4},{7,5},{8,10},{9,11},{10,... | collective-permute-start | bytes 1769480 | tf_op jit(solution)/shard_map/ppermute | solution.py:255
  55.6 29.6 %collective-permute-start.8 = (f32[16,64,256]{2,1,0:T(8,128)S(1)}, f32[16,64,256]{2,1,0:T(8,128)}, u32[]{:S(2)}, u32[]{:S(2)}) collective-permute-start(f32[16,64,256]{2,1,0:T(8,128)S(1)} %get-tuple-element.27), channel_id=1, source_target_pairs={{0,4},{1,5},{2,6},{3,7},{4,0},{5,1},{6,2},{7,3},{8,12},{9,13},{10,... | collective-permute-start | bytes 3145736 | tf_op jit(solution)/shard_map/ppermute | solution.py:255
  55.7 2.4 %collective-permute-start.13 = (f32[64,256]{1,0:T(8,128)S(1)}, f32[64,256]{1,0:T(8,128)S(1)}, u32[]{:S(2)}, u32[]{:S(2)}) collective-permute-start(f32[64,256]{1,0:T(8,128)S(1)} %add.91), channel_id=1, source_target_pairs={{0,4},{1,5},{2,6},{3,7},{4,0},{5,1},{6,2},{7,3},{8,12},{9,13},{10,... | collective-permute-start | bytes 196616 | tf_op jit(solution)/shard_map/ppermute | solution.py:255
  58.0 5.2 %collective-permute-start.14 = (f32[64,256]{1,0:T(8,128)S(1)}, f32[64,256]{1,0:T(8,128)S(1)}, u32[]{:S(2)}, u32[]{:S(2)}) collective-permute-start(f32[64,256]{1,0:T(8,128)S(1)} %add.92), channel_id=1, source_target_pairs={{0,8},{1,9},{2,10},{3,11},{4,12},{5,13},{6,14},{7,15},{8,0},{9,1},... | collective-permute-start | bytes 196616 | tf_op jit(solution)/shard_map/ppermute | solution.py:255
  63.3 5.7 %collective-permute-start.15 = (f32[64,256]{1,0:T(8,128)S(1)}, f32[64,256]{1,0:T(8,128)S(1)}, u32[]{:S(2)}, u32[]{:S(2)}) collective-permute-start(f32[64,256]{1,0:T(8,128)S(1)} %add.93), channel_id=1, source_target_pairs={{0,16},{1,17},{2,18},{3,19},{4,20},{5,21},{6,22},{7,23},{8,24},{9,... | collective-permute-start | bytes 196616 | tf_op jit(solution)/shard_map/ppermute | solution.py:255
  69.0 4.3 %collective-permute-start.16 = (f32[64,256]{1,0:T(8,128)S(1)}, f32[64,256]{1,0:T(8,128)S(1)}, u32[]{:S(2)}, u32[]{:S(2)}) collective-permute-start(f32[64,256]{1,0:T(8,128)S(1)} %add.94), channel_id=1, source_target_pairs={{0,1},{1,0},{2,3},{3,2},{4,5},{5,4},{6,7},{7,6},{8,9},{9,8},{10,11... | collective-permute-start | bytes 196616 | tf_op jit(solution)/shard_map/ppermute | solution.py:255
  70.9 16.6 %collective-permute-start.2 = (f32[16,64,256]{2,1,0:T(8,128)}, f32[16,64,256]{2,1,0:T(8,128)}, u32[]{:S(2)}, u32[]{:S(2)}) collective-permute-start(f32[16,64,256]{2,1,0:T(8,128)} %get-tuple-element.21), channel_id=1, source_target_pairs={{0,4},{1,5},{2,6},{3,7},{4,0},{5,1},{6,2},{7,3},{8,12},{9,13},{10,... | collective-permute-start | bytes 3145736 | tf_op jit(solution)/shard_map/ppermute | solution.py:255
  73.3 4.3 %collective-permute-start.17 = (f32[64,256]{1,0:T(8,128)S(1)}, f32[64,256]{1,0:T(8,128)S(1)}, u32[]{:S(2)}, u32[]{:S(2)}) collective-permute-start(f32[64,256]{1,0:T(8,128)S(1)} %add.95), channel_id=1, source_target_pairs={{0,2},{1,3},{2,0},{3,1},{4,6},{5,7},{6,4},{7,5},{8,10},{9,11},{10,... | collective-permute-start | bytes 196616 | tf_op jit(solution)/shard_map/ppermute | solution.py:255
  86.1 8.1 %collective-permute-start.10 = (f32[4,64,256]{2,1,0:T(8,128)S(1)}, f32[4,64,256]{2,1,0:T(8,128)S(1)}, u32[]{:S(2)}, u32[]{:S(2)}) collective-permute-start(f32[4,64,256]{2,1,0:T(8,128)S(1)} %slice_add_fusion), channel_id=1, source_target_pairs={{0,1},{1,0},{2,3},{3,2},{4,5},{5,4},{6,7},{7,6},{8,9},{9,8},{10,11... | collective-permute-start | bytes 786440 | tf_op jit(solution)/shard_map/ppermute | solution.py:255
  88.5 13.9 %collective-permute-start.4 = (f32[4,64,256]{2,1,0:T(8,128)S(1)}, f32[4,64,256]{2,1,0:T(8,128)S(1)}, u32[]{:S(2)}, u32[]{:S(2)}) collective-permute-start(f32[4,64,256]{2,1,0:T(8,128)S(1)} %slice_add_fusion.4), channel_id=1, source_target_pairs={{0,1},{1,0},{2,3},{3,2},{4,5},{5,4},{6,7},{7,6},{8,9},{9,8},{10,11... | collective-permute-start | bytes 786440 | tf_op jit(solution)/shard_map/ppermute | solution.py:255
  95.3 8.9 %collective-permute-start.9 = (f32[4,64,256]{2,1,0:T(8,128)S(1)}, f32[4,64,256]{2,1,0:T(8,128)S(1)}, u32[]{:S(2)}, u32[]{:S(2)}) collective-permute-start(f32[4,64,256]{2,1,0:T(8,128)S(1)} %get-tuple-element.33), channel_id=1, source_target_pairs={{0,2},{1,3},{2,0},{3,1},{4,6},{5,7},{6,4},{7,5},{8,10},{9,11},{10,... | collective-permute-start | bytes 786440 | tf_op jit(solution)/shard_map/ppermute | solution.py:255
  103.5 6.4 %collective-permute-start.3 = (f32[4,64,256]{2,1,0:T(8,128)S(1)}, f32[4,64,256]{2,1,0:T(8,128)S(1)}, u32[]{:S(2)}, u32[]{:S(2)}) collective-permute-start(f32[4,64,256]{2,1,0:T(8,128)S(1)} %get-tuple-element.35), channel_id=1, source_target_pairs={{0,2},{1,3},{2,0},{3,1},{4,6},{5,7},{6,4},{7,5},{8,10},{9,11},{10,... | collective-permute-start | bytes 786440 | tf_op jit(solution)/shard_map/ppermute | solution.py:255
  105.2 10.9 %collective-permute-start.12 = (f32[2,2,64,256]{3,2,1,0:T(8,128)S(1)}, f32[2,2,64,256]{3,2,1,0:T(8,128)S(1)}, u32[]{:S(2)}, u32[]{:S(2)}) collective-permute-start(f32[2,2,64,256]{3,2,1,0:T(8,128)S(1)} %get-tuple-element.36), channel_id=1, source_target_pairs={{0,24},{1,25},{2,26},{3,27},{4,28},{5,29},{6,30},{7,31},{8,16},{9,... | collective-permute-start | bytes 786440 | tf_op jit(solution)/shard_map/ppermute | solution.py:255
  109.3 15.4 %collective-permute-start.11 = (f32[2,2,64,256]{3,2,1,0:T(8,128)S(1)}, f32[2,2,64,256]{3,2,1,0:T(8,128)S(1)}, u32[]{:S(2)}, u32[]{:S(2)}) collective-permute-start(f32[2,2,64,256]{3,2,1,0:T(8,128)S(1)} %get-tuple-element.37), channel_id=1, source_target_pairs={{0,16},{1,17},{2,18},{3,19},{4,20},{5,21},{6,22},{7,23},{8,24},{9,... | collective-permute-start | bytes 786440 | tf_op jit(solution)/shard_map/ppermute | solution.py:255
  111.0 13.8 %collective-permute-start.5 = (f32[2,2,64,256]{3,2,1,0:T(8,128)S(1)}, f32[2,2,64,256]{3,2,1,0:T(8,128)S(1)}, u32[]{:S(2)}, u32[]{:S(2)}) collective-permute-start(f32[2,2,64,256]{3,2,1,0:T(8,128)S(1)} %get-tuple-element.38), channel_id=1, source_target_pairs={{0,8},{1,9},{2,10},{3,11},{4,12},{5,13},{6,14},{7,15},{8,0},{9,1},... | collective-permute-start | bytes 786440 | tf_op jit(solution)/shard_map/ppermute | solution.py:255

commit v2 on v0

v2 whole, which is shorter than its diff:
```python
import functools

import jax
import jax.numpy as jnp
from jax import lax
from jax.experimental import pallas as pl
from jax.experimental.pallas import tpu as pltpu
from jax.sharding import PartitionSpec as P

ROWS_DEV = 256
UNROLL = 8
F32 = jnp.float32
BF16 = jnp.bfloat16
AXES = ("term", "doc")
TOKEN = (8, 128)
LIMIT = pltpu.CompilerParams(vmem_limit_bytes=48 * 2**20)
TINY = pl.CostEstimate(flops=1, bytes_accessed=1, transcendentals=0)
ANY = pl.BlockSpec(memory_space=pl.ANY)
HBM = pl.BlockSpec(memory_space=pltpu.HBM)
SMEM = pl.BlockSpec(memory_space=pltpu.SMEM)
VMEM = pl.BlockSpec(memory_space=pltpu.VMEM)


def shaped(shape, dtype=F32):
    return jax.ShapeDtypeStruct(tuple(shape), dtype)


def split(v):
    hi = v.astype(BF16)
    lo = (v - hi.astype(F32)).astype(BF16)
    return hi, lo


def hdot(a, b, dims):
    return lax.dot_general(a, b, (dims, ((), ())), precision=lax.Precision.HIGHEST, preferred_element_type=F32)


def in_order(kernel, last, _token, *refs):
    kernel(*refs[:last], *refs[last + 1 :])
    refs[last][...] = jnp.zeros_like(refs[last])


class Queue:
    def __init__(self, token):
        self.token = token

    def call(self, name, kernel, out_shape, args):
        got = pl.pallas_call(
            functools.partial(in_order, kernel, len(args)),
            out_shape=(shaped(TOKEN),) + tuple(out_shape),
            in_specs=[VMEM] * (1 + len(args)),
            out_specs=(VMEM,) * (1 + len(out_shape)),
            compiler_params=LIMIT,
            cost_estimate=TINY,
            name=name,
        )(self.token, *args)
        self.token = got[0]
        return got[1:]


def products_kernel(geo, first, coords, anchors, me_ref, tiles, *rest):
    n_y, n_z, n_tiles, tile = geo
    if first:
        g_hbm, blocks, anchor_out, wide, buf, order, flag, in_sem, g_ref, g_sem = rest
        load = pltpu.make_async_copy(g_hbm, g_ref, g_sem)
        load.start()
    else:
        wide, anchor_in, blocks, anchor_out, token, buf, order, flag, in_sem = rest
        token[...] = jnp.zeros_like(token)
    n_doc = 2 * n_y
    slots = n_z * n_doc
    per = ROWS_DEV // tile
    me = me_ref[0]
    doc_base = me_ref[1]
    width = wide.shape[1] // 2

    def place(block):
        rel = lax.bitwise_xor(block // per, me)
        dc = (rel // n_doc) & 1
        mine = dc == (1 if first else 0)
        slot = (rel // (2 * n_doc)) * n_doc + lax.rem(rel, n_doc)
        return mine, slot

    def scan(k, count):
        order[count] = k
        return count + place(coords[0, k])[0].astype(jnp.int32)

    count = lax.fori_loop(0, n_tiles, scan, jnp.int32(0), unroll=8)
    groups = (count + UNROLL - 1) // UNROLL

    def entry(i):
        valid = i < count
        return valid, jnp.where(valid, order[jnp.minimum(i, n_tiles - 1)], 0)

    def fetch(j, u):
        at = lax.rem(j, 2) * UNROLL + u
        return pltpu.make_async_copy(tiles.at[entry(j * UNROLL + u)[1]], buf.at[at], in_sem.at[at])

    def fetch_group(j):
        @pl.when(j < groups)
        def _():
            for u in range(UNROLL):
                fetch(j, u).start()

    fetch_group(0)
    blocks[...] = jnp.zeros_like(blocks)
    flag[...] = jnp.zeros_like(flag)
    if first:
        load.wait()
        hi, lo = split(g_ref[...])
        wide[:, :width] = hi
        wide[:, width:] = lo

    def product(j, u):
        valid, k = entry(j * UNROLL + u)
        doc = coords[1, k] - doc_base
        hi, lo = split(buf[lax.rem(j, 2) * UNROLL + u])
        w = wide[pl.ds(pl.multiple_of(doc * tile, tile), tile), :]
        lhs = jnp.concatenate([hi, lo], axis=1)
        both = jnp.dot(lhs, jnp.concatenate([w, w], axis=0), preferred_element_type=F32)
        return both[:, :width] + both[:, width:]

    def group(j, carry):
        fetch_group(j + 1)
        for u in range(UNROLL):
            fetch(j, u).wait()
        prods = [product(j, u) for u in range(UNROLL)]
        for u, prod in enumerate(prods):
            valid, k = entry(j * UNROLL + u)
            block = coords[0, k]
            slot = jnp.where(valid, place(block)[1], slots)
            blocks[slot] += prod
            flag[pl.ds(slot, 1), :] = jnp.full((1, width), lax.rem(block, per).astype(F32), F32)
        return carry

    lax.fori_loop(0, groups, group, 0)
    if first:
        anchor_out[...] = jnp.zeros_like(anchor_out)
    else:
        anchor_out[...] = anchor_in[...]

    def pick(i, carry):
        row = anchors[i]
        block = row // tile
        mine, slot = place(block)

        @pl.when(mine)
        def _():
            value = blocks[slot, pl.ds(lax.rem(row, tile), 1), :]
            same = flag[pl.ds(slot, 1), :] == lax.rem(block, per).astype(F32)
            anchor_out[pl.ds(i, 1), :] = jnp.where(same, value, 0.0)

        return carry

    lax.fori_loop(0, anchors.shape[0], pick, 0)
    blocks[slots, pl.ds(0, slots), :] = flag[pl.ds(0, slots), :]


def products(n_y, n_z, coords, anchors, me, tiles, g=None, wide=None, anchor_in=None):
    n_tiles, tile = tiles.shape[:2]
    first = g is not None
    width = g.shape[1] if first else wide.shape[1] // 2
    slots = n_z * 2 * n_y
    outs = [shaped((slots + 1, tile, width)), shaped((anchors.shape[0], width))]
    scratch = [
        pltpu.VMEM((2 * UNROLL, tile, tile), F32),
        pltpu.SMEM((n_tiles + 8,), jnp.int32),
        pltpu.VMEM((slots + 8, width), F32),
        pltpu.SemaphoreType.DMA((2 * UNROLL,)),
    ]
    if first:
        outs.append(shaped((g.shape[0], 2 * width), BF16))
        scratch += [pltpu.VMEM(g.shape, F32), pltpu.SemaphoreType.DMA]
        more, specs = (g,), [HBM]
    else:
        outs.append(shaped(TOKEN))
        more, specs = (wide, anchor_in), [VMEM, VMEM]
    return pl.pallas_call(
        functools.partial(products_kernel, (n_y, n_z, n_tiles, tile), first),
        out_shape=outs,
        in_specs=[SMEM, SMEM, SMEM, HBM] + specs,
        out_specs=[VMEM] * 3,
        scratch_shapes=scratch,
        compiler_params=LIMIT,
        cost_estimate=pl.CostEstimate(flops=8 * 10**9, bytes_accessed=5 * 2**20, transcendentals=0),
        name="products_away" if first else "products_here",
    )(coords, anchors, me, tiles, *more)


def spread_kernel(dz, n_y, own, got, stay, send_x, *send_y):
    slots = own.shape[0] - 1
    half = own.shape[1] // 2
    for dy in range(n_y):
        for dx in range(2):
            slot = (dz * n_y + dy) * 2 + dx
            a, b = own[slot], got[slot]
            up_a = a * own[slots, pl.ds(slot, 1), :]
            up_b = b * got[slots, pl.ds(slot, 1), :]
            for s, value in enumerate(((a - up_a) + (b - up_b), up_a + up_b)):
                if dx:
                    send_x[2 * dy + s] = value[:half]
                else:
                    stay[2 * dy + s] = value[:half]
                if dy:
                    send_y[dy - 1][2 * dx + s] = value[half:]
                else:
                    stay[2 * n_y + 2 * dx + s] = value[half:]


def spread(queue, dz, n_y, own, got):
    half, width = own.shape[1] // 2, own.shape[2]
    outs = (shaped((2 * n_y + 4, half, width)), shaped((2 * n_y, half, width))) + (shaped((4, half, width)),) * (n_y - 1)
    stay, send_x, *send_y = queue.call("spread", functools.partial(spread_kernel, dz, n_y), outs, (own, got))
    return stay, send_x, send_y


def join_kernel(n_y, stay, got_x, *refs):
    got_y = refs[: n_y - 1]
    keep, send_x = refs[n_y - 1 : n_y + 1]
    send_y = refs[n_y + 1 :]
    for dy in range(n_y):
        for s in range(2):
            value = stay[2 * dy + s] + got_x[2 * dy + s]
            if dy:
                send_y[dy - 1][s] = value
            else:
                keep[s] = value
    for dx in range(2):
        for s in range(2):
            value = stay[2 * n_y + 2 * dx + s]
            for ref in got_y:
                value = value + ref[2 * dx + s]
            if dx:
                send_x[s] = value
            else:
                keep[2 + s] = value


def join(queue, n_y, stay, got_x, got_y):
    half, width = stay.shape[1:]
    outs = (shaped((4, half, width)),) + (shaped((2, half, width)),) * n_y
    keep, send_x, *send_y = queue.call("join", functools.partial(join_kernel, n_y), outs, (stay, got_x, *got_y))
    return keep, send_x, send_y


def merge_kernel(n_y, keep, got_x, *refs):
    got_y, far, out = refs[: n_y - 1], refs[n_y - 1 : -1], refs[-1]
    x, y = keep[:2], keep[2:] + got_x[...]
    for ref in got_y:
        x = x + ref[...]
    for ref in far:
        x = x + ref[:2]
        y = y + ref[2:]
    out[:2] = x
    out[2:] = y


def merge(queue, n_y, keep, got_x, got_y, far=()):
    return queue.call("merge", functools.partial(merge_kernel, n_y), (shaped(keep.shape),), (keep, got_x, *got_y, *far))[0]


def total_kernel(*refs):
    total = refs[0][...]
    for ref in refs[1:-1]:
        total = total + ref[...]
    refs[-1][...] = total


def total(queue, values):
    return queue.call("total", total_kernel, (shaped(values[0].shape),), values)[0]


def inverse_kernel(n_in, *refs):
    ins, (rows_ref, inv_ref) = refs[:n_in], refs[n_in:]
    rows = ins[0][...]
    for ref in ins[1:]:
        rows = rows + ref[...]
    rows_ref[...] = rows
    count = rows.shape[0]
    m = hdot(rows, rows, ((1,), (1,)))
    at_row = lax.broadcasted_iota(jnp.int32, (count, count), 0)
    at_col = lax.broadcasted_iota(jnp.int32, (count, count), 1)
    diagonal = at_row == at_col
    ridge = 0.001 * jnp.sum(jnp.where(diagonal, m, 0.0)) / count
    m = jnp.where(diagonal, m + ridge, m)
    for k in range(count):
        row = m[k : k + 1, :]
        col = m[:, k : k + 1]
        scale = 1.0 / m[k : k + 1, k : k + 1]
        row = jnp.where(at_col[:1] == k, 1.0, row) * scale
        m = jnp.where(at_row == k, row, jnp.where(at_col == k, 0.0, m) - col * row)
    inv_ref[...] = m


def inverse(queue, parts):
    count, width = parts[0].shape
    return queue.call("inverse", functools.partial(inverse_kernel, len(parts)), (shaped((count, width)), shaped((count, count))), parts)


def finish_kernel(n_far, near, *refs):
    x, y = near[:2], near[2:]
    for ref in refs[:n_far]:
        x = x + ref[:2]
        y = y + ref[2:]
    rows_ref, inv_ref, coef_ref, res_ref = refs[n_far:]
    owned = jnp.concatenate([x[0], y[0], x[1], y[1]], axis=0)
    rows = rows_ref[...]
    project = hdot(rows, owned, ((1,), (1,)))
    coef = hdot(inv_ref[...], project, ((1,), (0,)))
    coef_ref[...] = coef
    res_ref[...] = owned - hdot(coef, rows, ((0,), (0,)))


def finish(queue, near, far, rows, inv):
    half, width = near.shape[1:]
    outs = (shaped((rows.shape[0], 4 * half)), shaped((4 * half, width)))
    coef, res = queue.call("finish", functools.partial(finish_kernel, len(far)), outs, (near, *far, rows, inv))
    return coef.T, res


def body(n_term, n_doc, tiles, coords, sketch, anchors):
    devices = n_term * n_doc
    n_y, n_z = n_doc // 2, n_term // 2
    me = lax.axis_index(AXES).astype(jnp.int32)
    doc_base = lax.axis_index("doc").astype(jnp.int32) * (sketch.shape[0] // tiles.shape[1])
    where = jnp.stack([me, doc_base])

    def swap(v, mask):
        return lax.ppermute(v, AXES, [(i, i ^ mask) for i in range(devices)])

    def swap_y(values):
        return [swap(v, 2 * (k + 1)) for k, v in enumerate(values)]

    z_masks = [2 * n_doc * k for k in range(1, n_z)]
    away, part, wide = products(n_y, n_z, coords.T, anchors, where, tiles, g=sketch)
    got = swap(away, n_doc)
    here, part, token = products(n_y, n_z, coords.T, anchors, where, tiles, wide=wide, anchor_in=part)
    queue = Queue(token)
    first, second, far = {}, {}, {}

    def do_spread(dz):
        stay, send_x, send_y = spread(queue, dz, n_y, here, got)
        first[dz] = (stay, swap(send_x, 1), swap_y(send_y))

    def do_join(dz):
        keep, send_x, send_y = join(queue, n_y, *first.pop(dz))
        second[dz] = (keep, swap(send_x, 1), swap_y(send_y))

    def do_merge(dz, *more):
        far[dz] = swap(merge(queue, n_y, *second.pop(dz), more), 2 * n_doc * dz)

    top = n_z - 1
    do_spread(top)
    do_spread(top - 1)
    rounds = [part] + [swap(part, mask) for mask in z_masks]
    part = total(queue, rounds)
    rounds = [part] + [swap(part, mask) for mask in range(1, n_doc)]
    do_join(top)
    if top >= 2:
        do_spread(top - 2)
    do_join(top - 1)
    if top >= 3:
        do_spread(top - 3)
    for dz in range(top, 0, -1):
        do_merge(dz)
        if dz == top:
            part = total(queue, rounds)
            rounds = [part, swap(part, n_doc)]
        if dz >= 2:
            do_join(dz - 2)
        if dz >= 4:
            do_spread(dz - 4)
        if dz == 2:
            rows, inv = inverse(queue, rounds)
    if top < 2:
        rows, inv = inverse(queue, rounds)
    near = merge(queue, n_y, *second.pop(0), [far.pop(dz) for dz in range(top, 2, -1)])
    if 2 in far:
        near = total(queue, [near, far.pop(2)])
    return finish(queue, near, list(far.values()), rows, inv)


def solution(mesh):
    in_specs = (P(("term", "doc"), None, None), P(("term", "doc"), None), P("doc", None), P())
    out_specs = (P(("term", "doc"), None), P(("term", "doc"), None))
    run = functools.partial(body, mesh.shape["term"], mesh.shape["doc"])
    return jax.shard_map(run, mesh=mesh, in_specs=in_specs, out_specs=out_specs, check_vma=False)
```

time: 448 us -> 103 us (0.23)
  waiting for transfers between devices: 309 us -> 25.4 us
  matrix products: 67.7 us -> 0 us
  local copies, waits for them, and re-layouts: 43.1 us -> 2.92 us
  starting transfers between devices: 0.08 us -> 39 us
  Pallas kernels: 0 us -> 33.5 us
  between operations: 14.8 us -> 0.81 us
  other arithmetic: 12.1 us -> 0.08 us
    reduce_scatter x1 -> x0, waiting for transfers between devices: 186 us -> none  [body(): lax.psum_scatter(partial_value, ('term', 'doc'), scatter_dimension=0, til...]
    psum x1 -> x0, waiting for transfers between devices: 123 us -> none  [body(): anchor_rows = lax.psum(own_part, ('term', 'doc'))]
    dot_general x12 -> x0, matrix products: 67.3 us -> none  [the longest x4 30.6 us: step(): jnp.einsum('bk,kac->bac', onehot, prods, precision=lax.Precision.HIGHEST)]
    ppermute x0 -> x27, starting transfers between devices: none -> 39 us  [swap(): return lax.ppermute(v, AXES, [(i, i ^ mask) for i in range(devices)])]
    pallas_call x0 -> x19, Pallas kernels: none -> 33.5 us  [the longest x2 24.8 us: products(): pl.pallas_call(functools.partial(products_kernel, (n_y, n_z, n_tiles, til...]
    ppermute x0 -> x27, waiting for transfers between devices: none -> 25.4 us  [swap(): return lax.ppermute(v, AXES, [(i, i ^ mask) for i in range(devices)])]
    while x17 -> x0, local copies, waits for them, and re-layouts: 24.3 us -> none
    gather x4 -> x0, local copies, waits for them, and re-layouts: 17.3 us -> none  [step(): chosen = jnp.take(g_blocks, coords[:, 1] - doc_base, axis=0)]
  transfers between devices with their start and end apart: 2 -> 27, of which waited for: 2 -> 10; matrix products, arithmetic and copies ran while one was open for 0% -> 0% of each run, Pallas kernels for 0% -> 18%
where the time goes in v2:
time: 103 us; the launch traced here: 102 us
  starting transfers between devices  39 us (38%)
  Pallas kernels  33.5 us (33%)
  waiting for transfers between devices  25.4 us (25%)
  local copies, waits for them, and re-layouts  2.92 us (3%)
    ppermute x27, starting transfers between devices, swap(): return lax.ppermute(v, AXES, [(i, i ^ mask) for i in range(devices)])  39 us
    ppermute x27, waiting for transfers between devices, swap(): return lax.ppermute(v, AXES, [(i, i ^ mask) for i in range(devices)])  25.4 us
    pallas_call x2, Pallas kernels, products(): pl.pallas_call(functools.partial(products_kernel, (n_y, n_z, n_tiles, til...  24.8 us
    pallas_call x17, Pallas kernels, call(): pl.pallas_call(functools.partial(in_order, kernel, len(args)), out_shape=...  8.73 us
    unnamed x6, local copies, waits for them, and re-layouts  2.92 us
  transfers between devices with their start and end apart: 27, of which 10 were waited for; matrix products, arithmetic and copies ran while one was open for 0% of the time, Pallas kernels for 18%

profile of v2, /device:TPU:0, one launch (start us, length us, event | category | flops | bytes accessed | tf_op | source)
XLA Modules:
  0.0 101.6 jit_solution(7600586788335624605)
XLA Ops:
  0.7 1.6 %copy-done = f32[2048,256]{1,0:T(8,128)S(1)} copy-done((f32[2048,256]{1,0:T(8,128)S(1)}, f32[2048,256]{1,0:T(8,128)}, u32[]{:S(2)}) %copy-start) | copy-done | bytes 2097176
  3.6 12.6 %products_away.1 = (f32[17,128,256]{2,1,0:T(8,128)}, f32[64,256]{1,0:T(8,128)S(1)}, bf16[2048,512]{1,0:T(8,128)(2,1)S(1)}) custom-call(s32[2,128]{1,0:T(2,128)S(1)} %bitcast.4, s32[64]{0:T(128)S(1)} %copy-done.2, s32[2]{0:T(128)S(1)} %pad_add_fusion.me_ref, f32[128,128,128]{2,1,0:T(8,128)} %tiles.3, f32[2048,256]{1,0:T(8,128)S(1)} %copy-done), custom_call_target="tpu_custom_call" | custom-call | flops 8000000000 | bytes 5242880 | tf_op jit(solution)/shard_map/products_away/pallas_call | solution.py:178
  16.3 2.0 %collective-permute-start = (f32[17,128,256]{2,1,0:T(8,128)}, f32[17,128,256]{2,1,0:T(8,128)S(1)}, u32[]{:S(2)}, u32[]{:S(2)}) collective-permute-start(f32[17,128,256]{2,1,0:T(8,128)} %get-tuple-element.63), channel_id=1, source_target_pairs={{0,4},{1,5},{2,6},{3,7},{4,0},{5,1},{6,2},{7,3},{8,12},{9,13},{10,... | collective-permute-start | bytes 6684680 | tf_op jit(solution)/shard_map/ppermute | solution.py:329
  18.3 12.2 %products_here.1 = (f32[17,128,256]{2,1,0:T(8,128)S(1)}, f32[64,256]{1,0:T(8,128)S(1)}, f32[8,128]{1,0:T(8,128)S(1)}) custom-call(s32[2,128]{1,0:T(2,128)S(1)} %bitcast.5, s32[64]{0:T(128)S(1)} %copy-done.2, s32[2]{0:T(128)S(1)} %pad_add_fusion.me_ref, f32[128,128,128]{2,1,0:T(8,128)} %tiles.3, bf16[2048,512]{1,0:T(8,128)(2,1)S(1)} %get-tuple-element.59.rest_0_, ...), custom_call_target="tpu_custom_call" | custom-call | flops 8000000000 | bytes 5242880 | tf_op jit(solution)/shard_map/products_here/pallas_call | solution.py:178
  30.6 2.4 %collective-permute-start.4 = (f32[4,64,256]{2,1,0:T(8,128)S(1)}, f32[4,64,256]{2,1,0:T(8,128)S(1)}, u32[]{:S(2)}, u32[]{:S(2)}) collective-permute-start(f32[4,64,256]{2,1,0:T(8,128)S(1)} %get-tuple-element.69), channel_id=1, source_target_pairs={{0,1},{1,0},{2,3},{3,2},{4,5},{5,4},{6,7},{7,6},{8,9},{9,8},{10,11... | collective-permute-start | bytes 786440 | tf_op jit(solution)/shard_map/ppermute | solution.py:329
  32.9 2.7 %collective-permute-start.5 = (f32[4,64,256]{2,1,0:T(8,128)S(1)}, f32[4,64,256]{2,1,0:T(8,128)S(1)}, u32[]{:S(2)}, u32[]{:S(2)}) collective-permute-start(f32[4,64,256]{2,1,0:T(8,128)S(1)} %get-tuple-element.70), channel_id=1, source_target_pairs={{0,2},{1,3},{2,0},{3,1},{4,6},{5,7},{6,4},{7,5},{8,10},{9,11},{10,... | collective-permute-start | bytes 786440 | tf_op jit(solution)/shard_map/ppermute | solution.py:329
  35.7 1.2 %collective-permute-start.6 = (f32[4,64,256]{2,1,0:T(8,128)S(1)}, f32[4,64,256]{2,1,0:T(8,128)S(1)}, u32[]{:S(2)}, u32[]{:S(2)}) collective-permute-start(f32[4,64,256]{2,1,0:T(8,128)S(1)} %get-tuple-element.74), channel_id=1, source_target_pairs={{0,1},{1,0},{2,3},{3,2},{4,5},{5,4},{6,7},{7,6},{8,9},{9,8},{10,11... | collective-permute-start | bytes 786440 | tf_op jit(solution)/shard_map/ppermute | solution.py:329
  36.9 2.5 %collective-permute-start.2 = (f32[64,256]{1,0:T(8,128)S(1)}, f32[64,256]{1,0:T(8,128)S(1)}, u32[]{:S(2)}, u32[]{:S(2)}) collective-permute-start(f32[64,256]{1,0:T(8,128)S(1)} %get-tuple-element.66.refs_0_), channel_id=1, source_target_pairs={{0,16},{1,17},{2,18},{3,19},{4,20},{5,21},{6,22},{7,23},{8,24},{9,... | collective-permute-start | bytes 196616 | tf_op jit(solution)/shard_map/ppermute | solution.py:329
  40.4 1.7 %collective-permute-done.2.refs_2_ = f32[64,256]{1,0:T(8,128)S(1)} collective-permute-done((f32[64,256]{1,0:T(8,128)S(1)}, f32[64,256]{1,0:T(8,128)S(1)}, u32[]{:S(2)}, u32[]{:S(2)}) %collective-permute-start.2) | collective-permute-done | bytes 65568 | tf_op jit(solution)/shard_map/ppermute | solution.py:329
  42.1 5.5 %collective-permute-start.3 = (f32[64,256]{1,0:T(8,128)S(1)}, f32[64,256]{1,0:T(8,128)S(1)}, u32[]{:S(2)}, u32[]{:S(2)}) collective-permute-start(f32[64,256]{1,0:T(8,128)S(1)} %get-tuple-element.66.refs_0_), channel_id=1, source_target_pairs={{0,24},{1,25},{2,26},{3,27},{4,28},{5,29},{6,30},{7,31},{8,16},{9,... | collective-permute-start | bytes 196616 | tf_op jit(solution)/shard_map/ppermute | solution.py:329
  47.6 2.2 %collective-permute-done.3.refs_3_ = f32[64,256]{1,0:T(8,128)S(1)} collective-permute-done((f32[64,256]{1,0:T(8,128)S(1)}, f32[64,256]{1,0:T(8,128)S(1)}, u32[]{:S(2)}, u32[]{:S(2)}) %collective-permute-start.3) | collective-permute-done | bytes 65568 | tf_op jit(solution)/shard_map/ppermute | solution.py:329
  50.0 2.4 %collective-permute-start.11 = (f32[64,256]{1,0:T(8,128)S(1)}, f32[64,256]{1,0:T(8,128)S(1)}, u32[]{:S(2)}, u32[]{:S(2)}) collective-permute-start(f32[64,256]{1,0:T(8,128)S(1)} %get-tuple-element.82.refs_0_), channel_id=1, source_target_pairs={{0,2},{1,3},{2,0},{3,1},{4,6},{5,7},{6,4},{7,5},{8,10},{9,11},{10,... | collective-permute-start | bytes 196616 | tf_op jit(solution)/shard_map/ppermute | solution.py:329
  52.5 1.0 %collective-permute-start.13 = (f32[4,64,256]{2,1,0:T(8,128)S(1)}, f32[4,64,256]{2,1,0:T(8,128)S(1)}, u32[]{:S(2)}, u32[]{:S(2)}) collective-permute-start(f32[4,64,256]{2,1,0:T(8,128)S(1)} %get-tuple-element.85), channel_id=1, source_target_pairs={{0,1},{1,0},{2,3},{3,2},{4,5},{5,4},{6,7},{7,6},{8,9},{9,8},{10,11... | collective-permute-start | bytes 786440 | tf_op jit(solution)/shard_map/ppermute | solution.py:329
  54.6 1.1 %collective-permute-done.11.refs_2_ = f32[64,256]{1,0:T(8,128)S(1)} collective-permute-done((f32[64,256]{1,0:T(8,128)S(1)}, f32[64,256]{1,0:T(8,128)S(1)}, u32[]{:S(2)}, u32[]{:S(2)}) %collective-permute-start.11) | collective-permute-done | bytes 65568 | tf_op jit(solution)/shard_map/ppermute | solution.py:329
  55.7 1.3 %collective-permute-start.14 = (f32[4,64,256]{2,1,0:T(8,128)S(1)}, f32[4,64,256]{2,1,0:T(8,128)S(1)}, u32[]{:S(2)}, u32[]{:S(2)}) collective-permute-start(f32[4,64,256]{2,1,0:T(8,128)S(1)} %get-tuple-element.86), channel_id=1, source_target_pairs={{0,2},{1,3},{2,0},{3,1},{4,6},{5,7},{6,4},{7,5},{8,10},{9,11},{10,... | collective-permute-start | bytes 786440 | tf_op jit(solution)/shard_map/ppermute | solution.py:329
  57.7 1.4 %collective-permute-start.12 = (f32[64,256]{1,0:T(8,128)S(1)}, f32[64,256]{1,0:T(8,128)S(1)}, u32[]{:S(2)}, u32[]{:S(2)}) collective-permute-start(f32[64,256]{1,0:T(8,128)S(1)} %get-tuple-element.82.refs_0_), channel_id=1, source_target_pairs={{0,3},{1,2},{2,1},{3,0},{4,7},{5,6},{6,5},{7,4},{8,11},{9,10},{10,... | collective-permute-start | bytes 196616 | tf_op jit(solution)/shard_map/ppermute | solution.py:329
  59.3 5.1 %collective-permute-done.12.refs_3_ = f32[64,256]{1,0:T(8,128)S(1)} collective-permute-done((f32[64,256]{1,0:T(8,128)S(1)}, f32[64,256]{1,0:T(8,128)S(1)}, u32[]{:S(2)}, u32[]{:S(2)}) %collective-permute-start.12) | collective-permute-done | bytes 65568 | tf_op jit(solution)/shard_map/ppermute | solution.py:329
  64.4 2.6 %collective-permute-start.17 = (f32[4,64,256]{2,1,0:T(8,128)S(1)}, f32[4,64,256]{2,1,0:T(8,128)S(1)}, u32[]{:S(2)}, u32[]{:S(2)}) collective-permute-start(f32[4,64,256]{2,1,0:T(8,128)S(1)} %get-tuple-element.93), channel_id=1, source_target_pairs={{0,1},{1,0},{2,3},{3,2},{4,5},{5,4},{6,7},{7,6},{8,9},{9,8},{10,11... | collective-permute-start | bytes 786440 | tf_op jit(solution)/shard_map/ppermute | solution.py:329
  67.0 1.2 %collective-permute-start.18 = (f32[4,64,256]{2,1,0:T(8,128)S(1)}, f32[4,64,256]{2,1,0:T(8,128)S(1)}, u32[]{:S(2)}, u32[]{:S(2)}) collective-permute-start(f32[4,64,256]{2,1,0:T(8,128)S(1)} %get-tuple-element.94), channel_id=1, source_target_pairs={{0,2},{1,3},{2,0},{3,1},{4,6},{5,7},{6,4},{7,5},{8,10},{9,11},{10,... | collective-permute-start | bytes 786440 | tf_op jit(solution)/shard_map/ppermute | solution.py:329
  68.2 0.9 collective-permute-start.15
  69.3 2.0 %collective-permute-start.20 = (f32[2,64,256]{2,1,0:T(8,128)S(1)}, f32[2,64,256]{2,1,0:T(8,128)S(1)}, u32[]{:S(2)}, u32[]{:S(2)}) collective-permute-start(f32[2,64,256]{2,1,0:T(8,128)S(1)} %get-tuple-element.99), channel_id=1, source_target_pairs={{0,1},{1,0},{2,3},{3,2},{4,5},{5,4},{6,7},{7,6},{8,9},{9,8},{10,11... | collective-permute-start | bytes 393224 | tf_op jit(solution)/shard_map/ppermute | solution.py:329
  71.3 1.9 %collective-permute-done.15.refs_1_ = f32[2,64,256]{2,1,0:T(8,128)S(1)} collective-permute-done((f32[2,64,256]{2,1,0:T(8,128)S(1)}, f32[2,64,256]{2,1,0:T(8,128)S(1)}, u32[]{:S(2)}, u32[]{:S(2)}) %collective-permute-start.15) | collective-permute-done | bytes 131104 | tf_op jit(solution)/shard_map/ppermute | solution.py:329
  73.2 1.6 %collective-permute-start.21 = (f32[2,64,256]{2,1,0:T(8,128)S(1)}, f32[2,64,256]{2,1,0:T(8,128)S(1)}, u32[]{:S(2)}, u32[]{:S(2)}) collective-permute-start(f32[2,64,256]{2,1,0:T(8,128)S(1)} %get-tuple-element.100), channel_id=1, source_target_pairs={{0,2},{1,3},{2,0},{3,1},{4,6},{5,7},{6,4},{7,5},{8,10},{9,11},{10,... | collective-permute-start | bytes 393224 | tf_op jit(solution)/shard_map/ppermute | solution.py:329
  74.8 3.4 %collective-permute-start.24 = (f32[4,64,256]{2,1,0:T(8,128)S(1)}, f32[4,64,256]{2,1,0:T(8,128)S(1)}, u32[]{:S(2)}, u32[]{:S(2)}) collective-permute-start(f32[4,64,256]{2,1,0:T(8,128)S(1)} %get-tuple-element.105), channel_id=1, source_target_pairs={{0,24},{1,25},{2,26},{3,27},{4,28},{5,29},{6,30},{7,31},{8,16},{9,... | collective-permute-start | bytes 786440 | tf_op jit(solution)/shard_map/ppermute | solution.py:329
  78.3 5.7 %inverse.1 = (f32[8,128]{1,0:T(8,128)S(1)}, f32[64,256]{1,0:T(8,128)S(1)}, f32[64,64]{1,0:T(8,128)S(1)}) custom-call(f32[8,128]{1,0:T(8,128)S(1)} %get-tuple-element.95._token, f32[64,256]{1,0:T(8,128)S(1)} %get-tuple-element.96.refs_0_, f32[64,256]{1,0:T(8,128)S(1)} %collective-permute-done.19.refs_1_), custom_call_target="tpu_custom_call" | custom-call | flops 1 | bytes 1 | tf_op jit(solution)/shard_map/inverse/pallas_call | solution.py:48
  84.1 1.1 %collective-permute-start.26 = (f32[4,64,256]{2,1,0:T(8,128)S(1)}, f32[4,64,256]{2,1,0:T(8,128)S(1)}, u32[]{:S(2)}, u32[]{:S(2)}) collective-permute-start(f32[4,64,256]{2,1,0:T(8,128)S(1)} %get-tuple-element.111), channel_id=1, source_target_pairs={{0,8},{1,9},{2,10},{3,11},{4,12},{5,13},{6,14},{7,15},{8,0},{9,1},... | collective-permute-start | bytes 786440 | tf_op jit(solution)/shard_map/ppermute | solution.py:329
  85.2 1.2 %collective-permute-start.22 = (f32[2,64,256]{2,1,0:T(8,128)S(1)}, f32[2,64,256]{2,1,0:T(8,128)S(1)}, u32[]{:S(2)}, u32[]{:S(2)}) collective-permute-start(f32[2,64,256]{2,1,0:T(8,128)S(1)} %get-tuple-element.103), channel_id=1, source_target_pairs={{0,1},{1,0},{2,3},{3,2},{4,5},{5,4},{6,7},{7,6},{8,9},{9,8},{10,11... | collective-permute-start | bytes 393224 | tf_op jit(solution)/shard_map/ppermute | solution.py:329
  86.4 0.9 collective-permute-start.23
  87.3 3.0 %collective-permute-done.22.refs_1_ = f32[2,64,256]{2,1,0:T(8,128)S(1)} collective-permute-done((f32[2,64,256]{2,1,0:T(8,128)S(1)}, f32[2,64,256]{2,1,0:T(8,128)S(1)}, u32[]{:S(2)}, u32[]{:S(2)}) %collective-permute-start.22) | collective-permute-done | bytes 131104 | tf_op jit(solution)/shard_map/ppermute | solution.py:329
  90.3 1.1 %collective-permute-done.23.refs_2_ = f32[2,64,256]{2,1,0:T(8,128)S(1)} collective-permute-done((f32[2,64,256]{2,1,0:T(8,128)S(1)}, f32[2,64,256]{2,1,0:T(8,128)S(1)}, u32[]{:S(2)}, u32[]{:S(2)}) %collective-permute-start.23) | collective-permute-done | bytes 131104 | tf_op jit(solution)/shard_map/ppermute | solution.py:329
  91.4 8.1 %collective-permute-done.25.refs_1_ = f32[4,64,256]{2,1,0:T(8,128)S(1)} collective-permute-done((f32[4,64,256]{2,1,0:T(8,128)S(1)}, f32[4,64,256]{2,1,0:T(8,128)S(1)}, u32[]{:S(2)}, u32[]{:S(2)}) %collective-permute-start.25) | collective-permute-done | bytes 262176 | tf_op jit(solution)/shard_map/ppermute | solution.py:329
  99.6 2.0 %finish.1 = (f32[8,128]{1,0:T(8,128)}, f32[64,256]{1,0:T(8,128)}, f32[256,256]{1,0:T(8,128)}) custom-call(f32[8,128]{1,0:T(8,128)S(1)} %get-tuple-element.109._token, f32[4,64,256]{2,1,0:T(8,128)S(1)} %get-tuple-element.110.refs_0_, f32[4,64,256]{2,1,0:T(8,128)S(1)} %collective-permute-done.26.refs_1_, f32[64,256]{1,0:T(8,128)S(1)} %get-tuple-element.112.refs_2_, ...), custom_call_target="tpu_custom_call" | custom-call | flops 1 | bytes 1 | tf_op jit(solution)/shard_map/finish/pallas_call | solution.py:48
  (48 shorter events, 5.3 us)
Async XLA Ops:
  0.7 1.6 %copy-start = (f32[2048,256]{1,0:T(8,128)S(1)}, f32[2048,256]{1,0:T(8,128)}, u32[]{:S(2)}) copy-start(f32[2048,256]{1,0:T(8,128)} %rest_0_.1) | copy-start | bytes 6291460
  2.3 0.7 copy-start.1
  3.0 0.7 copy-start.2
  16.3 14.2 %collective-permute-start = (f32[17,128,256]{2,1,0:T(8,128)}, f32[17,128,256]{2,1,0:T(8,128)S(1)}, u32[]{:S(2)}, u32[]{:S(2)}) collective-permute-start(f32[17,128,256]{2,1,0:T(8,128)} %get-tuple-element.63), channel_id=1, source_target_pairs={{0,4},{1,5},{2,6},{3,7},{4,0},{5,1},{6,2},{7,3},{8,12},{9,13},{10,... | collective-permute-start | bytes 6684680 | tf_op jit(solution)/shard_map/ppermute | solution.py:329
  30.6 19.4 %collective-permute-start.4 = (f32[4,64,256]{2,1,0:T(8,128)S(1)}, f32[4,64,256]{2,1,0:T(8,128)S(1)}, u32[]{:S(2)}, u32[]{:S(2)}) collective-permute-start(f32[4,64,256]{2,1,0:T(8,128)S(1)} %get-tuple-element.69), channel_id=1, source_target_pairs={{0,1},{1,0},{2,3},{3,2},{4,5},{5,4},{6,7},{7,6},{8,9},{9,8},{10,11... | collective-permute-start | bytes 786440 | tf_op jit(solution)/shard_map/ppermute | solution.py:329
  32.9 19.4 %collective-permute-start.5 = (f32[4,64,256]{2,1,0:T(8,128)S(1)}, f32[4,64,256]{2,1,0:T(8,128)S(1)}, u32[]{:S(2)}, u32[]{:S(2)}) collective-permute-start(f32[4,64,256]{2,1,0:T(8,128)S(1)} %get-tuple-element.70), channel_id=1, source_target_pairs={{0,2},{1,3},{2,0},{3,1},{4,6},{5,7},{6,4},{7,5},{8,10},{9,11},{10,... | collective-permute-start | bytes 786440 | tf_op jit(solution)/shard_map/ppermute | solution.py:329
  35.6 4.3 %collective-permute-start.1 = (f32[64,256]{1,0:T(8,128)S(1)}, f32[64,256]{1,0:T(8,128)S(1)}, u32[]{:S(2)}, u32[]{:S(2)}) collective-permute-start(f32[64,256]{1,0:T(8,128)S(1)} %get-tuple-element.66.refs_0_), channel_id=1, source_target_pairs={{0,8},{1,9},{2,10},{3,11},{4,12},{5,13},{6,14},{7,15},{8,0},{9,1},... | collective-permute-start | bytes 196616 | tf_op jit(solution)/shard_map/ppermute | solution.py:329
  35.7 21.3 %collective-permute-start.6 = (f32[4,64,256]{2,1,0:T(8,128)S(1)}, f32[4,64,256]{2,1,0:T(8,128)S(1)}, u32[]{:S(2)}, u32[]{:S(2)}) collective-permute-start(f32[4,64,256]{2,1,0:T(8,128)S(1)} %get-tuple-element.74), channel_id=1, source_target_pairs={{0,1},{1,0},{2,3},{3,2},{4,5},{5,4},{6,7},{7,6},{8,9},{9,8},{10,11... | collective-permute-start | bytes 786440 | tf_op jit(solution)/shard_map/ppermute | solution.py:329
  36.9 5.2 %collective-permute-start.2 = (f32[64,256]{1,0:T(8,128)S(1)}, f32[64,256]{1,0:T(8,128)S(1)}, u32[]{:S(2)}, u32[]{:S(2)}) collective-permute-start(f32[64,256]{1,0:T(8,128)S(1)} %get-tuple-element.66.refs_0_), channel_id=1, source_target_pairs={{0,16},{1,17},{2,18},{3,19},{4,20},{5,21},{6,22},{7,23},{8,24},{9,... | collective-permute-start | bytes 196616 | tf_op jit(solution)/shard_map/ppermute | solution.py:329
  39.9 17.9 %collective-permute-start.7 = (f32[4,64,256]{2,1,0:T(8,128)S(1)}, f32[4,64,256]{2,1,0:T(8,128)S(1)}, u32[]{:S(2)}, u32[]{:S(2)}) collective-permute-start(f32[4,64,256]{2,1,0:T(8,128)S(1)} %get-tuple-element.75), channel_id=1, source_target_pairs={{0,2},{1,3},{2,0},{3,1},{4,6},{5,7},{6,4},{7,5},{8,10},{9,11},{10,... | collective-permute-start | bytes 786440 | tf_op jit(solution)/shard_map/ppermute | solution.py:329
  42.1 7.8 %collective-permute-start.3 = (f32[64,256]{1,0:T(8,128)S(1)}, f32[64,256]{1,0:T(8,128)S(1)}, u32[]{:S(2)}, u32[]{:S(2)}) collective-permute-start(f32[64,256]{1,0:T(8,128)S(1)} %get-tuple-element.66.refs_0_), channel_id=1, source_target_pairs={{0,24},{1,25},{2,26},{3,27},{4,28},{5,29},{6,30},{7,31},{8,16},{9,... | collective-permute-start | bytes 196616 | tf_op jit(solution)/shard_map/ppermute | solution.py:329
  49.9 4.3 %collective-permute-start.10 = (f32[64,256]{1,0:T(8,128)S(1)}, f32[64,256]{1,0:T(8,128)S(1)}, u32[]{:S(2)}, u32[]{:S(2)}) collective-permute-start(f32[64,256]{1,0:T(8,128)S(1)} %get-tuple-element.82.refs_0_), channel_id=1, source_target_pairs={{0,1},{1,0},{2,3},{3,2},{4,5},{5,4},{6,7},{7,6},{8,9},{9,8},{10,11... | collective-permute-start | bytes 196616 | tf_op jit(solution)/shard_map/ppermute | solution.py:329
  50.0 5.8 %collective-permute-start.11 = (f32[64,256]{1,0:T(8,128)S(1)}, f32[64,256]{1,0:T(8,128)S(1)}, u32[]{:S(2)}, u32[]{:S(2)}) collective-permute-start(f32[64,256]{1,0:T(8,128)S(1)} %get-tuple-element.82.refs_0_), channel_id=1, source_target_pairs={{0,2},{1,3},{2,0},{3,1},{4,6},{5,7},{6,4},{7,5},{8,10},{9,11},{10,... | collective-permute-start | bytes 196616 | tf_op jit(solution)/shard_map/ppermute | solution.py:329
  52.5 16.5 %collective-permute-start.13 = (f32[4,64,256]{2,1,0:T(8,128)S(1)}, f32[4,64,256]{2,1,0:T(8,128)S(1)}, u32[]{:S(2)}, u32[]{:S(2)}) collective-permute-start(f32[4,64,256]{2,1,0:T(8,128)S(1)} %get-tuple-element.85), channel_id=1, source_target_pairs={{0,1},{1,0},{2,3},{3,2},{4,5},{5,4},{6,7},{7,6},{8,9},{9,8},{10,11... | collective-permute-start | bytes 786440 | tf_op jit(solution)/shard_map/ppermute | solution.py:329
  54.2 12.8 %collective-permute-start.8 = (f32[2,64,256]{2,1,0:T(8,128)S(1)}, f32[2,64,256]{2,1,0:T(8,128)S(1)}, u32[]{:S(2)}, u32[]{:S(2)}) collective-permute-start(f32[2,64,256]{2,1,0:T(8,128)S(1)} %get-tuple-element.79), channel_id=1, source_target_pairs={{0,1},{1,0},{2,3},{3,2},{4,5},{5,4},{6,7},{7,6},{8,9},{9,8},{10,11... | collective-permute-start | bytes 393224 | tf_op jit(solution)/shard_map/ppermute | solution.py:329
  55.7 13.5 %collective-permute-start.14 = (f32[4,64,256]{2,1,0:T(8,128)S(1)}, f32[4,64,256]{2,1,0:T(8,128)S(1)}, u32[]{:S(2)}, u32[]{:S(2)}) collective-permute-start(f32[4,64,256]{2,1,0:T(8,128)S(1)} %get-tuple-element.86), channel_id=1, source_target_pairs={{0,2},{1,3},{2,0},{3,1},{4,6},{5,7},{6,4},{7,5},{8,10},{9,11},{10,... | collective-permute-start | bytes 786440 | tf_op jit(solution)/shard_map/ppermute | solution.py:329
  57.0 11.2 %collective-permute-start.9 = (f32[2,64,256]{2,1,0:T(8,128)S(1)}, f32[2,64,256]{2,1,0:T(8,128)S(1)}, u32[]{:S(2)}, u32[]{:S(2)}) collective-permute-start(f32[2,64,256]{2,1,0:T(8,128)S(1)} %get-tuple-element.80), channel_id=1, source_target_pairs={{0,2},{1,3},{2,0},{3,1},{4,6},{5,7},{6,4},{7,5},{8,10},{9,11},{10,... | collective-permute-start | bytes 393224 | tf_op jit(solution)/shard_map/ppermute | solution.py:329
  57.7 6.7 %collective-permute-start.12 = (f32[64,256]{1,0:T(8,128)S(1)}, f32[64,256]{1,0:T(8,128)S(1)}, u32[]{:S(2)}, u32[]{:S(2)}) collective-permute-start(f32[64,256]{1,0:T(8,128)S(1)} %get-tuple-element.82.refs_0_), channel_id=1, source_target_pairs={{0,3},{1,2},{2,1},{3,0},{4,7},{5,6},{6,5},{7,4},{8,11},{9,10},{10,... | collective-permute-start | bytes 196616 | tf_op jit(solution)/shard_map/ppermute | solution.py:329
  64.4 10.4 %collective-permute-start.17 = (f32[4,64,256]{2,1,0:T(8,128)S(1)}, f32[4,64,256]{2,1,0:T(8,128)S(1)}, u32[]{:S(2)}, u32[]{:S(2)}) collective-permute-start(f32[4,64,256]{2,1,0:T(8,128)S(1)} %get-tuple-element.93), channel_id=1, source_target_pairs={{0,1},{1,0},{2,3},{3,2},{4,5},{5,4},{6,7},{7,6},{8,9},{9,8},{10,11... | collective-permute-start | bytes 786440 | tf_op jit(solution)/shard_map/ppermute | solution.py:329
  67.0 11.3 %collective-permute-start.18 = (f32[4,64,256]{2,1,0:T(8,128)S(1)}, f32[4,64,256]{2,1,0:T(8,128)S(1)}, u32[]{:S(2)}, u32[]{:S(2)}) collective-permute-start(f32[4,64,256]{2,1,0:T(8,128)S(1)} %get-tuple-element.94), channel_id=1, source_target_pairs={{0,2},{1,3},{2,0},{3,1},{4,6},{5,7},{6,4},{7,5},{8,10},{9,11},{10,... | collective-permute-start | bytes 786440 | tf_op jit(solution)/shard_map/ppermute | solution.py:329
  68.2 5.0 %collective-permute-start.15 = (f32[2,64,256]{2,1,0:T(8,128)S(1)}, f32[2,64,256]{2,1,0:T(8,128)S(1)}, u32[]{:S(2)}, u32[]{:S(2)}) collective-permute-start(f32[2,64,256]{2,1,0:T(8,128)S(1)} %get-tuple-element.89), channel_id=1, source_target_pairs={{0,1},{1,0},{2,3},{3,2},{4,5},{5,4},{6,7},{7,6},{8,9},{9,8},{10,11... | collective-permute-start | bytes 393224 | tf_op jit(solution)/shard_map/ppermute | solution.py:329
  69.1 5.7 %collective-permute-start.16 = (f32[2,64,256]{2,1,0:T(8,128)S(1)}, f32[2,64,256]{2,1,0:T(8,128)S(1)}, u32[]{:S(2)}, u32[]{:S(2)}) collective-permute-start(f32[2,64,256]{2,1,0:T(8,128)S(1)} %get-tuple-element.90), channel_id=1, source_target_pairs={{0,2},{1,3},{2,0},{3,1},{4,6},{5,7},{6,4},{7,5},{8,10},{9,11},{10,... | collective-permute-start | bytes 393224 | tf_op jit(solution)/shard_map/ppermute | solution.py:329
  69.3 14.8 %collective-permute-start.20 = (f32[2,64,256]{2,1,0:T(8,128)S(1)}, f32[2,64,256]{2,1,0:T(8,128)S(1)}, u32[]{:S(2)}, u32[]{:S(2)}) collective-permute-start(f32[2,64,256]{2,1,0:T(8,128)S(1)} %get-tuple-element.99), channel_id=1, source_target_pairs={{0,1},{1,0},{2,3},{3,2},{4,5},{5,4},{6,7},{7,6},{8,9},{9,8},{10,11... | collective-permute-start | bytes 393224 | tf_op jit(solution)/shard_map/ppermute | solution.py:329
  73.2 10.9 %collective-permute-start.21 = (f32[2,64,256]{2,1,0:T(8,128)S(1)}, f32[2,64,256]{2,1,0:T(8,128)S(1)}, u32[]{:S(2)}, u32[]{:S(2)}) collective-permute-start(f32[2,64,256]{2,1,0:T(8,128)S(1)} %get-tuple-element.100), channel_id=1, source_target_pairs={{0,2},{1,3},{2,0},{3,1},{4,6},{5,7},{6,4},{7,5},{8,10},{9,11},{10,... | collective-permute-start | bytes 393224 | tf_op jit(solution)/shard_map/ppermute | solution.py:329
  74.8 3.5 %collective-permute-start.19 = (f32[64,256]{1,0:T(8,128)S(1)}, f32[64,256]{1,0:T(8,128)S(1)}, u32[]{:S(2)}, u32[]{:S(2)}) collective-permute-start(f32[64,256]{1,0:T(8,128)S(1)} %get-tuple-element.96.refs_0_), channel_id=1, source_target_pairs={{0,4},{1,5},{2,6},{3,7},{4,0},{5,1},{6,2},{7,3},{8,12},{9,13},{10,... | collective-permute-start | bytes 196616 | tf_op jit(solution)/shard_map/ppermute | solution.py:329
  74.8 16.5 %collective-permute-start.24 = (f32[4,64,256]{2,1,0:T(8,128)S(1)}, f32[4,64,256]{2,1,0:T(8,128)S(1)}, u32[]{:S(2)}, u32[]{:S(2)}) collective-permute-start(f32[4,64,256]{2,1,0:T(8,128)S(1)} %get-tuple-element.105), channel_id=1, source_target_pairs={{0,24},{1,25},{2,26},{3,27},{4,28},{5,29},{6,30},{7,31},{8,16},{9,... | collective-permute-start | bytes 786440 | tf_op jit(solution)/shard_map/ppermute | solution.py:329
  78.3 21.3 %collective-permute-start.25 = (f32[4,64,256]{2,1,0:T(8,128)S(1)}, f32[4,64,256]{2,1,0:T(8,128)S(1)}, u32[]{:S(2)}, u32[]{:S(2)}) collective-permute-start(f32[4,64,256]{2,1,0:T(8,128)S(1)} %get-tuple-element.108), channel_id=1, source_target_pairs={{0,16},{1,17},{2,18},{3,19},{4,20},{5,21},{6,22},{7,23},{8,24},{9,... | collective-permute-start | bytes 786440 | tf_op jit(solution)/shard_map/ppermute | solution.py:329
  84.1 15.4 %collective-permute-start.26 = (f32[4,64,256]{2,1,0:T(8,128)S(1)}, f32[4,64,256]{2,1,0:T(8,128)S(1)}, u32[]{:S(2)}, u32[]{:S(2)}) collective-permute-start(f32[4,64,256]{2,1,0:T(8,128)S(1)} %get-tuple-element.111), channel_id=1, source_target_pairs={{0,8},{1,9},{2,10},{3,11},{4,12},{5,13},{6,14},{7,15},{8,0},{9,1},... | collective-permute-start | bytes 786440 | tf_op jit(solution)/shard_map/ppermute | solution.py:329
  85.2 5.1 %collective-permute-start.22 = (f32[2,64,256]{2,1,0:T(8,128)S(1)}, f32[2,64,256]{2,1,0:T(8,128)S(1)}, u32[]{:S(2)}, u32[]{:S(2)}) collective-permute-start(f32[2,64,256]{2,1,0:T(8,128)S(1)} %get-tuple-element.103), channel_id=1, source_target_pairs={{0,1},{1,0},{2,3},{3,2},{4,5},{5,4},{6,7},{7,6},{8,9},{9,8},{10,11... | collective-permute-start | bytes 393224 | tf_op jit(solution)/shard_map/ppermute | solution.py:329
  86.4 5.0 %collective-permute-start.23 = (f32[2,64,256]{2,1,0:T(8,128)S(1)}, f32[2,64,256]{2,1,0:T(8,128)S(1)}, u32[]{:S(2)}, u32[]{:S(2)}) collective-permute-start(f32[2,64,256]{2,1,0:T(8,128)S(1)} %get-tuple-element.104), channel_id=1, source_target_pairs={{0,2},{1,3},{2,0},{3,1},{4,6},{5,7},{6,4},{7,5},{8,10},{9,11},{10,... | collective-permute-start | bytes 393224 | tf_op jit(solution)/shard_map/ppermute | solution.py:329

commit v3 on v0

v3 whole, which is shorter than its diff:
```python
import functools

import jax
import jax.numpy as jnp
from jax import lax
from jax.experimental import pallas as pl
from jax.experimental.pallas import tpu as pltpu
from jax.sharding import PartitionSpec as P

ROWS_DEV = 256
UNROLL = 8
F32 = jnp.float32
BF16 = jnp.bfloat16
AXES = ("term", "doc")
TOKEN = (8, 128)
LIMIT = pltpu.CompilerParams(vmem_limit_bytes=24 * 2**20)
LARGE = pltpu.CompilerParams(vmem_limit_bytes=44 * 2**20)
TINY = pl.CostEstimate(flops=1, bytes_accessed=1, transcendentals=0)
ANY = pl.BlockSpec(memory_space=pl.ANY)
HBM = pl.BlockSpec(memory_space=pltpu.HBM)
SMEM = pl.BlockSpec(memory_space=pltpu.SMEM)
VMEM = pl.BlockSpec(memory_space=pltpu.VMEM)


def shaped(shape, dtype=F32):
    return jax.ShapeDtypeStruct(tuple(shape), dtype)


def split(v):
    hi = v.astype(BF16)
    lo = (v - hi.astype(F32)).astype(BF16)
    return hi, lo


def hdot(a, b, dims):
    return lax.dot_general(a, b, (dims, ((), ())), precision=lax.Precision.HIGHEST, preferred_element_type=F32)


def in_order(kernel, last, _token, *refs):
    kernel(*refs[:last], *refs[last + 1 :])
    refs[last][...] = jnp.zeros_like(refs[last])


class Queue:
    def __init__(self, token):
        self.token = token

    def call(self, name, kernel, out_shape, args):
        got = pl.pallas_call(
            functools.partial(in_order, kernel, len(args)),
            out_shape=(shaped(TOKEN),) + tuple(out_shape),
            in_specs=[VMEM] * (1 + len(args)),
            out_specs=(VMEM,) * (1 + len(out_shape)),
            compiler_params=LIMIT,
            cost_estimate=TINY,
            name=name,
        )(self.token, *args)
        self.token = got[0]
        return got[1:]


def products_kernel(slots, code_ref, tiles, top_ref, low_ref, *rest):
    if len(rest) == 7:
        away, (blocks, anchor_out, buf, order, flag, in_sem) = True, rest[1:]
        anchor_out[...] = jnp.zeros_like(anchor_out)
    else:
        away, (anchor_in, blocks, anchor_out, token, buf, order, flag, in_sem) = False, rest
        token[...] = jnp.zeros_like(token)
        anchor_out[...] = anchor_in[...]
    n_tiles, tile = tiles.shape[:2]
    width = top_ref.shape[1]

    def wanted(code):
        return ((code >> 10) & 1) == (1 if away else 0)

    def fetch(k, i):
        return pltpu.make_async_copy(tiles.at[k], buf.at[i], in_sem.at[i])

    def scan(k, count):
        code = code_ref[k]
        mine = wanted(code)
        order[count] = code

        @pl.when(mine)
        def _():
            fetch(k, count).start()

        return count + mine.astype(jnp.int32)

    count = lax.fori_loop(0, n_tiles, scan, jnp.int32(0), unroll=4)
    blocks[...] = jnp.zeros_like(blocks)
    flag[...] = jnp.zeros_like(flag)

    def product(i, code):
        hi, lo = split(buf[i])
        rows = pl.ds(pl.multiple_of((code >> 12) * tile, tile), tile)
        w = jnp.concatenate([top_ref[rows, :], low_ref[rows, :]], axis=1)
        lhs = jnp.concatenate([hi, lo], axis=1)
        both = jnp.dot(lhs, jnp.concatenate([w, w], axis=0), preferred_element_type=F32)
        return both[:, :width] + both[:, width:]

    def put(code, prod):
        slot = code & 1023
        blocks[slot] += prod
        flag[pl.ds(slot, 1), :] = jnp.full((1, width), ((code >> 11) & 1).astype(F32), F32)

    def several(base, many):
        for u in range(many):
            fetch(0, base + u).wait()
        codes = [order[base + u] for u in range(many)]
        prods = [product(base + u, codes[u]) for u in range(many)]
        for code, prod in zip(codes, prods):
            put(code, prod)

    whole = count // UNROLL

    def group(j, carry):
        several(j * UNROLL, UNROLL)
        return carry

    def single(i, carry):
        several(i, 1)
        return carry

    lax.fori_loop(0, whole, group, 0)
    lax.fori_loop(whole * UNROLL, count, single, 0)

    def pick(i, carry):
        code = code_ref[n_tiles + i]

        @pl.when(wanted(code))
        def _():
            slot = code & 1023
            value = blocks[slot, pl.ds(code >> 12, 1), :]
            same = flag[pl.ds(slot, 1), :] == ((code >> 11) & 1).astype(F32)
            anchor_out[pl.ds(i, 1), :] = jnp.where(same, value, 0.0)

        return carry

    lax.fori_loop(0, anchor_out.shape[0], pick, 0)
    blocks[slots, pl.ds(0, slots), :] = flag[pl.ds(0, slots), :]


def products(slots, codes, tiles, top, low, more):
    n_tiles, tile = tiles.shape[:2]
    width = top.shape[1]
    away = len(more) == 0
    outs = [shaped((slots + 1, tile, width)), shaped((codes.shape[0] - n_tiles, width))]
    if not away:
        outs.append(shaped(TOKEN))
    return pl.pallas_call(
        functools.partial(products_kernel, slots),
        out_shape=outs,
        in_specs=[SMEM, HBM, VMEM, VMEM] + [VMEM] * max(1, len(more)),
        out_specs=[VMEM] * len(outs),
        scratch_shapes=[
            pltpu.VMEM((n_tiles, tile, tile), F32),
            pltpu.SMEM((n_tiles + 8,), jnp.int32),
            pltpu.VMEM((slots + 8, width), F32),
            pltpu.SemaphoreType.DMA((n_tiles,)),
        ],
        compiler_params=LARGE,
        cost_estimate=pl.CostEstimate(flops=8 * 10**9, bytes_accessed=5 * 2**20, transcendentals=0),
        name="products_away" if away else "products_here",
    )(codes, tiles, top, low, *(more or (jnp.zeros(TOKEN, F32),)))


def encode(n_doc, me, block, extra, per):
    rel = lax.bitwise_xor(block // per, me)
    core = (rel // n_doc) & 1
    slot = (rel // (2 * n_doc)) * n_doc + (rel & (n_doc - 1))
    return slot | (core << 10) | ((block % per) << 11) | (extra << 12)


def spread_kernel(zs, n_y, own, got, stay, send_x, *send_y):
    slots = own.shape[0] - 1
    half = own.shape[1] // 2
    n_x = len(zs) * 2 * n_y
    for i, dz in enumerate(zs):
        for dy in range(n_y):
            for dx in range(2):
                slot = (dz * n_y + dy) * 2 + dx
                a, b = own[slot], got[slot]
                up_a = a * own[slots, pl.ds(slot, 1), :]
                up_b = b * got[slots, pl.ds(slot, 1), :]
                for s, value in enumerate(((a - up_a) + (b - up_b), up_a + up_b)):
                    at = 2 * (i * n_y + dy) + s
                    if dx:
                        send_x[at] = value[:half]
                    else:
                        stay[at] = value[:half]
                    at = 2 * (i * 2 + dx) + s
                    if dy:
                        send_y[dy - 1][at] = value[half:]
                    else:
                        stay[n_x + at] = value[half:]


def spread(queue, zs, n_y, own, got):
    half, width = own.shape[1] // 2, own.shape[2]
    n_x, n_yy = len(zs) * 2 * n_y, len(zs) * 4
    outs = (shaped((n_x + n_yy, half, width)), shaped((n_x, half, width))) + (shaped((n_yy, half, width)),) * (n_y - 1)
    stay, send_x, *send_y = queue.call("spread", functools.partial(spread_kernel, zs, n_y), outs, (own, got))
    return stay, send_x, send_y


def join_kernel(n, n_y, stay, got_x, *refs):
    got_y = refs[: n_y - 1]
    keep, send_x = refs[n_y - 1 : n_y + 1]
    send_y = refs[n_y + 1 :]
    n_x = n * 2 * n_y
    for i in range(n):
        for s in range(2):
            for dy in range(n_y):
                at = 2 * (i * n_y + dy) + s
                value = stay[at] + got_x[at]
                if dy:
                    send_y[dy - 1][2 * i + s] = value
                else:
                    keep[4 * i + s] = value
            for dx in range(2):
                at = 2 * (i * 2 + dx) + s
                value = stay[n_x + at]
                for ref in got_y:
                    value = value + ref[at]
                if dx:
                    send_x[2 * i + s] = value
                else:
                    keep[4 * i + 2 + s] = value


def join(queue, n, n_y, stay, got_x, got_y):
    half, width = stay.shape[1:]
    outs = (shaped((4 * n, half, width)),) + (shaped((2 * n, half, width)),) * n_y
    keep, send_x, *send_y = queue.call("join", functools.partial(join_kernel, n, n_y), outs, (stay, got_x, *got_y))
    return keep, send_x, send_y


def merge_kernel(n, n_y, n_far, keep, got_x, *refs):
    got_y, far, outs = refs[: n_y - 1], refs[n_y - 1 : n_y - 1 + n_far], refs[n_y - 1 + n_far :]
    for i, out in enumerate(outs):
        for s in range(2):
            x = keep[4 * i + s]
            y = keep[4 * i + 2 + s] + got_x[2 * i + s]
            for ref in got_y:
                x = x + ref[2 * i + s]
            if i == n - 1:
                for ref in far:
                    x = x + ref[s]
                    y = y + ref[2 + s]
            out[s] = x
            out[2 + s] = y


def merge(queue, n, n_y, keep, got_x, got_y, far=()):
    outs = (shaped((4,) + keep.shape[1:]),) * n
    return queue.call("merge", functools.partial(merge_kernel, n, n_y, len(far)), outs, (keep, got_x, *got_y, *far))


def total_kernel(*refs):
    total = refs[0][...]
    for ref in refs[1:-1]:
        total = total + ref[...]
    refs[-1][...] = total


def total(queue, values):
    return queue.call("total", total_kernel, (shaped(values[0].shape),), values)[0]


def inverse_kernel(n_in, *refs):
    ins, (rows_ref, inv_ref) = refs[:n_in], refs[n_in:]
    rows = ins[0][...]
    for ref in ins[1:]:
        rows = rows + ref[...]
    rows_ref[...] = rows
    count = rows.shape[0]
    m = hdot(rows, rows, ((1,), (1,)))
    at_row = lax.broadcasted_iota(jnp.int32, (count, count), 0)
    at_col = lax.broadcasted_iota(jnp.int32, (count, count), 1)
    diagonal = at_row == at_col
    ridge = 0.001 * jnp.sum(jnp.where(diagonal, m, 0.0)) / count
    m = jnp.where(diagonal, m + ridge, m)
    for k in range(count):
        row = m[k : k + 1, :]
        col = m[:, k : k + 1]
        scale = 1.0 / m[k : k + 1, k : k + 1]
        row = jnp.where(at_col[:1] == k, 1.0, row) * scale
        m = jnp.where(at_row == k, row, jnp.where(at_col == k, 0.0, m) - col * row)
    inv_ref[...] = m


def inverse(queue, parts):
    count, width = parts[0].shape
    return queue.call("inverse", functools.partial(inverse_kernel, len(parts)), (shaped((count, width)), shaped((count, count))), parts)


def finish_kernel(n_far, near, *refs):
    x, y = near[:2], near[2:]
    for ref in refs[:n_far]:
        x = x + ref[:2]
        y = y + ref[2:]
    rows_ref, inv_ref, coef_ref, res_ref = refs[n_far:]
    owned = jnp.concatenate([x[0], y[0], x[1], y[1]], axis=0)
    rows = rows_ref[...]
    project = hdot(rows, owned, ((1,), (1,)))
    coef = hdot(inv_ref[...], project, ((1,), (0,)))
    coef_ref[...] = coef
    res_ref[...] = owned - hdot(coef, rows, ((0,), (0,)))


def finish(queue, near, far, rows, inv):
    half, width = near.shape[1:]
    outs = (shaped((rows.shape[0], 4 * half)), shaped((4 * half, width)))
    coef, res = queue.call("finish", functools.partial(finish_kernel, len(far)), outs, (near, *far, rows, inv))
    return coef.T, res


def body(n_term, n_doc, tiles, coords, sketch, anchors):
    devices = n_term * n_doc
    n_y, n_z = n_doc // 2, n_term // 2
    tile, width = tiles.shape[1], sketch.shape[1]
    per = ROWS_DEV // tile
    me = lax.axis_index(AXES).astype(jnp.int32)
    doc_base = lax.axis_index("doc").astype(jnp.int32) * (sketch.shape[0] // tile)

    def swap(v, mask):
        return lax.ppermute(v, AXES, [(i, i ^ mask) for i in range(devices)])

    def swap_y(values):
        return [swap(v, 2 * (k + 1)) for k, v in enumerate(values)]

    codes = jnp.concatenate([
        encode(n_doc, me, coords[:, 0], coords[:, 1] - doc_base, per),
        encode(n_doc, me, anchors // tile, anchors % tile, per),
    ])
    top = lax.reduce_precision(sketch, 8, 7)
    low = (sketch - top).astype(BF16)
    top = top.astype(BF16)
    slots = n_z * n_doc
    away, part = products(slots, codes, tiles, top, low, ())
    got = swap(away, n_doc)
    here, part, token = products(slots, codes, tiles, top, low, (part,))
    queue = Queue(token)

    def do_spread(zs):
        stay, send_x, send_y = spread(queue, zs, n_y, here, got)
        return stay, swap(send_x, 1), swap_y(send_y)

    def do_join(zs, state):
        keep, send_x, send_y = join(queue, len(zs), n_y, *state)
        return keep, swap(send_x, 1), swap_y(send_y)

    far_zs, mid_zs = tuple(range(n_z - 1, n_z // 2 - 1, -1)), tuple(range(n_z // 2 - 1, 0, -1))
    far_state = do_spread(far_zs)
    masks = [n_doc << b for b in range((n_term - 1).bit_length())]
    for mask in masks:
        part = total(queue, [part, swap(part, mask)])
    rounds = [part, swap(part, 1)]
    far_state = do_join(far_zs, far_state)
    mid_state = do_spread(mid_zs)
    near_state = do_spread((0,))
    part = total(queue, rounds)
    for b in range(1, (n_doc - 1).bit_length() - 1):
        part = total(queue, [part, swap(part, 1 << b)])
    rounds = [part, swap(part, n_doc // 2)]
    *relayed, far = merge(queue, len(far_zs), n_y, *far_state)
    relayed = [swap(v, 2 * n_doc * (dz - n_z // 2)) for v, dz in zip(relayed, far_zs)]
    mid_state = do_join(mid_zs, mid_state)
    far = swap(total(queue, [far, *relayed]), n_doc * n_z)
    near_state = do_join((0,), near_state)
    sends = merge(queue, len(mid_zs), n_y, *mid_state)
    last = [swap(v, 2 * n_doc * dz) for v, dz in zip(sends, mid_zs)]
    near, = merge(queue, 1, n_y, *near_state)
    rows, inv = inverse(queue, rounds)
    return finish(queue, near, [far, *last], rows, inv)


def solution(mesh):
    in_specs = (P(("term", "doc"), None, None), P(("term", "doc"), None), P("doc", None), P())
    out_specs = (P(("term", "doc"), None), P(("term", "doc"), None))
    run = functools.partial(body, mesh.shape["term"], mesh.shape["doc"])
    return jax.shard_map(run, mesh=mesh, in_specs=in_specs, out_specs=out_specs, check_vma=False)
```

time: 448 us -> 80.4 us (0.18)
  waiting for transfers between devices: 309 us -> 25.6 us
  matrix products: 67.7 us -> 0 us
  local copies, waits for them, and re-layouts: 43.1 us -> 0.01 us
  starting transfers between devices: 0.08 us -> 28.1 us
  Pallas kernels: 0 us -> 25.5 us
  between operations: 14.8 us -> 0.85 us
  other arithmetic: 12.1 us -> 1.98 us
    reduce_scatter x1 -> x0, waiting for transfers between devices: 186 us -> none  [body(): lax.psum_scatter(partial_value, ('term', 'doc'), scatter_dimension=0, til...]
    psum x1 -> x0, waiting for transfers between devices: 123 us -> none  [body(): anchor_rows = lax.psum(own_part, ('term', 'doc'))]
    dot_general x12 -> x0, matrix products: 67.3 us -> none  [the longest x4 30.6 us: step(): jnp.einsum('bk,kac->bac', onehot, prods, precision=lax.Precision.HIGHEST)]
    ppermute x0 -> x21, starting transfers between devices: none -> 28.1 us  [swap(): return lax.ppermute(v, AXES, [(i, i ^ mask) for i in range(devices)])]
    ppermute x0 -> x21, waiting for transfers between devices: none -> 25.6 us  [swap(): return lax.ppermute(v, AXES, [(i, i ^ mask) for i in range(devices)])]
    pallas_call x0 -> x18, Pallas kernels: none -> 25.5 us  [the longest x2 16.7 us: products(): pl.pallas_call(functools.partial(products_kernel, slots), out_shape=outs,...]
    while x17 -> x0, local copies, waits for them, and re-layouts: 24.3 us -> none
    gather x4 -> x0, local copies, waits for them, and re-layouts: 17.3 us -> none  [step(): chosen = jnp.take(g_blocks, coords[:, 1] - doc_base, axis=0)]
  transfers between devices with their start and end apart: 2 -> 21, of which waited for: 2 -> 11; matrix products, arithmetic and copies ran while one was open for 0% -> 0% of each run, Pallas kernels for 0% -> 19%
where the time goes in v3:
time: 80.4 us; the launch traced here: 82 us
  starting transfers between devices  28.1 us (35%)
  waiting for transfers between devices  25.6 us (32%)
  Pallas kernels  25.5 us (32%)
  other arithmetic  1.98 us (2%)
  between operations  0.85 us (1%)
    ppermute x21, starting transfers between devices, swap(): return lax.ppermute(v, AXES, [(i, i ^ mask) for i in range(devices)])  28.1 us
    ppermute x21, waiting for transfers between devices, swap(): return lax.ppermute(v, AXES, [(i, i ^ mask) for i in range(devices)])  25.6 us
    pallas_call x2, Pallas kernels, products(): pl.pallas_call(functools.partial(products_kernel, slots), out_shape=outs,...  16.7 us
    pallas_call x16, Pallas kernels, call(): pl.pallas_call(functools.partial(in_order, kernel, len(args)), out_shape=...  8.75 us
    convert_element_type x1, other arithmetic, body(): low = (sketch - top).astype(BF16)  1.91 us
  transfers between devices with their start and end apart: 21, of which 11 were waited for; matrix products, arithmetic and copies ran while one was open for 0% of the time, Pallas kernels for 19%

profile of v3, /device:TPU:0, one launch (start us, length us, event | category | flops | bytes accessed | tf_op | source)
XLA Modules:
  0.0 82.0 jit_solution(16610640621292663291)
XLA Ops:
  0.7 1.9 %fusion = (bf16[2048,256]{1,0:T(8,128)(2,1)S(1)}, bf16[2048,256]{1,0:T(8,128)(2,1)S(1)}) fusion(f32[2048,256]{1,0:T(8,128)} %param.6), kind=kLoop, calls=%fused_computation.2 | loop fusion | flops 2097152 | bytes 4194304 | tf_op jit(solution)/shard_map/convert_element_type | solution.py:338
  2.7 7.7 %products_away.1 = (f32[17,128,256]{2,1,0:T(8,128)S(1)}, f32[64,256]{1,0:T(8,128)S(1)}) custom-call(s32[192]{0:T(256)S(1)} %pad_add_fusion.code_ref, f32[128,128,128]{2,1,0:T(8,128)} %tiles.3, bf16[2048,256]{1,0:T(8,128)(2,1)S(1)} %get-tuple-element.105.top_ref, bf16[2048,256]{1,0:T(8,128)(2,1)S(1)} %get-tuple-element.104.low_ref, ...), custom_call_target="tpu_custom_call" | custom-call | flops 8000000000 | bytes 5242880 | tf_op jit(solution)/shard_map/products_away/pallas_call | solution.py:151
  10.4 2.3 %collective-permute-start = (f32[17,128,256]{2,1,0:T(8,128)S(1)}, f32[17,128,256]{2,1,0:T(8,128)S(1)}, u32[]{:S(2)}, u32[]{:S(2)}) collective-permute-start(f32[17,128,256]{2,1,0:T(8,128)S(1)} %get-tuple-element.56), channel_id=1, source_target_pairs={{0,4},{1,5},{2,6},{3,7},{4,0},{5,1},{6,2},{7,3},{8,12},{9,13},{10,... | collective-permute-start | bytes 6684680 | tf_op jit(solution)/shard_map/ppermute | solution.py:328
  12.7 9.1 %products_here.1 = (f32[17,128,256]{2,1,0:T(8,128)S(1)}, f32[64,256]{1,0:T(8,128)S(1)}, f32[8,128]{1,0:T(8,128)S(1)}) custom-call(s32[192]{0:T(256)S(1)} %pad_add_fusion.code_ref, f32[128,128,128]{2,1,0:T(8,128)} %tiles.3, bf16[2048,256]{1,0:T(8,128)(2,1)S(1)} %get-tuple-element.105.top_ref, bf16[2048,256]{1,0:T(8,128)(2,1)S(1)} %get-tuple-element.104.low_ref, ...), custom_call_target="tpu_custom_call" | custom-call | flops 8000000000 | bytes 5242880 | tf_op jit(solution)/shard_map/products_here/pallas_call | solution.py:151
  22.1 1.4 %collective-permute-start.4 = (f32[8,64,256]{2,1,0:T(8,128)S(1)}, f32[8,64,256]{2,1,0:T(8,128)S(1)}, u32[]{:S(2)}, u32[]{:S(2)}) collective-permute-start(f32[8,64,256]{2,1,0:T(8,128)S(1)} %get-tuple-element.65), channel_id=1, source_target_pairs={{0,1},{1,0},{2,3},{3,2},{4,5},{5,4},{6,7},{7,6},{8,9},{9,8},{10,11... | collective-permute-start | bytes 1572872 | tf_op jit(solution)/shard_map/ppermute | solution.py:328
  23.5 1.1 %collective-permute-start.5 = (f32[8,64,256]{2,1,0:T(8,128)S(1)}, f32[8,64,256]{2,1,0:T(8,128)S(1)}, u32[]{:S(2)}, u32[]{:S(2)}) collective-permute-start(f32[8,64,256]{2,1,0:T(8,128)S(1)} %get-tuple-element.66), channel_id=1, source_target_pairs={{0,2},{1,3},{2,0},{3,1},{4,6},{5,7},{6,4},{7,5},{8,10},{9,11},{10,... | collective-permute-start | bytes 1572872 | tf_op jit(solution)/shard_map/ppermute | solution.py:328
  24.6 1.3 %collective-permute-done.1.refs_1_ = f32[64,256]{1,0:T(8,128)S(1)} collective-permute-done((f32[64,256]{1,0:T(8,128)S(1)}, f32[64,256]{1,0:T(8,128)S(1)}, u32[]{:S(2)}, u32[]{:S(2)}) %collective-permute-start.1) | collective-permute-done | bytes 65568 | tf_op jit(solution)/shard_map/ppermute | solution.py:328
  25.9 2.7 %collective-permute-start.2 = (f32[64,256]{1,0:T(8,128)S(1)}, f32[64,256]{1,0:T(8,128)S(1)}, u32[]{:S(2)}, u32[]{:S(2)}) collective-permute-start(f32[64,256]{1,0:T(8,128)S(1)} %get-tuple-element.60.refs_0_), channel_id=1, source_target_pairs={{0,8},{1,9},{2,10},{3,11},{4,12},{5,13},{6,14},{7,15},{8,0},{9,1},... | collective-permute-start | bytes 196616 | tf_op jit(solution)/shard_map/ppermute | solution.py:328
  28.5 2.4 %collective-permute-done.2.refs_1_ = f32[64,256]{1,0:T(8,128)S(1)} collective-permute-done((f32[64,256]{1,0:T(8,128)S(1)}, f32[64,256]{1,0:T(8,128)S(1)}, u32[]{:S(2)}, u32[]{:S(2)}) %collective-permute-start.2) | collective-permute-done | bytes 65568 | tf_op jit(solution)/shard_map/ppermute | solution.py:328
  30.9 3.7 %collective-permute-start.3 = (f32[64,256]{1,0:T(8,128)S(1)}, f32[64,256]{1,0:T(8,128)S(1)}, u32[]{:S(2)}, u32[]{:S(2)}) collective-permute-start(f32[64,256]{1,0:T(8,128)S(1)} %get-tuple-element.62.refs_0_), channel_id=1, source_target_pairs={{0,16},{1,17},{2,18},{3,19},{4,20},{5,21},{6,22},{7,23},{8,24},{9,... | collective-permute-start | bytes 196616 | tf_op jit(solution)/shard_map/ppermute | solution.py:328
  34.6 3.0 %collective-permute-done.3.refs_1_ = f32[64,256]{1,0:T(8,128)S(1)} collective-permute-done((f32[64,256]{1,0:T(8,128)S(1)}, f32[64,256]{1,0:T(8,128)S(1)}, u32[]{:S(2)}, u32[]{:S(2)}) %collective-permute-start.3) | collective-permute-done | bytes 65568 | tf_op jit(solution)/shard_map/ppermute | solution.py:328
  37.8 0.6 collective-permute-start.8
  38.6 1.5 %collective-permute-start.10 = (f32[4,64,256]{2,1,0:T(8,128)S(1)}, f32[4,64,256]{2,1,0:T(8,128)S(1)}, u32[]{:S(2)}, u32[]{:S(2)}) collective-permute-start(f32[4,64,256]{2,1,0:T(8,128)S(1)} %get-tuple-element.78), channel_id=1, source_target_pairs={{0,2},{1,3},{2,0},{3,1},{4,6},{5,7},{6,4},{7,5},{8,10},{9,11},{10,... | collective-permute-start | bytes 786440 | tf_op jit(solution)/shard_map/ppermute | solution.py:328
  40.1 1.9 %collective-permute-start.9 = (f32[4,64,256]{2,1,0:T(8,128)S(1)}, f32[4,64,256]{2,1,0:T(8,128)S(1)}, u32[]{:S(2)}, u32[]{:S(2)}) collective-permute-start(f32[4,64,256]{2,1,0:T(8,128)S(1)} %get-tuple-element.77), channel_id=1, source_target_pairs={{0,1},{1,0},{2,3},{3,2},{4,5},{5,4},{6,7},{7,6},{8,9},{9,8},{10,11... | collective-permute-start | bytes 786440 | tf_op jit(solution)/shard_map/ppermute | solution.py:328
  42.3 9.2 %collective-permute-done.6.refs_1_ = f32[64,256]{1,0:T(8,128)S(1)} collective-permute-done((f32[64,256]{1,0:T(8,128)S(1)}, f32[64,256]{1,0:T(8,128)S(1)}, u32[]{:S(2)}, u32[]{:S(2)}) %collective-permute-start.6) | collective-permute-done | bytes 65568 | tf_op jit(solution)/shard_map/ppermute | solution.py:328
  51.6 0.6 collective-permute-start.11
  52.2 1.5 %collective-permute-start.12 = (f32[4,64,256]{2,1,0:T(8,128)S(1)}, f32[4,64,256]{2,1,0:T(8,128)S(1)}, u32[]{:S(2)}, u32[]{:S(2)}) collective-permute-start(f32[4,64,256]{2,1,0:T(8,128)S(1)} %get-tuple-element.84), channel_id=1, source_target_pairs={{0,1},{1,0},{2,3},{3,2},{4,5},{5,4},{6,7},{7,6},{8,9},{9,8},{10,11... | collective-permute-start | bytes 786440 | tf_op jit(solution)/shard_map/ppermute | solution.py:328
  53.7 1.0 %collective-permute-start.14 = (f32[2,64,256]{2,1,0:T(8,128)S(1)}, f32[2,64,256]{2,1,0:T(8,128)S(1)}, u32[]{:S(2)}, u32[]{:S(2)}) collective-permute-start(f32[2,64,256]{2,1,0:T(8,128)S(1)} %get-tuple-element.88), channel_id=1, source_target_pairs={{0,1},{1,0},{2,3},{3,2},{4,5},{5,4},{6,7},{7,6},{8,9},{9,8},{10,11... | collective-permute-start | bytes 393224 | tf_op jit(solution)/shard_map/ppermute | solution.py:328
  54.7 1.6 %collective-permute-start.15 = (f32[2,64,256]{2,1,0:T(8,128)S(1)}, f32[2,64,256]{2,1,0:T(8,128)S(1)}, u32[]{:S(2)}, u32[]{:S(2)}) collective-permute-start(f32[2,64,256]{2,1,0:T(8,128)S(1)} %get-tuple-element.89), channel_id=1, source_target_pairs={{0,2},{1,3},{2,0},{3,1},{4,6},{5,7},{6,4},{7,5},{8,10},{9,11},{10,... | collective-permute-start | bytes 393224 | tf_op jit(solution)/shard_map/ppermute | solution.py:328
  56.4 1.6 %collective-permute-done.11.refs_1_ = f32[4,64,256]{2,1,0:T(8,128)S(1)} collective-permute-done((f32[4,64,256]{2,1,0:T(8,128)S(1)}, f32[4,64,256]{2,1,0:T(8,128)S(1)}, u32[]{:S(2)}, u32[]{:S(2)}) %collective-permute-start.11) | collective-permute-done | bytes 262176 | tf_op jit(solution)/shard_map/ppermute | solution.py:328
  58.0 1.7 %collective-permute-done.12.refs_1_ = f32[4,64,256]{2,1,0:T(8,128)S(1)} collective-permute-done((f32[4,64,256]{2,1,0:T(8,128)S(1)}, f32[4,64,256]{2,1,0:T(8,128)S(1)}, u32[]{:S(2)}, u32[]{:S(2)}) %collective-permute-start.12) | collective-permute-done | bytes 262176 | tf_op jit(solution)/shard_map/ppermute | solution.py:328
  59.7 1.5 %collective-permute-done.13.refs_2_ = f32[4,64,256]{2,1,0:T(8,128)S(1)} collective-permute-done((f32[4,64,256]{2,1,0:T(8,128)S(1)}, f32[4,64,256]{2,1,0:T(8,128)S(1)}, u32[]{:S(2)}, u32[]{:S(2)}) %collective-permute-start.13) | collective-permute-done | bytes 262176 | tf_op jit(solution)/shard_map/ppermute | solution.py:328
  61.3 1.3 %collective-permute-done.15.refs_2_ = f32[2,64,256]{2,1,0:T(8,128)S(1)} collective-permute-done((f32[2,64,256]{2,1,0:T(8,128)S(1)}, f32[2,64,256]{2,1,0:T(8,128)S(1)}, u32[]{:S(2)}, u32[]{:S(2)}) %collective-permute-start.15) | collective-permute-done | bytes 131104 | tf_op jit(solution)/shard_map/ppermute | solution.py:328
  62.6 0.4 collective-permute-start.20
  63.0 3.9 %collective-permute-start.19 = (f32[4,64,256]{2,1,0:T(8,128)S(1)}, f32[4,64,256]{2,1,0:T(8,128)S(1)}, u32[]{:S(2)}, u32[]{:S(2)}) collective-permute-start(f32[4,64,256]{2,1,0:T(8,128)S(1)} %get-tuple-element.98), channel_id=1, source_target_pairs={{0,16},{1,17},{2,18},{3,19},{4,20},{5,21},{6,22},{7,23},{8,24},{9,... | collective-permute-start | bytes 786440 | tf_op jit(solution)/shard_map/ppermute | solution.py:328
  66.9 1.6 %collective-permute-start.16 = (f32[2,64,256]{2,1,0:T(8,128)S(1)}, f32[2,64,256]{2,1,0:T(8,128)S(1)}, u32[]{:S(2)}, u32[]{:S(2)}) collective-permute-start(f32[2,64,256]{2,1,0:T(8,128)S(1)} %get-tuple-element.92), channel_id=1, source_target_pairs={{0,1},{1,0},{2,3},{3,2},{4,5},{5,4},{6,7},{7,6},{8,9},{9,8},{10,11... | collective-permute-start | bytes 393224 | tf_op jit(solution)/shard_map/ppermute | solution.py:328
  68.8 1.7 %collective-permute-start.18 = (f32[64,256]{1,0:T(8,128)S(1)}, f32[64,256]{1,0:T(8,128)S(1)}, u32[]{:S(2)}, u32[]{:S(2)}) collective-permute-start(f32[64,256]{1,0:T(8,128)S(1)} %get-tuple-element.95.refs_0_), channel_id=1, source_target_pairs={{0,2},{1,3},{2,0},{3,1},{4,6},{5,7},{6,4},{7,5},{8,10},{9,11},{10,... | collective-permute-start | bytes 196616 | tf_op jit(solution)/shard_map/ppermute | solution.py:328
  70.6 1.3 %collective-permute-done.16.refs_1_ = f32[2,64,256]{2,1,0:T(8,128)S(1)} collective-permute-done((f32[2,64,256]{2,1,0:T(8,128)S(1)}, f32[2,64,256]{2,1,0:T(8,128)S(1)}, u32[]{:S(2)}, u32[]{:S(2)}) %collective-permute-start.16) | collective-permute-done | bytes 131104 | tf_op jit(solution)/shard_map/ppermute | solution.py:328
  71.9 1.6 %collective-permute-done.17.refs_2_ = f32[2,64,256]{2,1,0:T(8,128)S(1)} collective-permute-done((f32[2,64,256]{2,1,0:T(8,128)S(1)}, f32[2,64,256]{2,1,0:T(8,128)S(1)}, u32[]{:S(2)}, u32[]{:S(2)}) %collective-permute-start.17) | collective-permute-done | bytes 131104 | tf_op jit(solution)/shard_map/ppermute | solution.py:328
  73.5 0.7 collective-permute-done.18.refs_1_
  74.2 5.7 %inverse.1 = (f32[8,128]{1,0:T(8,128)S(1)}, f32[64,256]{1,0:T(8,128)S(1)}, f32[64,64]{1,0:T(8,128)S(1)}) custom-call(f32[8,128]{1,0:T(8,128)S(1)} %get-tuple-element.94._token, f32[64,256]{1,0:T(8,128)S(1)} %get-tuple-element.95.refs_0_, f32[64,256]{1,0:T(8,128)S(1)} %collective-permute-done.18.refs_1_), custom_call_target="tpu_custom_call" | custom-call | flops 1 | bytes 1 | tf_op jit(solution)/shard_map/inverse/pallas_call | solution.py:49
  80.0 2.0 %finish.1 = (f32[8,128]{1,0:T(8,128)}, f32[64,256]{1,0:T(8,128)}, f32[256,256]{1,0:T(8,128)}) custom-call(f32[8,128]{1,0:T(8,128)S(1)} %get-tuple-element.96._token, f32[4,64,256]{2,1,0:T(8,128)S(1)} %get-tuple-element.97.refs_0_, f32[4,64,256]{2,1,0:T(8,128)S(1)} %collective-permute-done.19.refs_1_, f32[4,64,256]{2,1,0:T(8,128)S(1)} %collective-permute-done.20.refs_2_, ...), custom_call_target="tpu_custom_call" | custom-call | flops 1 | bytes 1 | tf_op jit(solution)/shard_map/finish/pallas_call | solution.py:49
  (37 shorter events, 1.6 us)
Async XLA Ops:
  0.6 1.9 %copy-start.1 = (s32[64]{0:T(128)S(1)}, s32[64]{0:T(128)}, u32[]{:S(2)}) copy-start(s32[64]{0:T(128)} %param.7) | copy-start | bytes 772
  0.6 2.0 %copy-start = (s32[128,2]{0,1:T(2,128)S(1)}, s32[128,2]{0,1:T(2,128)}, u32[]{:S(2)}) copy-start(s32[128,2]{0,1:T(2,128)} %param.5) | copy-start | bytes 3076
  10.4 11.4 %collective-permute-start = (f32[17,128,256]{2,1,0:T(8,128)S(1)}, f32[17,128,256]{2,1,0:T(8,128)S(1)}, u32[]{:S(2)}, u32[]{:S(2)}) collective-permute-start(f32[17,128,256]{2,1,0:T(8,128)S(1)} %get-tuple-element.56), channel_id=1, source_target_pairs={{0,4},{1,5},{2,6},{3,7},{4,0},{5,1},{6,2},{7,3},{8,12},{9,13},{10,... | collective-permute-start | bytes 6684680 | tf_op jit(solution)/shard_map/ppermute | solution.py:328
  22.1 15.5 %collective-permute-start.4 = (f32[8,64,256]{2,1,0:T(8,128)S(1)}, f32[8,64,256]{2,1,0:T(8,128)S(1)}, u32[]{:S(2)}, u32[]{:S(2)}) collective-permute-start(f32[8,64,256]{2,1,0:T(8,128)S(1)} %get-tuple-element.65), channel_id=1, source_target_pairs={{0,1},{1,0},{2,3},{3,2},{4,5},{5,4},{6,7},{7,6},{8,9},{9,8},{10,11... | collective-permute-start | bytes 1572872 | tf_op jit(solution)/shard_map/ppermute | solution.py:328
  23.5 14.1 %collective-permute-start.5 = (f32[8,64,256]{2,1,0:T(8,128)S(1)}, f32[8,64,256]{2,1,0:T(8,128)S(1)}, u32[]{:S(2)}, u32[]{:S(2)}) collective-permute-start(f32[8,64,256]{2,1,0:T(8,128)S(1)} %get-tuple-element.66), channel_id=1, source_target_pairs={{0,2},{1,3},{2,0},{3,1},{4,6},{5,7},{6,4},{7,5},{8,10},{9,11},{10,... | collective-permute-start | bytes 1572872 | tf_op jit(solution)/shard_map/ppermute | solution.py:328
  24.6 1.3 %collective-permute-start.1 = (f32[64,256]{1,0:T(8,128)S(1)}, f32[64,256]{1,0:T(8,128)S(1)}, u32[]{:S(2)}, u32[]{:S(2)}) collective-permute-start(f32[64,256]{1,0:T(8,128)S(1)} %get-tuple-element.58.refs_0_), channel_id=1, source_target_pairs={{0,4},{1,5},{2,6},{3,7},{4,0},{5,1},{6,2},{7,3},{8,12},{9,13},{10,... | collective-permute-start | bytes 196616 | tf_op jit(solution)/shard_map/ppermute | solution.py:328
  25.9 5.1 %collective-permute-start.2 = (f32[64,256]{1,0:T(8,128)S(1)}, f32[64,256]{1,0:T(8,128)S(1)}, u32[]{:S(2)}, u32[]{:S(2)}) collective-permute-start(f32[64,256]{1,0:T(8,128)S(1)} %get-tuple-element.60.refs_0_), channel_id=1, source_target_pairs={{0,8},{1,9},{2,10},{3,11},{4,12},{5,13},{6,14},{7,15},{8,0},{9,1},... | collective-permute-start | bytes 196616 | tf_op jit(solution)/shard_map/ppermute | solution.py:328
  30.9 6.7 %collective-permute-start.3 = (f32[64,256]{1,0:T(8,128)S(1)}, f32[64,256]{1,0:T(8,128)S(1)}, u32[]{:S(2)}, u32[]{:S(2)}) collective-permute-start(f32[64,256]{1,0:T(8,128)S(1)} %get-tuple-element.62.refs_0_), channel_id=1, source_target_pairs={{0,16},{1,17},{2,18},{3,19},{4,20},{5,21},{6,22},{7,23},{8,24},{9,... | collective-permute-start | bytes 196616 | tf_op jit(solution)/shard_map/ppermute | solution.py:328
  37.7 13.7 %collective-permute-start.7 = (f32[4,64,256]{2,1,0:T(8,128)S(1)}, f32[4,64,256]{2,1,0:T(8,128)S(1)}, u32[]{:S(2)}, u32[]{:S(2)}) collective-permute-start(f32[4,64,256]{2,1,0:T(8,128)S(1)} %get-tuple-element.73), channel_id=1, source_target_pairs={{0,1},{1,0},{2,3},{3,2},{4,5},{5,4},{6,7},{7,6},{8,9},{9,8},{10,11... | collective-permute-start | bytes 786440 | tf_op jit(solution)/shard_map/ppermute | solution.py:328
  37.8 13.7 %collective-permute-start.8 = (f32[4,64,256]{2,1,0:T(8,128)S(1)}, f32[4,64,256]{2,1,0:T(8,128)S(1)}, u32[]{:S(2)}, u32[]{:S(2)}) collective-permute-start(f32[4,64,256]{2,1,0:T(8,128)S(1)} %get-tuple-element.74), channel_id=1, source_target_pairs={{0,2},{1,3},{2,0},{3,1},{4,6},{5,7},{6,4},{7,5},{8,10},{9,11},{10,... | collective-permute-start | bytes 786440 | tf_op jit(solution)/shard_map/ppermute | solution.py:328
  38.6 15.0 %collective-permute-start.10 = (f32[4,64,256]{2,1,0:T(8,128)S(1)}, f32[4,64,256]{2,1,0:T(8,128)S(1)}, u32[]{:S(2)}, u32[]{:S(2)}) collective-permute-start(f32[4,64,256]{2,1,0:T(8,128)S(1)} %get-tuple-element.78), channel_id=1, source_target_pairs={{0,2},{1,3},{2,0},{3,1},{4,6},{5,7},{6,4},{7,5},{8,10},{9,11},{10,... | collective-permute-start | bytes 786440 | tf_op jit(solution)/shard_map/ppermute | solution.py:328
  40.1 13.5 %collective-permute-start.9 = (f32[4,64,256]{2,1,0:T(8,128)S(1)}, f32[4,64,256]{2,1,0:T(8,128)S(1)}, u32[]{:S(2)}, u32[]{:S(2)}) collective-permute-start(f32[4,64,256]{2,1,0:T(8,128)S(1)} %get-tuple-element.77), channel_id=1, source_target_pairs={{0,1},{1,0},{2,3},{3,2},{4,5},{5,4},{6,7},{7,6},{8,9},{9,8},{10,11... | collective-permute-start | bytes 786440 | tf_op jit(solution)/shard_map/ppermute | solution.py:328
  42.1 9.4 %collective-permute-start.6 = (f32[64,256]{1,0:T(8,128)S(1)}, f32[64,256]{1,0:T(8,128)S(1)}, u32[]{:S(2)}, u32[]{:S(2)}) collective-permute-start(f32[64,256]{1,0:T(8,128)S(1)} %get-tuple-element.70.refs_0_), channel_id=1, source_target_pairs={{0,1},{1,0},{2,3},{3,2},{4,5},{5,4},{6,7},{7,6},{8,9},{9,8},{10,11... | collective-permute-start | bytes 196616 | tf_op jit(solution)/shard_map/ppermute | solution.py:328
  51.6 6.4 %collective-permute-start.11 = (f32[4,64,256]{2,1,0:T(8,128)S(1)}, f32[4,64,256]{2,1,0:T(8,128)S(1)}, u32[]{:S(2)}, u32[]{:S(2)}) collective-permute-start(f32[4,64,256]{2,1,0:T(8,128)S(1)} %get-tuple-element.81), channel_id=1, source_target_pairs={{0,8},{1,9},{2,10},{3,11},{4,12},{5,13},{6,14},{7,15},{8,0},{9,1},... | collective-permute-start | bytes 786440 | tf_op jit(solution)/shard_map/ppermute | solution.py:328
  52.2 7.6 %collective-permute-start.12 = (f32[4,64,256]{2,1,0:T(8,128)S(1)}, f32[4,64,256]{2,1,0:T(8,128)S(1)}, u32[]{:S(2)}, u32[]{:S(2)}) collective-permute-start(f32[4,64,256]{2,1,0:T(8,128)S(1)} %get-tuple-element.84), channel_id=1, source_target_pairs={{0,1},{1,0},{2,3},{3,2},{4,5},{5,4},{6,7},{7,6},{8,9},{9,8},{10,11... | collective-permute-start | bytes 786440 | tf_op jit(solution)/shard_map/ppermute | solution.py:328
  53.6 7.6 %collective-permute-start.13 = (f32[4,64,256]{2,1,0:T(8,128)S(1)}, f32[4,64,256]{2,1,0:T(8,128)S(1)}, u32[]{:S(2)}, u32[]{:S(2)}) collective-permute-start(f32[4,64,256]{2,1,0:T(8,128)S(1)} %get-tuple-element.85), channel_id=1, source_target_pairs={{0,2},{1,3},{2,0},{3,1},{4,6},{5,7},{6,4},{7,5},{8,10},{9,11},{10,... | collective-permute-start | bytes 786440 | tf_op jit(solution)/shard_map/ppermute | solution.py:328
  53.7 7.6 %collective-permute-start.14 = (f32[2,64,256]{2,1,0:T(8,128)S(1)}, f32[2,64,256]{2,1,0:T(8,128)S(1)}, u32[]{:S(2)}, u32[]{:S(2)}) collective-permute-start(f32[2,64,256]{2,1,0:T(8,128)S(1)} %get-tuple-element.88), channel_id=1, source_target_pairs={{0,1},{1,0},{2,3},{3,2},{4,5},{5,4},{6,7},{7,6},{8,9},{9,8},{10,11... | collective-permute-start | bytes 393224 | tf_op jit(solution)/shard_map/ppermute | solution.py:328
  54.7 7.9 %collective-permute-start.15 = (f32[2,64,256]{2,1,0:T(8,128)S(1)}, f32[2,64,256]{2,1,0:T(8,128)S(1)}, u32[]{:S(2)}, u32[]{:S(2)}) collective-permute-start(f32[2,64,256]{2,1,0:T(8,128)S(1)} %get-tuple-element.89), channel_id=1, source_target_pairs={{0,2},{1,3},{2,0},{3,1},{4,6},{5,7},{6,4},{7,5},{8,10},{9,11},{10,... | collective-permute-start | bytes 393224 | tf_op jit(solution)/shard_map/ppermute | solution.py:328
  62.6 17.3 %collective-permute-start.20 = (f32[4,64,256]{2,1,0:T(8,128)S(1)}, f32[4,64,256]{2,1,0:T(8,128)S(1)}, u32[]{:S(2)}, u32[]{:S(2)}) collective-permute-start(f32[4,64,256]{2,1,0:T(8,128)S(1)} %get-tuple-element.99), channel_id=1, source_target_pairs={{0,8},{1,9},{2,10},{3,11},{4,12},{5,13},{6,14},{7,15},{8,0},{9,1},... | collective-permute-start | bytes 786440 | tf_op jit(solution)/shard_map/ppermute | solution.py:328
  63.0 16.9 %collective-permute-start.19 = (f32[4,64,256]{2,1,0:T(8,128)S(1)}, f32[4,64,256]{2,1,0:T(8,128)S(1)}, u32[]{:S(2)}, u32[]{:S(2)}) collective-permute-start(f32[4,64,256]{2,1,0:T(8,128)S(1)} %get-tuple-element.98), channel_id=1, source_target_pairs={{0,16},{1,17},{2,18},{3,19},{4,20},{5,21},{6,22},{7,23},{8,24},{9,... | collective-permute-start | bytes 786440 | tf_op jit(solution)/shard_map/ppermute | solution.py:328
  66.9 5.0 %collective-permute-start.16 = (f32[2,64,256]{2,1,0:T(8,128)S(1)}, f32[2,64,256]{2,1,0:T(8,128)S(1)}, u32[]{:S(2)}, u32[]{:S(2)}) collective-permute-start(f32[2,64,256]{2,1,0:T(8,128)S(1)} %get-tuple-element.92), channel_id=1, source_target_pairs={{0,1},{1,0},{2,3},{3,2},{4,5},{5,4},{6,7},{7,6},{8,9},{9,8},{10,11... | collective-permute-start | bytes 393224 | tf_op jit(solution)/shard_map/ppermute | solution.py:328
  68.5 5.0 %collective-permute-start.17 = (f32[2,64,256]{2,1,0:T(8,128)S(1)}, f32[2,64,256]{2,1,0:T(8,128)S(1)}, u32[]{:S(2)}, u32[]{:S(2)}) collective-permute-start(f32[2,64,256]{2,1,0:T(8,128)S(1)} %get-tuple-element.93), channel_id=1, source_target_pairs={{0,2},{1,3},{2,0},{3,1},{4,6},{5,7},{6,4},{7,5},{8,10},{9,11},{10,... | collective-permute-start | bytes 393224 | tf_op jit(solution)/shard_map/ppermute | solution.py:328
  68.8 5.4 %collective-permute-start.18 = (f32[64,256]{1,0:T(8,128)S(1)}, f32[64,256]{1,0:T(8,128)S(1)}, u32[]{:S(2)}, u32[]{:S(2)}) collective-permute-start(f32[64,256]{1,0:T(8,128)S(1)} %get-tuple-element.95.refs_0_), channel_id=1, source_target_pairs={{0,2},{1,3},{2,0},{3,1},{4,6},{5,7},{6,4},{7,5},{8,10},{9,11},{10,... | collective-permute-start | bytes 196616 | tf_op jit(solution)/shard_map/ppermute | solution.py:328

commit v4 on v3

--- a/solution.py
+++ b/solution.py
@@ -8,13 +8,16 @@
 from jax.sharding import PartitionSpec as P
 
 ROWS_DEV = 256
-UNROLL = 8
+UNROLL = 16
+FETCHES = 4
+AWAY_MIB = 32
+HERE_MIB = 24
 F32 = jnp.float32
 BF16 = jnp.bfloat16
 AXES = ("term", "doc")
 TOKEN = (8, 128)
 LIMIT = pltpu.CompilerParams(vmem_limit_bytes=24 * 2**20)
-LARGE = pltpu.CompilerParams(vmem_limit_bytes=44 * 2**20)
+LARGE = pltpu.CompilerParams(vmem_limit_bytes=32 * 2**20)
 TINY = pl.CostEstimate(flops=1, bytes_accessed=1, transcendentals=0)
 ANY = pl.BlockSpec(memory_space=pl.ANY)
 HBM = pl.BlockSpec(memory_space=pltpu.HBM)
@@ -45,74 +48,65 @@
     def __init__(self, token):
         self.token = token
 
-    def call(self, name, kernel, out_shape, args):
+    def call(self, name, kernel, out_shape, args, smem=()):
         got = pl.pallas_call(
-            functools.partial(in_order, kernel, len(args)),
+            functools.partial(in_order, kernel, len(args) + len(smem)),
             out_shape=(shaped(TOKEN),) + tuple(out_shape),
-            in_specs=[VMEM] * (1 + len(args)),
+            in_specs=[VMEM] * (1 + len(args)) + [SMEM] * len(smem),
             out_specs=(VMEM,) * (1 + len(out_shape)),
             compiler_params=LIMIT,
             cost_estimate=TINY,
             name=name,
-        )(self.token, *args)
+        )(self.token, *args, *smem)
         self.token = got[0]
         return got[1:]
 
 
-def products_kernel(slots, code_ref, tiles, top_ref, low_ref, *rest):
-    if len(rest) == 7:
-        away, (blocks, anchor_out, buf, order, flag, in_sem) = True, rest[1:]
-        anchor_out[...] = jnp.zeros_like(anchor_out)
+def products_kernel(slots, away, code_ref, *refs):
+    if away:
+        tiles_in, g_ref, blocks, token, tiles, top_ref, low_ref, order, flag, in_sem = refs
     else:
-        away, (anchor_in, blocks, anchor_out, token, buf, order, flag, in_sem) = False, rest
-        token[...] = jnp.zeros_like(token)
-        anchor_out[...] = anchor_in[...]
+        tiles, top_ref, low_ref, blocks, token, order, flag = refs
     n_tiles, tile = tiles.shape[:2]
     width = top_ref.shape[1]
-
-    def wanted(code):
-        return ((code >> 10) & 1) == (1 if away else 0)
-
-    def fetch(k, i):
-        return pltpu.make_async_copy(tiles.at[k], buf.at[i], in_sem.at[i])
+    share = n_tiles // FETCHES
+    spans = [pl.ds(q * share, share) for q in range(FETCHES)]
+    if away:
+        loads = [pltpu.make_async_copy(tiles_in.at[span], tiles.at[span], in_sem.at[q]) for q, span in enumerate(spans)]
+        for load in loads:
+            load.start()
+    token[...] = jnp.zeros_like(token)
 
     def scan(k, count):
         code = code_ref[k]
-        mine = wanted(code)
-        order[count] = code
-
-        @pl.when(mine)
-        def _():
-            fetch(k, count).start()
-
-        return count + mine.astype(jnp.int32)
-
-    count = lax.fori_loop(0, n_tiles, scan, jnp.int32(0), unroll=4)
+        order[count] = code | (k << 16)
+        return count + (((code >> 10) & 1) == away).astype(jnp.int32)
+
+    counts = [jnp.int32(0)]
+    for q in range(FETCHES):
+        counts.append(lax.fori_loop(q * share, (q + 1) * share, scan, counts[-1], unroll=8))
     blocks[...] = jnp.zeros_like(blocks)
     flag[...] = jnp.zeros_like(flag)
-
-    def product(i, code):
-        hi, lo = split(buf[i])
-        rows = pl.ds(pl.multiple_of((code >> 12) * tile, tile), tile)
-        w = jnp.concatenate([top_ref[rows, :], low_ref[rows, :]], axis=1)
+    if away:
+        hi, lo = split(g_ref[...])
+        top_ref[...] = hi
+        low_ref[...] = lo
+
+    def product(code):
+        hi, lo = split(tiles[code >> 16])
+        rows = pl.ds(pl.multiple_of(((code >> 12) & 15) * tile, tile), tile)
+        top = top_ref[rows, :]
         lhs = jnp.concatenate([hi, lo], axis=1)
-        both = jnp.dot(lhs, jnp.concatenate([w, w], axis=0), preferred_element_type=F32)
-        return both[:, :width] + both[:, width:]
-
-    def put(code, prod):
-        slot = code & 1023
-        blocks[slot] += prod
-        flag[pl.ds(slot, 1), :] = jnp.full((1, width), ((code >> 11) & 1).astype(F32), F32)
+        both = jnp.dot(lhs, jnp.concatenate([top, top], axis=0), preferred_element_type=F32)
+        return both + jnp.dot(hi, low_ref[rows, :], preferred_element_type=F32)
 
     def several(base, many):
-        for u in range(many):
-            fetch(0, base + u).wait()
         codes = [order[base + u] for u in range(many)]
-        prods = [product(base + u, codes[u]) for u in range(many)]
+        prods = [product(code) for code in codes]
         for code, prod in zip(codes, prods):
-            put(code, prod)
-
-    whole = count // UNROLL
+            slot = code & 1023
+            blocks[slot] += prod
+            flag[pl.ds(slot, 1), :] = jnp.full((1, width), ((code >> 11) & 1).astype(F32), F32)
 
     def group(j, carry):
         several(j * UNROLL, UNROLL)
@@ -122,47 +116,69 @@
         several(i, 1)
         return carry
 
-    lax.fori_loop(0, whole, group, 0)
-    lax.fori_loop(whole * UNROLL, count, single, 0)
+    whole = [count // UNROLL for count in counts]
+    if away:
+        for q in range(FETCHES):
+            loads[q].wait()
+            lax.fori_loop(whole[q], whole[q + 1], group, 0)
+    else:
+        lax.fori_loop(0, whole[-1], group, 0)
+    lax.fori_loop(whole[-1] * UNROLL, counts[-1], single, 0)
+    blocks[slots, pl.ds(0, slots), :] = flag[pl.ds(0, slots), :]
+
+
+def products(slots, away, codes, tiles, *factors):
+    n_tiles, tile = tiles.shape[:2]
+    rows, width = factors[0].shape
+    outs = [shaped((slots + 1, tile, width)), shaped(TOKEN)]
+    scratch = [pltpu.SMEM((n_tiles + 8,), jnp.int32), pltpu.VMEM((slots + 8, width), F32)]
+    if away:
+        outs += [shaped(tiles.shape)] + [shaped((rows, width), BF16)] * 2
+        scratch.append(pltpu.SemaphoreType.DMA((FETCHES,)))
+    return pl.pallas_call(
+        functools.partial(products_kernel, slots, away),
+        out_shape=outs,
+        in_specs=[SMEM, HBM if away else VMEM] + [VMEM] * len(factors),
+        out_specs=[VMEM] * len(outs),
+        scratch_shapes=scratch,
+        compiler_params=pltpu.CompilerParams(vmem_limit_bytes=(AWAY_MIB if away else HERE_MIB) * 2**20),
+        cost_estimate=pl.CostEstimate(flops=8 * 10**9, bytes_accessed=5 * 2**20, transcendentals=0),
+        name="products_away" if away else "products_here",
+    )(codes, tiles, *factors)
+
+
+def encode(n_doc, me, block, extra, per):
+    rel = lax.bitwise_xor(block // per, me)
+    core = (rel // n_doc) & 1
+    slot = (rel // (2 * n_doc)) * n_doc + (rel & (n_doc - 1))
+    return slot | (core << 10) | ((block % per) << 11) | (extra << 12)
+
+
+def pick_kernel(n_tiles, away, here, code_ref, out):
+    slots = away.shape[0] - 1
+    out[...] = jnp.zeros_like(out)
+
+    def take(i, code, ref):
+        slot = code & 1023
+        value = ref[slot, pl.ds(code >> 12, 1), :]
+        same = ref[slots, pl.ds(slot, 1), :] == ((code >> 11) & 1).astype(F32)
+        out[pl.ds(i, 1), :] = jnp.where(same, value, 0.0)
 
     def pick(i, carry):
         code = code_ref[n_tiles + i]
-
-        @pl.when(wanted(code))
+        other = ((code >> 10) & 1) == 1
+
+        @pl.when(other)
         def _():
-            slot = code & 1023
-            value = blocks[slot, pl.ds(code >> 12, 1), :]
-            same = flag[pl.ds(slot, 1), :] == ((code >> 11) & 1).astype(F32)
-            anchor_out[pl.ds(i, 1), :] = jnp.where(same, value, 0.0)
+            take(i, code, away)
+
+        @pl.when(jnp.logical_not(other))
+        def _():
+            take(i, code, here)
 
         return carry
 
-    lax.fori_loop(0, anchor_out.shape[0], pick, 0)
-    blocks[slots, pl.ds(0, slots), :] = flag[pl.ds(0, slots), :]
-
-
-def products(slots, codes, tiles, top, low, more):
-    n_tiles, tile = tiles.shape[:2]
-    width = top.shape[1]
-    away = len(more) == 0
-    outs = [shaped((slots + 1, tile, width)), shaped((codes.shape[0] - n_tiles, width))]
-    if not away:
-        outs.append(shaped(TOKEN))
-    return pl.pallas_call(
-        functools.partial(products_kernel, slots),
-        out_shape=outs,
-        in_specs=[SMEM, HBM, VMEM, VMEM] + [VMEM] * max(1, len(more)),
-        out_specs=[VMEM] * len(outs),
-        scratch_shapes=[
-            pltpu.VMEM((n_tiles, tile, tile), F32),
-            pltpu.SMEM((n_tiles + 8,), jnp.int32),
-            pltpu.VMEM((slots + 8, width), F32),
-            pltpu.SemaphoreType.DMA((n_tiles,)),
-        ],
-        compiler_params=LARGE,
-        cost_estimate=pl.CostEstimate(flops=8 * 10**9, bytes_accessed=5 * 2**20, transcendentals=0),
-        name="products_away" if away else "products_here",
-    )(codes, tiles, top, low, *(more or (jnp.zeros(TOKEN, F32),)))
+    lax.fori_loop(0, out.shape[0], pick, 0, unroll=4)
 
 
 def encode(n_doc, me, block, extra, per):
@@ -268,31 +284,42 @@
     return queue.call("total", total_kernel, (shaped(values[0].shape),), values)[0]
 
 
-def inverse_kernel(n_in, *refs):
-    ins, (rows_ref, inv_ref) = refs[:n_in], refs[n_in:]
+def gram_kernel(n_in, *refs):
+    ins, (rows_ref, gram_ref) = refs[:n_in], refs[n_in:]
     rows = ins[0][...]
     for ref in ins[1:]:
         rows = rows + ref[...]
     rows_ref[...] = rows
     count = rows.shape[0]
-    m = hdot(rows, rows, ((1,), (1,)))
+    gram = hdot(rows, rows, ((1,), (1,)))
+    diagonal = lax.broadcasted_iota(jnp.int32, (count, count), 0) == lax.broadcasted_iota(jnp.int32, (count, count), 1)
+    ridge = 0.001 * jnp.sum(jnp.where(diagonal, gram, 0.0)) / count
+    gram_ref[...] = jnp.where(diagonal, gram + ridge, gram)
+
+
+def gram_of(queue, parts):
+    count, width = parts[0].shape
+    return queue.call("gram", functools.partial(gram_kernel, len(parts)), (shaped((count, width)), shaped((count, count))), parts)
+
+
+def eliminate_kernel(lo, hi, given, out):
+    m = given[...]
+    count = m.shape[0]
     at_row = lax.broadcasted_iota(jnp.int32, (count, count), 0)
     at_col = lax.broadcasted_iota(jnp.int32, (count, count), 1)
-    diagonal = at_row == at_col
-    ridge = 0.001 * jnp.sum(jnp.where(diagonal, m, 0.0)) / count
-    m = jnp.where(diagonal, m + ridge, m)
-    for k in range(count):
+    for k in range(lo, hi):
         row = m[k : k + 1, :]
         col = m[:, k : k + 1]
         scale = 1.0 / m[k : k + 1, k : k + 1]
         row = jnp.where(at_col[:1] == k, 1.0, row) * scale
         m = jnp.where(at_row == k, row, jnp.where(at_col == k, 0.0, m) - col * row)
-    inv_ref[...] = m
-
-
-def inverse(queue, parts):
-    count, width = parts[0].shape
-    return queue.call("inverse", functools.partial(inverse_kernel, len(parts)), (shaped((count, width)), shaped((count, count))), parts)
+    out[...] = m
+
+
+def eliminate(queue, m, part, parts):
+    count = m.shape[0]
+    lo, hi = count * part // parts, count * (part + 1) // parts
+    return queue.call("eliminate", functools.partial(eliminate_kernel, lo, hi), (shaped(m.shape),), (m,))[0]
 
 
 def finish_kernel(n_far, near, *refs):
@@ -334,13 +361,10 @@
         encode(n_doc, me, coords[:, 0], coords[:, 1] - doc_base, per),
         encode(n_doc, me, anchors // tile, anchors % tile, per),
     ])
-    top = lax.reduce_precision(sketch, 8, 7)
-    low = (sketch - top).astype(BF16)
-    top = top.astype(BF16)
     slots = n_z * n_doc
-    away, part = products(slots, codes, tiles, top, low, ())
+    away, _, tiles_here, top, low = products(slots, 1, codes, tiles, sketch)
     got = swap(away, n_doc)
-    here, part, token = products(slots, codes, tiles, top, low, (part,))
+    here, token = products(slots, 0, codes, tiles_here, top, low)
     queue = Queue(token)
 
     def do_spread(zs):
@@ -353,27 +377,35 @@
 
     far_zs, mid_zs = tuple(range(n_z - 1, n_z // 2 - 1, -1)), tuple(range(n_z // 2 - 1, 0, -1))
     far_state = do_spread(far_zs)
+    pick = functools.partial(pick_kernel, tiles.shape[0])
+    part, = queue.call("pick", pick, (shaped((anchors.shape[0], width)),), (away, here), (codes,))
     masks = [n_doc << b for b in range((n_term - 1).bit_length())]
-    for mask in masks:
+    for mask in masks[:-1]:
         part = total(queue, [part, swap(part, mask)])
+    rounds = [part, swap(part, masks[-1])]
+    far_state = do_join(far_zs, far_state)
+    part = total(queue, rounds)
     rounds = [part, swap(part, 1)]
-    far_state = do_join(far_zs, far_state)
     mid_state = do_spread(mid_zs)
     near_state = do_spread((0,))
+    *relayed, far = merge(queue, len(far_zs), n_y, *far_state)
+    relayed = [swap(v, 2 * n_doc * (dz - n_z // 2)) for v, dz in zip(relayed, far_zs)]
     part = total(queue, rounds)
     for b in range(1, (n_doc - 1).bit_length() - 1):
         part = total(queue, [part, swap(part, 1 << b)])
     rounds = [part, swap(part, n_doc // 2)]
-    *relayed, far = merge(queue, len(far_zs), n_y, *far_state)
-    relayed = [swap(v, 2 * n_doc * (dz - n_z // 2)) for v, dz in zip(relayed, far_zs)]
     mid_state = do_join(mid_zs, mid_state)
     far = swap(total(queue, [far, *relayed]), n_doc * n_z)
     near_state = do_join((0,), near_state)
+    rows, gram = gram_of(queue, rounds)
+    gram = eliminate(queue, gram, 0, 4)
     sends = merge(queue, len(mid_zs), n_y, *mid_state)
     last = [swap(v, 2 * n_doc * dz) for v, dz in zip(sends, mid_zs)]
+    gram = eliminate(queue, gram, 1, 4)
     near, = merge(queue, 1, n_y, *near_state)
-    rows, inv = inverse(queue, rounds)
-    return finish(queue, near, [far, *last], rows, inv)
+    for p in range(2, 4):
+        gram = eliminate(queue, gram, p, 4)
+    return finish(queue, near, [far, *last], rows, gram)
 
 
 def solution(mesh):

time: 80.4 us -> 78.5 us (0.976); the launches traced: 82 us -> 77.8 us
  Pallas kernels: 25.5 us -> 23.1 us
  waiting for transfers between devices: 25.6 us -> 24 us
  local copies, waits for them, and re-layouts: 0.01 us -> 1.59 us
  starting transfers between devices: 28.1 us -> 26.6 us
    pallas_call x18 -> x23, Pallas kernels: 25.5 us -> 23.1 us  [the longest x2 12.8 us: products(): pl.pallas_call(functools.partial(products_kernel, slots, away), out_shape...]
    convert_element_type x1 -> x0, other arithmetic: 1.91 us -> none  [body(): low = (sketch - top).astype(BF16)]
    unnamed x4 -> x2, local copies, waits for them, and re-layouts: 0.01 us -> 1.59 us
    ppermute x21, waiting for transfers between devices: 25.6 us -> 24 us  [swap(): return lax.ppermute(v, AXES, [(i, i ^ mask) for i in range(devices)])]
    ppermute x21, starting transfers between devices: 28.1 us -> 26.6 us  [swap(): return lax.ppermute(v, AXES, [(i, i ^ mask) for i in range(devices)])]
    or x2, other arithmetic: 0.06 us -> 1.47 us  [encode(): return slot | core << 10 | block % per << 11 | extra << 12]
  transfers between devices with their start and end apart: 21 -> 21, of which waited for: 11 -> 12; matrix products, arithmetic and copies ran while one was open for 0% -> 0% of each run, Pallas kernels for 19% -> 18%
where the time goes in v4:
time: 78.5 us; the launch traced here: 77.8 us
  starting transfers between devices  26.6 us (34%)
  waiting for transfers between devices  24 us (31%)
  Pallas kernels  23.1 us (29%)
  local copies, waits for them, and re-layouts  1.59 us (2%)
  other arithmetic  1.48 us (2%)
  between operations  0.85 us (1%)
    ppermute x21, starting transfers between devices, swap(): return lax.ppermute(v, AXES, [(i, i ^ mask) for i in range(devices)])  26.6 us
    ppermute x21, waiting for transfers between devices, swap(): return lax.ppermute(v, AXES, [(i, i ^ mask) for i in range(devices)])  24 us
    pallas_call x2, Pallas kernels, products(): pl.pallas_call(functools.partial(products_kernel, slots, away), out_shape...  12.8 us
    pallas_call x21, Pallas kernels, call(): pl.pallas_call(functools.partial(in_order, kernel, len(args) + len(smem))...  10.3 us
    unnamed x2, local copies, waits for them, and re-layouts  1.59 us
  transfers between devices with their start and end apart: 21, of which 12 were waited for; matrix products, arithmetic and copies ran while one was open for 0% of the time, Pallas kernels for 18%

profile of v4, /device:TPU:0, one launch (start us, length us, event | category | flops | bytes accessed | tf_op | source)
XLA Modules:
  0.0 77.8 jit_solution(64968397233881404)
XLA Ops:
  2.1 1.6 %copy-done = f32[2048,256]{1,0:T(8,128)S(1)} copy-done((f32[2048,256]{1,0:T(8,128)S(1)}, f32[2048,256]{1,0:T(8,128)}, u32[]{:S(2)}) %copy-start) | copy-done | bytes 2097176
  3.7 6.9 %products_away.1 = (f32[17,128,256]{2,1,0:T(8,128)S(1)}, f32[8,128]{1,0:T(8,128)}, f32[128,128,128]{2,1,0:T(8,128)S(1)}, bf16[2048,256]{1,0:T(8,128)(2,1)S(1)}, bf16[2048,256]{1,0:T(8,128)(2,1)S(1)}) custom-call(s32[192]{0:T(256)S(1)} %pad_add_fusion.code_ref.refs_2_, f32[128,128,128]{2,1,0:T(8,128)} %refs_0_.1, f32[2048,256]{1,0:T(8,128)S(1)} %copy-done), custom_call_target="tpu_custom_call" | custom-call | flops 8000000000 | bytes 5242880 | tf_op jit(solution)/shard_map/products_away/pallas_call | solution.py:138
  10.8 5.9 %products_here.1 = (f32[17,128,256]{2,1,0:T(8,128)S(1)}, f32[8,128]{1,0:T(8,128)S(1)}) custom-call(s32[192]{0:T(256)S(1)} %pad_add_fusion.code_ref.refs_2_, f32[128,128,128]{2,1,0:T(8,128)S(1)} %get-tuple-element.64.refs_0_, bf16[2048,256]{1,0:T(8,128)(2,1)S(1)} %get-tuple-element.65.refs_1_, bf16[2048,256]{1,0:T(8,128)(2,1)S(1)} %get-tuple-element.66.refs_2_), custom_call_target="tpu_custom_call" | custom-call | flops 8000000000 | bytes 5242880 | tf_op jit(solution)/shard_map/products_here/pallas_call | solution.py:138
  16.9 3.0 %collective-permute-start.3 = (f32[8,64,256]{2,1,0:T(8,128)S(1)}, f32[8,64,256]{2,1,0:T(8,128)S(1)}, u32[]{:S(2)}, u32[]{:S(2)}) collective-permute-start(f32[8,64,256]{2,1,0:T(8,128)S(1)} %get-tuple-element.77), channel_id=1, source_target_pairs={{0,1},{1,0},{2,3},{3,2},{4,5},{5,4},{6,7},{7,6},{8,9},{9,8},{10,11... | collective-permute-start | bytes 1572872 | tf_op jit(solution)/shard_map/ppermute | solution.py:355
  19.9 1.8 %collective-permute-start.4 = (f32[8,64,256]{2,1,0:T(8,128)S(1)}, f32[8,64,256]{2,1,0:T(8,128)S(1)}, u32[]{:S(2)}, u32[]{:S(2)}) collective-permute-start(f32[8,64,256]{2,1,0:T(8,128)S(1)} %get-tuple-element.78), channel_id=1, source_target_pairs={{0,2},{1,3},{2,0},{3,1},{4,6},{5,7},{6,4},{7,5},{8,10},{9,11},{10,... | collective-permute-start | bytes 1572872 | tf_op jit(solution)/shard_map/ppermute | solution.py:355
  21.8 1.8 %pick.1 = (f32[8,128]{1,0:T(8,128)S(1)}, f32[64,256]{1,0:T(8,128)S(1)}) custom-call(f32[8,128]{1,0:T(8,128)S(1)} %get-tuple-element.70._token, f32[17,128,256]{2,1,0:T(8,128)S(1)} %get-tuple-element.69.refs_0_, f32[17,128,256]{2,1,0:T(8,128)S(1)} %get-tuple-element.68.refs_0_.refs_1_, s32[192]{0:T(256)S(1)} %pad_add_fusion.code_ref.refs_2_), custom_call_target="tpu_custom_call" | custom-call | flops 1 | bytes 1 | tf_op jit(solution)/shard_map/pick/pallas_call | solution.py:52
  23.7 1.2 %collective-permute-done.1.refs_1_ = f32[64,256]{1,0:T(8,128)S(1)} collective-permute-done((f32[64,256]{1,0:T(8,128)S(1)}, f32[64,256]{1,0:T(8,128)S(1)}, u32[]{:S(2)}, u32[]{:S(2)}) %collective-permute-start.1) | collective-permute-done | bytes 65568 | tf_op jit(solution)/shard_map/ppermute | solution.py:355
  25.0 0.8 %collective-permute-start.2 = (f32[64,256]{1,0:T(8,128)S(1)}, f32[64,256]{1,0:T(8,128)S(1)}, u32[]{:S(2)}, u32[]{:S(2)}) collective-permute-start(f32[64,256]{1,0:T(8,128)S(1)} %get-tuple-element.74.refs_0_), channel_id=1, source_target_pairs={{0,8},{1,9},{2,10},{3,11},{4,12},{5,13},{6,14},{7,15},{8,0},{9,1},... | collective-permute-start | bytes 196616 | tf_op jit(solution)/shard_map/ppermute | solution.py:355
  25.8 3.5 %collective-permute-done.2.refs_1_ = f32[64,256]{1,0:T(8,128)S(1)} collective-permute-done((f32[64,256]{1,0:T(8,128)S(1)}, f32[64,256]{1,0:T(8,128)S(1)}, u32[]{:S(2)}, u32[]{:S(2)}) %collective-permute-start.2) | collective-permute-done | bytes 65568 | tf_op jit(solution)/shard_map/ppermute | solution.py:355
  29.3 3.0 %collective-permute-done.3.refs_1_ = f32[8,64,256]{2,1,0:T(8,128)S(1)} collective-permute-done((f32[8,64,256]{2,1,0:T(8,128)S(1)}, f32[8,64,256]{2,1,0:T(8,128)S(1)}, u32[]{:S(2)}, u32[]{:S(2)}) %collective-permute-start.3) | collective-permute-done | bytes 524320 | tf_op jit(solution)/shard_map/ppermute | solution.py:355
  32.3 1.5 %collective-permute-done.4.refs_2_ = f32[8,64,256]{2,1,0:T(8,128)S(1)} collective-permute-done((f32[8,64,256]{2,1,0:T(8,128)S(1)}, f32[8,64,256]{2,1,0:T(8,128)S(1)}, u32[]{:S(2)}, u32[]{:S(2)}) %collective-permute-start.4) | collective-permute-done | bytes 524320 | tf_op jit(solution)/shard_map/ppermute | solution.py:355
  34.3 0.8 %collective-permute-start.7 = (f32[4,64,256]{2,1,0:T(8,128)S(1)}, f32[4,64,256]{2,1,0:T(8,128)S(1)}, u32[]{:S(2)}, u32[]{:S(2)}) collective-permute-start(f32[4,64,256]{2,1,0:T(8,128)S(1)} %get-tuple-element.86), channel_id=1, source_target_pairs={{0,2},{1,3},{2,0},{3,1},{4,6},{5,7},{6,4},{7,5},{8,10},{9,11},{10,... | collective-permute-start | bytes 786440 | tf_op jit(solution)/shard_map/ppermute | solution.py:355
  35.1 4.3 %collective-permute-start.5 = (f32[64,256]{1,0:T(8,128)S(1)}, f32[64,256]{1,0:T(8,128)S(1)}, u32[]{:S(2)}, u32[]{:S(2)}) collective-permute-start(f32[64,256]{1,0:T(8,128)S(1)} %get-tuple-element.80.refs_0_), channel_id=1, source_target_pairs={{0,16},{1,17},{2,18},{3,19},{4,20},{5,21},{6,22},{7,23},{8,24},{9,... | collective-permute-start | bytes 196616 | tf_op jit(solution)/shard_map/ppermute | solution.py:355
  39.4 3.2 %collective-permute-done.5.refs_1_ = f32[64,256]{1,0:T(8,128)S(1)} collective-permute-done((f32[64,256]{1,0:T(8,128)S(1)}, f32[64,256]{1,0:T(8,128)S(1)}, u32[]{:S(2)}, u32[]{:S(2)}) %collective-permute-start.5) | collective-permute-done | bytes 65568 | tf_op jit(solution)/shard_map/ppermute | solution.py:355
  42.8 1.4 %collective-permute-start.9 = (f32[4,64,256]{2,1,0:T(8,128)S(1)}, f32[4,64,256]{2,1,0:T(8,128)S(1)}, u32[]{:S(2)}, u32[]{:S(2)}) collective-permute-start(f32[4,64,256]{2,1,0:T(8,128)S(1)} %get-tuple-element.91), channel_id=1, source_target_pairs={{0,1},{1,0},{2,3},{3,2},{4,5},{5,4},{6,7},{7,6},{8,9},{9,8},{10,11... | collective-permute-start | bytes 786440 | tf_op jit(solution)/shard_map/ppermute | solution.py:355
  44.2 1.0 %collective-permute-start.10 = (f32[4,64,256]{2,1,0:T(8,128)S(1)}, f32[4,64,256]{2,1,0:T(8,128)S(1)}, u32[]{:S(2)}, u32[]{:S(2)}) collective-permute-start(f32[4,64,256]{2,1,0:T(8,128)S(1)} %get-tuple-element.92), channel_id=1, source_target_pairs={{0,2},{1,3},{2,0},{3,1},{4,6},{5,7},{6,4},{7,5},{8,10},{9,11},{10,... | collective-permute-start | bytes 786440 | tf_op jit(solution)/shard_map/ppermute | solution.py:355
  45.5 1.2 %collective-permute-start.11 = (f32[4,64,256]{2,1,0:T(8,128)S(1)}, f32[4,64,256]{2,1,0:T(8,128)S(1)}, u32[]{:S(2)}, u32[]{:S(2)}) collective-permute-start(f32[4,64,256]{2,1,0:T(8,128)S(1)} %get-tuple-element.95), channel_id=1, source_target_pairs={{0,8},{1,9},{2,10},{3,11},{4,12},{5,13},{6,14},{7,15},{8,0},{9,1},... | collective-permute-start | bytes 786440 | tf_op jit(solution)/shard_map/ppermute | solution.py:355
  46.7 1.4 %collective-permute-start.12 = (f32[4,64,256]{2,1,0:T(8,128)S(1)}, f32[4,64,256]{2,1,0:T(8,128)S(1)}, u32[]{:S(2)}, u32[]{:S(2)}) collective-permute-start(f32[4,64,256]{2,1,0:T(8,128)S(1)} %get-tuple-element.98), channel_id=1, source_target_pairs={{0,1},{1,0},{2,3},{3,2},{4,5},{5,4},{6,7},{7,6},{8,9},{9,8},{10,11... | collective-permute-start | bytes 786440 | tf_op jit(solution)/shard_map/ppermute | solution.py:355
  48.1 5.4 %collective-permute-done.8.refs_1_ = f32[64,256]{1,0:T(8,128)S(1)} collective-permute-done((f32[64,256]{1,0:T(8,128)S(1)}, f32[64,256]{1,0:T(8,128)S(1)}, u32[]{:S(2)}, u32[]{:S(2)}) %collective-permute-start.8) | collective-permute-done | bytes 65568 | tf_op jit(solution)/shard_map/ppermute | solution.py:355
  53.6 1.8 %collective-permute-start.15 = (f32[2,64,256]{2,1,0:T(8,128)S(1)}, f32[2,64,256]{2,1,0:T(8,128)S(1)}, u32[]{:S(2)}, u32[]{:S(2)}) collective-permute-start(f32[2,64,256]{2,1,0:T(8,128)S(1)} %get-tuple-element.106), channel_id=1, source_target_pairs={{0,1},{1,0},{2,3},{3,2},{4,5},{5,4},{6,7},{7,6},{8,9},{9,8},{10,11... | collective-permute-start | bytes 393224 | tf_op jit(solution)/shard_map/ppermute | solution.py:355
  55.4 1.6 %collective-permute-start.16 = (f32[2,64,256]{2,1,0:T(8,128)S(1)}, f32[2,64,256]{2,1,0:T(8,128)S(1)}, u32[]{:S(2)}, u32[]{:S(2)}) collective-permute-start(f32[2,64,256]{2,1,0:T(8,128)S(1)} %get-tuple-element.107), channel_id=1, source_target_pairs={{0,2},{1,3},{2,0},{3,1},{4,6},{5,7},{6,4},{7,5},{8,10},{9,11},{10,... | collective-permute-start | bytes 393224 | tf_op jit(solution)/shard_map/ppermute | solution.py:355
  57.5 1.0 %collective-permute-done.12.refs_1_ = f32[4,64,256]{2,1,0:T(8,128)S(1)} collective-permute-done((f32[4,64,256]{2,1,0:T(8,128)S(1)}, f32[4,64,256]{2,1,0:T(8,128)S(1)}, u32[]{:S(2)}, u32[]{:S(2)}) %collective-permute-start.12) | collective-permute-done | bytes 262176 | tf_op jit(solution)/shard_map/ppermute | solution.py:355
  58.5 1.4 %collective-permute-done.13.refs_2_ = f32[4,64,256]{2,1,0:T(8,128)S(1)} collective-permute-done((f32[4,64,256]{2,1,0:T(8,128)S(1)}, f32[4,64,256]{2,1,0:T(8,128)S(1)}, u32[]{:S(2)}, u32[]{:S(2)}) %collective-permute-start.13) | collective-permute-done | bytes 262176 | tf_op jit(solution)/shard_map/ppermute | solution.py:355
  59.9 2.0 %collective-permute-done.14.refs_1_ = f32[64,256]{1,0:T(8,128)S(1)} collective-permute-done((f32[64,256]{1,0:T(8,128)S(1)}, f32[64,256]{1,0:T(8,128)S(1)}, u32[]{:S(2)}, u32[]{:S(2)}) %collective-permute-start.14) | collective-permute-done | bytes 65568 | tf_op jit(solution)/shard_map/ppermute | solution.py:355
  62.3 1.3 %eliminate.4 = (f32[8,128]{1,0:T(8,128)S(1)}, f32[64,64]{1,0:T(8,128)S(1)}) custom-call(f32[8,128]{1,0:T(8,128)S(1)} %get-tuple-element.102._token, f32[64,64]{1,0:T(8,128)S(1)} %get-tuple-element.103.refs_0_), custom_call_target="tpu_custom_call" | custom-call | flops 1 | bytes 1 | tf_op jit(solution)/shard_map/eliminate/pallas_call | solution.py:52
  64.0 3.3 %collective-permute-start.19 = (f32[4,64,256]{2,1,0:T(8,128)S(1)}, f32[4,64,256]{2,1,0:T(8,128)S(1)}, u32[]{:S(2)}, u32[]{:S(2)}) collective-permute-start(f32[4,64,256]{2,1,0:T(8,128)S(1)} %get-tuple-element.120), channel_id=1, source_target_pairs={{0,16},{1,17},{2,18},{3,19},{4,20},{5,21},{6,22},{7,23},{8,24},{9,... | collective-permute-start | bytes 786440 | tf_op jit(solution)/shard_map/ppermute | solution.py:355
  68.0 2.1 %collective-permute-start.18 = (f32[2,64,256]{2,1,0:T(8,128)S(1)}, f32[2,64,256]{2,1,0:T(8,128)S(1)}, u32[]{:S(2)}, u32[]{:S(2)}) collective-permute-start(f32[2,64,256]{2,1,0:T(8,128)S(1)} %get-tuple-element.113), channel_id=1, source_target_pairs={{0,2},{1,3},{2,0},{3,1},{4,6},{5,7},{6,4},{7,5},{8,10},{9,11},{10,... | collective-permute-start | bytes 393224 | tf_op jit(solution)/shard_map/ppermute | solution.py:355
  70.1 1.3 %eliminate.5 = (f32[8,128]{1,0:T(8,128)S(1)}, f32[64,64]{1,0:T(8,128)S(1)}) custom-call(f32[8,128]{1,0:T(8,128)S(1)} %get-tuple-element.108._token, f32[64,64]{1,0:T(8,128)S(1)} %get-tuple-element.109.refs_0_), custom_call_target="tpu_custom_call" | custom-call | flops 1 | bytes 1 | tf_op jit(solution)/shard_map/eliminate/pallas_call | solution.py:52
  71.4 1.0 %collective-permute-done.17.refs_1_ = f32[2,64,256]{2,1,0:T(8,128)S(1)} collective-permute-done((f32[2,64,256]{2,1,0:T(8,128)S(1)}, f32[2,64,256]{2,1,0:T(8,128)S(1)}, u32[]{:S(2)}, u32[]{:S(2)}) %collective-permute-start.17) | collective-permute-done | bytes 131104 | tf_op jit(solution)/shard_map/ppermute | solution.py:355
  73.1 1.3 %eliminate.6 = (f32[8,128]{1,0:T(8,128)S(1)}, f32[64,64]{1,0:T(8,128)S(1)}) custom-call(f32[8,128]{1,0:T(8,128)S(1)} %get-tuple-element.114._token, f32[64,64]{1,0:T(8,128)S(1)} %get-tuple-element.115.refs_0_), custom_call_target="tpu_custom_call" | custom-call | flops 1 | bytes 1 | tf_op jit(solution)/shard_map/eliminate/pallas_call | solution.py:52
  74.3 1.3 %eliminate.7 = (f32[8,128]{1,0:T(8,128)S(1)}, f32[64,64]{1,0:T(8,128)S(1)}) custom-call(f32[8,128]{1,0:T(8,128)S(1)} %get-tuple-element.116._token, f32[64,64]{1,0:T(8,128)S(1)} %get-tuple-element.117.refs_0_), custom_call_target="tpu_custom_call" | custom-call | flops 1 | bytes 1 | tf_op jit(solution)/shard_map/eliminate/pallas_call | solution.py:52
  75.7 2.0 %finish.1 = (f32[8,128]{1,0:T(8,128)}, f32[64,256]{1,0:T(8,128)}, f32[256,256]{1,0:T(8,128)}) custom-call(f32[8,128]{1,0:T(8,128)S(1)} %get-tuple-element.118._token, f32[4,64,256]{2,1,0:T(8,128)S(1)} %get-tuple-element.119.refs_0_, f32[4,64,256]{2,1,0:T(8,128)S(1)} %collective-permute-done.19.refs_1_, f32[4,64,256]{2,1,0:T(8,128)S(1)} %collective-permute-done.20.refs_2_, ...), custom_call_target="tpu_custom_call" | custom-call | flops 1 | bytes 1 | tf_op jit(solution)/shard_map/finish/pallas_call | solution.py:52
  (38 shorter events, 5.6 us)
Async XLA Ops:
  2.1 1.6 %copy-start = (f32[2048,256]{1,0:T(8,128)S(1)}, f32[2048,256]{1,0:T(8,128)}, u32[]{:S(2)}) copy-start(f32[2048,256]{1,0:T(8,128)} %refs_1_.1) | copy-start | bytes 6291460
  10.7 6.0 %collective-permute-start = (f32[17,128,256]{2,1,0:T(8,128)S(1)}, f32[17,128,256]{2,1,0:T(8,128)S(1)}, u32[]{:S(2)}, u32[]{:S(2)}) collective-permute-start(f32[17,128,256]{2,1,0:T(8,128)S(1)} %get-tuple-element.69.refs_0_), channel_id=1, source_target_pairs={{0,4},{1,5},{2,6},{3,7},{4,0},{5,1},{6,2},{7,3},{8,12},{9,13},{10,... | collective-permute-start | bytes 6684680 | tf_op jit(solution)/shard_map/ppermute | solution.py:355
  16.9 15.3 %collective-permute-start.3 = (f32[8,64,256]{2,1,0:T(8,128)S(1)}, f32[8,64,256]{2,1,0:T(8,128)S(1)}, u32[]{:S(2)}, u32[]{:S(2)}) collective-permute-start(f32[8,64,256]{2,1,0:T(8,128)S(1)} %get-tuple-element.77), channel_id=1, source_target_pairs={{0,1},{1,0},{2,3},{3,2},{4,5},{5,4},{6,7},{7,6},{8,9},{9,8},{10,11... | collective-permute-start | bytes 1572872 | tf_op jit(solution)/shard_map/ppermute | solution.py:355
  19.9 13.8 %collective-permute-start.4 = (f32[8,64,256]{2,1,0:T(8,128)S(1)}, f32[8,64,256]{2,1,0:T(8,128)S(1)}, u32[]{:S(2)}, u32[]{:S(2)}) collective-permute-start(f32[8,64,256]{2,1,0:T(8,128)S(1)} %get-tuple-element.78), channel_id=1, source_target_pairs={{0,2},{1,3},{2,0},{3,1},{4,6},{5,7},{6,4},{7,5},{8,10},{9,11},{10,... | collective-permute-start | bytes 1572872 | tf_op jit(solution)/shard_map/ppermute | solution.py:355
  23.6 1.3 %collective-permute-start.1 = (f32[64,256]{1,0:T(8,128)S(1)}, f32[64,256]{1,0:T(8,128)S(1)}, u32[]{:S(2)}, u32[]{:S(2)}) collective-permute-start(f32[64,256]{1,0:T(8,128)S(1)} %get-tuple-element.72.refs_0_), channel_id=1, source_target_pairs={{0,4},{1,5},{2,6},{3,7},{4,0},{5,1},{6,2},{7,3},{8,12},{9,13},{10,... | collective-permute-start | bytes 196616 | tf_op jit(solution)/shard_map/ppermute | solution.py:355
  25.0 4.3 %collective-permute-start.2 = (f32[64,256]{1,0:T(8,128)S(1)}, f32[64,256]{1,0:T(8,128)S(1)}, u32[]{:S(2)}, u32[]{:S(2)}) collective-permute-start(f32[64,256]{1,0:T(8,128)S(1)} %get-tuple-element.74.refs_0_), channel_id=1, source_target_pairs={{0,8},{1,9},{2,10},{3,11},{4,12},{5,13},{6,14},{7,15},{8,0},{9,1},... | collective-permute-start | bytes 196616 | tf_op jit(solution)/shard_map/ppermute | solution.py:355
  33.8 11.6 %collective-permute-start.6 = (f32[4,64,256]{2,1,0:T(8,128)S(1)}, f32[4,64,256]{2,1,0:T(8,128)S(1)}, u32[]{:S(2)}, u32[]{:S(2)}) collective-permute-start(f32[4,64,256]{2,1,0:T(8,128)S(1)} %get-tuple-element.85), channel_id=1, source_target_pairs={{0,1},{1,0},{2,3},{3,2},{4,5},{5,4},{6,7},{7,6},{8,9},{9,8},{10,11... | collective-permute-start | bytes 786440 | tf_op jit(solution)/shard_map/ppermute | solution.py:355
  34.3 11.2 %collective-permute-start.7 = (f32[4,64,256]{2,1,0:T(8,128)S(1)}, f32[4,64,256]{2,1,0:T(8,128)S(1)}, u32[]{:S(2)}, u32[]{:S(2)}) collective-permute-start(f32[4,64,256]{2,1,0:T(8,128)S(1)} %get-tuple-element.86), channel_id=1, source_target_pairs={{0,2},{1,3},{2,0},{3,1},{4,6},{5,7},{6,4},{7,5},{8,10},{9,11},{10,... | collective-permute-start | bytes 786440 | tf_op jit(solution)/shard_map/ppermute | solution.py:355
  35.1 7.5 %collective-permute-start.5 = (f32[64,256]{1,0:T(8,128)S(1)}, f32[64,256]{1,0:T(8,128)S(1)}, u32[]{:S(2)}, u32[]{:S(2)}) collective-permute-start(f32[64,256]{1,0:T(8,128)S(1)} %get-tuple-element.80.refs_0_), channel_id=1, source_target_pairs={{0,16},{1,17},{2,18},{3,19},{4,20},{5,21},{6,22},{7,23},{8,24},{9,... | collective-permute-start | bytes 196616 | tf_op jit(solution)/shard_map/ppermute | solution.py:355
  42.8 10.7 %collective-permute-start.9 = (f32[4,64,256]{2,1,0:T(8,128)S(1)}, f32[4,64,256]{2,1,0:T(8,128)S(1)}, u32[]{:S(2)}, u32[]{:S(2)}) collective-permute-start(f32[4,64,256]{2,1,0:T(8,128)S(1)} %get-tuple-element.91), channel_id=1, source_target_pairs={{0,1},{1,0},{2,3},{3,2},{4,5},{5,4},{6,7},{7,6},{8,9},{9,8},{10,11... | collective-permute-start | bytes 786440 | tf_op jit(solution)/shard_map/ppermute | solution.py:355
  44.2 9.3 %collective-permute-start.10 = (f32[4,64,256]{2,1,0:T(8,128)S(1)}, f32[4,64,256]{2,1,0:T(8,128)S(1)}, u32[]{:S(2)}, u32[]{:S(2)}) collective-permute-start(f32[4,64,256]{2,1,0:T(8,128)S(1)} %get-tuple-element.92), channel_id=1, source_target_pairs={{0,2},{1,3},{2,0},{3,1},{4,6},{5,7},{6,4},{7,5},{8,10},{9,11},{10,... | collective-permute-start | bytes 786440 | tf_op jit(solution)/shard_map/ppermute | solution.py:355
  45.2 8.3 %collective-permute-start.8 = (f32[64,256]{1,0:T(8,128)S(1)}, f32[64,256]{1,0:T(8,128)S(1)}, u32[]{:S(2)}, u32[]{:S(2)}) collective-permute-start(f32[64,256]{1,0:T(8,128)S(1)} %get-tuple-element.88.refs_0_), channel_id=1, source_target_pairs={{0,1},{1,0},{2,3},{3,2},{4,5},{5,4},{6,7},{7,6},{8,9},{9,8},{10,11... | collective-permute-start | bytes 196616 | tf_op jit(solution)/shard_map/ppermute | solution.py:355
  45.5 11.5 %collective-permute-start.11 = (f32[4,64,256]{2,1,0:T(8,128)S(1)}, f32[4,64,256]{2,1,0:T(8,128)S(1)}, u32[]{:S(2)}, u32[]{:S(2)}) collective-permute-start(f32[4,64,256]{2,1,0:T(8,128)S(1)} %get-tuple-element.95), channel_id=1, source_target_pairs={{0,8},{1,9},{2,10},{3,11},{4,12},{5,13},{6,14},{7,15},{8,0},{9,1},... | collective-permute-start | bytes 786440 | tf_op jit(solution)/shard_map/ppermute | solution.py:355
  46.7 11.7 %collective-permute-start.12 = (f32[4,64,256]{2,1,0:T(8,128)S(1)}, f32[4,64,256]{2,1,0:T(8,128)S(1)}, u32[]{:S(2)}, u32[]{:S(2)}) collective-permute-start(f32[4,64,256]{2,1,0:T(8,128)S(1)} %get-tuple-element.98), channel_id=1, source_target_pairs={{0,1},{1,0},{2,3},{3,2},{4,5},{5,4},{6,7},{7,6},{8,9},{9,8},{10,11... | collective-permute-start | bytes 786440 | tf_op jit(solution)/shard_map/ppermute | solution.py:355
  53.5 6.4 %collective-permute-start.13 = (f32[4,64,256]{2,1,0:T(8,128)S(1)}, f32[4,64,256]{2,1,0:T(8,128)S(1)}, u32[]{:S(2)}, u32[]{:S(2)}) collective-permute-start(f32[4,64,256]{2,1,0:T(8,128)S(1)} %get-tuple-element.99), channel_id=1, source_target_pairs={{0,2},{1,3},{2,0},{3,1},{4,6},{5,7},{6,4},{7,5},{8,10},{9,11},{10,... | collective-permute-start | bytes 786440 | tf_op jit(solution)/shard_map/ppermute | solution.py:355
  53.6 10.0 %collective-permute-start.15 = (f32[2,64,256]{2,1,0:T(8,128)S(1)}, f32[2,64,256]{2,1,0:T(8,128)S(1)}, u32[]{:S(2)}, u32[]{:S(2)}) collective-permute-start(f32[2,64,256]{2,1,0:T(8,128)S(1)} %get-tuple-element.106), channel_id=1, source_target_pairs={{0,1},{1,0},{2,3},{3,2},{4,5},{5,4},{6,7},{7,6},{8,9},{9,8},{10,11... | collective-permute-start | bytes 393224 | tf_op jit(solution)/shard_map/ppermute | solution.py:355
  55.4 8.2 %collective-permute-start.16 = (f32[2,64,256]{2,1,0:T(8,128)S(1)}, f32[2,64,256]{2,1,0:T(8,128)S(1)}, u32[]{:S(2)}, u32[]{:S(2)}) collective-permute-start(f32[2,64,256]{2,1,0:T(8,128)S(1)} %get-tuple-element.107), channel_id=1, source_target_pairs={{0,2},{1,3},{2,0},{3,1},{4,6},{5,7},{6,4},{7,5},{8,10},{9,11},{10,... | collective-permute-start | bytes 393224 | tf_op jit(solution)/shard_map/ppermute | solution.py:355
  57.0 4.9 %collective-permute-start.14 = (f32[64,256]{1,0:T(8,128)S(1)}, f32[64,256]{1,0:T(8,128)S(1)}, u32[]{:S(2)}, u32[]{:S(2)}) collective-permute-start(f32[64,256]{1,0:T(8,128)S(1)} %get-tuple-element.101.refs_0_), channel_id=1, source_target_pairs={{0,2},{1,3},{2,0},{3,1},{4,6},{5,7},{6,4},{7,5},{8,10},{9,11},{10,... | collective-permute-start | bytes 196616 | tf_op jit(solution)/shard_map/ppermute | solution.py:355
  63.7 12.0 %collective-permute-start.20 = (f32[4,64,256]{2,1,0:T(8,128)S(1)}, f32[4,64,256]{2,1,0:T(8,128)S(1)}, u32[]{:S(2)}, u32[]{:S(2)}) collective-permute-start(f32[4,64,256]{2,1,0:T(8,128)S(1)} %get-tuple-element.121), channel_id=1, source_target_pairs={{0,8},{1,9},{2,10},{3,11},{4,12},{5,13},{6,14},{7,15},{8,0},{9,1},... | collective-permute-start | bytes 786440 | tf_op jit(solution)/shard_map/ppermute | solution.py:355
  64.0 11.7 %collective-permute-start.19 = (f32[4,64,256]{2,1,0:T(8,128)S(1)}, f32[4,64,256]{2,1,0:T(8,128)S(1)}, u32[]{:S(2)}, u32[]{:S(2)}) collective-permute-start(f32[4,64,256]{2,1,0:T(8,128)S(1)} %get-tuple-element.120), channel_id=1, source_target_pairs={{0,16},{1,17},{2,18},{3,19},{4,20},{5,21},{6,22},{7,23},{8,24},{9,... | collective-permute-start | bytes 786440 | tf_op jit(solution)/shard_map/ppermute | solution.py:355
  67.4 5.0 %collective-permute-start.17 = (f32[2,64,256]{2,1,0:T(8,128)S(1)}, f32[2,64,256]{2,1,0:T(8,128)S(1)}, u32[]{:S(2)}, u32[]{:S(2)}) collective-permute-start(f32[2,64,256]{2,1,0:T(8,128)S(1)} %get-tuple-element.112), channel_id=1, source_target_pairs={{0,1},{1,0},{2,3},{3,2},{4,5},{5,4},{6,7},{7,6},{8,9},{9,8},{10,11... | collective-permute-start | bytes 393224 | tf_op jit(solution)/shard_map/ppermute | solution.py:355
  68.0 5.1 %collective-permute-start.18 = (f32[2,64,256]{2,1,0:T(8,128)S(1)}, f32[2,64,256]{2,1,0:T(8,128)S(1)}, u32[]{:S(2)}, u32[]{:S(2)}) collective-permute-start(f32[2,64,256]{2,1,0:T(8,128)S(1)} %get-tuple-element.113), channel_id=1, source_target_pairs={{0,2},{1,3},{2,0},{3,1},{4,6},{5,7},{6,4},{7,5},{8,10},{9,11},{10,... | collective-permute-start | bytes 393224 | tf_op jit(solution)/shard_map/ppermute | solution.py:355

commit v5 on v4

v5 whole, which is shorter than its diff:
```python
import functools

import jax
import jax.numpy as jnp
from jax import lax
from jax.experimental import pallas as pl
from jax.experimental.pallas import tpu as pltpu
from jax.sharding import PartitionSpec as P

ROWS_DEV = 256
UNROLL = 16
FETCHES = 8
AWAY_MIB = 32
HERE_MIB = 24
F32 = jnp.float32
BF16 = jnp.bfloat16
AXES = ("term", "doc")
TOKEN = (8, 128)
LIMIT = pltpu.CompilerParams(vmem_limit_bytes=24 * 2**20)
LARGE = pltpu.CompilerParams(vmem_limit_bytes=32 * 2**20)
TINY = pl.CostEstimate(flops=1, bytes_accessed=1, transcendentals=0)
LONG = pl.CostEstimate(flops=4 * 10**9, bytes_accessed=1, transcendentals=0)
ANY = pl.BlockSpec(memory_space=pl.ANY)
HBM = pl.BlockSpec(memory_space=pltpu.HBM)
SMEM = pl.BlockSpec(memory_space=pltpu.SMEM)
VMEM = pl.BlockSpec(memory_space=pltpu.VMEM)


def shaped(shape, dtype=F32):
    return jax.ShapeDtypeStruct(tuple(shape), dtype)


def split(v):
    hi = v.astype(BF16)
    lo = (v - hi.astype(F32)).astype(BF16)
    return hi, lo


def hdot(a, b, dims):
    return lax.dot_general(a, b, (dims, ((), ())), precision=lax.Precision.HIGHEST, preferred_element_type=F32)


def in_order(kernel, last, _token, *refs):
    kernel(*refs[:last], *refs[last + 1 :])
    refs[last][...] = jnp.zeros_like(refs[last])


class Queue:
    def __init__(self, token):
        self.token = token

    def call(self, name, kernel, out_shape, args, smem=(), cost=TINY):
        got = pl.pallas_call(
            functools.partial(in_order, kernel, len(args) + len(smem)),
            out_shape=(shaped(TOKEN),) + tuple(out_shape),
            in_specs=[VMEM] * (1 + len(args)) + [SMEM] * len(smem),
            out_specs=(VMEM,) * (1 + len(out_shape)),
            compiler_params=LIMIT,
            cost_estimate=cost,
            name=name,
        )(self.token, *args, *smem)
        self.token = got[0]
        return got[1:]


def products_kernel(slots, away, code_ref, *refs):
    if away:
        tiles_in, g_ref, blocks, token, tiles, top_ref, low_ref, order, flag, in_sem = refs
    else:
        tiles, top_ref, low_ref, blocks, token, order, flag = refs
    n_tiles, tile = tiles.shape[:2]
    width = top_ref.shape[1]
    share = n_tiles // FETCHES
    spans = [pl.ds(q * share, share) for q in range(FETCHES)]
    if away:
        loads = [pltpu.make_async_copy(tiles_in.at[span], tiles.at[span], in_sem.at[q]) for q, span in enumerate(spans)]
        for load in loads:
            load.start()
    token[...] = jnp.zeros_like(token)

    def scan(k, count):
        code = code_ref[k]
        order[count] = code | (k << 16)
        return count + (((code >> 10) & 1) == away).astype(jnp.int32)

    counts = [jnp.int32(0)]
    for q in range(FETCHES):
        counts.append(lax.fori_loop(q * share, (q + 1) * share, scan, counts[-1], unroll=8))
    for u in range(UNROLL):
        order[counts[-1] + u] = slots
    blocks[...] = jnp.zeros_like(blocks)
    flag[...] = jnp.zeros_like(flag)
    if away:
        hi, lo = split(g_ref[...])
        top_ref[...] = hi
        low_ref[...] = lo

    def product(code):
        hi, lo = split(tiles[code >> 16])
        rows = pl.ds(pl.multiple_of(((code >> 12) & 15) * tile, tile), tile)
        top = top_ref[rows, :]
        lhs = jnp.concatenate([hi, lo], axis=1)
        both = jnp.dot(lhs, jnp.concatenate([top, top], axis=0), preferred_element_type=F32)
        return both + jnp.dot(hi, low_ref[rows, :], preferred_element_type=F32)

    def several(base, many):
        codes = [order[base + u] for u in range(many)]
        prods = [product(code) for code in codes]
        for code, prod in zip(codes, prods):
            slot = code & 1023
            blocks[slot] += prod
            flag[pl.ds(slot, 1), :] = jnp.full((1, width), ((code >> 11) & 1).astype(F32), F32)

    def group(j, carry):
        several(j * UNROLL, UNROLL)
        return carry

    whole = [count // UNROLL for count in counts[:-1]] + [(counts[-1] + UNROLL - 1) // UNROLL]
    if away:
        for q in range(FETCHES):
            loads[q].wait()
            lax.fori_loop(whole[q], whole[q + 1], group, 0)
    else:
        lax.fori_loop(0, whole[-1], group, 0)
    blocks[slots, pl.ds(0, slots), :] = flag[pl.ds(0, slots), :]


def products(slots, away, codes, tiles, *factors):
    n_tiles, tile = tiles.shape[:2]
    rows, width = factors[0].shape
    outs = [shaped((slots + 1, tile, width)), shaped(TOKEN)]
    scratch = [pltpu.SMEM((n_tiles + UNROLL,), jnp.int32), pltpu.VMEM((slots + 8, width), F32)]
    if away:
        outs += [shaped(tiles.shape)] + [shaped((rows, width), BF16)] * 2
        scratch.append(pltpu.SemaphoreType.DMA((FETCHES,)))
    return pl.pallas_call(
        functools.partial(products_kernel, slots, away),
        out_shape=outs,
        in_specs=[SMEM, HBM if away else VMEM] + [VMEM] * len(factors),
        out_specs=[VMEM] * len(outs),
        scratch_shapes=scratch,
        compiler_params=pltpu.CompilerParams(vmem_limit_bytes=(AWAY_MIB if away else HERE_MIB) * 2**20),
        cost_estimate=pl.CostEstimate(flops=8 * 10**9, bytes_accessed=5 * 2**20, transcendentals=0),
        name="products_away" if away else "products_here",
    )(codes, tiles, *factors)


def encode(n_doc, me, block, per):
    rel = lax.bitwise_xor(block // per, me)
    core = (rel // n_doc) & 1
    slot = (rel // (2 * n_doc)) * n_doc + (rel & (n_doc - 1))
    return slot | (core << 10) | ((block % per) << 11)


def pick_kernel(n_tiles, away, here, code_ref, out):
    slots = away.shape[0] - 1
    for i in range(out.shape[0]):
        code = code_ref[n_tiles + i]
        slot, row = code & 1023, code >> 12
        bit = ((code >> 11) & 1).astype(F32)
        other = ((code >> 10) & 1) == 1
        value = jnp.where(other, away[slot, pl.ds(row, 1), :], here[slot, pl.ds(row, 1), :])
        which = jnp.where(other, away[slots, pl.ds(slot, 1), :], here[slots, pl.ds(slot, 1), :])
        out[i : i + 1, :] = jnp.where(which == bit, value, 0.0)


def spread_kernel(groups, n_y, own, got, stay, *sends):
    slots = own.shape[0] - 1
    half = own.shape[1] // 2
    n_x = sum(len(zs) for zs in groups) * 2 * n_y
    i = 0
    for g, zs in enumerate(groups):
        send_x, *send_y = sends[g * n_y : (g + 1) * n_y]
        for j, dz in enumerate(zs):
            for dy in range(n_y):
                for dx in range(2):
                    slot = (dz * n_y + dy) * 2 + dx
                    a, b = own[slot], got[slot]
                    up_a = a * own[slots, pl.ds(slot, 1), :]
                    up_b = b * got[slots, pl.ds(slot, 1), :]
                    for s, value in enumerate(((a - up_a) + (b - up_b), up_a + up_b)):
                        if dx:
                            send_x[2 * (j * n_y + dy) + s] = value[:half]
                        else:
                            stay[2 * (i * n_y + dy) + s] = value[:half]
                        if dy:
                            send_y[dy - 1][2 * (j * 2 + dx) + s] = value[half:]
                        else:
                            stay[n_x + 2 * (i * 2 + dx) + s] = value[half:]
            i += 1


def spread(queue, groups, n_y, own, got):
    half, width = own.shape[1] // 2, own.shape[2]
    n = sum(len(zs) for zs in groups)
    outs = [shaped((n * (2 * n_y + 4), half, width))]
    for zs in groups:
        outs += [shaped((len(zs) * 2 * n_y, half, width))] + [shaped((len(zs) * 4, half, width))] * (n_y - 1)
    return queue.call("spread", functools.partial(spread_kernel, groups, n_y), outs, (own, got))


def join_kernel(groups, n_y, n_parts, ride_x, stay, *refs):
    n = sum(len(zs) for zs in groups)
    came = refs[: len(groups) * n_y]
    parts = refs[len(came) : len(came) + n_parts]
    keep, rows, send_x, *send_y = refs[len(came) + n_parts :]
    n_x = n * 2 * n_y
    i = 0
    for g, zs in enumerate(groups):
        got_x, *got_y = came[g * n_y : (g + 1) * n_y]
        for j in range(len(zs)):
            for s in range(2):
                for dy in range(n_y):
                    value = stay[2 * (i * n_y + dy) + s] + got_x[2 * (j * n_y + dy) + s]
                    if dy:
                        send_y[dy - 1][2 * i + s] = value
                    else:
                        keep[4 * i + s] = value
                for dx in range(2):
                    value = stay[n_x + 2 * (i * 2 + dx) + s]
                    for ref in got_y:
                        value = value + ref[2 * (j * 2 + dx) + s]
                    if dx:
                        send_x[2 * i + s] = value
                    else:
                        keep[4 * i + 2 + s] = value
            i += 1
    total = parts[0][...]
    for ref in parts[1:]:
        total = total + ref[...]
    rows[...] = total
    for ref in [send_x] if ride_x else send_y:
        ref[2 * n] = total


def join(queue, groups, n_y, state, parts, ride_x):
    stay = state[0]
    half, width = stay.shape[1:]
    n = sum(len(zs) for zs in groups)
    pairs = [shaped((2 * n + (1 if ride_x == (k == 0) else 0), half, width)) for k in range(n_y)]
    outs = [shaped((4 * n, half, width)), shaped((half, width))] + pairs
    kernel = functools.partial(join_kernel, groups, n_y, len(parts), ride_x)
    return queue.call("join", kernel, outs, (*state, *parts))


def merge_kernel(n, n_y, ride_x, keep, rows, got_x, *refs):
    got_y, total, outs = refs[: n_y - 1], refs[n_y - 1], refs[n_y:]
    for i, out in enumerate(outs):
        for s in range(2):
            x = keep[4 * i + s]
            for ref in got_y:
                x = x + ref[2 * i + s]
            out[s] = x
            out[2 + s] = keep[4 * i + 2 + s] + got_x[2 * i + s]
    value = rows[...]
    for ref in [got_x] if ride_x else got_y:
        value = value + ref[2 * n]
    total[...] = value


def merge(queue, n, n_y, keep, rows, came, ride_x):
    outs = (shaped(rows.shape),) + (shaped((4,) + keep.shape[1:]),) * n
    return queue.call("merge", functools.partial(merge_kernel, n, n_y, ride_x), outs, (keep, rows, *came))


def total_kernel(*refs):
    total = refs[0][...]
    for ref in refs[1:-1]:
        total = total + ref[...]
    refs[-1][...] = total


def total(queue, values):
    return queue.call("total", total_kernel, (shaped(values[0].shape),), values)[0]


def gram_kernel(rows_ref, gram_ref):
    rows = rows_ref[...]
    count = rows.shape[0]
    gram = hdot(rows, rows, ((1,), (1,)))
    diagonal = lax.broadcasted_iota(jnp.int32, (count, count), 0) == lax.broadcasted_iota(jnp.int32, (count, count), 1)
    ridge = 0.001 * jnp.sum(jnp.where(diagonal, gram, 0.0)) / count
    gram_ref[...] = jnp.where(diagonal, gram + ridge, gram)


def gram_of(queue, rows):
    return queue.call("gram", gram_kernel, (shaped((rows.shape[0],) * 2),), (rows,))[0]


def eliminate_kernel(lo, hi, given, out):
    m = given[...]
    count = m.shape[0]
    at_row = lax.broadcasted_iota(jnp.int32, (count, count), 0)
    at_col = lax.broadcasted_iota(jnp.int32, (count, count), 1)
    for k in range(lo, hi):
        row = m[k : k + 1, :]
        col = m[:, k : k + 1]
        scale = 1.0 / m[k : k + 1, k : k + 1]
        row = jnp.where(at_col[:1] == k, 1.0, row) * scale
        m = jnp.where(at_row == k, row, jnp.where(at_col == k, 0.0, m) - col * row)
    out[...] = m


def eliminate(queue, m, part, cost):
    half = m.shape[0] // 2
    kernel = functools.partial(eliminate_kernel, part * half, (part + 1) * half)
    return queue.call("eliminate", kernel, (shaped(m.shape),), (m,), cost=cost)[0]


def solver_kernel(rows, inv, out):
    out[...] = hdot(rows[...], inv[...], ((0,), (0,)))


def solver(queue, rows, inv):
    return queue.call("solver", solver_kernel, (shaped(rows.shape[::-1]),), (rows, inv))[0]


def finish_kernel(n_far, near, *refs):
    x, y = near[:2], near[2:]
    for ref in refs[:n_far]:
        x = x + ref[:2]
        y = y + ref[2:]
    rows_ref, solve_ref, coef_ref, res_ref = refs[n_far:]
    owned = jnp.concatenate([x[0], y[0], x[1], y[1]], axis=0)
    coef = hdot(owned, solve_ref[...], ((1,), (0,)))
    res_ref[...] = owned - hdot(coef, rows_ref[...], ((1,), (0,)))
    coef_ref[...] = coef.T


def finish(queue, near, far, rows, solve):
    half, width = near.shape[1:]
    outs = (shaped((rows.shape[0], 4 * half)), shaped((4 * half, width)))
    coef, res = queue.call("finish", functools.partial(finish_kernel, len(far)), outs, (near, *far, rows, solve))
    return coef.T, res


def body(n_term, n_doc, tiles, coords, sketch, anchors):
    devices = n_term * n_doc
    n_y, n_z = n_doc // 2, n_term // 2
    tile, width = tiles.shape[1], sketch.shape[1]
    per = ROWS_DEV // tile
    me = lax.axis_index(AXES).astype(jnp.int32)
    doc_base = lax.axis_index("doc").astype(jnp.int32) * (sketch.shape[0] // tile)

    def swap(v, mask):
        return lax.ppermute(v, AXES, [(i, i ^ mask) for i in range(devices)])

    def swap_y(values):
        return [swap(v, 2 * (k + 1)) for k, v in enumerate(values)]

    n_tiles, count = coords.shape[0], anchors.shape[0]
    is_block = lax.broadcasted_iota(jnp.int32, (2, n_tiles + count), 0) == 0
    anchor = jnp.where(is_block[:, :count], anchors // tile, anchors % tile + doc_base)
    pair = jnp.pad(coords.T, ((0, 0), (0, count))) + jnp.pad(anchor, ((0, 0), (n_tiles, 0)))
    codes = jnp.sum(jnp.where(is_block, encode(n_doc, me, pair, per), (pair - doc_base) << 12), axis=0)
    slots = n_z * n_doc
    away, _, tiles_here, top, low = products(slots, 1, codes, tiles, sketch)
    got = swap(away, n_doc)
    here, token = products(slots, 0, codes, tiles_here, top, low)
    queue = Queue(token)

    def swaps(values):
        return [swap(v, 2 * k if k else 1) for k, v in enumerate(values)]

    def do_spread(groups):
        stay, *sends = spread(queue, groups, n_y, here, got)
        came = []
        for g in range(len(groups)):
            came += swaps(sends[g * n_y : (g + 1) * n_y])
        return [stay, *came]

    def do_join(groups, state, parts, ride_x):
        keep, rows, *sends = join(queue, groups, n_y, state, parts, ride_x)
        return keep, rows, swaps(sends)

    mid = tuple(range(n_z // 2 - 1, 0, -1))
    far_groups = (tuple(range(n_z - 1, n_z // 2 - 1, -1)),)
    near_groups = (mid + (0,),)
    state = do_spread(far_groups)
    pick = functools.partial(pick_kernel, n_tiles)
    part, = queue.call("pick", pick, (shaped((count, width)),), (away, here), (codes,))
    masks = [n_doc << b for b in range((n_term - 1).bit_length())]
    for mask in masks[:-1]:
        part = total(queue, [part, swap(part, mask)])
    joined = do_join(far_groups, state, (part, swap(part, masks[-1])), True)
    state = do_spread(near_groups)
    rows, *relayed, far = merge(queue, len(far_groups[0]), n_y, *joined, True)
    relayed = [swap(v, 2 * n_doc * (dz - n_z // 2)) for v, dz in zip(relayed, far_groups[0])]
    far = swap(total(queue, [far, *relayed]), n_doc * n_z)
    joined = do_join(near_groups, state, (rows,), False)
    rows, *sends, near = merge(queue, len(mid) + 1, n_y, *joined, False)
    last = [swap(v, 2 * n_doc * dz) for v, dz in zip(sends, mid)]
    gram = gram_of(queue, rows)
    gram = eliminate(queue, gram, 0, TINY)
    near = total(queue, [near, far])
    gram = eliminate(queue, gram, 1, LONG)
    solve = solver(queue, rows, gram)
    return finish(queue, near, last, rows, solve)


def solution(mesh):
    in_specs = (P(("term", "doc"), None, None), P(("term", "doc"), None), P("doc", None), P())
    out_specs = (P(("term", "doc"), None), P(("term", "doc"), None))
    run = functools.partial(body, mesh.shape["term"], mesh.shape["doc"])
    return jax.shard_map(run, mesh=mesh, in_specs=in_specs, out_specs=out_specs, check_vma=False)
```

time: 78.5 us -> 71.3 us (0.908)
  starting transfers between devices: 26.6 us -> 22.1 us
  Pallas kernels: 23.1 us -> 21.2 us
    ppermute x21 -> x15, starting transfers between devices: 26.6 us -> 22.1 us  [swap(): return lax.ppermute(v, AXES, [(i, i ^ mask) for i in range(devices)])]
    or x2 -> x0, other arithmetic: 1.47 us -> none  [encode(): return slot | core << 10 | block % per << 11 | extra << 12]
    pallas_call x2, Pallas kernels: 12.8 us -> 11.6 us  [products(): pl.pallas_call(functools.partial(products_kernel, slots, away), out_shape...]
    pallas_call x21 -> x16, Pallas kernels: 10.3 us -> 9.67 us  [call(): pl.pallas_call(functools.partial(in_order, kernel, len(args) + len(smem))...]
    ppermute x21 -> x15, waiting for transfers between devices: 24 us -> 23.8 us  [swap(): return lax.ppermute(v, AXES, [(i, i ^ mask) for i in range(devices)])]
  transfers between devices with their start and end apart: 21 -> 15, of which waited for: 12 -> 9; matrix products, arithmetic and copies ran while one was open for 0% -> 0% of each run, Pallas kernels for 18% -> 19%
where the time goes in v5:
time: 71.3 us; the launch traced here: 71 us
  waiting for transfers between devices  23.8 us (33%)
  starting transfers between devices  22.1 us (31%)
  Pallas kernels  21.2 us (30%)
  local copies, waits for them, and re-layouts  1.58 us (2%)
  other arithmetic  1.51 us (2%)
  between operations  0.79 us (1%)
    ppermute x15, waiting for transfers between devices, swap(): return lax.ppermute(v, AXES, [(i, i ^ mask) for i in range(devices)])  23.8 us
    ppermute x15, starting transfers between devices, swap(): return lax.ppermute(v, AXES, [(i, i ^ mask) for i in range(devices)])  22.1 us
    pallas_call x2, Pallas kernels, products(): pl.pallas_call(functools.partial(products_kernel, slots, away), out_shape...  11.6 us
    pallas_call x16, Pallas kernels, call(): pl.pallas_call(functools.partial(in_order, kernel, len(args) + len(smem))...  9.67 us
    unnamed x2, local copies, waits for them, and re-layouts  1.58 us
  transfers between devices with their start and end apart: 15, of which 9 were waited for; matrix products, arithmetic and copies ran while one was open for 0% of the time, Pallas kernels for 19%

profile of v5, /device:TPU:0, one launch (start us, length us, event | category | flops | bytes accessed | tf_op | source)
XLA Modules:
  0.0 71.0 jit_solution(9937796065511911170)
XLA Ops:
  0.7 0.7 and_select_fusion.5
  1.4 0.8 %fusion.3.code_ref.refs_2_ = s32[192]{0:T(256)S(1)} fusion(s32[2,64]{1,0:T(2,128)S(1)} %broadcast_select_fusion, s32[2,128]{1,0:T(2,128)} %bitcast.2, pred[2]{0:T(512)(128)(4,1)S(1)} %iota_compare_fusion, s32[]{:T(128)S(6)} %mul.12, s32[]{:T(128)S(6)} %add.39), kind=kLoop, calls=%fused_computation.15 | loop fusion | flops 22080 | bytes 2314 | tf_op jit(solution)/shard_map/reduce_sum | solution.py:355
  2.2 1.6 %copy-done = f32[2048,256]{1,0:T(8,128)S(1)} copy-done((f32[2048,256]{1,0:T(8,128)S(1)}, f32[2048,256]{1,0:T(8,128)}, u32[]{:S(2)}) %copy-start) | copy-done | bytes 2097176
  3.8 5.6 %products_away.1 = (f32[17,128,256]{2,1,0:T(8,128)S(1)}, f32[8,128]{1,0:T(8,128)}, f32[128,128,128]{2,1,0:T(8,128)S(1)}, bf16[2048,256]{1,0:T(8,128)(2,1)S(1)}, bf16[2048,256]{1,0:T(8,128)(2,1)S(1)}) custom-call(s32[192]{0:T(256)S(1)} %fusion.3.code_ref.refs_2_, f32[128,128,128]{2,1,0:T(8,128)} %refs_0_.1, f32[2048,256]{1,0:T(8,128)S(1)} %copy-done), custom_call_target="tpu_custom_call" | custom-call | flops 8000000000 | bytes 5242880 | tf_op jit(solution)/shard_map/products_away/pallas_call | solution.py:136
  9.4 1.4 %collective-permute-start = (f32[17,128,256]{2,1,0:T(8,128)S(1)}, f32[17,128,256]{2,1,0:T(8,128)S(1)}, u32[]{:S(2)}, u32[]{:S(2)}) collective-permute-start(f32[17,128,256]{2,1,0:T(8,128)S(1)} %get-tuple-element.59.refs_0_), channel_id=1, source_target_pairs={{0,4},{1,5},{2,6},{3,7},{4,0},{5,1},{6,2},{7,3},{8,12},{9,13},{10,... | collective-permute-start | bytes 6684680 | tf_op jit(solution)/shard_map/ppermute | solution.py:346
  10.8 5.9 %products_here.1 = (f32[17,128,256]{2,1,0:T(8,128)S(1)}, f32[8,128]{1,0:T(8,128)S(1)}) custom-call(s32[192]{0:T(256)S(1)} %fusion.3.code_ref.refs_2_, f32[128,128,128]{2,1,0:T(8,128)S(1)} %get-tuple-element.54.refs_0_, bf16[2048,256]{1,0:T(8,128)(2,1)S(1)} %get-tuple-element.55.refs_1_, bf16[2048,256]{1,0:T(8,128)(2,1)S(1)} %get-tuple-element.56.refs_2_), custom_call_target="tpu_custom_call" | custom-call | flops 8000000000 | bytes 5242880 | tf_op jit(solution)/shard_map/products_here/pallas_call | solution.py:136
  17.0 1.6 %collective-permute-start.3 = (f32[8,64,256]{2,1,0:T(8,128)S(1)}, f32[8,64,256]{2,1,0:T(8,128)S(1)}, u32[]{:S(2)}, u32[]{:S(2)}) collective-permute-start(f32[8,64,256]{2,1,0:T(8,128)S(1)} %get-tuple-element.67), channel_id=1, source_target_pairs={{0,1},{1,0},{2,3},{3,2},{4,5},{5,4},{6,7},{7,6},{8,9},{9,8},{10,11... | collective-permute-start | bytes 1572872 | tf_op jit(solution)/shard_map/ppermute | solution.py:346
  18.7 1.5 %collective-permute-start.4 = (f32[8,64,256]{2,1,0:T(8,128)S(1)}, f32[8,64,256]{2,1,0:T(8,128)S(1)}, u32[]{:S(2)}, u32[]{:S(2)}) collective-permute-start(f32[8,64,256]{2,1,0:T(8,128)S(1)} %get-tuple-element.68), channel_id=1, source_target_pairs={{0,2},{1,3},{2,0},{3,1},{4,6},{5,7},{6,4},{7,5},{8,10},{9,11},{10,... | collective-permute-start | bytes 1572872 | tf_op jit(solution)/shard_map/ppermute | solution.py:346
  20.2 0.9 %pick.1 = (f32[8,128]{1,0:T(8,128)S(1)}, f32[64,256]{1,0:T(8,128)S(1)}) custom-call(f32[8,128]{1,0:T(8,128)S(1)} %get-tuple-element.60._token, f32[17,128,256]{2,1,0:T(8,128)S(1)} %get-tuple-element.59.refs_0_, f32[17,128,256]{2,1,0:T(8,128)S(1)} %get-tuple-element.58.refs_0_.refs_1_, s32[192]{0:T(256)S(1)} %fusion.3.code_ref.refs_2_), custom_call_target="tpu_custom_call" | custom-call | flops 1 | bytes 1 | tf_op jit(solution)/shard_map/pick/pallas_call | solution.py:53
  21.2 1.2 %collective-permute-done.1.refs_1_ = f32[64,256]{1,0:T(8,128)S(1)} collective-permute-done((f32[64,256]{1,0:T(8,128)S(1)}, f32[64,256]{1,0:T(8,128)S(1)}, u32[]{:S(2)}, u32[]{:S(2)}) %collective-permute-start.1) | collective-permute-done | bytes 65568 | tf_op jit(solution)/shard_map/ppermute | solution.py:346
  22.5 1.9 %collective-permute-start.2 = (f32[64,256]{1,0:T(8,128)S(1)}, f32[64,256]{1,0:T(8,128)S(1)}, u32[]{:S(2)}, u32[]{:S(2)}) collective-permute-start(f32[64,256]{1,0:T(8,128)S(1)} %get-tuple-element.64.refs_0_), channel_id=1, source_target_pairs={{0,8},{1,9},{2,10},{3,11},{4,12},{5,13},{6,14},{7,15},{8,0},{9,1},... | collective-permute-start | bytes 196616 | tf_op jit(solution)/shard_map/ppermute | solution.py:346
  24.4 2.4 %collective-permute-done.2.refs_1_ = f32[64,256]{1,0:T(8,128)S(1)} collective-permute-done((f32[64,256]{1,0:T(8,128)S(1)}, f32[64,256]{1,0:T(8,128)S(1)}, u32[]{:S(2)}, u32[]{:S(2)}) %collective-permute-start.2) | collective-permute-done | bytes 65568 | tf_op jit(solution)/shard_map/ppermute | solution.py:346
  26.8 2.9 %collective-permute-start.5 = (f32[64,256]{1,0:T(8,128)S(1)}, f32[64,256]{1,0:T(8,128)S(1)}, u32[]{:S(2)}, u32[]{:S(2)}) collective-permute-start(f32[64,256]{1,0:T(8,128)S(1)} %get-tuple-element.69.refs_3_), channel_id=1, source_target_pairs={{0,16},{1,17},{2,18},{3,19},{4,20},{5,21},{6,22},{7,23},{8,24},{9,... | collective-permute-start | bytes 196616 | tf_op jit(solution)/shard_map/ppermute | solution.py:346
  29.8 2.6 %collective-permute-done.5.refs_4_ = f32[64,256]{1,0:T(8,128)S(1)} collective-permute-done((f32[64,256]{1,0:T(8,128)S(1)}, f32[64,256]{1,0:T(8,128)S(1)}, u32[]{:S(2)}, u32[]{:S(2)}) %collective-permute-start.5) | collective-permute-done | bytes 65568 | tf_op jit(solution)/shard_map/ppermute | solution.py:346
  32.8 1.6 %collective-permute-start.7 = (f32[4,64,256]{2,1,0:T(8,128)S(1)}, f32[4,64,256]{2,1,0:T(8,128)S(1)}, u32[]{:S(2)}, u32[]{:S(2)}) collective-permute-start(f32[4,64,256]{2,1,0:T(8,128)S(1)} %get-tuple-element.75), channel_id=1, source_target_pairs={{0,2},{1,3},{2,0},{3,1},{4,6},{5,7},{6,4},{7,5},{8,10},{9,11},{10,... | collective-permute-start | bytes 786440 | tf_op jit(solution)/shard_map/ppermute | solution.py:346
  34.6 1.2 %collective-permute-start.9 = (f32[8,64,256]{2,1,0:T(8,128)S(1)}, f32[8,64,256]{2,1,0:T(8,128)S(1)}, u32[]{:S(2)}, u32[]{:S(2)}) collective-permute-start(f32[8,64,256]{2,1,0:T(8,128)S(1)} %get-tuple-element.81), channel_id=1, source_target_pairs={{0,1},{1,0},{2,3},{3,2},{4,5},{5,4},{6,7},{7,6},{8,9},{9,8},{10,11... | collective-permute-start | bytes 1572872 | tf_op jit(solution)/shard_map/ppermute | solution.py:346
  35.9 1.1 %collective-permute-start.10 = (f32[8,64,256]{2,1,0:T(8,128)S(1)}, f32[8,64,256]{2,1,0:T(8,128)S(1)}, u32[]{:S(2)}, u32[]{:S(2)}) collective-permute-start(f32[8,64,256]{2,1,0:T(8,128)S(1)} %get-tuple-element.82), channel_id=1, source_target_pairs={{0,2},{1,3},{2,0},{3,1},{4,6},{5,7},{6,4},{7,5},{8,10},{9,11},{10,... | collective-permute-start | bytes 1572872 | tf_op jit(solution)/shard_map/ppermute | solution.py:346
  37.0 5.1 %collective-permute-done.7.refs_3_ = f32[4,64,256]{2,1,0:T(8,128)S(1)} collective-permute-done((f32[4,64,256]{2,1,0:T(8,128)S(1)}, f32[4,64,256]{2,1,0:T(8,128)S(1)}, u32[]{:S(2)}, u32[]{:S(2)}) %collective-permute-start.7) | collective-permute-done | bytes 262176 | tf_op jit(solution)/shard_map/ppermute | solution.py:346
  42.0 1.2 %collective-permute-done.6.refs_2_ = f32[5,64,256]{2,1,0:T(8,128)S(1)} collective-permute-done((f32[5,64,256]{2,1,0:T(8,128)S(1)}, f32[5,64,256]{2,1,0:T(8,128)S(1)}, u32[]{:S(2)}, u32[]{:S(2)}) %collective-permute-start.6) | collective-permute-done | bytes 327712 | tf_op jit(solution)/shard_map/ppermute | solution.py:346
  43.3 1.6 %collective-permute-start.8 = (f32[4,64,256]{2,1,0:T(8,128)S(1)}, f32[4,64,256]{2,1,0:T(8,128)S(1)}, u32[]{:S(2)}, u32[]{:S(2)}) collective-permute-start(f32[4,64,256]{2,1,0:T(8,128)S(1)} %get-tuple-element.78), channel_id=1, source_target_pairs={{0,8},{1,9},{2,10},{3,11},{4,12},{5,13},{6,14},{7,15},{8,0},{9,1},... | collective-permute-start | bytes 786440 | tf_op jit(solution)/shard_map/ppermute | solution.py:346
  44.9 4.8 %collective-permute-done.8.refs_1_ = f32[4,64,256]{2,1,0:T(8,128)S(1)} collective-permute-done((f32[4,64,256]{2,1,0:T(8,128)S(1)}, f32[4,64,256]{2,1,0:T(8,128)S(1)}, u32[]{:S(2)}, u32[]{:S(2)}) %collective-permute-start.8) | collective-permute-done | bytes 262176 | tf_op jit(solution)/shard_map/ppermute | solution.py:346
  49.8 1.7 %collective-permute-done.9.refs_1_ = f32[8,64,256]{2,1,0:T(8,128)S(1)} collective-permute-done((f32[8,64,256]{2,1,0:T(8,128)S(1)}, f32[8,64,256]{2,1,0:T(8,128)S(1)}, u32[]{:S(2)}, u32[]{:S(2)}) %collective-permute-start.9) | collective-permute-done | bytes 524320 | tf_op jit(solution)/shard_map/ppermute | solution.py:346
  51.6 1.1 %collective-permute-start.12 = (f32[5,64,256]{2,1,0:T(8,128)S(1)}, f32[5,64,256]{2,1,0:T(8,128)S(1)}, u32[]{:S(2)}, u32[]{:S(2)}) collective-permute-start(f32[5,64,256]{2,1,0:T(8,128)S(1)} %get-tuple-element.88), channel_id=1, source_target_pairs={{0,2},{1,3},{2,0},{3,1},{4,6},{5,7},{6,4},{7,5},{8,10},{9,11},{10,... | collective-permute-start | bytes 983048 | tf_op jit(solution)/shard_map/ppermute | solution.py:346
  52.7 1.4 %collective-permute-start.11 = (f32[4,64,256]{2,1,0:T(8,128)S(1)}, f32[4,64,256]{2,1,0:T(8,128)S(1)}, u32[]{:S(2)}, u32[]{:S(2)}) collective-permute-start(f32[4,64,256]{2,1,0:T(8,128)S(1)} %get-tuple-element.87), channel_id=1, source_target_pairs={{0,1},{1,0},{2,3},{3,2},{4,5},{5,4},{6,7},{7,6},{8,9},{9,8},{10,11... | collective-permute-start | bytes 786440 | tf_op jit(solution)/shard_map/ppermute | solution.py:346
  54.1 1.7 %collective-permute-start.13 = (f32[4,64,256]{2,1,0:T(8,128)S(1)}, f32[4,64,256]{2,1,0:T(8,128)S(1)}, u32[]{:S(2)}, u32[]{:S(2)}) collective-permute-start(f32[4,64,256]{2,1,0:T(8,128)S(1)} %get-tuple-element.95), channel_id=1, source_target_pairs={{0,16},{1,17},{2,18},{3,19},{4,20},{5,21},{6,22},{7,23},{8,24},{9,... | collective-permute-start | bytes 786440 | tf_op jit(solution)/shard_map/ppermute | solution.py:346
  55.8 3.3 %collective-permute-done.11.refs_2_ = f32[4,64,256]{2,1,0:T(8,128)S(1)} collective-permute-done((f32[4,64,256]{2,1,0:T(8,128)S(1)}, f32[4,64,256]{2,1,0:T(8,128)S(1)}, u32[]{:S(2)}, u32[]{:S(2)}) %collective-permute-start.11) | collective-permute-done | bytes 262176 | tf_op jit(solution)/shard_map/ppermute | solution.py:346
  59.2 2.6 %collective-permute-start.14 = (f32[4,64,256]{2,1,0:T(8,128)S(1)}, f32[4,64,256]{2,1,0:T(8,128)S(1)}, u32[]{:S(2)}, u32[]{:S(2)}) collective-permute-start(f32[4,64,256]{2,1,0:T(8,128)S(1)} %get-tuple-element.102), channel_id=1, source_target_pairs={{0,8},{1,9},{2,10},{3,11},{4,12},{5,13},{6,14},{7,15},{8,0},{9,1},... | collective-permute-start | bytes 786440 | tf_op jit(solution)/shard_map/ppermute | solution.py:346
  61.8 0.3 gram.1
  62.1 2.7 %eliminate.2 = (f32[8,128]{1,0:T(8,128)S(1)}, f32[64,64]{1,0:T(8,128)S(1)}) custom-call(f32[8,128]{1,0:T(8,128)S(1)} %get-tuple-element.91._token, f32[64,64]{1,0:T(8,128)S(1)} %get-tuple-element.92.refs_0_), custom_call_target="tpu_custom_call" | custom-call | flops 1 | bytes 1 | tf_op jit(solution)/shard_map/eliminate/pallas_call | solution.py:53
  64.8 1.4 %collective-permute-done.13.refs_1_ = f32[4,64,256]{2,1,0:T(8,128)S(1)} collective-permute-done((f32[4,64,256]{2,1,0:T(8,128)S(1)}, f32[4,64,256]{2,1,0:T(8,128)S(1)}, u32[]{:S(2)}, u32[]{:S(2)}) %collective-permute-start.13) | collective-permute-done | bytes 262176 | tf_op jit(solution)/shard_map/ppermute | solution.py:346
  66.3 2.7 %eliminate.3 = (f32[8,128]{1,0:T(8,128)S(1)}, f32[64,64]{1,0:T(8,128)S(1)}) custom-call(f32[8,128]{1,0:T(8,128)S(1)} %get-tuple-element.96._token, f32[64,64]{1,0:T(8,128)S(1)} %get-tuple-element.97.refs_0_), custom_call_target="tpu_custom_call" | custom-call | flops 4000000000 | bytes 1 | tf_op jit(solution)/shard_map/eliminate/pallas_call | solution.py:53
  69.3 1.7 %finish.1 = (f32[8,128]{1,0:T(8,128)}, f32[64,256]{1,0:T(8,128)}, f32[256,256]{1,0:T(8,128)}) custom-call(f32[8,128]{1,0:T(8,128)S(1)} %get-tuple-element.100._token, f32[4,64,256]{2,1,0:T(8,128)S(1)} %get-tuple-element.101.refs_0_, f32[4,64,256]{2,1,0:T(8,128)S(1)} %collective-permute-done.14.refs_1_, f32[64,256]{1,0:T(8,128)S(1)} %get-tuple-element.90.refs_0_.refs_2_, ...), custom_call_target="tpu_custom_call" | custom-call | flops 1 | bytes 1 | tf_op jit(solution)/shard_map/finish/pallas_call | solution.py:53
  (22 shorter events, 1.8 us)
Async XLA Ops:
  2.2 1.6 %copy-start = (f32[2048,256]{1,0:T(8,128)S(1)}, f32[2048,256]{1,0:T(8,128)}, u32[]{:S(2)}) copy-start(f32[2048,256]{1,0:T(8,128)} %refs_1_.1) | copy-start | bytes 6291460
  9.4 7.3 %collective-permute-start = (f32[17,128,256]{2,1,0:T(8,128)S(1)}, f32[17,128,256]{2,1,0:T(8,128)S(1)}, u32[]{:S(2)}, u32[]{:S(2)}) collective-permute-start(f32[17,128,256]{2,1,0:T(8,128)S(1)} %get-tuple-element.59.refs_0_), channel_id=1, source_target_pairs={{0,4},{1,5},{2,6},{3,7},{4,0},{5,1},{6,2},{7,3},{8,12},{9,13},{10,... | collective-permute-start | bytes 6684680 | tf_op jit(solution)/shard_map/ppermute | solution.py:346
  17.0 15.4 %collective-permute-start.3 = (f32[8,64,256]{2,1,0:T(8,128)S(1)}, f32[8,64,256]{2,1,0:T(8,128)S(1)}, u32[]{:S(2)}, u32[]{:S(2)}) collective-permute-start(f32[8,64,256]{2,1,0:T(8,128)S(1)} %get-tuple-element.67), channel_id=1, source_target_pairs={{0,1},{1,0},{2,3},{3,2},{4,5},{5,4},{6,7},{7,6},{8,9},{9,8},{10,11... | collective-permute-start | bytes 1572872 | tf_op jit(solution)/shard_map/ppermute | solution.py:346
  18.7 13.7 %collective-permute-start.4 = (f32[8,64,256]{2,1,0:T(8,128)S(1)}, f32[8,64,256]{2,1,0:T(8,128)S(1)}, u32[]{:S(2)}, u32[]{:S(2)}) collective-permute-start(f32[8,64,256]{2,1,0:T(8,128)S(1)} %get-tuple-element.68), channel_id=1, source_target_pairs={{0,2},{1,3},{2,0},{3,1},{4,6},{5,7},{6,4},{7,5},{8,10},{9,11},{10,... | collective-permute-start | bytes 1572872 | tf_op jit(solution)/shard_map/ppermute | solution.py:346
  21.1 1.3 %collective-permute-start.1 = (f32[64,256]{1,0:T(8,128)S(1)}, f32[64,256]{1,0:T(8,128)S(1)}, u32[]{:S(2)}, u32[]{:S(2)}) collective-permute-start(f32[64,256]{1,0:T(8,128)S(1)} %get-tuple-element.62.refs_0_), channel_id=1, source_target_pairs={{0,4},{1,5},{2,6},{3,7},{4,0},{5,1},{6,2},{7,3},{8,12},{9,13},{10,... | collective-permute-start | bytes 196616 | tf_op jit(solution)/shard_map/ppermute | solution.py:346
  22.5 4.4 %collective-permute-start.2 = (f32[64,256]{1,0:T(8,128)S(1)}, f32[64,256]{1,0:T(8,128)S(1)}, u32[]{:S(2)}, u32[]{:S(2)}) collective-permute-start(f32[64,256]{1,0:T(8,128)S(1)} %get-tuple-element.64.refs_0_), channel_id=1, source_target_pairs={{0,8},{1,9},{2,10},{3,11},{4,12},{5,13},{6,14},{7,15},{8,0},{9,1},... | collective-permute-start | bytes 196616 | tf_op jit(solution)/shard_map/ppermute | solution.py:346
  26.8 5.6 %collective-permute-start.5 = (f32[64,256]{1,0:T(8,128)S(1)}, f32[64,256]{1,0:T(8,128)S(1)}, u32[]{:S(2)}, u32[]{:S(2)}) collective-permute-start(f32[64,256]{1,0:T(8,128)S(1)} %get-tuple-element.69.refs_3_), channel_id=1, source_target_pairs={{0,16},{1,17},{2,18},{3,19},{4,20},{5,21},{6,22},{7,23},{8,24},{9,... | collective-permute-start | bytes 196616 | tf_op jit(solution)/shard_map/ppermute | solution.py:346
  32.5 10.7 %collective-permute-start.6 = (f32[5,64,256]{2,1,0:T(8,128)S(1)}, f32[5,64,256]{2,1,0:T(8,128)S(1)}, u32[]{:S(2)}, u32[]{:S(2)}) collective-permute-start(f32[5,64,256]{2,1,0:T(8,128)S(1)} %get-tuple-element.74), channel_id=1, source_target_pairs={{0,1},{1,0},{2,3},{3,2},{4,5},{5,4},{6,7},{7,6},{8,9},{9,8},{10,11... | collective-permute-start | bytes 983048 | tf_op jit(solution)/shard_map/ppermute | solution.py:346
  32.8 9.2 %collective-permute-start.7 = (f32[4,64,256]{2,1,0:T(8,128)S(1)}, f32[4,64,256]{2,1,0:T(8,128)S(1)}, u32[]{:S(2)}, u32[]{:S(2)}) collective-permute-start(f32[4,64,256]{2,1,0:T(8,128)S(1)} %get-tuple-element.75), channel_id=1, source_target_pairs={{0,2},{1,3},{2,0},{3,1},{4,6},{5,7},{6,4},{7,5},{8,10},{9,11},{10,... | collective-permute-start | bytes 786440 | tf_op jit(solution)/shard_map/ppermute | solution.py:346
  34.6 16.8 %collective-permute-start.9 = (f32[8,64,256]{2,1,0:T(8,128)S(1)}, f32[8,64,256]{2,1,0:T(8,128)S(1)}, u32[]{:S(2)}, u32[]{:S(2)}) collective-permute-start(f32[8,64,256]{2,1,0:T(8,128)S(1)} %get-tuple-element.81), channel_id=1, source_target_pairs={{0,1},{1,0},{2,3},{3,2},{4,5},{5,4},{6,7},{7,6},{8,9},{9,8},{10,11... | collective-permute-start | bytes 1572872 | tf_op jit(solution)/shard_map/ppermute | solution.py:346
  35.9 15.6 %collective-permute-start.10 = (f32[8,64,256]{2,1,0:T(8,128)S(1)}, f32[8,64,256]{2,1,0:T(8,128)S(1)}, u32[]{:S(2)}, u32[]{:S(2)}) collective-permute-start(f32[8,64,256]{2,1,0:T(8,128)S(1)} %get-tuple-element.82), channel_id=1, source_target_pairs={{0,2},{1,3},{2,0},{3,1},{4,6},{5,7},{6,4},{7,5},{8,10},{9,11},{10,... | collective-permute-start | bytes 1572872 | tf_op jit(solution)/shard_map/ppermute | solution.py:346
  43.3 6.4 %collective-permute-start.8 = (f32[4,64,256]{2,1,0:T(8,128)S(1)}, f32[4,64,256]{2,1,0:T(8,128)S(1)}, u32[]{:S(2)}, u32[]{:S(2)}) collective-permute-start(f32[4,64,256]{2,1,0:T(8,128)S(1)} %get-tuple-element.78), channel_id=1, source_target_pairs={{0,8},{1,9},{2,10},{3,11},{4,12},{5,13},{6,14},{7,15},{8,0},{9,1},... | collective-permute-start | bytes 786440 | tf_op jit(solution)/shard_map/ppermute | solution.py:346
  51.6 7.5 %collective-permute-start.12 = (f32[5,64,256]{2,1,0:T(8,128)S(1)}, f32[5,64,256]{2,1,0:T(8,128)S(1)}, u32[]{:S(2)}, u32[]{:S(2)}) collective-permute-start(f32[5,64,256]{2,1,0:T(8,128)S(1)} %get-tuple-element.88), channel_id=1, source_target_pairs={{0,2},{1,3},{2,0},{3,1},{4,6},{5,7},{6,4},{7,5},{8,10},{9,11},{10,... | collective-permute-start | bytes 983048 | tf_op jit(solution)/shard_map/ppermute | solution.py:346
  52.7 6.4 %collective-permute-start.11 = (f32[4,64,256]{2,1,0:T(8,128)S(1)}, f32[4,64,256]{2,1,0:T(8,128)S(1)}, u32[]{:S(2)}, u32[]{:S(2)}) collective-permute-start(f32[4,64,256]{2,1,0:T(8,128)S(1)} %get-tuple-element.87), channel_id=1, source_target_pairs={{0,1},{1,0},{2,3},{3,2},{4,5},{5,4},{6,7},{7,6},{8,9},{9,8},{10,11... | collective-permute-start | bytes 786440 | tf_op jit(solution)/shard_map/ppermute | solution.py:346
  54.1 12.1 %collective-permute-start.13 = (f32[4,64,256]{2,1,0:T(8,128)S(1)}, f32[4,64,256]{2,1,0:T(8,128)S(1)}, u32[]{:S(2)}, u32[]{:S(2)}) collective-permute-start(f32[4,64,256]{2,1,0:T(8,128)S(1)} %get-tuple-element.95), channel_id=1, source_target_pairs={{0,16},{1,17},{2,18},{3,19},{4,20},{5,21},{6,22},{7,23},{8,24},{9,... | collective-permute-start | bytes 786440 | tf_op jit(solution)/shard_map/ppermute | solution.py:346
  59.2 10.1 %collective-permute-start.14 = (f32[4,64,256]{2,1,0:T(8,128)S(1)}, f32[4,64,256]{2,1,0:T(8,128)S(1)}, u32[]{:S(2)}, u32[]{:S(2)}) collective-permute-start(f32[4,64,256]{2,1,0:T(8,128)S(1)} %get-tuple-element.102), channel_id=1, source_target_pairs={{0,8},{1,9},{2,10},{3,11},{4,12},{5,13},{6,14},{7,15},{8,0},{9,1},... | collective-permute-start | bytes 786440 | tf_op jit(solution)/shard_map/ppermute | solution.py:346

commit v6 on v5

--- a/solution.py
+++ b/solution.py
@@ -199,21 +199,24 @@
     return queue.call("spread", functools.partial(spread_kernel, groups, n_y), outs, (own, got))
 
 
-def join_kernel(groups, n_y, n_parts, ride_x, stay, *refs):
+def join_kernel(groups, n_y, n_parts, ride_x, cuts, stay, *refs):
     n = sum(len(zs) for zs in groups)
     came = refs[: len(groups) * n_y]
     parts = refs[len(came) : len(came) + n_parts]
-    keep, rows, send_x, *send_y = refs[len(came) + n_parts :]
+    keep, rows, *sends = refs[len(came) + n_parts :]
+    at = [(c, m) for c, cut in enumerate(cuts) for m in range(cut)]
     n_x = n * 2 * n_y
     i = 0
     for g, zs in enumerate(groups):
         got_x, *got_y = came[g * n_y : (g + 1) * n_y]
         for j in range(len(zs)):
+            cut, m = at[i]
+            send_x, *send_y = sends[cut * n_y : (cut + 1) * n_y]
             for s in range(2):
                 for dy in range(n_y):
                     value = stay[2 * (i * n_y + dy) + s] + got_x[2 * (j * n_y + dy) + s]
                     if dy:
-                        send_y[dy - 1][2 * i + s] = value
+                        send_y[dy - 1][2 * m + s] = value
                     else:
                         keep[4 * i + s] = value
                 for dx in range(2):
@@ -221,7 +224,7 @@
                     for ref in got_y:
                         value = value + ref[2 * (j * 2 + dx) + s]
                     if dx:
-                        send_x[2 * i + s] = value
+                        send_x[2 * m + s] = value
                     else:
                         keep[4 * i + 2 + s] = value
             i += 1
@@ -229,38 +232,49 @@
     for ref in parts[1:]:
         total = total + ref[...]
     rows[...] = total
-    for ref in [send_x] if ride_x else send_y:
-        ref[2 * n] = total
-
-
-def join(queue, groups, n_y, state, parts, ride_x):
+    for ref in sends[:1] if ride_x else sends[1:n_y]:
+        ref[2 * cuts[0]] = total
+
+
+def join(queue, groups, n_y, state, parts, ride_x, cuts):
     stay = state[0]
     half, width = stay.shape[1:]
     n = sum(len(zs) for zs in groups)
-    pairs = [shaped((2 * n + (1 if ride_x == (k == 0) else 0), half, width)) for k in range(n_y)]
-    outs = [shaped((4 * n, half, width)), shaped((half, width))] + pairs
-    kernel = functools.partial(join_kernel, groups, n_y, len(parts), ride_x)
+    outs = [shaped((4 * n, half, width)), shaped((half, width))]
+    for c, cut in enumerate(cuts):
+        outs += [shaped((2 * cut + (1 if c == 0 and ride_x == (k == 0) else 0), half, width)) for k in range(n_y)]
+    kernel = functools.partial(join_kernel, groups, n_y, len(parts), ride_x, cuts)
     return queue.call("join", kernel, outs, (*state, *parts))
 
 
-def merge_kernel(n, n_y, ride_x, keep, rows, got_x, *refs):
-    got_y, total, outs = refs[: n_y - 1], refs[n_y - 1], refs[n_y:]
+def merge_kernel(start, n, n_y, ride, keep, got_x, *refs):
+    got_y, refs = refs[: n_y - 1], refs[n_y - 1 :]
+    if ride is None:
+        far, outs = refs[:-n], refs[-n:]
+    else:
+        far, (rows, total, *outs) = (), refs
+        value = rows[...]
+        for ref in [got_x] if ride else got_y:
+            value = value + ref[2 * n]
+        total[...] = value
     for i, out in enumerate(outs):
         for s in range(2):
-            x = keep[4 * i + s]
+            x = keep[4 * (start + i) + s]
+            y = keep[4 * (start + i) + 2 + s] + got_x[2 * i + s]
             for ref in got_y:
                 x = x + ref[2 * i + s]
+            for ref in far:
+                x = x + ref[s]
+                y = y + ref[2 + s]
             out[s] = x
-            out[2 + s] = keep[4 * i + 2 + s] + got_x[2 * i + s]
-    value = rows[...]
-    for ref in [got_x] if ride_x else got_y:
-        value = value + ref[2 * n]
-    total[...] = value
-
-
-def merge(queue, n, n_y, keep, rows, came, ride_x):
-    outs = (shaped(rows.shape),) + (shaped((4,) + keep.shape[1:]),) * n
-    return queue.call("merge", functools.partial(merge_kernel, n, n_y, ride_x), outs, (keep, rows, *came))
+            out[2 + s] = y
+
+
+def merge(queue, start, n, n_y, keep, came, ride, more):
+    outs = (shaped((4,) + keep.shape[1:]),) * n
+    if ride is not None:
+        outs = (shaped(more[0].shape),) + outs
+    return queue.call("merge", functools.partial(merge_kernel, start, n, n_y, ride), outs, (keep, *came, *more))
 
 
 def total_kernel(*refs):
@@ -369,9 +383,9 @@
             came += swaps(sends[g * n_y : (g + 1) * n_y])
         return [stay, *came]
 
-    def do_join(groups, state, parts, ride_x):
-        keep, rows, *sends = join(queue, groups, n_y, state, parts, ride_x)
-        return keep, rows, swaps(sends)
+    def do_join(groups, state, parts, ride_x, cuts):
+        keep, rows, *sends = join(queue, groups, n_y, state, parts, ride_x, cuts)
+        return keep, rows, [swaps(sends[c * n_y : (c + 1) * n_y]) for c in range(len(cuts))]
 
     mid = tuple(range(n_z // 2 - 1, 0, -1))
     far_groups = (tuple(range(n_z - 1, n_z // 2 - 1, -1)),)
@@ -382,17 +396,18 @@
     masks = [n_doc << b for b in range((n_term - 1).bit_length())]
     for mask in masks[:-1]:
         part = total(queue, [part, swap(part, mask)])
-    joined = do_join(far_groups, state, (part, swap(part, masks[-1])), True)
+    n_far, n_mid = len(far_groups[0]), len(mid)
+    keep, rows, came = do_join(far_groups, state, (part, swap(part, masks[-1])), True, (n_far,))
     state = do_spread(near_groups)
-    rows, *relayed, far = merge(queue, len(far_groups[0]), n_y, *joined, True)
+    rows, *relayed, far = merge(queue, 0, n_far, n_y, keep, came[0], True, (rows,))
     relayed = [swap(v, 2 * n_doc * (dz - n_z // 2)) for v, dz in zip(relayed, far_groups[0])]
     far = swap(total(queue, [far, *relayed]), n_doc * n_z)
-    joined = do_join(near_groups, state, (rows,), False)
-    rows, *sends, near = merge(queue, len(mid) + 1, n_y, *joined, False)
+    keep, rows, came = do_join(near_groups, state, (rows,), False, (n_mid, 1))
+    rows, *sends = merge(queue, 0, n_mid, n_y, keep, came[0], False, (rows,))
     last = [swap(v, 2 * n_doc * dz) for v, dz in zip(sends, mid)]
     gram = gram_of(queue, rows)
     gram = eliminate(queue, gram, 0, TINY)
-    near = total(queue, [near, far])
+    near, = merge(queue, n_mid, 1, n_y, keep, came[1], None, (far,))
     gram = eliminate(queue, gram, 1, LONG)
     solve = solver(queue, rows, gram)
     return finish(queue, near, last, rows, solve)

time: 71.3 us -> 70.3 us (0.986)
  starting transfers between devices: 22.1 us -> 21.2 us
    ppermute x15 -> x17, starting transfers between devices: 22.1 us -> 21.2 us  [swap(): return lax.ppermute(v, AXES, [(i, i ^ mask) for i in range(devices)])]
    ppermute x15 -> x17, waiting for transfers between devices: 23.8 us -> 23.6 us  [swap(): return lax.ppermute(v, AXES, [(i, i ^ mask) for i in range(devices)])]
  transfers between devices with their start and end apart: 15 -> 17, of which waited for: 9 -> 8; matrix products, arithmetic and copies ran while one was open for 0% -> 0% of each run, Pallas kernels for 19% -> 18%
where the time goes in v6:
time: 70.3 us; the launch traced here: 69.7 us
  waiting for transfers between devices  23.6 us (34%)
  starting transfers between devices  21.2 us (30%)
  Pallas kernels  20.9 us (30%)
  local copies, waits for them, and re-layouts  1.58 us (2%)
  other arithmetic  1.51 us (2%)
  between operations  0.82 us (1%)
    ppermute x17, waiting for transfers between devices, swap(): return lax.ppermute(v, AXES, [(i, i ^ mask) for i in range(devices)])  23.6 us
    ppermute x17, starting transfers between devices, swap(): return lax.ppermute(v, AXES, [(i, i ^ mask) for i in range(devices)])  21.2 us
    pallas_call x2, Pallas kernels, products(): pl.pallas_call(functools.partial(products_kernel, slots, away), out_shape...  11.2 us
    pallas_call x16, Pallas kernels, call(): pl.pallas_call(functools.partial(in_order, kernel, len(args) + len(smem))...  9.64 us
    unnamed x2, local copies, waits for them, and re-layouts  1.58 us
  transfers between devices with their start and end apart: 17, of which 8 were waited for; matrix products, arithmetic and copies ran while one was open for 0% of the time, Pallas kernels for 18%

profile of v6, /device:TPU:0, one launch (start us, length us, event | category | flops | bytes accessed | tf_op | source)
XLA Modules:
  0.0 69.7 jit_solution(9638608828673361281)
XLA Ops:
  0.7 0.7 and_select_fusion.5
  1.4 0.8 %fusion.3.code_ref.refs_2_ = s32[192]{0:T(256)S(1)} fusion(s32[2,64]{1,0:T(2,128)S(1)} %broadcast_select_fusion, s32[2,128]{1,0:T(2,128)} %bitcast.2, pred[2]{0:T(512)(128)(4,1)S(1)} %iota_compare_fusion, s32[]{:T(128)S(6)} %mul.12, s32[]{:T(128)S(6)} %add.39), kind=kLoop, calls=%fused_computation.15 | loop fusion | flops 22080 | bytes 2314 | tf_op jit(solution)/shard_map/reduce_sum | solution.py:369
  2.2 1.6 %copy-done = f32[2048,256]{1,0:T(8,128)S(1)} copy-done((f32[2048,256]{1,0:T(8,128)S(1)}, f32[2048,256]{1,0:T(8,128)}, u32[]{:S(2)}) %copy-start) | copy-done | bytes 2097176
  3.8 6.1 %products_away.1 = (f32[17,128,256]{2,1,0:T(8,128)S(1)}, f32[8,128]{1,0:T(8,128)}, f32[128,128,128]{2,1,0:T(8,128)S(1)}, bf16[2048,256]{1,0:T(8,128)(2,1)S(1)}, bf16[2048,256]{1,0:T(8,128)(2,1)S(1)}) custom-call(s32[192]{0:T(256)S(1)} %fusion.3.code_ref.refs_2_, f32[128,128,128]{2,1,0:T(8,128)} %refs_0_.1, f32[2048,256]{1,0:T(8,128)S(1)} %copy-done), custom_call_target="tpu_custom_call" | custom-call | flops 8000000000 | bytes 5242880 | tf_op jit(solution)/shard_map/products_away/pallas_call | solution.py:136
  9.8 0.5 collective-permute-start
  10.4 5.2 %products_here.1 = (f32[17,128,256]{2,1,0:T(8,128)S(1)}, f32[8,128]{1,0:T(8,128)S(1)}) custom-call(s32[192]{0:T(256)S(1)} %fusion.3.code_ref.refs_2_, f32[128,128,128]{2,1,0:T(8,128)S(1)} %get-tuple-element.55.refs_0_, bf16[2048,256]{1,0:T(8,128)(2,1)S(1)} %get-tuple-element.56.refs_1_, bf16[2048,256]{1,0:T(8,128)(2,1)S(1)} %get-tuple-element.57.refs_2_), custom_call_target="tpu_custom_call" | custom-call | flops 8000000000 | bytes 5242880 | tf_op jit(solution)/shard_map/products_here/pallas_call | solution.py:136
  15.8 3.6 %collective-permute-start.3 = (f32[8,64,256]{2,1,0:T(8,128)S(1)}, f32[8,64,256]{2,1,0:T(8,128)S(1)}, u32[]{:S(2)}, u32[]{:S(2)}) collective-permute-start(f32[8,64,256]{2,1,0:T(8,128)S(1)} %get-tuple-element.68), channel_id=1, source_target_pairs={{0,1},{1,0},{2,3},{3,2},{4,5},{5,4},{6,7},{7,6},{8,9},{9,8},{10,11... | collective-permute-start | bytes 1572872 | tf_op jit(solution)/shard_map/ppermute | solution.py:360
  19.4 0.8 %collective-permute-start.4 = (f32[8,64,256]{2,1,0:T(8,128)S(1)}, f32[8,64,256]{2,1,0:T(8,128)S(1)}, u32[]{:S(2)}, u32[]{:S(2)}) collective-permute-start(f32[8,64,256]{2,1,0:T(8,128)S(1)} %get-tuple-element.69), channel_id=1, source_target_pairs={{0,2},{1,3},{2,0},{3,1},{4,6},{5,7},{6,4},{7,5},{8,10},{9,11},{10,... | collective-permute-start | bytes 1572872 | tf_op jit(solution)/shard_map/ppermute | solution.py:360
  20.2 0.9 %pick.1 = (f32[8,128]{1,0:T(8,128)S(1)}, f32[64,256]{1,0:T(8,128)S(1)}) custom-call(f32[8,128]{1,0:T(8,128)S(1)} %get-tuple-element.61._token, f32[17,128,256]{2,1,0:T(8,128)S(1)} %get-tuple-element.60.refs_0_, f32[17,128,256]{2,1,0:T(8,128)S(1)} %get-tuple-element.59.refs_0_.refs_1_, s32[192]{0:T(256)S(1)} %fusion.3.code_ref.refs_2_), custom_call_target="tpu_custom_call" | custom-call | flops 1 | bytes 1 | tf_op jit(solution)/shard_map/pick/pallas_call | solution.py:53
  21.2 1.2 %collective-permute-done.1.refs_1_ = f32[64,256]{1,0:T(8,128)S(1)} collective-permute-done((f32[64,256]{1,0:T(8,128)S(1)}, f32[64,256]{1,0:T(8,128)S(1)}, u32[]{:S(2)}, u32[]{:S(2)}) %collective-permute-start.1) | collective-permute-done | bytes 65568 | tf_op jit(solution)/shard_map/ppermute | solution.py:360
  22.5 1.2 %collective-permute-start.2 = (f32[64,256]{1,0:T(8,128)S(1)}, f32[64,256]{1,0:T(8,128)S(1)}, u32[]{:S(2)}, u32[]{:S(2)}) collective-permute-start(f32[64,256]{1,0:T(8,128)S(1)} %get-tuple-element.65.refs_0_), channel_id=1, source_target_pairs={{0,8},{1,9},{2,10},{3,11},{4,12},{5,13},{6,14},{7,15},{8,0},{9,1},... | collective-permute-start | bytes 196616 | tf_op jit(solution)/shard_map/ppermute | solution.py:360
  23.7 3.1 %collective-permute-done.2.refs_1_ = f32[64,256]{1,0:T(8,128)S(1)} collective-permute-done((f32[64,256]{1,0:T(8,128)S(1)}, f32[64,256]{1,0:T(8,128)S(1)}, u32[]{:S(2)}, u32[]{:S(2)}) %collective-permute-start.2) | collective-permute-done | bytes 65568 | tf_op jit(solution)/shard_map/ppermute | solution.py:360
  26.8 2.6 %collective-permute-start.5 = (f32[64,256]{1,0:T(8,128)S(1)}, f32[64,256]{1,0:T(8,128)S(1)}, u32[]{:S(2)}, u32[]{:S(2)}) collective-permute-start(f32[64,256]{1,0:T(8,128)S(1)} %get-tuple-element.70.refs_3_), channel_id=1, source_target_pairs={{0,16},{1,17},{2,18},{3,19},{4,20},{5,21},{6,22},{7,23},{8,24},{9,... | collective-permute-start | bytes 196616 | tf_op jit(solution)/shard_map/ppermute | solution.py:360
  29.5 3.3 %collective-permute-done.5.refs_4_ = f32[64,256]{1,0:T(8,128)S(1)} collective-permute-done((f32[64,256]{1,0:T(8,128)S(1)}, f32[64,256]{1,0:T(8,128)S(1)}, u32[]{:S(2)}, u32[]{:S(2)}) %collective-permute-start.5) | collective-permute-done | bytes 65568 | tf_op jit(solution)/shard_map/ppermute | solution.py:360
  32.9 0.6 collective-permute-start.6
  33.5 0.6 collective-permute-start.7
  34.3 1.7 %collective-permute-start.9 = (f32[8,64,256]{2,1,0:T(8,128)S(1)}, f32[8,64,256]{2,1,0:T(8,128)S(1)}, u32[]{:S(2)}, u32[]{:S(2)}) collective-permute-start(f32[8,64,256]{2,1,0:T(8,128)S(1)} %get-tuple-element.82), channel_id=1, source_target_pairs={{0,1},{1,0},{2,3},{3,2},{4,5},{5,4},{6,7},{7,6},{8,9},{9,8},{10,11... | collective-permute-start | bytes 1572872 | tf_op jit(solution)/shard_map/ppermute | solution.py:360
  36.1 1.3 %collective-permute-start.10 = (f32[8,64,256]{2,1,0:T(8,128)S(1)}, f32[8,64,256]{2,1,0:T(8,128)S(1)}, u32[]{:S(2)}, u32[]{:S(2)}) collective-permute-start(f32[8,64,256]{2,1,0:T(8,128)S(1)} %get-tuple-element.83), channel_id=1, source_target_pairs={{0,2},{1,3},{2,0},{3,1},{4,6},{5,7},{6,4},{7,5},{8,10},{9,11},{10,... | collective-permute-start | bytes 1572872 | tf_op jit(solution)/shard_map/ppermute | solution.py:360
  37.4 5.3 %collective-permute-done.7.refs_2_ = f32[4,64,256]{2,1,0:T(8,128)S(1)} collective-permute-done((f32[4,64,256]{2,1,0:T(8,128)S(1)}, f32[4,64,256]{2,1,0:T(8,128)S(1)}, u32[]{:S(2)}, u32[]{:S(2)}) %collective-permute-start.7) | collective-permute-done | bytes 262176 | tf_op jit(solution)/shard_map/ppermute | solution.py:360
  42.7 0.9 %collective-permute-done.6.refs_1_ = f32[5,64,256]{2,1,0:T(8,128)S(1)} collective-permute-done((f32[5,64,256]{2,1,0:T(8,128)S(1)}, f32[5,64,256]{2,1,0:T(8,128)S(1)}, u32[]{:S(2)}, u32[]{:S(2)}) %collective-permute-start.6) | collective-permute-done | bytes 327712 | tf_op jit(solution)/shard_map/ppermute | solution.py:360
  43.7 0.9 %collective-permute-start.8 = (f32[4,64,256]{2,1,0:T(8,128)S(1)}, f32[4,64,256]{2,1,0:T(8,128)S(1)}, u32[]{:S(2)}, u32[]{:S(2)}) collective-permute-start(f32[4,64,256]{2,1,0:T(8,128)S(1)} %get-tuple-element.79), channel_id=1, source_target_pairs={{0,8},{1,9},{2,10},{3,11},{4,12},{5,13},{6,14},{7,15},{8,0},{9,1},... | collective-permute-start | bytes 786440 | tf_op jit(solution)/shard_map/ppermute | solution.py:360
  44.6 8.1 %collective-permute-done.8.refs_1_ = f32[4,64,256]{2,1,0:T(8,128)S(1)} collective-permute-done((f32[4,64,256]{2,1,0:T(8,128)S(1)}, f32[4,64,256]{2,1,0:T(8,128)S(1)}, u32[]{:S(2)}, u32[]{:S(2)}) %collective-permute-start.8) | collective-permute-done | bytes 262176 | tf_op jit(solution)/shard_map/ppermute | solution.py:360
  52.7 1.1 %collective-permute-start.15 = (f32[4,64,256]{2,1,0:T(8,128)S(1)}, f32[4,64,256]{2,1,0:T(8,128)S(1)}, u32[]{:S(2)}, u32[]{:S(2)}) collective-permute-start(f32[4,64,256]{2,1,0:T(8,128)S(1)} %get-tuple-element.97), channel_id=1, source_target_pairs={{0,16},{1,17},{2,18},{3,19},{4,20},{5,21},{6,22},{7,23},{8,24},{9,... | collective-permute-start | bytes 786440 | tf_op jit(solution)/shard_map/ppermute | solution.py:360
  54.2 0.9 %collective-permute-start.11 = (f32[2,64,256]{2,1,0:T(8,128)S(1)}, f32[2,64,256]{2,1,0:T(8,128)S(1)}, u32[]{:S(2)}, u32[]{:S(2)}) collective-permute-start(f32[2,64,256]{2,1,0:T(8,128)S(1)} %get-tuple-element.87), channel_id=1, source_target_pairs={{0,1},{1,0},{2,3},{3,2},{4,5},{5,4},{6,7},{7,6},{8,9},{9,8},{10,11... | collective-permute-start | bytes 393224 | tf_op jit(solution)/shard_map/ppermute | solution.py:360
  55.0 1.2 %collective-permute-start.13 = (f32[2,64,256]{2,1,0:T(8,128)S(1)}, f32[2,64,256]{2,1,0:T(8,128)S(1)}, u32[]{:S(2)}, u32[]{:S(2)}) collective-permute-start(f32[2,64,256]{2,1,0:T(8,128)S(1)} %get-tuple-element.95), channel_id=1, source_target_pairs={{0,1},{1,0},{2,3},{3,2},{4,5},{5,4},{6,7},{7,6},{8,9},{9,8},{10,11... | collective-permute-start | bytes 393224 | tf_op jit(solution)/shard_map/ppermute | solution.py:360
  56.2 1.9 %collective-permute-start.14 = (f32[2,64,256]{2,1,0:T(8,128)S(1)}, f32[2,64,256]{2,1,0:T(8,128)S(1)}, u32[]{:S(2)}, u32[]{:S(2)}) collective-permute-start(f32[2,64,256]{2,1,0:T(8,128)S(1)} %get-tuple-element.96), channel_id=1, source_target_pairs={{0,2},{1,3},{2,0},{3,1},{4,6},{5,7},{6,4},{7,5},{8,10},{9,11},{10,... | collective-permute-start | bytes 393224 | tf_op jit(solution)/shard_map/ppermute | solution.py:360
  58.1 1.1 %collective-permute-done.11.refs_1_ = f32[2,64,256]{2,1,0:T(8,128)S(1)} collective-permute-done((f32[2,64,256]{2,1,0:T(8,128)S(1)}, f32[2,64,256]{2,1,0:T(8,128)S(1)}, u32[]{:S(2)}, u32[]{:S(2)}) %collective-permute-start.11) | collective-permute-done | bytes 131104 | tf_op jit(solution)/shard_map/ppermute | solution.py:360
  59.2 0.5 collective-permute-done.12.refs_2_
  59.7 2.1 %collective-permute-start.16 = (f32[4,64,256]{2,1,0:T(8,128)S(1)}, f32[4,64,256]{2,1,0:T(8,128)S(1)}, u32[]{:S(2)}, u32[]{:S(2)}) collective-permute-start(f32[4,64,256]{2,1,0:T(8,128)S(1)} %get-tuple-element.104), channel_id=1, source_target_pairs={{0,8},{1,9},{2,10},{3,11},{4,12},{5,13},{6,14},{7,15},{8,0},{9,1},... | collective-permute-start | bytes 786440 | tf_op jit(solution)/shard_map/ppermute | solution.py:360
  62.2 2.7 %eliminate.2 = (f32[8,128]{1,0:T(8,128)S(1)}, f32[64,64]{1,0:T(8,128)S(1)}) custom-call(f32[8,128]{1,0:T(8,128)S(1)} %get-tuple-element.92._token, f32[64,64]{1,0:T(8,128)S(1)} %get-tuple-element.93.refs_0_), custom_call_target="tpu_custom_call" | custom-call | flops 1 | bytes 1 | tf_op jit(solution)/shard_map/eliminate/pallas_call | solution.py:53
  64.9 2.7 %eliminate.3 = (f32[8,128]{1,0:T(8,128)S(1)}, f32[64,64]{1,0:T(8,128)S(1)}) custom-call(f32[8,128]{1,0:T(8,128)S(1)} %get-tuple-element.98._token, f32[64,64]{1,0:T(8,128)S(1)} %get-tuple-element.99.refs_0_), custom_call_target="tpu_custom_call" | custom-call | flops 4000000000 | bytes 1 | tf_op jit(solution)/shard_map/eliminate/pallas_call | solution.py:53
  68.0 1.7 %finish.1 = (f32[8,128]{1,0:T(8,128)}, f32[64,256]{1,0:T(8,128)}, f32[256,256]{1,0:T(8,128)}) custom-call(f32[8,128]{1,0:T(8,128)S(1)} %get-tuple-element.102._token, f32[4,64,256]{2,1,0:T(8,128)S(1)} %get-tuple-element.103.refs_0_, f32[4,64,256]{2,1,0:T(8,128)S(1)} %collective-permute-done.16.refs_1_, f32[64,256]{1,0:T(8,128)S(1)} %get-tuple-element.91.refs_0_.refs_2_, ...), custom_call_target="tpu_custom_call" | custom-call | flops 1 | bytes 1 | tf_op jit(solution)/shard_map/finish/pallas_call | solution.py:53
  (26 shorter events, 2.1 us)
Async XLA Ops:
  2.2 1.6 %copy-start = (f32[2048,256]{1,0:T(8,128)S(1)}, f32[2048,256]{1,0:T(8,128)}, u32[]{:S(2)}) copy-start(f32[2048,256]{1,0:T(8,128)} %refs_1_.1) | copy-start | bytes 6291460
  9.8 5.7 %collective-permute-start = (f32[17,128,256]{2,1,0:T(8,128)S(1)}, f32[17,128,256]{2,1,0:T(8,128)S(1)}, u32[]{:S(2)}, u32[]{:S(2)}) collective-permute-start(f32[17,128,256]{2,1,0:T(8,128)S(1)} %get-tuple-element.60.refs_0_), channel_id=1, source_target_pairs={{0,4},{1,5},{2,6},{3,7},{4,0},{5,1},{6,2},{7,3},{8,12},{9,13},{10,... | collective-permute-start | bytes 6684680 | tf_op jit(solution)/shard_map/ppermute | solution.py:360
  15.8 16.9 %collective-permute-start.3 = (f32[8,64,256]{2,1,0:T(8,128)S(1)}, f32[8,64,256]{2,1,0:T(8,128)S(1)}, u32[]{:S(2)}, u32[]{:S(2)}) collective-permute-start(f32[8,64,256]{2,1,0:T(8,128)S(1)} %get-tuple-element.68), channel_id=1, source_target_pairs={{0,1},{1,0},{2,3},{3,2},{4,5},{5,4},{6,7},{7,6},{8,9},{9,8},{10,11... | collective-permute-start | bytes 1572872 | tf_op jit(solution)/shard_map/ppermute | solution.py:360
  19.4 13.4 %collective-permute-start.4 = (f32[8,64,256]{2,1,0:T(8,128)S(1)}, f32[8,64,256]{2,1,0:T(8,128)S(1)}, u32[]{:S(2)}, u32[]{:S(2)}) collective-permute-start(f32[8,64,256]{2,1,0:T(8,128)S(1)} %get-tuple-element.69), channel_id=1, source_target_pairs={{0,2},{1,3},{2,0},{3,1},{4,6},{5,7},{6,4},{7,5},{8,10},{9,11},{10,... | collective-permute-start | bytes 1572872 | tf_op jit(solution)/shard_map/ppermute | solution.py:360
  21.2 1.3 %collective-permute-start.1 = (f32[64,256]{1,0:T(8,128)S(1)}, f32[64,256]{1,0:T(8,128)S(1)}, u32[]{:S(2)}, u32[]{:S(2)}) collective-permute-start(f32[64,256]{1,0:T(8,128)S(1)} %get-tuple-element.63.refs_0_), channel_id=1, source_target_pairs={{0,4},{1,5},{2,6},{3,7},{4,0},{5,1},{6,2},{7,3},{8,12},{9,13},{10,... | collective-permute-start | bytes 196616 | tf_op jit(solution)/shard_map/ppermute | solution.py:360
  22.5 4.3 %collective-permute-start.2 = (f32[64,256]{1,0:T(8,128)S(1)}, f32[64,256]{1,0:T(8,128)S(1)}, u32[]{:S(2)}, u32[]{:S(2)}) collective-permute-start(f32[64,256]{1,0:T(8,128)S(1)} %get-tuple-element.65.refs_0_), channel_id=1, source_target_pairs={{0,8},{1,9},{2,10},{3,11},{4,12},{5,13},{6,14},{7,15},{8,0},{9,1},... | collective-permute-start | bytes 196616 | tf_op jit(solution)/shard_map/ppermute | solution.py:360
  26.8 5.9 %collective-permute-start.5 = (f32[64,256]{1,0:T(8,128)S(1)}, f32[64,256]{1,0:T(8,128)S(1)}, u32[]{:S(2)}, u32[]{:S(2)}) collective-permute-start(f32[64,256]{1,0:T(8,128)S(1)} %get-tuple-element.70.refs_3_), channel_id=1, source_target_pairs={{0,16},{1,17},{2,18},{3,19},{4,20},{5,21},{6,22},{7,23},{8,24},{9,... | collective-permute-start | bytes 196616 | tf_op jit(solution)/shard_map/ppermute | solution.py:360
  32.9 10.7 %collective-permute-start.6 = (f32[5,64,256]{2,1,0:T(8,128)S(1)}, f32[5,64,256]{2,1,0:T(8,128)S(1)}, u32[]{:S(2)}, u32[]{:S(2)}) collective-permute-start(f32[5,64,256]{2,1,0:T(8,128)S(1)} %get-tuple-element.74), channel_id=1, source_target_pairs={{0,1},{1,0},{2,3},{3,2},{4,5},{5,4},{6,7},{7,6},{8,9},{9,8},{10,11... | collective-permute-start | bytes 983048 | tf_op jit(solution)/shard_map/ppermute | solution.py:360
  33.5 9.2 %collective-permute-start.7 = (f32[4,64,256]{2,1,0:T(8,128)S(1)}, f32[4,64,256]{2,1,0:T(8,128)S(1)}, u32[]{:S(2)}, u32[]{:S(2)}) collective-permute-start(f32[4,64,256]{2,1,0:T(8,128)S(1)} %get-tuple-element.75), channel_id=1, source_target_pairs={{0,2},{1,3},{2,0},{3,1},{4,6},{5,7},{6,4},{7,5},{8,10},{9,11},{10,... | collective-permute-start | bytes 786440 | tf_op jit(solution)/shard_map/ppermute | solution.py:360
  34.3 19.5 %collective-permute-start.9 = (f32[8,64,256]{2,1,0:T(8,128)S(1)}, f32[8,64,256]{2,1,0:T(8,128)S(1)}, u32[]{:S(2)}, u32[]{:S(2)}) collective-permute-start(f32[8,64,256]{2,1,0:T(8,128)S(1)} %get-tuple-element.82), channel_id=1, source_target_pairs={{0,1},{1,0},{2,3},{3,2},{4,5},{5,4},{6,7},{7,6},{8,9},{9,8},{10,11... | collective-permute-start | bytes 1572872 | tf_op jit(solution)/shard_map/ppermute | solution.py:360
  36.1 17.8 %collective-permute-start.10 = (f32[8,64,256]{2,1,0:T(8,128)S(1)}, f32[8,64,256]{2,1,0:T(8,128)S(1)}, u32[]{:S(2)}, u32[]{:S(2)}) collective-permute-start(f32[8,64,256]{2,1,0:T(8,128)S(1)} %get-tuple-element.83), channel_id=1, source_target_pairs={{0,2},{1,3},{2,0},{3,1},{4,6},{5,7},{6,4},{7,5},{8,10},{9,11},{10,... | collective-permute-start | bytes 1572872 | tf_op jit(solution)/shard_map/ppermute | solution.py:360
  43.7 9.0 %collective-permute-start.8 = (f32[4,64,256]{2,1,0:T(8,128)S(1)}, f32[4,64,256]{2,1,0:T(8,128)S(1)}, u32[]{:S(2)}, u32[]{:S(2)}) collective-permute-start(f32[4,64,256]{2,1,0:T(8,128)S(1)} %get-tuple-element.79), channel_id=1, source_target_pairs={{0,8},{1,9},{2,10},{3,11},{4,12},{5,13},{6,14},{7,15},{8,0},{9,1},... | collective-permute-start | bytes 786440 | tf_op jit(solution)/shard_map/ppermute | solution.py:360
  52.7 12.1 %collective-permute-start.15 = (f32[4,64,256]{2,1,0:T(8,128)S(1)}, f32[4,64,256]{2,1,0:T(8,128)S(1)}, u32[]{:S(2)}, u32[]{:S(2)}) collective-permute-start(f32[4,64,256]{2,1,0:T(8,128)S(1)} %get-tuple-element.97), channel_id=1, source_target_pairs={{0,16},{1,17},{2,18},{3,19},{4,20},{5,21},{6,22},{7,23},{8,24},{9,... | collective-permute-start | bytes 786440 | tf_op jit(solution)/shard_map/ppermute | solution.py:360
  54.0 5.7 %collective-permute-start.12 = (f32[3,64,256]{2,1,0:T(8,128)S(1)}, f32[3,64,256]{2,1,0:T(8,128)S(1)}, u32[]{:S(2)}, u32[]{:S(2)}) collective-permute-start(f32[3,64,256]{2,1,0:T(8,128)S(1)} %get-tuple-element.88), channel_id=1, source_target_pairs={{0,2},{1,3},{2,0},{3,1},{4,6},{5,7},{6,4},{7,5},{8,10},{9,11},{10,... | collective-permute-start | bytes 589832 | tf_op jit(solution)/shard_map/ppermute | solution.py:360
  54.2 5.0 %collective-permute-start.11 = (f32[2,64,256]{2,1,0:T(8,128)S(1)}, f32[2,64,256]{2,1,0:T(8,128)S(1)}, u32[]{:S(2)}, u32[]{:S(2)}) collective-permute-start(f32[2,64,256]{2,1,0:T(8,128)S(1)} %get-tuple-element.87), channel_id=1, source_target_pairs={{0,1},{1,0},{2,3},{3,2},{4,5},{5,4},{6,7},{7,6},{8,9},{9,8},{10,11... | collective-permute-start | bytes 393224 | tf_op jit(solution)/shard_map/ppermute | solution.py:360
  55.0 9.8 %collective-permute-start.13 = (f32[2,64,256]{2,1,0:T(8,128)S(1)}, f32[2,64,256]{2,1,0:T(8,128)S(1)}, u32[]{:S(2)}, u32[]{:S(2)}) collective-permute-start(f32[2,64,256]{2,1,0:T(8,128)S(1)} %get-tuple-element.95), channel_id=1, source_target_pairs={{0,1},{1,0},{2,3},{3,2},{4,5},{5,4},{6,7},{7,6},{8,9},{9,8},{10,11... | collective-permute-start | bytes 393224 | tf_op jit(solution)/shard_map/ppermute | solution.py:360
  56.2 8.7 %collective-permute-start.14 = (f32[2,64,256]{2,1,0:T(8,128)S(1)}, f32[2,64,256]{2,1,0:T(8,128)S(1)}, u32[]{:S(2)}, u32[]{:S(2)}) collective-permute-start(f32[2,64,256]{2,1,0:T(8,128)S(1)} %get-tuple-element.96), channel_id=1, source_target_pairs={{0,2},{1,3},{2,0},{3,1},{4,6},{5,7},{6,4},{7,5},{8,10},{9,11},{10,... | collective-permute-start | bytes 393224 | tf_op jit(solution)/shard_map/ppermute | solution.py:360
  59.7 8.2 %collective-permute-start.16 = (f32[4,64,256]{2,1,0:T(8,128)S(1)}, f32[4,64,256]{2,1,0:T(8,128)S(1)}, u32[]{:S(2)}, u32[]{:S(2)}) collective-permute-start(f32[4,64,256]{2,1,0:T(8,128)S(1)} %get-tuple-element.104), channel_id=1, source_target_pairs={{0,8},{1,9},{2,10},{3,11},{4,12},{5,13},{6,14},{7,15},{8,0},{9,1},... | collective-permute-start | bytes 786440 | tf_op jit(solution)/shard_map/ppermute | solution.py:360

commit v7 on v6

--- a/solution.py
+++ b/solution.py
@@ -306,12 +306,20 @@
     count = m.shape[0]
     at_row = lax.broadcasted_iota(jnp.int32, (count, count), 0)
     at_col = lax.broadcasted_iota(jnp.int32, (count, count), 1)
-    for k in range(lo, hi):
-        row = m[k : k + 1, :]
-        col = m[:, k : k + 1]
-        scale = 1.0 / m[k : k + 1, k : k + 1]
-        row = jnp.where(at_col[:1] == k, 1.0, row) * scale
-        m = jnp.where(at_row == k, row, jnp.where(at_col == k, 0.0, m) - col * row)
+    for k in range(lo, hi, 2):
+        first, second = m[k : k + 1, :], m[k + 1 : k + 2, :]
+        col, next_col = m[:, k : k + 1], m[:, k + 1 : k + 2]
+        left = 1.0 / first[:, k : k + 1]
+        up = first[:, k + 1 : k + 2] * left
+        down = second[:, k : k + 1] * left
+        right = 1.0 / (second[:, k + 1 : k + 2] - second[:, k : k + 1] * up)
+        place = at_col[:1]
+        first = jnp.where(place == k, 1.0, jnp.where(place == k + 1, 0.0, first))
+        second = jnp.where(place == k + 1, 1.0, jnp.where(place == k, 0.0, second))
+        second = (second - down * first) * right
+        first = left * first - up * second
+        rest = jnp.where((at_col == k) | (at_col == k + 1), 0.0, m) - col * first - next_col * second
+        m = jnp.where(at_row == k, first, jnp.where(at_row == k + 1, second, rest))
     out[...] = m
 
 

time: 70.3 us -> 74.8 us (1.064); the launches traced: 69.7 us -> 75.2 us
  Pallas kernels: 20.9 us -> 25.3 us
  waiting for transfers between devices: 23.6 us -> 25.5 us
    pallas_call x16, Pallas kernels: 9.64 us -> 14 us  [call(): pl.pallas_call(functools.partial(in_order, kernel, len(args) + len(smem))...]
    ppermute x17, waiting for transfers between devices: 23.6 us -> 25.5 us  [swap(): return lax.ppermute(v, AXES, [(i, i ^ mask) for i in range(devices)])]
  transfers between devices with their start and end apart: 17 -> 17, of which waited for: 8 -> 8; matrix products, arithmetic and copies ran while one was open for 0% -> 0% of each run, Pallas kernels for 18% -> 23%
where the time goes in v7:
time: 74.8 us; the launch traced here: 75.2 us
  waiting for transfers between devices  25.5 us (34%)
  Pallas kernels  25.3 us (34%)
  starting transfers between devices  20.5 us (27%)
  local copies, waits for them, and re-layouts  1.58 us (2%)
  other arithmetic  1.51 us (2%)
  between operations  0.82 us (1%)
    ppermute x17, waiting for transfers between devices, swap(): return lax.ppermute(v, AXES, [(i, i ^ mask) for i in range(devices)])  25.5 us
    ppermute x17, starting transfers between devices, swap(): return lax.ppermute(v, AXES, [(i, i ^ mask) for i in range(devices)])  20.5 us
    pallas_call x16, Pallas kernels, call(): pl.pallas_call(functools.partial(in_order, kernel, len(args) + len(smem))...  14 us
    pallas_call x2, Pallas kernels, products(): pl.pallas_call(functools.partial(products_kernel, slots, away), out_shape...  11.2 us
    unnamed x2, local copies, waits for them, and re-layouts  1.58 us
  transfers between devices with their start and end apart: 17, of which 8 were waited for; matrix products, arithmetic and copies ran while one was open for 0% of the time, Pallas kernels for 23%

profile of v7, /device:TPU:0, one launch (start us, length us, event | category | flops | bytes accessed | tf_op | source)
XLA Modules:
  0.0 75.2 jit_solution(16817512299003089344)
XLA Ops:
  0.7 0.7 and_select_fusion.5
  1.4 0.8 %fusion.3.code_ref.refs_2_ = s32[192]{0:T(256)S(1)} fusion(s32[2,64]{1,0:T(2,128)S(1)} %broadcast_select_fusion, s32[2,128]{1,0:T(2,128)} %bitcast.2, pred[2]{0:T(512)(128)(4,1)S(1)} %iota_compare_fusion, s32[]{:T(128)S(6)} %mul.12, s32[]{:T(128)S(6)} %add.39), kind=kLoop, calls=%fused_computation.15 | loop fusion | flops 22080 | bytes 2314 | tf_op jit(solution)/shard_map/reduce_sum | solution.py:377
  2.2 1.6 %copy-done = f32[2048,256]{1,0:T(8,128)S(1)} copy-done((f32[2048,256]{1,0:T(8,128)S(1)}, f32[2048,256]{1,0:T(8,128)}, u32[]{:S(2)}) %copy-start) | copy-done | bytes 2097176
  3.8 6.1 %products_away.1 = (f32[17,128,256]{2,1,0:T(8,128)S(1)}, f32[8,128]{1,0:T(8,128)}, f32[128,128,128]{2,1,0:T(8,128)S(1)}, bf16[2048,256]{1,0:T(8,128)(2,1)S(1)}, bf16[2048,256]{1,0:T(8,128)(2,1)S(1)}) custom-call(s32[192]{0:T(256)S(1)} %fusion.3.code_ref.refs_2_, f32[128,128,128]{2,1,0:T(8,128)} %refs_0_.1, f32[2048,256]{1,0:T(8,128)S(1)} %copy-done), custom_call_target="tpu_custom_call" | custom-call | flops 8000000000 | bytes 5242880 | tf_op jit(solution)/shard_map/products_away/pallas_call | solution.py:136
  9.8 1.0 %collective-permute-start = (f32[17,128,256]{2,1,0:T(8,128)S(1)}, f32[17,128,256]{2,1,0:T(8,128)S(1)}, u32[]{:S(2)}, u32[]{:S(2)}) collective-permute-start(f32[17,128,256]{2,1,0:T(8,128)S(1)} %get-tuple-element.60.refs_0_), channel_id=1, source_target_pairs={{0,4},{1,5},{2,6},{3,7},{4,0},{5,1},{6,2},{7,3},{8,12},{9,13},{10,... | collective-permute-start | bytes 6684680 | tf_op jit(solution)/shard_map/ppermute | solution.py:368
  10.8 5.2 %products_here.1 = (f32[17,128,256]{2,1,0:T(8,128)S(1)}, f32[8,128]{1,0:T(8,128)S(1)}) custom-call(s32[192]{0:T(256)S(1)} %fusion.3.code_ref.refs_2_, f32[128,128,128]{2,1,0:T(8,128)S(1)} %get-tuple-element.55.refs_0_, bf16[2048,256]{1,0:T(8,128)(2,1)S(1)} %get-tuple-element.56.refs_1_, bf16[2048,256]{1,0:T(8,128)(2,1)S(1)} %get-tuple-element.57.refs_2_), custom_call_target="tpu_custom_call" | custom-call | flops 8000000000 | bytes 5242880 | tf_op jit(solution)/shard_map/products_here/pallas_call | solution.py:136
  16.3 2.4 %collective-permute-start.3 = (f32[8,64,256]{2,1,0:T(8,128)S(1)}, f32[8,64,256]{2,1,0:T(8,128)S(1)}, u32[]{:S(2)}, u32[]{:S(2)}) collective-permute-start(f32[8,64,256]{2,1,0:T(8,128)S(1)} %get-tuple-element.68), channel_id=1, source_target_pairs={{0,1},{1,0},{2,3},{3,2},{4,5},{5,4},{6,7},{7,6},{8,9},{9,8},{10,11... | collective-permute-start | bytes 1572872 | tf_op jit(solution)/shard_map/ppermute | solution.py:368
  18.7 2.3 %collective-permute-start.4 = (f32[8,64,256]{2,1,0:T(8,128)S(1)}, f32[8,64,256]{2,1,0:T(8,128)S(1)}, u32[]{:S(2)}, u32[]{:S(2)}) collective-permute-start(f32[8,64,256]{2,1,0:T(8,128)S(1)} %get-tuple-element.69), channel_id=1, source_target_pairs={{0,2},{1,3},{2,0},{3,1},{4,6},{5,7},{6,4},{7,5},{8,10},{9,11},{10,... | collective-permute-start | bytes 1572872 | tf_op jit(solution)/shard_map/ppermute | solution.py:368
  20.9 0.9 %pick.1 = (f32[8,128]{1,0:T(8,128)S(1)}, f32[64,256]{1,0:T(8,128)S(1)}) custom-call(f32[8,128]{1,0:T(8,128)S(1)} %get-tuple-element.61._token, f32[17,128,256]{2,1,0:T(8,128)S(1)} %get-tuple-element.60.refs_0_, f32[17,128,256]{2,1,0:T(8,128)S(1)} %get-tuple-element.59.refs_0_.refs_1_, s32[192]{0:T(256)S(1)} %fusion.3.code_ref.refs_2_), custom_call_target="tpu_custom_call" | custom-call | flops 1 | bytes 1 | tf_op jit(solution)/shard_map/pick/pallas_call | solution.py:53
  21.9 1.2 %collective-permute-done.1.refs_1_ = f32[64,256]{1,0:T(8,128)S(1)} collective-permute-done((f32[64,256]{1,0:T(8,128)S(1)}, f32[64,256]{1,0:T(8,128)S(1)}, u32[]{:S(2)}, u32[]{:S(2)}) %collective-permute-start.1) | collective-permute-done | bytes 65568 | tf_op jit(solution)/shard_map/ppermute | solution.py:368
  23.2 0.5 collective-permute-start.2
  23.7 3.9 %collective-permute-done.2.refs_1_ = f32[64,256]{1,0:T(8,128)S(1)} collective-permute-done((f32[64,256]{1,0:T(8,128)S(1)}, f32[64,256]{1,0:T(8,128)S(1)}, u32[]{:S(2)}, u32[]{:S(2)}) %collective-permute-start.2) | collective-permute-done | bytes 65568 | tf_op jit(solution)/shard_map/ppermute | solution.py:368
  27.5 1.9 %collective-permute-start.5 = (f32[64,256]{1,0:T(8,128)S(1)}, f32[64,256]{1,0:T(8,128)S(1)}, u32[]{:S(2)}, u32[]{:S(2)}) collective-permute-start(f32[64,256]{1,0:T(8,128)S(1)} %get-tuple-element.70.refs_3_), channel_id=1, source_target_pairs={{0,16},{1,17},{2,18},{3,19},{4,20},{5,21},{6,22},{7,23},{8,24},{9,... | collective-permute-start | bytes 196616 | tf_op jit(solution)/shard_map/ppermute | solution.py:368
  29.5 4.0 %collective-permute-done.5.refs_4_ = f32[64,256]{1,0:T(8,128)S(1)} collective-permute-done((f32[64,256]{1,0:T(8,128)S(1)}, f32[64,256]{1,0:T(8,128)S(1)}, u32[]{:S(2)}, u32[]{:S(2)}) %collective-permute-start.5) | collective-permute-done | bytes 65568 | tf_op jit(solution)/shard_map/ppermute | solution.py:368
  33.6 0.6 collective-permute-start.7
  34.5 1.7 %collective-permute-start.9 = (f32[8,64,256]{2,1,0:T(8,128)S(1)}, f32[8,64,256]{2,1,0:T(8,128)S(1)}, u32[]{:S(2)}, u32[]{:S(2)}) collective-permute-start(f32[8,64,256]{2,1,0:T(8,128)S(1)} %get-tuple-element.82), channel_id=1, source_target_pairs={{0,1},{1,0},{2,3},{3,2},{4,5},{5,4},{6,7},{7,6},{8,9},{9,8},{10,11... | collective-permute-start | bytes 1572872 | tf_op jit(solution)/shard_map/ppermute | solution.py:368
  36.2 1.8 %collective-permute-start.10 = (f32[8,64,256]{2,1,0:T(8,128)S(1)}, f32[8,64,256]{2,1,0:T(8,128)S(1)}, u32[]{:S(2)}, u32[]{:S(2)}) collective-permute-start(f32[8,64,256]{2,1,0:T(8,128)S(1)} %get-tuple-element.83), channel_id=1, source_target_pairs={{0,2},{1,3},{2,0},{3,1},{4,6},{5,7},{6,4},{7,5},{8,10},{9,11},{10,... | collective-permute-start | bytes 1572872 | tf_op jit(solution)/shard_map/ppermute | solution.py:368
  38.0 4.9 %collective-permute-done.7.refs_2_ = f32[4,64,256]{2,1,0:T(8,128)S(1)} collective-permute-done((f32[4,64,256]{2,1,0:T(8,128)S(1)}, f32[4,64,256]{2,1,0:T(8,128)S(1)}, u32[]{:S(2)}, u32[]{:S(2)}) %collective-permute-start.7) | collective-permute-done | bytes 262176 | tf_op jit(solution)/shard_map/ppermute | solution.py:368
  42.9 1.3 %collective-permute-done.6.refs_1_ = f32[5,64,256]{2,1,0:T(8,128)S(1)} collective-permute-done((f32[5,64,256]{2,1,0:T(8,128)S(1)}, f32[5,64,256]{2,1,0:T(8,128)S(1)}, u32[]{:S(2)}, u32[]{:S(2)}) %collective-permute-start.6) | collective-permute-done | bytes 327712 | tf_op jit(solution)/shard_map/ppermute | solution.py:368
  44.4 8.5 %collective-permute-done.8.refs_1_ = f32[4,64,256]{2,1,0:T(8,128)S(1)} collective-permute-done((f32[4,64,256]{2,1,0:T(8,128)S(1)}, f32[4,64,256]{2,1,0:T(8,128)S(1)}, u32[]{:S(2)}, u32[]{:S(2)}) %collective-permute-start.8) | collective-permute-done | bytes 262176 | tf_op jit(solution)/shard_map/ppermute | solution.py:368
  53.0 1.3 %collective-permute-start.15 = (f32[4,64,256]{2,1,0:T(8,128)S(1)}, f32[4,64,256]{2,1,0:T(8,128)S(1)}, u32[]{:S(2)}, u32[]{:S(2)}) collective-permute-start(f32[4,64,256]{2,1,0:T(8,128)S(1)} %get-tuple-element.97), channel_id=1, source_target_pairs={{0,16},{1,17},{2,18},{3,19},{4,20},{5,21},{6,22},{7,23},{8,24},{9,... | collective-permute-start | bytes 786440 | tf_op jit(solution)/shard_map/ppermute | solution.py:368
  54.5 0.5 collective-permute-start.12
  55.0 0.8 %collective-permute-start.11 = (f32[2,64,256]{2,1,0:T(8,128)S(1)}, f32[2,64,256]{2,1,0:T(8,128)S(1)}, u32[]{:S(2)}, u32[]{:S(2)}) collective-permute-start(f32[2,64,256]{2,1,0:T(8,128)S(1)} %get-tuple-element.87), channel_id=1, source_target_pairs={{0,1},{1,0},{2,3},{3,2},{4,5},{5,4},{6,7},{7,6},{8,9},{9,8},{10,11... | collective-permute-start | bytes 393224 | tf_op jit(solution)/shard_map/ppermute | solution.py:368
  55.7 1.3 %collective-permute-start.13 = (f32[2,64,256]{2,1,0:T(8,128)S(1)}, f32[2,64,256]{2,1,0:T(8,128)S(1)}, u32[]{:S(2)}, u32[]{:S(2)}) collective-permute-start(f32[2,64,256]{2,1,0:T(8,128)S(1)} %get-tuple-element.95), channel_id=1, source_target_pairs={{0,1},{1,0},{2,3},{3,2},{4,5},{5,4},{6,7},{7,6},{8,9},{9,8},{10,11... | collective-permute-start | bytes 393224 | tf_op jit(solution)/shard_map/ppermute | solution.py:368
  57.0 1.6 %collective-permute-start.14 = (f32[2,64,256]{2,1,0:T(8,128)S(1)}, f32[2,64,256]{2,1,0:T(8,128)S(1)}, u32[]{:S(2)}, u32[]{:S(2)}) collective-permute-start(f32[2,64,256]{2,1,0:T(8,128)S(1)} %get-tuple-element.96), channel_id=1, source_target_pairs={{0,2},{1,3},{2,0},{3,1},{4,6},{5,7},{6,4},{7,5},{8,10},{9,11},{10,... | collective-permute-start | bytes 393224 | tf_op jit(solution)/shard_map/ppermute | solution.py:368
  58.6 1.4 %collective-permute-done.11.refs_1_ = f32[2,64,256]{2,1,0:T(8,128)S(1)} collective-permute-done((f32[2,64,256]{2,1,0:T(8,128)S(1)}, f32[2,64,256]{2,1,0:T(8,128)S(1)}, u32[]{:S(2)}, u32[]{:S(2)}) %collective-permute-start.11) | collective-permute-done | bytes 131104 | tf_op jit(solution)/shard_map/ppermute | solution.py:368
  60.2 2.7 %collective-permute-start.16 = (f32[4,64,256]{2,1,0:T(8,128)S(1)}, f32[4,64,256]{2,1,0:T(8,128)S(1)}, u32[]{:S(2)}, u32[]{:S(2)}) collective-permute-start(f32[4,64,256]{2,1,0:T(8,128)S(1)} %get-tuple-element.104), channel_id=1, source_target_pairs={{0,8},{1,9},{2,10},{3,11},{4,12},{5,13},{6,14},{7,15},{8,0},{9,1},... | collective-permute-start | bytes 786440 | tf_op jit(solution)/shard_map/ppermute | solution.py:368
  63.0 0.3 gram.1
  63.3 4.9 %eliminate.2 = (f32[8,128]{1,0:T(8,128)S(1)}, f32[64,64]{1,0:T(8,128)S(1)}) custom-call(f32[8,128]{1,0:T(8,128)S(1)} %get-tuple-element.92._token, f32[64,64]{1,0:T(8,128)S(1)} %get-tuple-element.93.refs_0_), custom_call_target="tpu_custom_call" | custom-call | flops 1 | bytes 1 | tf_op jit(solution)/shard_map/eliminate/pallas_call | solution.py:53
  68.2 4.9 %eliminate.3 = (f32[8,128]{1,0:T(8,128)S(1)}, f32[64,64]{1,0:T(8,128)S(1)}) custom-call(f32[8,128]{1,0:T(8,128)S(1)} %get-tuple-element.98._token, f32[64,64]{1,0:T(8,128)S(1)} %get-tuple-element.99.refs_0_), custom_call_target="tpu_custom_call" | custom-call | flops 4000000000 | bytes 1 | tf_op jit(solution)/shard_map/eliminate/pallas_call | solution.py:53
  73.1 0.3 solver.1
  73.4 1.7 %finish.1 = (f32[8,128]{1,0:T(8,128)}, f32[64,256]{1,0:T(8,128)}, f32[256,256]{1,0:T(8,128)}) custom-call(f32[8,128]{1,0:T(8,128)S(1)} %get-tuple-element.102._token, f32[4,64,256]{2,1,0:T(8,128)S(1)} %get-tuple-element.103.refs_0_, f32[4,64,256]{2,1,0:T(8,128)S(1)} %collective-permute-done.16.refs_1_, f32[64,256]{1,0:T(8,128)S(1)} %get-tuple-element.91.refs_0_.refs_2_, ...), custom_call_target="tpu_custom_call" | custom-call | flops 1 | bytes 1 | tf_op jit(solution)/shard_map/finish/pallas_call | solution.py:53
  (26 shorter events, 1.6 us)
Async XLA Ops:
  2.2 1.6 %copy-start = (f32[2048,256]{1,0:T(8,128)S(1)}, f32[2048,256]{1,0:T(8,128)}, u32[]{:S(2)}) copy-start(f32[2048,256]{1,0:T(8,128)} %refs_1_.1) | copy-start | bytes 6291460
  9.8 6.2 %collective-permute-start = (f32[17,128,256]{2,1,0:T(8,128)S(1)}, f32[17,128,256]{2,1,0:T(8,128)S(1)}, u32[]{:S(2)}, u32[]{:S(2)}) collective-permute-start(f32[17,128,256]{2,1,0:T(8,128)S(1)} %get-tuple-element.60.refs_0_), channel_id=1, source_target_pairs={{0,4},{1,5},{2,6},{3,7},{4,0},{5,1},{6,2},{7,3},{8,12},{9,13},{10,... | collective-permute-start | bytes 6684680 | tf_op jit(solution)/shard_map/ppermute | solution.py:368
  16.3 17.1 %collective-permute-start.3 = (f32[8,64,256]{2,1,0:T(8,128)S(1)}, f32[8,64,256]{2,1,0:T(8,128)S(1)}, u32[]{:S(2)}, u32[]{:S(2)}) collective-permute-start(f32[8,64,256]{2,1,0:T(8,128)S(1)} %get-tuple-element.68), channel_id=1, source_target_pairs={{0,1},{1,0},{2,3},{3,2},{4,5},{5,4},{6,7},{7,6},{8,9},{9,8},{10,11... | collective-permute-start | bytes 1572872 | tf_op jit(solution)/shard_map/ppermute | solution.py:368
  18.7 14.8 %collective-permute-start.4 = (f32[8,64,256]{2,1,0:T(8,128)S(1)}, f32[8,64,256]{2,1,0:T(8,128)S(1)}, u32[]{:S(2)}, u32[]{:S(2)}) collective-permute-start(f32[8,64,256]{2,1,0:T(8,128)S(1)} %get-tuple-element.69), channel_id=1, source_target_pairs={{0,2},{1,3},{2,0},{3,1},{4,6},{5,7},{6,4},{7,5},{8,10},{9,11},{10,... | collective-permute-start | bytes 1572872 | tf_op jit(solution)/shard_map/ppermute | solution.py:368
  21.9 1.3 %collective-permute-start.1 = (f32[64,256]{1,0:T(8,128)S(1)}, f32[64,256]{1,0:T(8,128)S(1)}, u32[]{:S(2)}, u32[]{:S(2)}) collective-permute-start(f32[64,256]{1,0:T(8,128)S(1)} %get-tuple-element.63.refs_0_), channel_id=1, source_target_pairs={{0,4},{1,5},{2,6},{3,7},{4,0},{5,1},{6,2},{7,3},{8,12},{9,13},{10,... | collective-permute-start | bytes 196616 | tf_op jit(solution)/shard_map/ppermute | solution.py:368
  23.2 4.3 %collective-permute-start.2 = (f32[64,256]{1,0:T(8,128)S(1)}, f32[64,256]{1,0:T(8,128)S(1)}, u32[]{:S(2)}, u32[]{:S(2)}) collective-permute-start(f32[64,256]{1,0:T(8,128)S(1)} %get-tuple-element.65.refs_0_), channel_id=1, source_target_pairs={{0,8},{1,9},{2,10},{3,11},{4,12},{5,13},{6,14},{7,15},{8,0},{9,1},... | collective-permute-start | bytes 196616 | tf_op jit(solution)/shard_map/ppermute | solution.py:368
  27.5 5.9 %collective-permute-start.5 = (f32[64,256]{1,0:T(8,128)S(1)}, f32[64,256]{1,0:T(8,128)S(1)}, u32[]{:S(2)}, u32[]{:S(2)}) collective-permute-start(f32[64,256]{1,0:T(8,128)S(1)} %get-tuple-element.70.refs_3_), channel_id=1, source_target_pairs={{0,16},{1,17},{2,18},{3,19},{4,20},{5,21},{6,22},{7,23},{8,24},{9,... | collective-permute-start | bytes 196616 | tf_op jit(solution)/shard_map/ppermute | solution.py:368
  33.5 10.7 %collective-permute-start.6 = (f32[5,64,256]{2,1,0:T(8,128)S(1)}, f32[5,64,256]{2,1,0:T(8,128)S(1)}, u32[]{:S(2)}, u32[]{:S(2)}) collective-permute-start(f32[5,64,256]{2,1,0:T(8,128)S(1)} %get-tuple-element.74), channel_id=1, source_target_pairs={{0,1},{1,0},{2,3},{3,2},{4,5},{5,4},{6,7},{7,6},{8,9},{9,8},{10,11... | collective-permute-start | bytes 983048 | tf_op jit(solution)/shard_map/ppermute | solution.py:368
  33.6 9.3 %collective-permute-start.7 = (f32[4,64,256]{2,1,0:T(8,128)S(1)}, f32[4,64,256]{2,1,0:T(8,128)S(1)}, u32[]{:S(2)}, u32[]{:S(2)}) collective-permute-start(f32[4,64,256]{2,1,0:T(8,128)S(1)} %get-tuple-element.75), channel_id=1, source_target_pairs={{0,2},{1,3},{2,0},{3,1},{4,6},{5,7},{6,4},{7,5},{8,10},{9,11},{10,... | collective-permute-start | bytes 786440 | tf_op jit(solution)/shard_map/ppermute | solution.py:368
  34.5 19.9 %collective-permute-start.9 = (f32[8,64,256]{2,1,0:T(8,128)S(1)}, f32[8,64,256]{2,1,0:T(8,128)S(1)}, u32[]{:S(2)}, u32[]{:S(2)}) collective-permute-start(f32[8,64,256]{2,1,0:T(8,128)S(1)} %get-tuple-element.82), channel_id=1, source_target_pairs={{0,1},{1,0},{2,3},{3,2},{4,5},{5,4},{6,7},{7,6},{8,9},{9,8},{10,11... | collective-permute-start | bytes 1572872 | tf_op jit(solution)/shard_map/ppermute | solution.py:368
  36.2 18.1 %collective-permute-start.10 = (f32[8,64,256]{2,1,0:T(8,128)S(1)}, f32[8,64,256]{2,1,0:T(8,128)S(1)}, u32[]{:S(2)}, u32[]{:S(2)}) collective-permute-start(f32[8,64,256]{2,1,0:T(8,128)S(1)} %get-tuple-element.83), channel_id=1, source_target_pairs={{0,2},{1,3},{2,0},{3,1},{4,6},{5,7},{6,4},{7,5},{8,10},{9,11},{10,... | collective-permute-start | bytes 1572872 | tf_op jit(solution)/shard_map/ppermute | solution.py:368
  44.3 8.6 %collective-permute-start.8 = (f32[4,64,256]{2,1,0:T(8,128)S(1)}, f32[4,64,256]{2,1,0:T(8,128)S(1)}, u32[]{:S(2)}, u32[]{:S(2)}) collective-permute-start(f32[4,64,256]{2,1,0:T(8,128)S(1)} %get-tuple-element.79), channel_id=1, source_target_pairs={{0,8},{1,9},{2,10},{3,11},{4,12},{5,13},{6,14},{7,15},{8,0},{9,1},... | collective-permute-start | bytes 786440 | tf_op jit(solution)/shard_map/ppermute | solution.py:368
  53.0 15.2 %collective-permute-start.15 = (f32[4,64,256]{2,1,0:T(8,128)S(1)}, f32[4,64,256]{2,1,0:T(8,128)S(1)}, u32[]{:S(2)}, u32[]{:S(2)}) collective-permute-start(f32[4,64,256]{2,1,0:T(8,128)S(1)} %get-tuple-element.97), channel_id=1, source_target_pairs={{0,16},{1,17},{2,18},{3,19},{4,20},{5,21},{6,22},{7,23},{8,24},{9,... | collective-permute-start | bytes 786440 | tf_op jit(solution)/shard_map/ppermute | solution.py:368
  54.5 5.7 %collective-permute-start.12 = (f32[3,64,256]{2,1,0:T(8,128)S(1)}, f32[3,64,256]{2,1,0:T(8,128)S(1)}, u32[]{:S(2)}, u32[]{:S(2)}) collective-permute-start(f32[3,64,256]{2,1,0:T(8,128)S(1)} %get-tuple-element.88), channel_id=1, source_target_pairs={{0,2},{1,3},{2,0},{3,1},{4,6},{5,7},{6,4},{7,5},{8,10},{9,11},{10,... | collective-permute-start | bytes 589832 | tf_op jit(solution)/shard_map/ppermute | solution.py:368
  55.0 5.0 %collective-permute-start.11 = (f32[2,64,256]{2,1,0:T(8,128)S(1)}, f32[2,64,256]{2,1,0:T(8,128)S(1)}, u32[]{:S(2)}, u32[]{:S(2)}) collective-permute-start(f32[2,64,256]{2,1,0:T(8,128)S(1)} %get-tuple-element.87), channel_id=1, source_target_pairs={{0,1},{1,0},{2,3},{3,2},{4,5},{5,4},{6,7},{7,6},{8,9},{9,8},{10,11... | collective-permute-start | bytes 393224 | tf_op jit(solution)/shard_map/ppermute | solution.py:368
  55.7 12.4 %collective-permute-start.13 = (f32[2,64,256]{2,1,0:T(8,128)S(1)}, f32[2,64,256]{2,1,0:T(8,128)S(1)}, u32[]{:S(2)}, u32[]{:S(2)}) collective-permute-start(f32[2,64,256]{2,1,0:T(8,128)S(1)} %get-tuple-element.95), channel_id=1, source_target_pairs={{0,1},{1,0},{2,3},{3,2},{4,5},{5,4},{6,7},{7,6},{8,9},{9,8},{10,11... | collective-permute-start | bytes 393224 | tf_op jit(solution)/shard_map/ppermute | solution.py:368
  57.0 11.2 %collective-permute-start.14 = (f32[2,64,256]{2,1,0:T(8,128)S(1)}, f32[2,64,256]{2,1,0:T(8,128)S(1)}, u32[]{:S(2)}, u32[]{:S(2)}) collective-permute-start(f32[2,64,256]{2,1,0:T(8,128)S(1)} %get-tuple-element.96), channel_id=1, source_target_pairs={{0,2},{1,3},{2,0},{3,1},{4,6},{5,7},{6,4},{7,5},{8,10},{9,11},{10,... | collective-permute-start | bytes 393224 | tf_op jit(solution)/shard_map/ppermute | solution.py:368
  60.2 13.2 %collective-permute-start.16 = (f32[4,64,256]{2,1,0:T(8,128)S(1)}, f32[4,64,256]{2,1,0:T(8,128)S(1)}, u32[]{:S(2)}, u32[]{:S(2)}) collective-permute-start(f32[4,64,256]{2,1,0:T(8,128)S(1)} %get-tuple-element.104), channel_id=1, source_target_pairs={{0,8},{1,9},{2,10},{3,11},{4,12},{5,13},{6,14},{7,15},{8,0},{9,1},... | collective-permute-start | bytes 786440 | tf_op jit(solution)/shard_map/ppermute | solution.py:368

commit v8 on v6

--- a/solution.py
+++ b/solution.py
@@ -203,7 +203,9 @@
     n = sum(len(zs) for zs in groups)
     came = refs[: len(groups) * n_y]
     parts = refs[len(came) : len(came) + n_parts]
-    keep, rows, *sends = refs[len(came) + n_parts :]
+    keep, *sends = refs[len(came) + n_parts :]
+    if n_parts:
+        rows, *sends = sends
     at = [(c, m) for c, cut in enumerate(cuts) for m in range(cut)]
     n_x = n * 2 * n_y
     i = 0
@@ -228,21 +230,22 @@
                     else:
                         keep[4 * i + 2 + s] = value
             i += 1
-    total = parts[0][...]
-    for ref in parts[1:]:
-        total = total + ref[...]
-    rows[...] = total
-    for ref in sends[:1] if ride_x else sends[1:n_y]:
-        ref[2 * cuts[0]] = total
+    if n_parts:
+        total = parts[0][...]
+        for ref in parts[1:]:
+            total = total + ref[...]
+        rows[...] = total
+        for ref in sends[:1] if ride_x else sends[1:n_y]:
+            ref[2 * cuts[0]] = total
 
 
 def join(queue, groups, n_y, state, parts, ride_x, cuts):
     stay = state[0]
     half, width = stay.shape[1:]
     n = sum(len(zs) for zs in groups)
-    outs = [shaped((4 * n, half, width)), shaped((half, width))]
+    outs = [shaped((4 * n, half, width))] + [shaped((half, width))] * bool(parts)
     for c, cut in enumerate(cuts):
-        outs += [shaped((2 * cut + (1 if c == 0 and ride_x == (k == 0) else 0), half, width)) for k in range(n_y)]
+        outs += [shaped((2 * cut + (1 if c == 0 and parts and ride_x == (k == 0) else 0), half, width)) for k in range(n_y)]
     kernel = functools.partial(join_kernel, groups, n_y, len(parts), ride_x, cuts)
     return queue.call("join", kernel, outs, (*state, *parts))
 
@@ -384,12 +387,12 @@
         return [stay, *came]
 
     def do_join(groups, state, parts, ride_x, cuts):
-        keep, rows, *sends = join(queue, groups, n_y, state, parts, ride_x, cuts)
+        keep, *sends = join(queue, groups, n_y, state, parts, ride_x, cuts)
+        rows = sends.pop(0) if parts else None
         return keep, rows, [swaps(sends[c * n_y : (c + 1) * n_y]) for c in range(len(cuts))]
 
     mid = tuple(range(n_z // 2 - 1, 0, -1))
     far_groups = (tuple(range(n_z - 1, n_z // 2 - 1, -1)),)
-    near_groups = (mid + (0,),)
     state = do_spread(far_groups)
     pick = functools.partial(pick_kernel, n_tiles)
     part, = queue.call("pick", pick, (shaped((count, width)),), (away, here), (codes,))
@@ -398,16 +401,18 @@
         part = total(queue, [part, swap(part, mask)])
     n_far, n_mid = len(far_groups[0]), len(mid)
     keep, rows, came = do_join(far_groups, state, (part, swap(part, masks[-1])), True, (n_far,))
-    state = do_spread(near_groups)
+    mid_state = do_spread((mid,))
+    near_state = do_spread(((0,),))
     rows, *relayed, far = merge(queue, 0, n_far, n_y, keep, came[0], True, (rows,))
     relayed = [swap(v, 2 * n_doc * (dz - n_z // 2)) for v, dz in zip(relayed, far_groups[0])]
+    mid_keep, rows, mid_came = do_join((mid,), mid_state, (rows,), False, (n_mid,))
     far = swap(total(queue, [far, *relayed]), n_doc * n_z)
-    keep, rows, came = do_join(near_groups, state, (rows,), False, (n_mid, 1))
-    rows, *sends = merge(queue, 0, n_mid, n_y, keep, came[0], False, (rows,))
+    keep, _, came = do_join(((0,),), near_state, (), None, (1,))
+    rows, *sends = merge(queue, 0, n_mid, n_y, mid_keep, mid_came[0], False, (rows,))
     last = [swap(v, 2 * n_doc * dz) for v, dz in zip(sends, mid)]
     gram = gram_of(queue, rows)
     gram = eliminate(queue, gram, 0, TINY)
-    near, = merge(queue, n_mid, 1, n_y, keep, came[1], None, (far,))
+    near, = merge(queue, 0, 1, n_y, keep, came[0], None, (far,))
     gram = eliminate(queue, gram, 1, LONG)
     solve = solver(queue, rows, gram)
     return finish(queue, near, last, rows, solve)

time: 70.3 us -> 70 us (level); the launches traced: 69.7 us -> 70.5 us
  starting transfers between devices: 21.2 us -> 27 us
  waiting for transfers between devices: 23.6 us -> 18.5 us
    ppermute x17 -> x19, starting transfers between devices: 21.2 us -> 27 us  [swap(): return lax.ppermute(v, AXES, [(i, i ^ mask) for i in range(devices)])]
    ppermute x17 -> x19, waiting for transfers between devices: 23.6 us -> 18.5 us  [swap(): return lax.ppermute(v, AXES, [(i, i ^ mask) for i in range(devices)])]
    pallas_call x16 -> x18, Pallas kernels: 9.64 us -> 9.65 us  [call(): pl.pallas_call(functools.partial(in_order, kernel, len(args) + len(smem))...]
  transfers between devices with their start and end apart: 17 -> 19, of which waited for: 8 -> 10; matrix products, arithmetic and copies ran while one was open for 0% -> 0% of each run, Pallas kernels for 18% -> 18%
where the time goes in v8:
time: 70 us; the launch traced here: 70.5 us
  starting transfers between devices  27 us (39%)
  Pallas kernels  21.1 us (30%)
  waiting for transfers between devices  18.5 us (26%)
  local copies, waits for them, and re-layouts  1.58 us (2%)
  other arithmetic  1.51 us (2%)
  between operations  0.83 us (1%)
    ppermute x19, starting transfers between devices, swap(): return lax.ppermute(v, AXES, [(i, i ^ mask) for i in range(devices)])  27 us
    ppermute x19, waiting for transfers between devices, swap(): return lax.ppermute(v, AXES, [(i, i ^ mask) for i in range(devices)])  18.5 us
    pallas_call x2, Pallas kernels, products(): pl.pallas_call(functools.partial(products_kernel, slots, away), out_shape...  11.4 us
    pallas_call x18, Pallas kernels, call(): pl.pallas_call(functools.partial(in_order, kernel, len(args) + len(smem))...  9.65 us
    unnamed x2, local copies, waits for them, and re-layouts  1.58 us
  transfers between devices with their start and end apart: 19, of which 10 were waited for; matrix products, arithmetic and copies ran while one was open for 0% of the time, Pallas kernels for 18%

profile of v8, /device:TPU:0, one launch (start us, length us, event | category | flops | bytes accessed | tf_op | source)
XLA Modules:
  0.0 70.5 jit_solution(6460305534839145559)
XLA Ops:
  1.4 0.8 %fusion.3.code_ref.refs_2_ = s32[192]{0:T(256)S(1)} fusion(s32[2,64]{1,0:T(2,128)S(1)} %broadcast_select_fusion, s32[2,128]{1,0:T(2,128)} %bitcast.2, pred[2]{0:T(512)(128)(4,1)S(1)} %iota_compare_fusion, s32[]{:T(128)S(6)} %mul.12, s32[]{:T(128)S(6)} %add.39), kind=kLoop, calls=%fused_computation.15 | loop fusion | flops 22080 | bytes 2314 | tf_op jit(solution)/shard_map/reduce_sum | solution.py:372
  2.2 1.6 %copy-done = f32[2048,256]{1,0:T(8,128)S(1)} copy-done((f32[2048,256]{1,0:T(8,128)S(1)}, f32[2048,256]{1,0:T(8,128)}, u32[]{:S(2)}) %copy-start) | copy-done | bytes 2097176
  3.8 6.3 %products_away.1 = (f32[17,128,256]{2,1,0:T(8,128)S(1)}, f32[8,128]{1,0:T(8,128)}, f32[128,128,128]{2,1,0:T(8,128)S(1)}, bf16[2048,256]{1,0:T(8,128)(2,1)S(1)}, bf16[2048,256]{1,0:T(8,128)(2,1)S(1)}) custom-call(s32[192]{0:T(256)S(1)} %fusion.3.code_ref.refs_2_, f32[128,128,128]{2,1,0:T(8,128)} %refs_0_.1, f32[2048,256]{1,0:T(8,128)S(1)} %copy-done), custom_call_target="tpu_custom_call" | custom-call | flops 8000000000 | bytes 5242880 | tf_op jit(solution)/shard_map/products_away/pallas_call | solution.py:136
  10.0 0.8 %collective-permute-start = (f32[17,128,256]{2,1,0:T(8,128)S(1)}, f32[17,128,256]{2,1,0:T(8,128)S(1)}, u32[]{:S(2)}, u32[]{:S(2)}) collective-permute-start(f32[17,128,256]{2,1,0:T(8,128)S(1)} %get-tuple-element.66.refs_0_), channel_id=1, source_target_pairs={{0,4},{1,5},{2,6},{3,7},{4,0},{5,1},{6,2},{7,3},{8,12},{9,13},{10,... | collective-permute-start | bytes 6684680 | tf_op jit(solution)/shard_map/ppermute | solution.py:363
  10.8 5.2 %products_here.1 = (f32[17,128,256]{2,1,0:T(8,128)S(1)}, f32[8,128]{1,0:T(8,128)S(1)}) custom-call(s32[192]{0:T(256)S(1)} %fusion.3.code_ref.refs_2_, f32[128,128,128]{2,1,0:T(8,128)S(1)} %get-tuple-element.61.refs_0_, bf16[2048,256]{1,0:T(8,128)(2,1)S(1)} %get-tuple-element.62.refs_1_, bf16[2048,256]{1,0:T(8,128)(2,1)S(1)} %get-tuple-element.63.refs_2_), custom_call_target="tpu_custom_call" | custom-call | flops 8000000000 | bytes 5242880 | tf_op jit(solution)/shard_map/products_here/pallas_call | solution.py:136
  16.3 2.7 %collective-permute-start.3 = (f32[8,64,256]{2,1,0:T(8,128)S(1)}, f32[8,64,256]{2,1,0:T(8,128)S(1)}, u32[]{:S(2)}, u32[]{:S(2)}) collective-permute-start(f32[8,64,256]{2,1,0:T(8,128)S(1)} %get-tuple-element.74), channel_id=1, source_target_pairs={{0,1},{1,0},{2,3},{3,2},{4,5},{5,4},{6,7},{7,6},{8,9},{9,8},{10,11... | collective-permute-start | bytes 1572872 | tf_op jit(solution)/shard_map/ppermute | solution.py:363
  19.0 1.0 %collective-permute-start.4 = (f32[8,64,256]{2,1,0:T(8,128)S(1)}, f32[8,64,256]{2,1,0:T(8,128)S(1)}, u32[]{:S(2)}, u32[]{:S(2)}) collective-permute-start(f32[8,64,256]{2,1,0:T(8,128)S(1)} %get-tuple-element.75), channel_id=1, source_target_pairs={{0,2},{1,3},{2,0},{3,1},{4,6},{5,7},{6,4},{7,5},{8,10},{9,11},{10,... | collective-permute-start | bytes 1572872 | tf_op jit(solution)/shard_map/ppermute | solution.py:363
  19.9 0.9 %pick.1 = (f32[8,128]{1,0:T(8,128)S(1)}, f32[64,256]{1,0:T(8,128)S(1)}) custom-call(f32[8,128]{1,0:T(8,128)S(1)} %get-tuple-element.67._token, f32[17,128,256]{2,1,0:T(8,128)S(1)} %get-tuple-element.66.refs_0_, f32[17,128,256]{2,1,0:T(8,128)S(1)} %get-tuple-element.65.refs_0_.refs_1_, s32[192]{0:T(256)S(1)} %fusion.3.code_ref.refs_2_), custom_call_target="tpu_custom_call" | custom-call | flops 1 | bytes 1 | tf_op jit(solution)/shard_map/pick/pallas_call | solution.py:53
  21.0 1.2 %collective-permute-done.1.refs_1_ = f32[64,256]{1,0:T(8,128)S(1)} collective-permute-done((f32[64,256]{1,0:T(8,128)S(1)}, f32[64,256]{1,0:T(8,128)S(1)}, u32[]{:S(2)}, u32[]{:S(2)}) %collective-permute-start.1) | collective-permute-done | bytes 65568 | tf_op jit(solution)/shard_map/ppermute | solution.py:363
  22.2 1.4 %collective-permute-start.2 = (f32[64,256]{1,0:T(8,128)S(1)}, f32[64,256]{1,0:T(8,128)S(1)}, u32[]{:S(2)}, u32[]{:S(2)}) collective-permute-start(f32[64,256]{1,0:T(8,128)S(1)} %get-tuple-element.71.refs_0_), channel_id=1, source_target_pairs={{0,8},{1,9},{2,10},{3,11},{4,12},{5,13},{6,14},{7,15},{8,0},{9,1},... | collective-permute-start | bytes 196616 | tf_op jit(solution)/shard_map/ppermute | solution.py:363
  23.7 2.9 %collective-permute-done.2.refs_1_ = f32[64,256]{1,0:T(8,128)S(1)} collective-permute-done((f32[64,256]{1,0:T(8,128)S(1)}, f32[64,256]{1,0:T(8,128)S(1)}, u32[]{:S(2)}, u32[]{:S(2)}) %collective-permute-start.2) | collective-permute-done | bytes 65568 | tf_op jit(solution)/shard_map/ppermute | solution.py:363
  26.6 2.9 %collective-permute-start.5 = (f32[64,256]{1,0:T(8,128)S(1)}, f32[64,256]{1,0:T(8,128)S(1)}, u32[]{:S(2)}, u32[]{:S(2)}) collective-permute-start(f32[64,256]{1,0:T(8,128)S(1)} %get-tuple-element.76.refs_3_), channel_id=1, source_target_pairs={{0,16},{1,17},{2,18},{3,19},{4,20},{5,21},{6,22},{7,23},{8,24},{9,... | collective-permute-start | bytes 196616 | tf_op jit(solution)/shard_map/ppermute | solution.py:363
  29.5 2.3 %collective-permute-done.5.refs_4_ = f32[64,256]{1,0:T(8,128)S(1)} collective-permute-done((f32[64,256]{1,0:T(8,128)S(1)}, f32[64,256]{1,0:T(8,128)S(1)}, u32[]{:S(2)}, u32[]{:S(2)}) %collective-permute-start.5) | collective-permute-done | bytes 65568 | tf_op jit(solution)/shard_map/ppermute | solution.py:363
  32.8 1.7 %collective-permute-start.7 = (f32[4,64,256]{2,1,0:T(8,128)S(1)}, f32[4,64,256]{2,1,0:T(8,128)S(1)}, u32[]{:S(2)}, u32[]{:S(2)}) collective-permute-start(f32[4,64,256]{2,1,0:T(8,128)S(1)} %get-tuple-element.82), channel_id=1, source_target_pairs={{0,2},{1,3},{2,0},{3,1},{4,6},{5,7},{6,4},{7,5},{8,10},{9,11},{10,... | collective-permute-start | bytes 786440 | tf_op jit(solution)/shard_map/ppermute | solution.py:363
  34.7 1.7 %collective-permute-start.8 = (f32[4,64,256]{2,1,0:T(8,128)S(1)}, f32[4,64,256]{2,1,0:T(8,128)S(1)}, u32[]{:S(2)}, u32[]{:S(2)}) collective-permute-start(f32[4,64,256]{2,1,0:T(8,128)S(1)} %get-tuple-element.86), channel_id=1, source_target_pairs={{0,1},{1,0},{2,3},{3,2},{4,5},{5,4},{6,7},{7,6},{8,9},{9,8},{10,11... | collective-permute-start | bytes 786440 | tf_op jit(solution)/shard_map/ppermute | solution.py:363
  36.8 5.2 %collective-permute-done.7.refs_2_ = f32[4,64,256]{2,1,0:T(8,128)S(1)} collective-permute-done((f32[4,64,256]{2,1,0:T(8,128)S(1)}, f32[4,64,256]{2,1,0:T(8,128)S(1)}, u32[]{:S(2)}, u32[]{:S(2)}) %collective-permute-start.7) | collective-permute-done | bytes 262176 | tf_op jit(solution)/shard_map/ppermute | solution.py:363
  42.1 1.0 %collective-permute-done.6.refs_1_ = f32[5,64,256]{2,1,0:T(8,128)S(1)} collective-permute-done((f32[5,64,256]{2,1,0:T(8,128)S(1)}, f32[5,64,256]{2,1,0:T(8,128)S(1)}, u32[]{:S(2)}, u32[]{:S(2)}) %collective-permute-start.6) | collective-permute-done | bytes 327712 | tf_op jit(solution)/shard_map/ppermute | solution.py:363
  43.1 1.3 %collective-permute-start.10 = (f32[4,64,256]{2,1,0:T(8,128)S(1)}, f32[4,64,256]{2,1,0:T(8,128)S(1)}, u32[]{:S(2)}, u32[]{:S(2)}) collective-permute-start(f32[4,64,256]{2,1,0:T(8,128)S(1)} %get-tuple-element.91), channel_id=1, source_target_pairs={{0,8},{1,9},{2,10},{3,11},{4,12},{5,13},{6,14},{7,15},{8,0},{9,1},... | collective-permute-start | bytes 786440 | tf_op jit(solution)/shard_map/ppermute | solution.py:363
  44.4 0.7 collective-permute-start.11
  45.1 1.7 %collective-permute-start.12 = (f32[4,64,256]{2,1,0:T(8,128)S(1)}, f32[4,64,256]{2,1,0:T(8,128)S(1)}, u32[]{:S(2)}, u32[]{:S(2)}) collective-permute-start(f32[4,64,256]{2,1,0:T(8,128)S(1)} %get-tuple-element.95), channel_id=1, source_target_pairs={{0,2},{1,3},{2,0},{3,1},{4,6},{5,7},{6,4},{7,5},{8,10},{9,11},{10,... | collective-permute-start | bytes 786440 | tf_op jit(solution)/shard_map/ppermute | solution.py:363
  46.8 1.9 %collective-permute-done.8.refs_1_ = f32[4,64,256]{2,1,0:T(8,128)S(1)} collective-permute-done((f32[4,64,256]{2,1,0:T(8,128)S(1)}, f32[4,64,256]{2,1,0:T(8,128)S(1)}, u32[]{:S(2)}, u32[]{:S(2)}) %collective-permute-start.8) | collective-permute-done | bytes 262176 | tf_op jit(solution)/shard_map/ppermute | solution.py:363
  48.8 1.9 %collective-permute-done.10.refs_1_ = f32[4,64,256]{2,1,0:T(8,128)S(1)} collective-permute-done((f32[4,64,256]{2,1,0:T(8,128)S(1)}, f32[4,64,256]{2,1,0:T(8,128)S(1)}, u32[]{:S(2)}, u32[]{:S(2)}) %collective-permute-start.10) | collective-permute-done | bytes 262176 | tf_op jit(solution)/shard_map/ppermute | solution.py:363
  50.7 3.7 %collective-permute-start.17 = (f32[4,64,256]{2,1,0:T(8,128)S(1)}, f32[4,64,256]{2,1,0:T(8,128)S(1)}, u32[]{:S(2)}, u32[]{:S(2)}) collective-permute-start(f32[4,64,256]{2,1,0:T(8,128)S(1)} %get-tuple-element.109), channel_id=1, source_target_pairs={{0,16},{1,17},{2,18},{3,19},{4,20},{5,21},{6,22},{7,23},{8,24},{9,... | collective-permute-start | bytes 786440 | tf_op jit(solution)/shard_map/ppermute | solution.py:363
  54.4 1.2 %collective-permute-start.13 = (f32[2,64,256]{2,1,0:T(8,128)S(1)}, f32[2,64,256]{2,1,0:T(8,128)S(1)}, u32[]{:S(2)}, u32[]{:S(2)}) collective-permute-start(f32[2,64,256]{2,1,0:T(8,128)S(1)} %get-tuple-element.98), channel_id=1, source_target_pairs={{0,1},{1,0},{2,3},{3,2},{4,5},{5,4},{6,7},{7,6},{8,9},{9,8},{10,11... | collective-permute-start | bytes 393224 | tf_op jit(solution)/shard_map/ppermute | solution.py:363
  55.7 0.9 %collective-permute-start.15 = (f32[2,64,256]{2,1,0:T(8,128)S(1)}, f32[2,64,256]{2,1,0:T(8,128)S(1)}, u32[]{:S(2)}, u32[]{:S(2)}) collective-permute-start(f32[2,64,256]{2,1,0:T(8,128)S(1)} %get-tuple-element.107), channel_id=1, source_target_pairs={{0,1},{1,0},{2,3},{3,2},{4,5},{5,4},{6,7},{7,6},{8,9},{9,8},{10,11... | collective-permute-start | bytes 393224 | tf_op jit(solution)/shard_map/ppermute | solution.py:363
  56.6 2.0 %collective-permute-start.16 = (f32[2,64,256]{2,1,0:T(8,128)S(1)}, f32[2,64,256]{2,1,0:T(8,128)S(1)}, u32[]{:S(2)}, u32[]{:S(2)}) collective-permute-start(f32[2,64,256]{2,1,0:T(8,128)S(1)} %get-tuple-element.108), channel_id=1, source_target_pairs={{0,2},{1,3},{2,0},{3,1},{4,6},{5,7},{6,4},{7,5},{8,10},{9,11},{10,... | collective-permute-start | bytes 393224 | tf_op jit(solution)/shard_map/ppermute | solution.py:363
  58.6 0.8 %collective-permute-done.13.refs_1_ = f32[2,64,256]{2,1,0:T(8,128)S(1)} collective-permute-done((f32[2,64,256]{2,1,0:T(8,128)S(1)}, f32[2,64,256]{2,1,0:T(8,128)S(1)}, u32[]{:S(2)}, u32[]{:S(2)}) %collective-permute-start.13) | collective-permute-done | bytes 131104 | tf_op jit(solution)/shard_map/ppermute | solution.py:363
  59.4 0.7 collective-permute-done.14.refs_2_
  60.1 2.6 %collective-permute-start.18 = (f32[4,64,256]{2,1,0:T(8,128)S(1)}, f32[4,64,256]{2,1,0:T(8,128)S(1)}, u32[]{:S(2)}, u32[]{:S(2)}) collective-permute-start(f32[4,64,256]{2,1,0:T(8,128)S(1)} %get-tuple-element.116), channel_id=1, source_target_pairs={{0,8},{1,9},{2,10},{3,11},{4,12},{5,13},{6,14},{7,15},{8,0},{9,1},... | collective-permute-start | bytes 786440 | tf_op jit(solution)/shard_map/ppermute | solution.py:363
  63.0 2.7 %eliminate.2 = (f32[8,128]{1,0:T(8,128)S(1)}, f32[64,64]{1,0:T(8,128)S(1)}) custom-call(f32[8,128]{1,0:T(8,128)S(1)} %get-tuple-element.103._token, f32[64,64]{1,0:T(8,128)S(1)} %get-tuple-element.104.refs_0_), custom_call_target="tpu_custom_call" | custom-call | flops 1 | bytes 1 | tf_op jit(solution)/shard_map/eliminate/pallas_call | solution.py:53
  65.8 2.7 %eliminate.3 = (f32[8,128]{1,0:T(8,128)S(1)}, f32[64,64]{1,0:T(8,128)S(1)}) custom-call(f32[8,128]{1,0:T(8,128)S(1)} %get-tuple-element.110._token, f32[64,64]{1,0:T(8,128)S(1)} %get-tuple-element.111.refs_0_), custom_call_target="tpu_custom_call" | custom-call | flops 4000000000 | bytes 1 | tf_op jit(solution)/shard_map/eliminate/pallas_call | solution.py:53
  68.8 1.7 %finish.1 = (f32[8,128]{1,0:T(8,128)}, f32[64,256]{1,0:T(8,128)}, f32[256,256]{1,0:T(8,128)}) custom-call(f32[8,128]{1,0:T(8,128)S(1)} %get-tuple-element.114._token, f32[4,64,256]{2,1,0:T(8,128)S(1)} %get-tuple-element.115.refs_0_, f32[4,64,256]{2,1,0:T(8,128)S(1)} %collective-permute-done.18.refs_1_, f32[64,256]{1,0:T(8,128)S(1)} %get-tuple-element.102.refs_0_.refs_2_, ...), custom_call_target="tpu_custom_call" | custom-call | flops 1 | bytes 1 | tf_op jit(solution)/shard_map/finish/pallas_call | solution.py:53
  (32 shorter events, 3.7 us)
Async XLA Ops:
  2.2 1.6 %copy-start = (f32[2048,256]{1,0:T(8,128)S(1)}, f32[2048,256]{1,0:T(8,128)}, u32[]{:S(2)}) copy-start(f32[2048,256]{1,0:T(8,128)} %refs_1_.1) | copy-start | bytes 6291460
  10.0 5.9 %collective-permute-start = (f32[17,128,256]{2,1,0:T(8,128)S(1)}, f32[17,128,256]{2,1,0:T(8,128)S(1)}, u32[]{:S(2)}, u32[]{:S(2)}) collective-permute-start(f32[17,128,256]{2,1,0:T(8,128)S(1)} %get-tuple-element.66.refs_0_), channel_id=1, source_target_pairs={{0,4},{1,5},{2,6},{3,7},{4,0},{5,1},{6,2},{7,3},{8,12},{9,13},{10,... | collective-permute-start | bytes 6684680 | tf_op jit(solution)/shard_map/ppermute | solution.py:363
  16.3 15.5 %collective-permute-start.3 = (f32[8,64,256]{2,1,0:T(8,128)S(1)}, f32[8,64,256]{2,1,0:T(8,128)S(1)}, u32[]{:S(2)}, u32[]{:S(2)}) collective-permute-start(f32[8,64,256]{2,1,0:T(8,128)S(1)} %get-tuple-element.74), channel_id=1, source_target_pairs={{0,1},{1,0},{2,3},{3,2},{4,5},{5,4},{6,7},{7,6},{8,9},{9,8},{10,11... | collective-permute-start | bytes 1572872 | tf_op jit(solution)/shard_map/ppermute | solution.py:363
  19.0 13.3 %collective-permute-start.4 = (f32[8,64,256]{2,1,0:T(8,128)S(1)}, f32[8,64,256]{2,1,0:T(8,128)S(1)}, u32[]{:S(2)}, u32[]{:S(2)}) collective-permute-start(f32[8,64,256]{2,1,0:T(8,128)S(1)} %get-tuple-element.75), channel_id=1, source_target_pairs={{0,2},{1,3},{2,0},{3,1},{4,6},{5,7},{6,4},{7,5},{8,10},{9,11},{10,... | collective-permute-start | bytes 1572872 | tf_op jit(solution)/shard_map/ppermute | solution.py:363
  20.9 1.3 %collective-permute-start.1 = (f32[64,256]{1,0:T(8,128)S(1)}, f32[64,256]{1,0:T(8,128)S(1)}, u32[]{:S(2)}, u32[]{:S(2)}) collective-permute-start(f32[64,256]{1,0:T(8,128)S(1)} %get-tuple-element.69.refs_0_), channel_id=1, source_target_pairs={{0,4},{1,5},{2,6},{3,7},{4,0},{5,1},{6,2},{7,3},{8,12},{9,13},{10,... | collective-permute-start | bytes 196616 | tf_op jit(solution)/shard_map/ppermute | solution.py:363
  22.2 4.3 %collective-permute-start.2 = (f32[64,256]{1,0:T(8,128)S(1)}, f32[64,256]{1,0:T(8,128)S(1)}, u32[]{:S(2)}, u32[]{:S(2)}) collective-permute-start(f32[64,256]{1,0:T(8,128)S(1)} %get-tuple-element.71.refs_0_), channel_id=1, source_target_pairs={{0,8},{1,9},{2,10},{3,11},{4,12},{5,13},{6,14},{7,15},{8,0},{9,1},... | collective-permute-start | bytes 196616 | tf_op jit(solution)/shard_map/ppermute | solution.py:363
  26.6 5.2 %collective-permute-start.5 = (f32[64,256]{1,0:T(8,128)S(1)}, f32[64,256]{1,0:T(8,128)S(1)}, u32[]{:S(2)}, u32[]{:S(2)}) collective-permute-start(f32[64,256]{1,0:T(8,128)S(1)} %get-tuple-element.76.refs_3_), channel_id=1, source_target_pairs={{0,16},{1,17},{2,18},{3,19},{4,20},{5,21},{6,22},{7,23},{8,24},{9,... | collective-permute-start | bytes 196616 | tf_op jit(solution)/shard_map/ppermute | solution.py:363
  32.4 10.7 %collective-permute-start.6 = (f32[5,64,256]{2,1,0:T(8,128)S(1)}, f32[5,64,256]{2,1,0:T(8,128)S(1)}, u32[]{:S(2)}, u32[]{:S(2)}) collective-permute-start(f32[5,64,256]{2,1,0:T(8,128)S(1)} %get-tuple-element.81), channel_id=1, source_target_pairs={{0,1},{1,0},{2,3},{3,2},{4,5},{5,4},{6,7},{7,6},{8,9},{9,8},{10,11... | collective-permute-start | bytes 983048 | tf_op jit(solution)/shard_map/ppermute | solution.py:363
  32.8 9.2 %collective-permute-start.7 = (f32[4,64,256]{2,1,0:T(8,128)S(1)}, f32[4,64,256]{2,1,0:T(8,128)S(1)}, u32[]{:S(2)}, u32[]{:S(2)}) collective-permute-start(f32[4,64,256]{2,1,0:T(8,128)S(1)} %get-tuple-element.82), channel_id=1, source_target_pairs={{0,2},{1,3},{2,0},{3,1},{4,6},{5,7},{6,4},{7,5},{8,10},{9,11},{10,... | collective-permute-start | bytes 786440 | tf_op jit(solution)/shard_map/ppermute | solution.py:363
  34.7 14.0 %collective-permute-start.8 = (f32[4,64,256]{2,1,0:T(8,128)S(1)}, f32[4,64,256]{2,1,0:T(8,128)S(1)}, u32[]{:S(2)}, u32[]{:S(2)}) collective-permute-start(f32[4,64,256]{2,1,0:T(8,128)S(1)} %get-tuple-element.86), channel_id=1, source_target_pairs={{0,1},{1,0},{2,3},{3,2},{4,5},{5,4},{6,7},{7,6},{8,9},{9,8},{10,11... | collective-permute-start | bytes 786440 | tf_op jit(solution)/shard_map/ppermute | solution.py:363
  36.4 12.3 %collective-permute-start.9 = (f32[4,64,256]{2,1,0:T(8,128)S(1)}, f32[4,64,256]{2,1,0:T(8,128)S(1)}, u32[]{:S(2)}, u32[]{:S(2)}) collective-permute-start(f32[4,64,256]{2,1,0:T(8,128)S(1)} %get-tuple-element.87), channel_id=1, source_target_pairs={{0,2},{1,3},{2,0},{3,1},{4,6},{5,7},{6,4},{7,5},{8,10},{9,11},{10,... | collective-permute-start | bytes 786440 | tf_op jit(solution)/shard_map/ppermute | solution.py:363
  43.1 7.6 %collective-permute-start.10 = (f32[4,64,256]{2,1,0:T(8,128)S(1)}, f32[4,64,256]{2,1,0:T(8,128)S(1)}, u32[]{:S(2)}, u32[]{:S(2)}) collective-permute-start(f32[4,64,256]{2,1,0:T(8,128)S(1)} %get-tuple-element.91), channel_id=1, source_target_pairs={{0,8},{1,9},{2,10},{3,11},{4,12},{5,13},{6,14},{7,15},{8,0},{9,1},... | collective-permute-start | bytes 786440 | tf_op jit(solution)/shard_map/ppermute | solution.py:363
  44.4 11.2 %collective-permute-start.11 = (f32[4,64,256]{2,1,0:T(8,128)S(1)}, f32[4,64,256]{2,1,0:T(8,128)S(1)}, u32[]{:S(2)}, u32[]{:S(2)}) collective-permute-start(f32[4,64,256]{2,1,0:T(8,128)S(1)} %get-tuple-element.94), channel_id=1, source_target_pairs={{0,1},{1,0},{2,3},{3,2},{4,5},{5,4},{6,7},{7,6},{8,9},{9,8},{10,11... | collective-permute-start | bytes 786440 | tf_op jit(solution)/shard_map/ppermute | solution.py:363
  45.1 10.5 %collective-permute-start.12 = (f32[4,64,256]{2,1,0:T(8,128)S(1)}, f32[4,64,256]{2,1,0:T(8,128)S(1)}, u32[]{:S(2)}, u32[]{:S(2)}) collective-permute-start(f32[4,64,256]{2,1,0:T(8,128)S(1)} %get-tuple-element.95), channel_id=1, source_target_pairs={{0,2},{1,3},{2,0},{3,1},{4,6},{5,7},{6,4},{7,5},{8,10},{9,11},{10,... | collective-permute-start | bytes 786440 | tf_op jit(solution)/shard_map/ppermute | solution.py:363
  50.7 15.0 %collective-permute-start.17 = (f32[4,64,256]{2,1,0:T(8,128)S(1)}, f32[4,64,256]{2,1,0:T(8,128)S(1)}, u32[]{:S(2)}, u32[]{:S(2)}) collective-permute-start(f32[4,64,256]{2,1,0:T(8,128)S(1)} %get-tuple-element.109), channel_id=1, source_target_pairs={{0,16},{1,17},{2,18},{3,19},{4,20},{5,21},{6,22},{7,23},{8,24},{9,... | collective-permute-start | bytes 786440 | tf_op jit(solution)/shard_map/ppermute | solution.py:363
  54.4 5.7 %collective-permute-start.14 = (f32[3,64,256]{2,1,0:T(8,128)S(1)}, f32[3,64,256]{2,1,0:T(8,128)S(1)}, u32[]{:S(2)}, u32[]{:S(2)}) collective-permute-start(f32[3,64,256]{2,1,0:T(8,128)S(1)} %get-tuple-element.99), channel_id=1, source_target_pairs={{0,2},{1,3},{2,0},{3,1},{4,6},{5,7},{6,4},{7,5},{8,10},{9,11},{10,... | collective-permute-start | bytes 589832 | tf_op jit(solution)/shard_map/ppermute | solution.py:363
  54.4 5.0 %collective-permute-start.13 = (f32[2,64,256]{2,1,0:T(8,128)S(1)}, f32[2,64,256]{2,1,0:T(8,128)S(1)}, u32[]{:S(2)}, u32[]{:S(2)}) collective-permute-start(f32[2,64,256]{2,1,0:T(8,128)S(1)} %get-tuple-element.98), channel_id=1, source_target_pairs={{0,1},{1,0},{2,3},{3,2},{4,5},{5,4},{6,7},{7,6},{8,9},{9,8},{10,11... | collective-permute-start | bytes 393224 | tf_op jit(solution)/shard_map/ppermute | solution.py:363
  55.7 10.0 %collective-permute-start.15 = (f32[2,64,256]{2,1,0:T(8,128)S(1)}, f32[2,64,256]{2,1,0:T(8,128)S(1)}, u32[]{:S(2)}, u32[]{:S(2)}) collective-permute-start(f32[2,64,256]{2,1,0:T(8,128)S(1)} %get-tuple-element.107), channel_id=1, source_target_pairs={{0,1},{1,0},{2,3},{3,2},{4,5},{5,4},{6,7},{7,6},{8,9},{9,8},{10,11... | collective-permute-start | bytes 393224 | tf_op jit(solution)/shard_map/ppermute | solution.py:363
  56.6 9.1 %collective-permute-start.16 = (f32[2,64,256]{2,1,0:T(8,128)S(1)}, f32[2,64,256]{2,1,0:T(8,128)S(1)}, u32[]{:S(2)}, u32[]{:S(2)}) collective-permute-start(f32[2,64,256]{2,1,0:T(8,128)S(1)} %get-tuple-element.108), channel_id=1, source_target_pairs={{0,2},{1,3},{2,0},{3,1},{4,6},{5,7},{6,4},{7,5},{8,10},{9,11},{10,... | collective-permute-start | bytes 393224 | tf_op jit(solution)/shard_map/ppermute | solution.py:363
  60.1 8.7 %collective-permute-start.18 = (f32[4,64,256]{2,1,0:T(8,128)S(1)}, f32[4,64,256]{2,1,0:T(8,128)S(1)}, u32[]{:S(2)}, u32[]{:S(2)}) collective-permute-start(f32[4,64,256]{2,1,0:T(8,128)S(1)} %get-tuple-element.116), channel_id=1, source_target_pairs={{0,8},{1,9},{2,10},{3,11},{4,12},{5,13},{6,14},{7,15},{8,0},{9,1},... | collective-permute-start | bytes 786440 | tf_op jit(solution)/shard_map/ppermute | solution.py:363

commit v9 on v8

--- a/solution.py
+++ b/solution.py
@@ -145,17 +145,17 @@
     )(codes, tiles, *factors)
 
 
-def encode(n_doc, me, block, per):
+def encode(n_doc, me, block, extra, per):
     rel = lax.bitwise_xor(block // per, me)
     core = (rel // n_doc) & 1
     slot = (rel // (2 * n_doc)) * n_doc + (rel & (n_doc - 1))
-    return slot | (core << 10) | ((block % per) << 11)
-
-
-def pick_kernel(n_tiles, away, here, code_ref, out):
+    return slot | (core << 10) | ((block % per) << 11) | (extra << 12)
+
+
+def pick_kernel(away, here, code_ref, out):
     slots = away.shape[0] - 1
     for i in range(out.shape[0]):
-        code = code_ref[n_tiles + i]
+        code = code_ref[i]
         slot, row = code & 1023, code >> 12
         bit = ((code >> 11) & 1).astype(F32)
         other = ((code >> 10) & 1) == 1
@@ -365,11 +365,9 @@
     def swap_y(values):
         return [swap(v, 2 * (k + 1)) for k, v in enumerate(values)]
 
-    n_tiles, count = coords.shape[0], anchors.shape[0]
-    is_block = lax.broadcasted_iota(jnp.int32, (2, n_tiles + count), 0) == 0
-    anchor = jnp.where(is_block[:, :count], anchors // tile, anchors % tile + doc_base)
-    pair = jnp.pad(coords.T, ((0, 0), (0, count))) + jnp.pad(anchor, ((0, 0), (n_tiles, 0)))
-    codes = jnp.sum(jnp.where(is_block, encode(n_doc, me, pair, per), (pair - doc_base) << 12), axis=0)
+    count = anchors.shape[0]
+    codes = encode(n_doc, me, coords[:, 0], coords[:, 1] - doc_base, per)
+    anchor_codes = encode(n_doc, me, anchors // tile, anchors % tile, per)
     slots = n_z * n_doc
     away, _, tiles_here, top, low = products(slots, 1, codes, tiles, sketch)
     got = swap(away, n_doc)
@@ -394,8 +392,7 @@
     mid = tuple(range(n_z // 2 - 1, 0, -1))
     far_groups = (tuple(range(n_z - 1, n_z // 2 - 1, -1)),)
     state = do_spread(far_groups)
-    pick = functools.partial(pick_kernel, n_tiles)
-    part, = queue.call("pick", pick, (shaped((count, width)),), (away, here), (codes,))
+    part, = queue.call("pick", pick_kernel, (shaped((count, width)),), (away, here), (anchor_codes,))
     masks = [n_doc << b for b in range((n_term - 1).bit_length())]
     for mask in masks[:-1]:
         part = total(queue, [part, swap(part, mask)])

time: 70 us -> 70.1 us (level)
  waiting for transfers between devices: 18.5 us -> 23.9 us
  starting transfers between devices: 27 us -> 21.9 us
    ppermute x19, waiting for transfers between devices: 18.5 us -> 23.9 us  [swap(): return lax.ppermute(v, AXES, [(i, i ^ mask) for i in range(devices)])]
    ppermute x19, starting transfers between devices: 27 us -> 21.9 us  [swap(): return lax.ppermute(v, AXES, [(i, i ^ mask) for i in range(devices)])]
    or x0 -> x2, other arithmetic: none -> 0.81 us  [encode(): return slot | core << 10 | block % per << 11 | extra << 12]
    reduce_sum x1 -> x0, other arithmetic: 0.76 us -> none  [body(): jnp.sum(jnp.where(is_block, encode(n_doc, me, pair, per), pair - doc_base...]
    select_n x2 -> x0, other arithmetic: 0.74 us -> none  [the longest x1 0.67 us: body(): anchors // tile]
    unnamed x2 -> x4, local copies, waits for them, and re-layouts: 1.58 us -> 1.59 us
  transfers between devices with their start and end apart: 19 -> 19, of which waited for: 10 -> 9; matrix products, arithmetic and copies ran while one was open for 0% -> 0% of each run, Pallas kernels for 18% -> 18%
where the time goes in v9:
time: 70.1 us; the launch traced here: 69.9 us
  waiting for transfers between devices  23.9 us (34%)
  starting transfers between devices  21.9 us (31%)
  Pallas kernels  20.9 us (30%)
  local copies, waits for them, and re-layouts  1.59 us (2%)
  between operations  0.85 us (1%)
  other arithmetic  0.81 us (1%)
    ppermute x19, waiting for transfers between devices, swap(): return lax.ppermute(v, AXES, [(i, i ^ mask) for i in range(devices)])  23.9 us
    ppermute x19, starting transfers between devices, swap(): return lax.ppermute(v, AXES, [(i, i ^ mask) for i in range(devices)])  21.9 us
    pallas_call x2, Pallas kernels, products(): pl.pallas_call(functools.partial(products_kernel, slots, away), out_shape...  11.2 us
    pallas_call x18, Pallas kernels, call(): pl.pallas_call(functools.partial(in_order, kernel, len(args) + len(smem))...  9.64 us
    unnamed x4, local copies, waits for them, and re-layouts  1.59 us
  transfers between devices with their start and end apart: 19, of which 9 were waited for; matrix products, arithmetic and copies ran while one was open for 0% of the time, Pallas kernels for 18%

profile of v9, /device:TPU:0, one launch (start us, length us, event | category | flops | bytes accessed | tf_op | source)
XLA Modules:
  0.0 69.9 jit_solution(2820641739055014374)
XLA Ops:
  0.6 0.8 %fusion.2.code_ref = s32[128]{0:T(128)S(1)} fusion(s32[128,2]{0,1:T(2,128)} %param.5, s32[]{:T(128)S(6)} %mul.21, s32[]{:T(128)S(6)} %add.32), kind=kLoop, calls=%fused_computation.31 | loop fusion | flops 7168 | bytes 1544 | tf_op jit(solution)/shard_map/or | solution.py:152
  1.4 1.6 %copy-done = f32[2048,256]{1,0:T(8,128)S(1)} copy-done((f32[2048,256]{1,0:T(8,128)S(1)}, f32[2048,256]{1,0:T(8,128)}, u32[]{:S(2)}) %copy-start) | copy-done | bytes 2097176
  3.0 6.1 %products_away.1 = (f32[17,128,256]{2,1,0:T(8,128)S(1)}, f32[8,128]{1,0:T(8,128)}, f32[128,128,128]{2,1,0:T(8,128)S(1)}, bf16[2048,256]{1,0:T(8,128)(2,1)S(1)}, bf16[2048,256]{1,0:T(8,128)(2,1)S(1)}) custom-call(s32[128]{0:T(128)S(1)} %fusion.2.code_ref, f32[128,128,128]{2,1,0:T(8,128)} %refs_0_.1, f32[2048,256]{1,0:T(8,128)S(1)} %copy-done), custom_call_target="tpu_custom_call" | custom-call | flops 8000000000 | bytes 5242880 | tf_op jit(solution)/shard_map/products_away/pallas_call | solution.py:136
  9.1 1.0 %collective-permute-start = (f32[17,128,256]{2,1,0:T(8,128)S(1)}, f32[17,128,256]{2,1,0:T(8,128)S(1)}, u32[]{:S(2)}, u32[]{:S(2)}) collective-permute-start(f32[17,128,256]{2,1,0:T(8,128)S(1)} %get-tuple-element.66.refs_0_), channel_id=1, source_target_pairs={{0,4},{1,5},{2,6},{3,7},{4,0},{5,1},{6,2},{7,3},{8,12},{9,13},{10,... | collective-permute-start | bytes 6684680 | tf_op jit(solution)/shard_map/ppermute | solution.py:363
  10.0 5.1 %products_here.1 = (f32[17,128,256]{2,1,0:T(8,128)S(1)}, f32[8,128]{1,0:T(8,128)S(1)}) custom-call(s32[128]{0:T(128)S(1)} %fusion.2.code_ref, f32[128,128,128]{2,1,0:T(8,128)S(1)} %get-tuple-element.61.refs_0_, bf16[2048,256]{1,0:T(8,128)(2,1)S(1)} %get-tuple-element.62.refs_1_, bf16[2048,256]{1,0:T(8,128)(2,1)S(1)} %get-tuple-element.63.refs_2_), custom_call_target="tpu_custom_call" | custom-call | flops 8000000000 | bytes 5242880 | tf_op jit(solution)/shard_map/products_here/pallas_call | solution.py:136
  15.5 2.4 %collective-permute-start.3 = (f32[8,64,256]{2,1,0:T(8,128)S(1)}, f32[8,64,256]{2,1,0:T(8,128)S(1)}, u32[]{:S(2)}, u32[]{:S(2)}) collective-permute-start(f32[8,64,256]{2,1,0:T(8,128)S(1)} %get-tuple-element.74), channel_id=1, source_target_pairs={{0,1},{1,0},{2,3},{3,2},{4,5},{5,4},{6,7},{7,6},{8,9},{9,8},{10,11... | collective-permute-start | bytes 1572872 | tf_op jit(solution)/shard_map/ppermute | solution.py:363
  17.9 2.3 %collective-permute-start.4 = (f32[8,64,256]{2,1,0:T(8,128)S(1)}, f32[8,64,256]{2,1,0:T(8,128)S(1)}, u32[]{:S(2)}, u32[]{:S(2)}) collective-permute-start(f32[8,64,256]{2,1,0:T(8,128)S(1)} %get-tuple-element.75), channel_id=1, source_target_pairs={{0,2},{1,3},{2,0},{3,1},{4,6},{5,7},{6,4},{7,5},{8,10},{9,11},{10,... | collective-permute-start | bytes 1572872 | tf_op jit(solution)/shard_map/ppermute | solution.py:363
  20.2 0.9 %pick.1 = (f32[8,128]{1,0:T(8,128)S(1)}, f32[64,256]{1,0:T(8,128)S(1)}) custom-call(f32[8,128]{1,0:T(8,128)S(1)} %get-tuple-element.67._token, f32[17,128,256]{2,1,0:T(8,128)S(1)} %get-tuple-element.66.refs_0_, f32[17,128,256]{2,1,0:T(8,128)S(1)} %get-tuple-element.65.refs_0_.refs_1_, s32[64]{0:T(128)S(1)} %fusion.5.refs_2_), custom_call_target="tpu_custom_call" | custom-call | flops 1 | bytes 1 | tf_op jit(solution)/shard_map/pick/pallas_call | solution.py:53
  21.2 1.2 %collective-permute-done.1.refs_1_ = f32[64,256]{1,0:T(8,128)S(1)} collective-permute-done((f32[64,256]{1,0:T(8,128)S(1)}, f32[64,256]{1,0:T(8,128)S(1)}, u32[]{:S(2)}, u32[]{:S(2)}) %collective-permute-start.1) | collective-permute-done | bytes 65568 | tf_op jit(solution)/shard_map/ppermute | solution.py:363
  22.6 4.3 %collective-permute-done.2.refs_1_ = f32[64,256]{1,0:T(8,128)S(1)} collective-permute-done((f32[64,256]{1,0:T(8,128)S(1)}, f32[64,256]{1,0:T(8,128)S(1)}, u32[]{:S(2)}, u32[]{:S(2)}) %collective-permute-start.2) | collective-permute-done | bytes 65568 | tf_op jit(solution)/shard_map/ppermute | solution.py:363
  26.8 1.9 %collective-permute-start.5 = (f32[64,256]{1,0:T(8,128)S(1)}, f32[64,256]{1,0:T(8,128)S(1)}, u32[]{:S(2)}, u32[]{:S(2)}) collective-permute-start(f32[64,256]{1,0:T(8,128)S(1)} %get-tuple-element.76.refs_3_), channel_id=1, source_target_pairs={{0,16},{1,17},{2,18},{3,19},{4,20},{5,21},{6,22},{7,23},{8,24},{9,... | collective-permute-start | bytes 196616 | tf_op jit(solution)/shard_map/ppermute | solution.py:363
  28.7 4.0 %collective-permute-done.5.refs_4_ = f32[64,256]{1,0:T(8,128)S(1)} collective-permute-done((f32[64,256]{1,0:T(8,128)S(1)}, f32[64,256]{1,0:T(8,128)S(1)}, u32[]{:S(2)}, u32[]{:S(2)}) %collective-permute-start.5) | collective-permute-done | bytes 65568 | tf_op jit(solution)/shard_map/ppermute | solution.py:363
  32.9 0.4 collective-permute-start.7
  33.5 1.6 %collective-permute-start.8 = (f32[4,64,256]{2,1,0:T(8,128)S(1)}, f32[4,64,256]{2,1,0:T(8,128)S(1)}, u32[]{:S(2)}, u32[]{:S(2)}) collective-permute-start(f32[4,64,256]{2,1,0:T(8,128)S(1)} %get-tuple-element.86), channel_id=1, source_target_pairs={{0,1},{1,0},{2,3},{3,2},{4,5},{5,4},{6,7},{7,6},{8,9},{9,8},{10,11... | collective-permute-start | bytes 786440 | tf_op jit(solution)/shard_map/ppermute | solution.py:363
  35.1 2.0 %collective-permute-start.9 = (f32[4,64,256]{2,1,0:T(8,128)S(1)}, f32[4,64,256]{2,1,0:T(8,128)S(1)}, u32[]{:S(2)}, u32[]{:S(2)}) collective-permute-start(f32[4,64,256]{2,1,0:T(8,128)S(1)} %get-tuple-element.87), channel_id=1, source_target_pairs={{0,2},{1,3},{2,0},{3,1},{4,6},{5,7},{6,4},{7,5},{8,10},{9,11},{10,... | collective-permute-start | bytes 786440 | tf_op jit(solution)/shard_map/ppermute | solution.py:363
  37.3 4.9 %collective-permute-done.7.refs_2_ = f32[4,64,256]{2,1,0:T(8,128)S(1)} collective-permute-done((f32[4,64,256]{2,1,0:T(8,128)S(1)}, f32[4,64,256]{2,1,0:T(8,128)S(1)}, u32[]{:S(2)}, u32[]{:S(2)}) %collective-permute-start.7) | collective-permute-done | bytes 262176 | tf_op jit(solution)/shard_map/ppermute | solution.py:363
  42.2 1.3 %collective-permute-done.6.refs_1_ = f32[5,64,256]{2,1,0:T(8,128)S(1)} collective-permute-done((f32[5,64,256]{2,1,0:T(8,128)S(1)}, f32[5,64,256]{2,1,0:T(8,128)S(1)}, u32[]{:S(2)}, u32[]{:S(2)}) %collective-permute-start.6) | collective-permute-done | bytes 327712 | tf_op jit(solution)/shard_map/ppermute | solution.py:363
  43.7 1.0 %collective-permute-start.11 = (f32[4,64,256]{2,1,0:T(8,128)S(1)}, f32[4,64,256]{2,1,0:T(8,128)S(1)}, u32[]{:S(2)}, u32[]{:S(2)}) collective-permute-start(f32[4,64,256]{2,1,0:T(8,128)S(1)} %get-tuple-element.94), channel_id=1, source_target_pairs={{0,1},{1,0},{2,3},{3,2},{4,5},{5,4},{6,7},{7,6},{8,9},{9,8},{10,11... | collective-permute-start | bytes 786440 | tf_op jit(solution)/shard_map/ppermute | solution.py:363
  44.7 1.4 %collective-permute-start.12 = (f32[4,64,256]{2,1,0:T(8,128)S(1)}, f32[4,64,256]{2,1,0:T(8,128)S(1)}, u32[]{:S(2)}, u32[]{:S(2)}) collective-permute-start(f32[4,64,256]{2,1,0:T(8,128)S(1)} %get-tuple-element.95), channel_id=1, source_target_pairs={{0,2},{1,3},{2,0},{3,1},{4,6},{5,7},{6,4},{7,5},{8,10},{9,11},{10,... | collective-permute-start | bytes 786440 | tf_op jit(solution)/shard_map/ppermute | solution.py:363
  46.1 3.1 %collective-permute-done.8.refs_1_ = f32[4,64,256]{2,1,0:T(8,128)S(1)} collective-permute-done((f32[4,64,256]{2,1,0:T(8,128)S(1)}, f32[4,64,256]{2,1,0:T(8,128)S(1)}, u32[]{:S(2)}, u32[]{:S(2)}) %collective-permute-start.8) | collective-permute-done | bytes 262176 | tf_op jit(solution)/shard_map/ppermute | solution.py:363
  49.2 3.6 %collective-permute-done.10.refs_1_ = f32[4,64,256]{2,1,0:T(8,128)S(1)} collective-permute-done((f32[4,64,256]{2,1,0:T(8,128)S(1)}, f32[4,64,256]{2,1,0:T(8,128)S(1)}, u32[]{:S(2)}, u32[]{:S(2)}) %collective-permute-start.10) | collective-permute-done | bytes 262176 | tf_op jit(solution)/shard_map/ppermute | solution.py:363
  52.9 0.8 %collective-permute-start.17 = (f32[4,64,256]{2,1,0:T(8,128)S(1)}, f32[4,64,256]{2,1,0:T(8,128)S(1)}, u32[]{:S(2)}, u32[]{:S(2)}) collective-permute-start(f32[4,64,256]{2,1,0:T(8,128)S(1)} %get-tuple-element.109), channel_id=1, source_target_pairs={{0,16},{1,17},{2,18},{3,19},{4,20},{5,21},{6,22},{7,23},{8,24},{9,... | collective-permute-start | bytes 786440 | tf_op jit(solution)/shard_map/ppermute | solution.py:363
  53.7 0.8 %collective-permute-start.13 = (f32[2,64,256]{2,1,0:T(8,128)S(1)}, f32[2,64,256]{2,1,0:T(8,128)S(1)}, u32[]{:S(2)}, u32[]{:S(2)}) collective-permute-start(f32[2,64,256]{2,1,0:T(8,128)S(1)} %get-tuple-element.98), channel_id=1, source_target_pairs={{0,1},{1,0},{2,3},{3,2},{4,5},{5,4},{6,7},{7,6},{8,9},{9,8},{10,11... | collective-permute-start | bytes 393224 | tf_op jit(solution)/shard_map/ppermute | solution.py:363
  54.5 1.3 %collective-permute-start.15 = (f32[2,64,256]{2,1,0:T(8,128)S(1)}, f32[2,64,256]{2,1,0:T(8,128)S(1)}, u32[]{:S(2)}, u32[]{:S(2)}) collective-permute-start(f32[2,64,256]{2,1,0:T(8,128)S(1)} %get-tuple-element.107), channel_id=1, source_target_pairs={{0,1},{1,0},{2,3},{3,2},{4,5},{5,4},{6,7},{7,6},{8,9},{9,8},{10,11... | collective-permute-start | bytes 393224 | tf_op jit(solution)/shard_map/ppermute | solution.py:363
  55.8 2.0 %collective-permute-start.16 = (f32[2,64,256]{2,1,0:T(8,128)S(1)}, f32[2,64,256]{2,1,0:T(8,128)S(1)}, u32[]{:S(2)}, u32[]{:S(2)}) collective-permute-start(f32[2,64,256]{2,1,0:T(8,128)S(1)} %get-tuple-element.108), channel_id=1, source_target_pairs={{0,2},{1,3},{2,0},{3,1},{4,6},{5,7},{6,4},{7,5},{8,10},{9,11},{10,... | collective-permute-start | bytes 393224 | tf_op jit(solution)/shard_map/ppermute | solution.py:363
  57.8 0.8 %collective-permute-done.13.refs_1_ = f32[2,64,256]{2,1,0:T(8,128)S(1)} collective-permute-done((f32[2,64,256]{2,1,0:T(8,128)S(1)}, f32[2,64,256]{2,1,0:T(8,128)S(1)}, u32[]{:S(2)}, u32[]{:S(2)}) %collective-permute-start.13) | collective-permute-done | bytes 131104 | tf_op jit(solution)/shard_map/ppermute | solution.py:363
  58.6 0.7 collective-permute-done.14.refs_2_
  59.4 2.7 %collective-permute-start.18 = (f32[4,64,256]{2,1,0:T(8,128)S(1)}, f32[4,64,256]{2,1,0:T(8,128)S(1)}, u32[]{:S(2)}, u32[]{:S(2)}) collective-permute-start(f32[4,64,256]{2,1,0:T(8,128)S(1)} %get-tuple-element.116), channel_id=1, source_target_pairs={{0,8},{1,9},{2,10},{3,11},{4,12},{5,13},{6,14},{7,15},{8,0},{9,1},... | collective-permute-start | bytes 786440 | tf_op jit(solution)/shard_map/ppermute | solution.py:363
  62.1 0.3 gram.1
  62.4 2.7 %eliminate.2 = (f32[8,128]{1,0:T(8,128)S(1)}, f32[64,64]{1,0:T(8,128)S(1)}) custom-call(f32[8,128]{1,0:T(8,128)S(1)} %get-tuple-element.103._token, f32[64,64]{1,0:T(8,128)S(1)} %get-tuple-element.104.refs_0_), custom_call_target="tpu_custom_call" | custom-call | flops 1 | bytes 1 | tf_op jit(solution)/shard_map/eliminate/pallas_call | solution.py:53
  65.2 2.7 %eliminate.3 = (f32[8,128]{1,0:T(8,128)S(1)}, f32[64,64]{1,0:T(8,128)S(1)}) custom-call(f32[8,128]{1,0:T(8,128)S(1)} %get-tuple-element.110._token, f32[64,64]{1,0:T(8,128)S(1)} %get-tuple-element.111.refs_0_), custom_call_target="tpu_custom_call" | custom-call | flops 4000000000 | bytes 1 | tf_op jit(solution)/shard_map/eliminate/pallas_call | solution.py:53
  68.2 1.7 %finish.1 = (f32[8,128]{1,0:T(8,128)}, f32[64,256]{1,0:T(8,128)}, f32[256,256]{1,0:T(8,128)}) custom-call(f32[8,128]{1,0:T(8,128)S(1)} %get-tuple-element.114._token, f32[4,64,256]{2,1,0:T(8,128)S(1)} %get-tuple-element.115.refs_0_, f32[4,64,256]{2,1,0:T(8,128)S(1)} %collective-permute-done.18.refs_1_, f32[64,256]{1,0:T(8,128)S(1)} %get-tuple-element.102.refs_0_.refs_2_, ...), custom_call_target="tpu_custom_call" | custom-call | flops 1 | bytes 1 | tf_op jit(solution)/shard_map/finish/pallas_call | solution.py:53
  (32 shorter events, 1.7 us)
Async XLA Ops:
  1.4 1.6 %copy-start = (f32[2048,256]{1,0:T(8,128)S(1)}, f32[2048,256]{1,0:T(8,128)}, u32[]{:S(2)}) copy-start(f32[2048,256]{1,0:T(8,128)} %refs_1_.1) | copy-start | bytes 6291460
  9.1 6.1 %collective-permute-start = (f32[17,128,256]{2,1,0:T(8,128)S(1)}, f32[17,128,256]{2,1,0:T(8,128)S(1)}, u32[]{:S(2)}, u32[]{:S(2)}) collective-permute-start(f32[17,128,256]{2,1,0:T(8,128)S(1)} %get-tuple-element.66.refs_0_), channel_id=1, source_target_pairs={{0,4},{1,5},{2,6},{3,7},{4,0},{5,1},{6,2},{7,3},{8,12},{9,13},{10,... | collective-permute-start | bytes 6684680 | tf_op jit(solution)/shard_map/ppermute | solution.py:363
  15.2 5.0 %copy-start.1 = (s32[64]{0:T(128)S(1)}, s32[64]{0:T(128)}, u32[]{:S(2)}) copy-start(s32[64]{0:T(128)} %param.7) | copy-start | bytes 772
  15.5 17.2 %collective-permute-start.3 = (f32[8,64,256]{2,1,0:T(8,128)S(1)}, f32[8,64,256]{2,1,0:T(8,128)S(1)}, u32[]{:S(2)}, u32[]{:S(2)}) collective-permute-start(f32[8,64,256]{2,1,0:T(8,128)S(1)} %get-tuple-element.74), channel_id=1, source_target_pairs={{0,1},{1,0},{2,3},{3,2},{4,5},{5,4},{6,7},{7,6},{8,9},{9,8},{10,11... | collective-permute-start | bytes 1572872 | tf_op jit(solution)/shard_map/ppermute | solution.py:363
  17.9 14.8 %collective-permute-start.4 = (f32[8,64,256]{2,1,0:T(8,128)S(1)}, f32[8,64,256]{2,1,0:T(8,128)S(1)}, u32[]{:S(2)}, u32[]{:S(2)}) collective-permute-start(f32[8,64,256]{2,1,0:T(8,128)S(1)} %get-tuple-element.75), channel_id=1, source_target_pairs={{0,2},{1,3},{2,0},{3,1},{4,6},{5,7},{6,4},{7,5},{8,10},{9,11},{10,... | collective-permute-start | bytes 1572872 | tf_op jit(solution)/shard_map/ppermute | solution.py:363
  21.2 1.3 %collective-permute-start.1 = (f32[64,256]{1,0:T(8,128)S(1)}, f32[64,256]{1,0:T(8,128)S(1)}, u32[]{:S(2)}, u32[]{:S(2)}) collective-permute-start(f32[64,256]{1,0:T(8,128)S(1)} %get-tuple-element.69.refs_0_), channel_id=1, source_target_pairs={{0,4},{1,5},{2,6},{3,7},{4,0},{5,1},{6,2},{7,3},{8,12},{9,13},{10,... | collective-permute-start | bytes 196616 | tf_op jit(solution)/shard_map/ppermute | solution.py:363
  22.5 4.3 %collective-permute-start.2 = (f32[64,256]{1,0:T(8,128)S(1)}, f32[64,256]{1,0:T(8,128)S(1)}, u32[]{:S(2)}, u32[]{:S(2)}) collective-permute-start(f32[64,256]{1,0:T(8,128)S(1)} %get-tuple-element.71.refs_0_), channel_id=1, source_target_pairs={{0,8},{1,9},{2,10},{3,11},{4,12},{5,13},{6,14},{7,15},{8,0},{9,1},... | collective-permute-start | bytes 196616 | tf_op jit(solution)/shard_map/ppermute | solution.py:363
  26.8 5.8 %collective-permute-start.5 = (f32[64,256]{1,0:T(8,128)S(1)}, f32[64,256]{1,0:T(8,128)S(1)}, u32[]{:S(2)}, u32[]{:S(2)}) collective-permute-start(f32[64,256]{1,0:T(8,128)S(1)} %get-tuple-element.76.refs_3_), channel_id=1, source_target_pairs={{0,16},{1,17},{2,18},{3,19},{4,20},{5,21},{6,22},{7,23},{8,24},{9,... | collective-permute-start | bytes 196616 | tf_op jit(solution)/shard_map/ppermute | solution.py:363
  32.8 10.7 %collective-permute-start.6 = (f32[5,64,256]{2,1,0:T(8,128)S(1)}, f32[5,64,256]{2,1,0:T(8,128)S(1)}, u32[]{:S(2)}, u32[]{:S(2)}) collective-permute-start(f32[5,64,256]{2,1,0:T(8,128)S(1)} %get-tuple-element.81), channel_id=1, source_target_pairs={{0,1},{1,0},{2,3},{3,2},{4,5},{5,4},{6,7},{7,6},{8,9},{9,8},{10,11... | collective-permute-start | bytes 983048 | tf_op jit(solution)/shard_map/ppermute | solution.py:363
  32.9 9.3 %collective-permute-start.7 = (f32[4,64,256]{2,1,0:T(8,128)S(1)}, f32[4,64,256]{2,1,0:T(8,128)S(1)}, u32[]{:S(2)}, u32[]{:S(2)}) collective-permute-start(f32[4,64,256]{2,1,0:T(8,128)S(1)} %get-tuple-element.82), channel_id=1, source_target_pairs={{0,2},{1,3},{2,0},{3,1},{4,6},{5,7},{6,4},{7,5},{8,10},{9,11},{10,... | collective-permute-start | bytes 786440 | tf_op jit(solution)/shard_map/ppermute | solution.py:363
  33.5 15.7 %collective-permute-start.8 = (f32[4,64,256]{2,1,0:T(8,128)S(1)}, f32[4,64,256]{2,1,0:T(8,128)S(1)}, u32[]{:S(2)}, u32[]{:S(2)}) collective-permute-start(f32[4,64,256]{2,1,0:T(8,128)S(1)} %get-tuple-element.86), channel_id=1, source_target_pairs={{0,1},{1,0},{2,3},{3,2},{4,5},{5,4},{6,7},{7,6},{8,9},{9,8},{10,11... | collective-permute-start | bytes 786440 | tf_op jit(solution)/shard_map/ppermute | solution.py:363
  35.1 14.0 %collective-permute-start.9 = (f32[4,64,256]{2,1,0:T(8,128)S(1)}, f32[4,64,256]{2,1,0:T(8,128)S(1)}, u32[]{:S(2)}, u32[]{:S(2)}) collective-permute-start(f32[4,64,256]{2,1,0:T(8,128)S(1)} %get-tuple-element.87), channel_id=1, source_target_pairs={{0,2},{1,3},{2,0},{3,1},{4,6},{5,7},{6,4},{7,5},{8,10},{9,11},{10,... | collective-permute-start | bytes 786440 | tf_op jit(solution)/shard_map/ppermute | solution.py:363
  43.6 9.2 %collective-permute-start.10 = (f32[4,64,256]{2,1,0:T(8,128)S(1)}, f32[4,64,256]{2,1,0:T(8,128)S(1)}, u32[]{:S(2)}, u32[]{:S(2)}) collective-permute-start(f32[4,64,256]{2,1,0:T(8,128)S(1)} %get-tuple-element.91), channel_id=1, source_target_pairs={{0,8},{1,9},{2,10},{3,11},{4,12},{5,13},{6,14},{7,15},{8,0},{9,1},... | collective-permute-start | bytes 786440 | tf_op jit(solution)/shard_map/ppermute | solution.py:363
  43.7 10.7 %collective-permute-start.11 = (f32[4,64,256]{2,1,0:T(8,128)S(1)}, f32[4,64,256]{2,1,0:T(8,128)S(1)}, u32[]{:S(2)}, u32[]{:S(2)}) collective-permute-start(f32[4,64,256]{2,1,0:T(8,128)S(1)} %get-tuple-element.94), channel_id=1, source_target_pairs={{0,1},{1,0},{2,3},{3,2},{4,5},{5,4},{6,7},{7,6},{8,9},{9,8},{10,11... | collective-permute-start | bytes 786440 | tf_op jit(solution)/shard_map/ppermute | solution.py:363
  44.7 9.7 %collective-permute-start.12 = (f32[4,64,256]{2,1,0:T(8,128)S(1)}, f32[4,64,256]{2,1,0:T(8,128)S(1)}, u32[]{:S(2)}, u32[]{:S(2)}) collective-permute-start(f32[4,64,256]{2,1,0:T(8,128)S(1)} %get-tuple-element.95), channel_id=1, source_target_pairs={{0,2},{1,3},{2,0},{3,1},{4,6},{5,7},{6,4},{7,5},{8,10},{9,11},{10,... | collective-permute-start | bytes 786440 | tf_op jit(solution)/shard_map/ppermute | solution.py:363
  52.9 12.2 %collective-permute-start.17 = (f32[4,64,256]{2,1,0:T(8,128)S(1)}, f32[4,64,256]{2,1,0:T(8,128)S(1)}, u32[]{:S(2)}, u32[]{:S(2)}) collective-permute-start(f32[4,64,256]{2,1,0:T(8,128)S(1)} %get-tuple-element.109), channel_id=1, source_target_pairs={{0,16},{1,17},{2,18},{3,19},{4,20},{5,21},{6,22},{7,23},{8,24},{9,... | collective-permute-start | bytes 786440 | tf_op jit(solution)/shard_map/ppermute | solution.py:363
  53.7 5.7 %collective-permute-start.14 = (f32[3,64,256]{2,1,0:T(8,128)S(1)}, f32[3,64,256]{2,1,0:T(8,128)S(1)}, u32[]{:S(2)}, u32[]{:S(2)}) collective-permute-start(f32[3,64,256]{2,1,0:T(8,128)S(1)} %get-tuple-element.99), channel_id=1, source_target_pairs={{0,2},{1,3},{2,0},{3,1},{4,6},{5,7},{6,4},{7,5},{8,10},{9,11},{10,... | collective-permute-start | bytes 589832 | tf_op jit(solution)/shard_map/ppermute | solution.py:363
  53.7 5.0 %collective-permute-start.13 = (f32[2,64,256]{2,1,0:T(8,128)S(1)}, f32[2,64,256]{2,1,0:T(8,128)S(1)}, u32[]{:S(2)}, u32[]{:S(2)}) collective-permute-start(f32[2,64,256]{2,1,0:T(8,128)S(1)} %get-tuple-element.98), channel_id=1, source_target_pairs={{0,1},{1,0},{2,3},{3,2},{4,5},{5,4},{6,7},{7,6},{8,9},{9,8},{10,11... | collective-permute-start | bytes 393224 | tf_op jit(solution)/shard_map/ppermute | solution.py:363
  54.5 10.6 %collective-permute-start.15 = (f32[2,64,256]{2,1,0:T(8,128)S(1)}, f32[2,64,256]{2,1,0:T(8,128)S(1)}, u32[]{:S(2)}, u32[]{:S(2)}) collective-permute-start(f32[2,64,256]{2,1,0:T(8,128)S(1)} %get-tuple-element.107), channel_id=1, source_target_pairs={{0,1},{1,0},{2,3},{3,2},{4,5},{5,4},{6,7},{7,6},{8,9},{9,8},{10,11... | collective-permute-start | bytes 393224 | tf_op jit(solution)/shard_map/ppermute | solution.py:363
  55.8 9.3 %collective-permute-start.16 = (f32[2,64,256]{2,1,0:T(8,128)S(1)}, f32[2,64,256]{2,1,0:T(8,128)S(1)}, u32[]{:S(2)}, u32[]{:S(2)}) collective-permute-start(f32[2,64,256]{2,1,0:T(8,128)S(1)} %get-tuple-element.108), channel_id=1, source_target_pairs={{0,2},{1,3},{2,0},{3,1},{4,6},{5,7},{6,4},{7,5},{8,10},{9,11},{10,... | collective-permute-start | bytes 393224 | tf_op jit(solution)/shard_map/ppermute | solution.py:363
  59.4 8.8 %collective-permute-start.18 = (f32[4,64,256]{2,1,0:T(8,128)S(1)}, f32[4,64,256]{2,1,0:T(8,128)S(1)}, u32[]{:S(2)}, u32[]{:S(2)}) collective-permute-start(f32[4,64,256]{2,1,0:T(8,128)S(1)} %get-tuple-element.116), channel_id=1, source_target_pairs={{0,8},{1,9},{2,10},{3,11},{4,12},{5,13},{6,14},{7,15},{8,0},{9,1},... | collective-permute-start | bytes 786440 | tf_op jit(solution)/shard_map/ppermute | solution.py:363

commit v10 on v9

--- a/solution.py
+++ b/solution.py
@@ -291,21 +291,7 @@
     return queue.call("total", total_kernel, (shaped(values[0].shape),), values)[0]
 
 
-def gram_kernel(rows_ref, gram_ref):
-    rows = rows_ref[...]
-    count = rows.shape[0]
-    gram = hdot(rows, rows, ((1,), (1,)))
-    diagonal = lax.broadcasted_iota(jnp.int32, (count, count), 0) == lax.broadcasted_iota(jnp.int32, (count, count), 1)
-    ridge = 0.001 * jnp.sum(jnp.where(diagonal, gram, 0.0)) / count
-    gram_ref[...] = jnp.where(diagonal, gram + ridge, gram)
-
-
-def gram_of(queue, rows):
-    return queue.call("gram", gram_kernel, (shaped((rows.shape[0],) * 2),), (rows,))[0]
-
-
-def eliminate_kernel(lo, hi, given, out):
-    m = given[...]
+def eliminate_steps(m, lo, hi):
     count = m.shape[0]
     at_row = lax.broadcasted_iota(jnp.int32, (count, count), 0)
     at_col = lax.broadcasted_iota(jnp.int32, (count, count), 1)
@@ -315,21 +301,21 @@
         scale = 1.0 / m[k : k + 1, k : k + 1]
         row = jnp.where(at_col[:1] == k, 1.0, row) * scale
         m = jnp.where(at_row == k, row, jnp.where(at_col == k, 0.0, m) - col * row)
-    out[...] = m
-
-
-def eliminate(queue, m, part, cost):
-    half = m.shape[0] // 2
-    kernel = functools.partial(eliminate_kernel, part * half, (part + 1) * half)
-    return queue.call("eliminate", kernel, (shaped(m.shape),), (m,), cost=cost)[0]
-
-
-def solver_kernel(rows, inv, out):
-    out[...] = hdot(rows[...], inv[...], ((0,), (0,)))
-
-
-def solver(queue, rows, inv):
-    return queue.call("solver", solver_kernel, (shaped(rows.shape[::-1]),), (rows, inv))[0]
+    return m
+
+
+def gram_kernel(rows_ref, out):
+    rows = rows_ref[...]
+    count = rows.shape[0]
+    gram = hdot(rows, rows, ((1,), (1,)))
+    diagonal = lax.broadcasted_iota(jnp.int32, (count, count), 0) == lax.broadcasted_iota(jnp.int32, (count, count), 1)
+    ridge = 0.001 * jnp.sum(jnp.where(diagonal, gram, 0.0)) / count
+    out[...] = eliminate_steps(jnp.where(diagonal, gram + ridge, gram), 0, count // 2)
+
+
+def solver_kernel(rows, given, out):
+    count = rows.shape[0]
+    out[...] = hdot(rows[...], eliminate_steps(given[...], count // 2, count), ((0,), (0,)))
 
 
 def finish_kernel(n_far, near, *refs):
@@ -407,11 +393,9 @@
     keep, _, came = do_join(((0,),), near_state, (), None, (1,))
     rows, *sends = merge(queue, 0, n_mid, n_y, mid_keep, mid_came[0], False, (rows,))
     last = [swap(v, 2 * n_doc * dz) for v, dz in zip(sends, mid)]
-    gram = gram_of(queue, rows)
-    gram = eliminate(queue, gram, 0, TINY)
+    half_way, = queue.call("gram", gram_kernel, (shaped((count, count)),), (rows,))
     near, = merge(queue, 0, 1, n_y, keep, came[0], None, (far,))
-    gram = eliminate(queue, gram, 1, LONG)
-    solve = solver(queue, rows, gram)
+    solve, = queue.call("solver", solver_kernel, (shaped((width, count)),), (rows, half_way), cost=LONG)
     return finish(queue, near, last, rows, solve)
 
 

time: 70.1 us -> 68.8 us (0.981)
  waiting for transfers between devices: 23.9 us -> 21.9 us
  starting transfers between devices: 21.9 us -> 22.7 us
    ppermute x19, waiting for transfers between devices: 23.9 us -> 21.9 us  [swap(): return lax.ppermute(v, AXES, [(i, i ^ mask) for i in range(devices)])]
    ppermute x19, starting transfers between devices: 21.9 us -> 22.7 us  [swap(): return lax.ppermute(v, AXES, [(i, i ^ mask) for i in range(devices)])]
    pallas_call x18 -> x16, Pallas kernels: 9.64 us -> 9.61 us  [call(): pl.pallas_call(functools.partial(in_order, kernel, len(args) + len(smem))...]
where the time goes in v10:
time: 68.8 us; the launch traced here: 68.6 us
  starting transfers between devices  22.7 us (33%)
  waiting for transfers between devices  21.9 us (32%)
  Pallas kernels  20.8 us (30%)
  local copies, waits for them, and re-layouts  1.59 us (2%)
  other arithmetic  0.81 us (1%)
  between operations  0.81 us (1%)
    ppermute x19, starting transfers between devices, swap(): return lax.ppermute(v, AXES, [(i, i ^ mask) for i in range(devices)])  22.7 us
    ppermute x19, waiting for transfers between devices, swap(): return lax.ppermute(v, AXES, [(i, i ^ mask) for i in range(devices)])  21.9 us
    pallas_call x2, Pallas kernels, products(): pl.pallas_call(functools.partial(products_kernel, slots, away), out_shape...  11.2 us
    pallas_call x16, Pallas kernels, call(): pl.pallas_call(functools.partial(in_order, kernel, len(args) + len(smem))...  9.61 us
    unnamed x4, local copies, waits for them, and re-layouts  1.59 us
  transfers between devices with their start and end apart: 19, of which 9 were waited for; matrix products, arithmetic and copies ran while one was open for 0% of the time, Pallas kernels for 18%

profile of v10, /device:TPU:0, one launch (start us, length us, event | category | flops | bytes accessed | tf_op | source)
XLA Modules:
  0.0 68.6 jit_solution(2106081323504937058)
XLA Ops:
  0.6 0.8 %fusion.2.code_ref = s32[128]{0:T(128)S(1)} fusion(s32[128,2]{0,1:T(2,128)} %param.5, s32[]{:T(128)S(6)} %mul.21, s32[]{:T(128)S(6)} %add.32), kind=kLoop, calls=%fused_computation.31 | loop fusion | flops 7168 | bytes 1544 | tf_op jit(solution)/shard_map/or | solution.py:152
  1.4 1.6 %copy-done = f32[2048,256]{1,0:T(8,128)S(1)} copy-done((f32[2048,256]{1,0:T(8,128)S(1)}, f32[2048,256]{1,0:T(8,128)}, u32[]{:S(2)}) %copy-start) | copy-done | bytes 2097176
  3.0 6.1 %products_away.1 = (f32[17,128,256]{2,1,0:T(8,128)S(1)}, f32[8,128]{1,0:T(8,128)}, f32[128,128,128]{2,1,0:T(8,128)S(1)}, bf16[2048,256]{1,0:T(8,128)(2,1)S(1)}, bf16[2048,256]{1,0:T(8,128)(2,1)S(1)}) custom-call(s32[128]{0:T(128)S(1)} %fusion.2.code_ref, f32[128,128,128]{2,1,0:T(8,128)} %refs_0_.1, f32[2048,256]{1,0:T(8,128)S(1)} %copy-done), custom_call_target="tpu_custom_call" | custom-call | flops 8000000000 | bytes 5242880 | tf_op jit(solution)/shard_map/products_away/pallas_call | solution.py:136
  9.1 1.3 %collective-permute-start = (f32[17,128,256]{2,1,0:T(8,128)S(1)}, f32[17,128,256]{2,1,0:T(8,128)S(1)}, u32[]{:S(2)}, u32[]{:S(2)}) collective-permute-start(f32[17,128,256]{2,1,0:T(8,128)S(1)} %get-tuple-element.62.refs_0_), channel_id=1, source_target_pairs={{0,4},{1,5},{2,6},{3,7},{4,0},{5,1},{6,2},{7,3},{8,12},{9,13},{10,... | collective-permute-start | bytes 6684680 | tf_op jit(solution)/shard_map/ppermute | solution.py:349
  10.4 5.1 %products_here.1 = (f32[17,128,256]{2,1,0:T(8,128)S(1)}, f32[8,128]{1,0:T(8,128)S(1)}) custom-call(s32[128]{0:T(128)S(1)} %fusion.2.code_ref, f32[128,128,128]{2,1,0:T(8,128)S(1)} %get-tuple-element.57.refs_0_, bf16[2048,256]{1,0:T(8,128)(2,1)S(1)} %get-tuple-element.58.refs_1_, bf16[2048,256]{1,0:T(8,128)(2,1)S(1)} %get-tuple-element.59.refs_2_), custom_call_target="tpu_custom_call" | custom-call | flops 8000000000 | bytes 5242880 | tf_op jit(solution)/shard_map/products_here/pallas_call | solution.py:136
  15.5 0.3 spread.3
  15.8 2.1 %collective-permute-start.3 = (f32[8,64,256]{2,1,0:T(8,128)S(1)}, f32[8,64,256]{2,1,0:T(8,128)S(1)}, u32[]{:S(2)}, u32[]{:S(2)}) collective-permute-start(f32[8,64,256]{2,1,0:T(8,128)S(1)} %get-tuple-element.70), channel_id=1, source_target_pairs={{0,1},{1,0},{2,3},{3,2},{4,5},{5,4},{6,7},{7,6},{8,9},{9,8},{10,11... | collective-permute-start | bytes 1572872 | tf_op jit(solution)/shard_map/ppermute | solution.py:349
  17.9 2.3 %collective-permute-start.4 = (f32[8,64,256]{2,1,0:T(8,128)S(1)}, f32[8,64,256]{2,1,0:T(8,128)S(1)}, u32[]{:S(2)}, u32[]{:S(2)}) collective-permute-start(f32[8,64,256]{2,1,0:T(8,128)S(1)} %get-tuple-element.71), channel_id=1, source_target_pairs={{0,2},{1,3},{2,0},{3,1},{4,6},{5,7},{6,4},{7,5},{8,10},{9,11},{10,... | collective-permute-start | bytes 1572872 | tf_op jit(solution)/shard_map/ppermute | solution.py:349
  20.2 0.9 %pick.1 = (f32[8,128]{1,0:T(8,128)S(1)}, f32[64,256]{1,0:T(8,128)S(1)}) custom-call(f32[8,128]{1,0:T(8,128)S(1)} %get-tuple-element.63._token, f32[17,128,256]{2,1,0:T(8,128)S(1)} %get-tuple-element.62.refs_0_, f32[17,128,256]{2,1,0:T(8,128)S(1)} %get-tuple-element.61.refs_0_.refs_1_, s32[64]{0:T(128)S(1)} %fusion.5.refs_2_), custom_call_target="tpu_custom_call" | custom-call | flops 1 | bytes 1 | tf_op jit(solution)/shard_map/pick/pallas_call | solution.py:53
  21.2 1.2 %collective-permute-done.1.refs_1_ = f32[64,256]{1,0:T(8,128)S(1)} collective-permute-done((f32[64,256]{1,0:T(8,128)S(1)}, f32[64,256]{1,0:T(8,128)S(1)}, u32[]{:S(2)}, u32[]{:S(2)}) %collective-permute-start.1) | collective-permute-done | bytes 65568 | tf_op jit(solution)/shard_map/ppermute | solution.py:349
  22.5 1.2 %collective-permute-start.2 = (f32[64,256]{1,0:T(8,128)S(1)}, f32[64,256]{1,0:T(8,128)S(1)}, u32[]{:S(2)}, u32[]{:S(2)}) collective-permute-start(f32[64,256]{1,0:T(8,128)S(1)} %get-tuple-element.67.refs_0_), channel_id=1, source_target_pairs={{0,8},{1,9},{2,10},{3,11},{4,12},{5,13},{6,14},{7,15},{8,0},{9,1},... | collective-permute-start | bytes 196616 | tf_op jit(solution)/shard_map/ppermute | solution.py:349
  23.7 3.1 %collective-permute-done.2.refs_1_ = f32[64,256]{1,0:T(8,128)S(1)} collective-permute-done((f32[64,256]{1,0:T(8,128)S(1)}, f32[64,256]{1,0:T(8,128)S(1)}, u32[]{:S(2)}, u32[]{:S(2)}) %collective-permute-start.2) | collective-permute-done | bytes 65568 | tf_op jit(solution)/shard_map/ppermute | solution.py:349
  26.8 1.9 %collective-permute-start.5 = (f32[64,256]{1,0:T(8,128)S(1)}, f32[64,256]{1,0:T(8,128)S(1)}, u32[]{:S(2)}, u32[]{:S(2)}) collective-permute-start(f32[64,256]{1,0:T(8,128)S(1)} %get-tuple-element.72.refs_3_), channel_id=1, source_target_pairs={{0,16},{1,17},{2,18},{3,19},{4,20},{5,21},{6,22},{7,23},{8,24},{9,... | collective-permute-start | bytes 196616 | tf_op jit(solution)/shard_map/ppermute | solution.py:349
  28.7 4.0 %collective-permute-done.5.refs_4_ = f32[64,256]{1,0:T(8,128)S(1)} collective-permute-done((f32[64,256]{1,0:T(8,128)S(1)}, f32[64,256]{1,0:T(8,128)S(1)}, u32[]{:S(2)}, u32[]{:S(2)}) %collective-permute-start.5) | collective-permute-done | bytes 65568 | tf_op jit(solution)/shard_map/ppermute | solution.py:349
  33.6 1.7 %collective-permute-start.8 = (f32[4,64,256]{2,1,0:T(8,128)S(1)}, f32[4,64,256]{2,1,0:T(8,128)S(1)}, u32[]{:S(2)}, u32[]{:S(2)}) collective-permute-start(f32[4,64,256]{2,1,0:T(8,128)S(1)} %get-tuple-element.82), channel_id=1, source_target_pairs={{0,1},{1,0},{2,3},{3,2},{4,5},{5,4},{6,7},{7,6},{8,9},{9,8},{10,11... | collective-permute-start | bytes 786440 | tf_op jit(solution)/shard_map/ppermute | solution.py:349
  35.3 1.9 %collective-permute-start.9 = (f32[4,64,256]{2,1,0:T(8,128)S(1)}, f32[4,64,256]{2,1,0:T(8,128)S(1)}, u32[]{:S(2)}, u32[]{:S(2)}) collective-permute-start(f32[4,64,256]{2,1,0:T(8,128)S(1)} %get-tuple-element.83), channel_id=1, source_target_pairs={{0,2},{1,3},{2,0},{3,1},{4,6},{5,7},{6,4},{7,5},{8,10},{9,11},{10,... | collective-permute-start | bytes 786440 | tf_op jit(solution)/shard_map/ppermute | solution.py:349
  37.4 5.0 %collective-permute-done.7.refs_2_ = f32[4,64,256]{2,1,0:T(8,128)S(1)} collective-permute-done((f32[4,64,256]{2,1,0:T(8,128)S(1)}, f32[4,64,256]{2,1,0:T(8,128)S(1)}, u32[]{:S(2)}, u32[]{:S(2)}) %collective-permute-start.7) | collective-permute-done | bytes 262176 | tf_op jit(solution)/shard_map/ppermute | solution.py:349
  42.4 1.2 %collective-permute-done.6.refs_1_ = f32[5,64,256]{2,1,0:T(8,128)S(1)} collective-permute-done((f32[5,64,256]{2,1,0:T(8,128)S(1)}, f32[5,64,256]{2,1,0:T(8,128)S(1)}, u32[]{:S(2)}, u32[]{:S(2)}) %collective-permute-start.6) | collective-permute-done | bytes 327712 | tf_op jit(solution)/shard_map/ppermute | solution.py:349
  43.7 0.6 collective-permute-start.10
  44.3 1.2 %collective-permute-start.11 = (f32[4,64,256]{2,1,0:T(8,128)S(1)}, f32[4,64,256]{2,1,0:T(8,128)S(1)}, u32[]{:S(2)}, u32[]{:S(2)}) collective-permute-start(f32[4,64,256]{2,1,0:T(8,128)S(1)} %get-tuple-element.90), channel_id=1, source_target_pairs={{0,1},{1,0},{2,3},{3,2},{4,5},{5,4},{6,7},{7,6},{8,9},{9,8},{10,11... | collective-permute-start | bytes 786440 | tf_op jit(solution)/shard_map/ppermute | solution.py:349
  45.7 3.4 %collective-permute-done.8.refs_1_ = f32[4,64,256]{2,1,0:T(8,128)S(1)} collective-permute-done((f32[4,64,256]{2,1,0:T(8,128)S(1)}, f32[4,64,256]{2,1,0:T(8,128)S(1)}, u32[]{:S(2)}, u32[]{:S(2)}) %collective-permute-start.8) | collective-permute-done | bytes 262176 | tf_op jit(solution)/shard_map/ppermute | solution.py:349
  49.2 2.3 %collective-permute-done.10.refs_1_ = f32[4,64,256]{2,1,0:T(8,128)S(1)} collective-permute-done((f32[4,64,256]{2,1,0:T(8,128)S(1)}, f32[4,64,256]{2,1,0:T(8,128)S(1)}, u32[]{:S(2)}, u32[]{:S(2)}) %collective-permute-start.10) | collective-permute-done | bytes 262176 | tf_op jit(solution)/shard_map/ppermute | solution.py:349
  51.6 2.9 %collective-permute-start.17 = (f32[4,64,256]{2,1,0:T(8,128)S(1)}, f32[4,64,256]{2,1,0:T(8,128)S(1)}, u32[]{:S(2)}, u32[]{:S(2)}) collective-permute-start(f32[4,64,256]{2,1,0:T(8,128)S(1)} %get-tuple-element.103), channel_id=1, source_target_pairs={{0,16},{1,17},{2,18},{3,19},{4,20},{5,21},{6,22},{7,23},{8,24},{9,... | collective-permute-start | bytes 786440 | tf_op jit(solution)/shard_map/ppermute | solution.py:349
  54.6 0.4 collective-permute-start.13
  55.1 1.7 %collective-permute-start.15 = (f32[2,64,256]{2,1,0:T(8,128)S(1)}, f32[2,64,256]{2,1,0:T(8,128)S(1)}, u32[]{:S(2)}, u32[]{:S(2)}) collective-permute-start(f32[2,64,256]{2,1,0:T(8,128)S(1)} %get-tuple-element.101), channel_id=1, source_target_pairs={{0,1},{1,0},{2,3},{3,2},{4,5},{5,4},{6,7},{7,6},{8,9},{9,8},{10,11... | collective-permute-start | bytes 393224 | tf_op jit(solution)/shard_map/ppermute | solution.py:349
  56.8 1.9 %collective-permute-start.16 = (f32[2,64,256]{2,1,0:T(8,128)S(1)}, f32[2,64,256]{2,1,0:T(8,128)S(1)}, u32[]{:S(2)}, u32[]{:S(2)}) collective-permute-start(f32[2,64,256]{2,1,0:T(8,128)S(1)} %get-tuple-element.102), channel_id=1, source_target_pairs={{0,2},{1,3},{2,0},{3,1},{4,6},{5,7},{6,4},{7,5},{8,10},{9,11},{10,... | collective-permute-start | bytes 393224 | tf_op jit(solution)/shard_map/ppermute | solution.py:349
  58.7 0.9 %collective-permute-done.13.refs_1_ = f32[2,64,256]{2,1,0:T(8,128)S(1)} collective-permute-done((f32[2,64,256]{2,1,0:T(8,128)S(1)}, f32[2,64,256]{2,1,0:T(8,128)S(1)}, u32[]{:S(2)}, u32[]{:S(2)}) %collective-permute-start.13) | collective-permute-done | bytes 131104 | tf_op jit(solution)/shard_map/ppermute | solution.py:349
  59.6 0.6 collective-permute-done.14.refs_2_
  60.2 0.6 collective-permute-start.18
  60.9 3.0 %gram.1 = (f32[8,128]{1,0:T(8,128)S(1)}, f32[64,64]{1,0:T(8,128)S(1)}) custom-call(f32[8,128]{1,0:T(8,128)S(1)} %get-tuple-element.97._token, f32[64,256]{1,0:T(8,128)S(1)} %get-tuple-element.98.refs_0_.refs_2_), custom_call_target="tpu_custom_call" | custom-call | flops 1 | bytes 1 | tf_op jit(solution)/shard_map/gram/pallas_call | solution.py:53
  63.9 3.0 %solver.1 = (f32[8,128]{1,0:T(8,128)S(1)}, f32[256,64]{1,0:T(8,128)S(1)}) custom-call(f32[8,128]{1,0:T(8,128)S(1)} %get-tuple-element.104._token, f32[64,256]{1,0:T(8,128)S(1)} %get-tuple-element.98.refs_0_.refs_2_, f32[64,64]{1,0:T(8,128)S(1)} %get-tuple-element.105.refs_1_), custom_call_target="tpu_custom_call" | custom-call | flops 4000000000 | bytes 1 | tf_op jit(solution)/shard_map/solver/pallas_call | solution.py:53
  66.9 1.7 %finish.1 = (f32[8,128]{1,0:T(8,128)}, f32[64,256]{1,0:T(8,128)}, f32[256,256]{1,0:T(8,128)}) custom-call(f32[8,128]{1,0:T(8,128)S(1)} %get-tuple-element.106._token, f32[4,64,256]{2,1,0:T(8,128)S(1)} %get-tuple-element.107.refs_0_, f32[4,64,256]{2,1,0:T(8,128)S(1)} %collective-permute-done.18.refs_1_, f32[64,256]{1,0:T(8,128)S(1)} %get-tuple-element.98.refs_0_.refs_2_, ...), custom_call_target="tpu_custom_call" | custom-call | flops 1 | bytes 1 | tf_op jit(solution)/shard_map/finish/pallas_call | solution.py:53
  (30 shorter events, 1.8 us)
Async XLA Ops:
  1.4 1.6 %copy-start = (f32[2048,256]{1,0:T(8,128)S(1)}, f32[2048,256]{1,0:T(8,128)}, u32[]{:S(2)}) copy-start(f32[2048,256]{1,0:T(8,128)} %refs_1_.1) | copy-start | bytes 6291460
  9.1 6.4 %collective-permute-start = (f32[17,128,256]{2,1,0:T(8,128)S(1)}, f32[17,128,256]{2,1,0:T(8,128)S(1)}, u32[]{:S(2)}, u32[]{:S(2)}) collective-permute-start(f32[17,128,256]{2,1,0:T(8,128)S(1)} %get-tuple-element.62.refs_0_), channel_id=1, source_target_pairs={{0,4},{1,5},{2,6},{3,7},{4,0},{5,1},{6,2},{7,3},{8,12},{9,13},{10,... | collective-permute-start | bytes 6684680 | tf_op jit(solution)/shard_map/ppermute | solution.py:349
  15.5 4.7 %copy-start.1 = (s32[64]{0:T(128)S(1)}, s32[64]{0:T(128)}, u32[]{:S(2)}) copy-start(s32[64]{0:T(128)} %param.7) | copy-start | bytes 772
  15.8 16.9 %collective-permute-start.3 = (f32[8,64,256]{2,1,0:T(8,128)S(1)}, f32[8,64,256]{2,1,0:T(8,128)S(1)}, u32[]{:S(2)}, u32[]{:S(2)}) collective-permute-start(f32[8,64,256]{2,1,0:T(8,128)S(1)} %get-tuple-element.70), channel_id=1, source_target_pairs={{0,1},{1,0},{2,3},{3,2},{4,5},{5,4},{6,7},{7,6},{8,9},{9,8},{10,11... | collective-permute-start | bytes 1572872 | tf_op jit(solution)/shard_map/ppermute | solution.py:349
  17.9 14.9 %collective-permute-start.4 = (f32[8,64,256]{2,1,0:T(8,128)S(1)}, f32[8,64,256]{2,1,0:T(8,128)S(1)}, u32[]{:S(2)}, u32[]{:S(2)}) collective-permute-start(f32[8,64,256]{2,1,0:T(8,128)S(1)} %get-tuple-element.71), channel_id=1, source_target_pairs={{0,2},{1,3},{2,0},{3,1},{4,6},{5,7},{6,4},{7,5},{8,10},{9,11},{10,... | collective-permute-start | bytes 1572872 | tf_op jit(solution)/shard_map/ppermute | solution.py:349
  21.2 1.3 %collective-permute-start.1 = (f32[64,256]{1,0:T(8,128)S(1)}, f32[64,256]{1,0:T(8,128)S(1)}, u32[]{:S(2)}, u32[]{:S(2)}) collective-permute-start(f32[64,256]{1,0:T(8,128)S(1)} %get-tuple-element.65.refs_0_), channel_id=1, source_target_pairs={{0,4},{1,5},{2,6},{3,7},{4,0},{5,1},{6,2},{7,3},{8,12},{9,13},{10,... | collective-permute-start | bytes 196616 | tf_op jit(solution)/shard_map/ppermute | solution.py:349
  22.5 4.3 %collective-permute-start.2 = (f32[64,256]{1,0:T(8,128)S(1)}, f32[64,256]{1,0:T(8,128)S(1)}, u32[]{:S(2)}, u32[]{:S(2)}) collective-permute-start(f32[64,256]{1,0:T(8,128)S(1)} %get-tuple-element.67.refs_0_), channel_id=1, source_target_pairs={{0,8},{1,9},{2,10},{3,11},{4,12},{5,13},{6,14},{7,15},{8,0},{9,1},... | collective-permute-start | bytes 196616 | tf_op jit(solution)/shard_map/ppermute | solution.py:349
  26.8 5.9 %collective-permute-start.5 = (f32[64,256]{1,0:T(8,128)S(1)}, f32[64,256]{1,0:T(8,128)S(1)}, u32[]{:S(2)}, u32[]{:S(2)}) collective-permute-start(f32[64,256]{1,0:T(8,128)S(1)} %get-tuple-element.72.refs_3_), channel_id=1, source_target_pairs={{0,16},{1,17},{2,18},{3,19},{4,20},{5,21},{6,22},{7,23},{8,24},{9,... | collective-permute-start | bytes 196616 | tf_op jit(solution)/shard_map/ppermute | solution.py:349
  32.9 10.7 %collective-permute-start.6 = (f32[5,64,256]{2,1,0:T(8,128)S(1)}, f32[5,64,256]{2,1,0:T(8,128)S(1)}, u32[]{:S(2)}, u32[]{:S(2)}) collective-permute-start(f32[5,64,256]{2,1,0:T(8,128)S(1)} %get-tuple-element.77), channel_id=1, source_target_pairs={{0,1},{1,0},{2,3},{3,2},{4,5},{5,4},{6,7},{7,6},{8,9},{9,8},{10,11... | collective-permute-start | bytes 983048 | tf_op jit(solution)/shard_map/ppermute | solution.py:349
  33.2 9.2 %collective-permute-start.7 = (f32[4,64,256]{2,1,0:T(8,128)S(1)}, f32[4,64,256]{2,1,0:T(8,128)S(1)}, u32[]{:S(2)}, u32[]{:S(2)}) collective-permute-start(f32[4,64,256]{2,1,0:T(8,128)S(1)} %get-tuple-element.78), channel_id=1, source_target_pairs={{0,2},{1,3},{2,0},{3,1},{4,6},{5,7},{6,4},{7,5},{8,10},{9,11},{10,... | collective-permute-start | bytes 786440 | tf_op jit(solution)/shard_map/ppermute | solution.py:349
  33.6 15.6 %collective-permute-start.8 = (f32[4,64,256]{2,1,0:T(8,128)S(1)}, f32[4,64,256]{2,1,0:T(8,128)S(1)}, u32[]{:S(2)}, u32[]{:S(2)}) collective-permute-start(f32[4,64,256]{2,1,0:T(8,128)S(1)} %get-tuple-element.82), channel_id=1, source_target_pairs={{0,1},{1,0},{2,3},{3,2},{4,5},{5,4},{6,7},{7,6},{8,9},{9,8},{10,11... | collective-permute-start | bytes 786440 | tf_op jit(solution)/shard_map/ppermute | solution.py:349
  35.3 13.8 %collective-permute-start.9 = (f32[4,64,256]{2,1,0:T(8,128)S(1)}, f32[4,64,256]{2,1,0:T(8,128)S(1)}, u32[]{:S(2)}, u32[]{:S(2)}) collective-permute-start(f32[4,64,256]{2,1,0:T(8,128)S(1)} %get-tuple-element.83), channel_id=1, source_target_pairs={{0,2},{1,3},{2,0},{3,1},{4,6},{5,7},{6,4},{7,5},{8,10},{9,11},{10,... | collective-permute-start | bytes 786440 | tf_op jit(solution)/shard_map/ppermute | solution.py:349
  43.7 7.9 %collective-permute-start.10 = (f32[4,64,256]{2,1,0:T(8,128)S(1)}, f32[4,64,256]{2,1,0:T(8,128)S(1)}, u32[]{:S(2)}, u32[]{:S(2)}) collective-permute-start(f32[4,64,256]{2,1,0:T(8,128)S(1)} %get-tuple-element.87), channel_id=1, source_target_pairs={{0,8},{1,9},{2,10},{3,11},{4,12},{5,13},{6,14},{7,15},{8,0},{9,1},... | collective-permute-start | bytes 786440 | tf_op jit(solution)/shard_map/ppermute | solution.py:349
  44.3 10.8 %collective-permute-start.11 = (f32[4,64,256]{2,1,0:T(8,128)S(1)}, f32[4,64,256]{2,1,0:T(8,128)S(1)}, u32[]{:S(2)}, u32[]{:S(2)}) collective-permute-start(f32[4,64,256]{2,1,0:T(8,128)S(1)} %get-tuple-element.90), channel_id=1, source_target_pairs={{0,1},{1,0},{2,3},{3,2},{4,5},{5,4},{6,7},{7,6},{8,9},{9,8},{10,11... | collective-permute-start | bytes 786440 | tf_op jit(solution)/shard_map/ppermute | solution.py:349
  45.5 9.6 %collective-permute-start.12 = (f32[4,64,256]{2,1,0:T(8,128)S(1)}, f32[4,64,256]{2,1,0:T(8,128)S(1)}, u32[]{:S(2)}, u32[]{:S(2)}) collective-permute-start(f32[4,64,256]{2,1,0:T(8,128)S(1)} %get-tuple-element.91), channel_id=1, source_target_pairs={{0,2},{1,3},{2,0},{3,1},{4,6},{5,7},{6,4},{7,5},{8,10},{9,11},{10,... | collective-permute-start | bytes 786440 | tf_op jit(solution)/shard_map/ppermute | solution.py:349
  51.6 12.3 %collective-permute-start.17 = (f32[4,64,256]{2,1,0:T(8,128)S(1)}, f32[4,64,256]{2,1,0:T(8,128)S(1)}, u32[]{:S(2)}, u32[]{:S(2)}) collective-permute-start(f32[4,64,256]{2,1,0:T(8,128)S(1)} %get-tuple-element.103), channel_id=1, source_target_pairs={{0,16},{1,17},{2,18},{3,19},{4,20},{5,21},{6,22},{7,23},{8,24},{9,... | collective-permute-start | bytes 786440 | tf_op jit(solution)/shard_map/ppermute | solution.py:349
  54.5 5.7 %collective-permute-start.14 = (f32[3,64,256]{2,1,0:T(8,128)S(1)}, f32[3,64,256]{2,1,0:T(8,128)S(1)}, u32[]{:S(2)}, u32[]{:S(2)}) collective-permute-start(f32[3,64,256]{2,1,0:T(8,128)S(1)} %get-tuple-element.95), channel_id=1, source_target_pairs={{0,2},{1,3},{2,0},{3,1},{4,6},{5,7},{6,4},{7,5},{8,10},{9,11},{10,... | collective-permute-start | bytes 589832 | tf_op jit(solution)/shard_map/ppermute | solution.py:349
  54.6 5.0 %collective-permute-start.13 = (f32[2,64,256]{2,1,0:T(8,128)S(1)}, f32[2,64,256]{2,1,0:T(8,128)S(1)}, u32[]{:S(2)}, u32[]{:S(2)}) collective-permute-start(f32[2,64,256]{2,1,0:T(8,128)S(1)} %get-tuple-element.94), channel_id=1, source_target_pairs={{0,1},{1,0},{2,3},{3,2},{4,5},{5,4},{6,7},{7,6},{8,9},{9,8},{10,11... | collective-permute-start | bytes 393224 | tf_op jit(solution)/shard_map/ppermute | solution.py:349
  55.1 8.7 %collective-permute-start.15 = (f32[2,64,256]{2,1,0:T(8,128)S(1)}, f32[2,64,256]{2,1,0:T(8,128)S(1)}, u32[]{:S(2)}, u32[]{:S(2)}) collective-permute-start(f32[2,64,256]{2,1,0:T(8,128)S(1)} %get-tuple-element.101), channel_id=1, source_target_pairs={{0,1},{1,0},{2,3},{3,2},{4,5},{5,4},{6,7},{7,6},{8,9},{9,8},{10,11... | collective-permute-start | bytes 393224 | tf_op jit(solution)/shard_map/ppermute | solution.py:349
  56.8 7.1 %collective-permute-start.16 = (f32[2,64,256]{2,1,0:T(8,128)S(1)}, f32[2,64,256]{2,1,0:T(8,128)S(1)}, u32[]{:S(2)}, u32[]{:S(2)}) collective-permute-start(f32[2,64,256]{2,1,0:T(8,128)S(1)} %get-tuple-element.102), channel_id=1, source_target_pairs={{0,2},{1,3},{2,0},{3,1},{4,6},{5,7},{6,4},{7,5},{8,10},{9,11},{10,... | collective-permute-start | bytes 393224 | tf_op jit(solution)/shard_map/ppermute | solution.py:349
  60.2 6.7 %collective-permute-start.18 = (f32[4,64,256]{2,1,0:T(8,128)S(1)}, f32[4,64,256]{2,1,0:T(8,128)S(1)}, u32[]{:S(2)}, u32[]{:S(2)}) collective-permute-start(f32[4,64,256]{2,1,0:T(8,128)S(1)} %get-tuple-element.108), channel_id=1, source_target_pairs={{0,8},{1,9},{2,10},{3,11},{4,12},{5,13},{6,14},{7,15},{8,0},{9,1},... | collective-permute-start | bytes 786440 | tf_op jit(solution)/shard_map/ppermute | solution.py:349
